TPU v7x, 32 devices: a whole 2x2x4 slice. The times are simulated.
32 devices in a mesh: groups: 2 (over y), seq: 16 (over z, x, core).
Axes of the slice: x: 2, y: 2, z: 4, core: 2. Of those that a mesh axis runs over, the one named last changes fastest.
Arguments:
- inputs: bfloat16 [4096, 2048], P(('groups', 'seq')), parts along dimension 0, may hold values from -6 to 6
- gate_in: bfloat16 [4096, 2048], P(('groups', 'seq')), parts along dimension 0, may hold values from -6 to 6
- value_weight: bfloat16 [2048, 2048], P('seq'), may hold values from -0.125 to 0.125
- short_taps: float32 [3, 2048], replicated, may hold values from -3 to 3
- filter_taps: bfloat16 [2048, 2048], P('seq'), may hold values from -0.125 to 0.125
- skip_scale: float32 [2048], replicated, may hold values from -5 to 5
- output_weight: bfloat16 [2048, 2048], P('seq'), may hold values from -0.125 to 0.125
Outputs:
- layer_out: bfloat16 [4096, 2048], P(('groups', 'seq')), parts along dimension 0
There are 2 independent parts, one for each index of `groups`. A program takes and returns all parts, laid end to end along the dimension named above; an argument that names none is the same for every part. Nothing has to cross between parts.
All inputs are finite; a program needn't handle non-finite values.
Results may differ from a plain program's by a relative error of at most 0.0095.
Values may be sent and summed in bfloat16 or wider, within the bound.
No kernel may reach another device: no remote copies, remote signals or barrier semaphores. Data moves between devices by JAX's collectives and lax.ppermute only.
A program may use at most 128 MiB of HBM per device.

v0:
```python
import math

import jax
import jax.numpy as jnp
from jax import lax
from jax.sharding import PartitionSpec as P


def passed_along(block, axis, distance):
    devices = range(lax.axis_size(axis))
    route = [(i - distance, i) for i in devices if i - distance in devices]
    return lax.ppermute(block, axis, route)


def turning(index, count):
    return jnp.float32(2.0 * math.pi) * index.astype(jnp.float32) / jnp.float32(count)


def wide_tables(count):
    grid = jnp.arange(count, dtype=jnp.int32)
    angle = turning(grid[:, None] * grid[None, :] % count, count)
    return (jnp.cos(angle), jnp.sin(angle))


def tables(count):
    cos_table, sin_table = wide_tables(count)
    return (cos_table.astype(jnp.bfloat16), sin_table.astype(jnp.bfloat16))


def matmul(left, right):
    return jnp.dot(left, right, preferred_element_type=jnp.float32)


def first_section(columns, cos_wide, sin_wide, offsets, length):
    data = columns.astype(jnp.float32)
    first_re = jnp.einsum("fb,mbc->fmc", cos_wide, data, precision=lax.Precision.HIGHEST)
    first_im = -jnp.einsum("fb,mbc->fmc", sin_wide, data, precision=lax.Precision.HIGHEST)
    freq_index = jnp.arange(cos_wide.shape[0], dtype=jnp.int32)
    angle = turning(freq_index[:, None] * offsets[None, :], length)[:, :, None]
    cos_turn = jnp.cos(angle)
    sin_turn = jnp.sin(angle)
    partial_re = (first_re * cos_turn + first_im * sin_turn).astype(jnp.bfloat16)
    partial_im = (first_im * cos_turn - first_re * sin_turn).astype(jnp.bfloat16)
    return (partial_re, partial_im)


def local_section(gathered_re, gathered_im, cos_local, sin_local):
    spec_re = (
        jnp.einsum("km,jmc->jkc", cos_local, gathered_re, preferred_element_type=jnp.float32)
        + jnp.einsum("km,jmc->jkc", sin_local, gathered_im, preferred_element_type=jnp.float32)
    ).astype(jnp.bfloat16)
    spec_im = (
        jnp.einsum("km,jmc->jkc", cos_local, gathered_im, preferred_element_type=jnp.float32)
        - jnp.einsum("km,jmc->jkc", sin_local, gathered_re, preferred_element_type=jnp.float32)
    ).astype(jnp.bfloat16)
    return (spec_re.astype(jnp.float32), spec_im.astype(jnp.float32))


def local(inputs, gate_in, value_weight, short_taps, filter_taps, skip_scale, output_weight):
    row_count = inputs.shape[0]
    channels = value_weight.shape[1]
    blocks = lax.axis_size("seq")
    per_block = row_count // blocks
    length = 2 * row_count * blocks
    device = lax.axis_index("seq")
    columns = inputs
    projected = matmul(columns, lax.all_gather(value_weight, "seq", axis=0, tiled=True)).astype(
        jnp.bfloat16
    )
    earlier = passed_along(projected[row_count - 2 :], "seq", 1)
    extended = jnp.concatenate([earlier, projected], 0)
    value = (
        short_taps[0] * extended[2:]
        + short_taps[1] * extended[1:-1]
        + short_taps[2] * extended[:-2]
    ).astype(jnp.bfloat16)
    cos_full, sin_full = wide_tables(2 * blocks)
    cos_wide = cos_full[:, :blocks]
    sin_wide = sin_full[:, :blocks]
    cos_narrow = cos_full[:blocks, :]
    sin_narrow = sin_full[:blocks, :]
    cos_local, sin_local = tables(row_count)
    offsets = device * per_block + jnp.arange(per_block, dtype=jnp.int32)

    def transform(signal):
        columns = lax.all_to_all(
            signal.reshape(row_count, 1, channels), "seq", split_axis=0, concat_axis=1, tiled=True
        )
        partial_re, partial_im = first_section(columns, cos_wide, sin_wide, offsets, length)
        gathered_re, gathered_im = (
            lax.all_to_all(partial_re, "seq", split_axis=0, concat_axis=1, tiled=True),
            lax.all_to_all(partial_im, "seq", split_axis=0, concat_axis=1, tiled=True),
        )
        return local_section(gathered_re, gathered_im, cos_local, sin_local)

    resp_re, resp_im = transform(filter_taps)
    value_re, value_im = transform(value)
    product_re = (value_re * resp_re - value_im * resp_im).astype(jnp.bfloat16)
    product_im = (value_re * resp_im + value_im * resp_re).astype(jnp.bfloat16)
    back_re = (
        jnp.einsum("mk,jkc->jmc", cos_local, product_re, preferred_element_type=jnp.float32)
        - jnp.einsum("mk,jkc->jmc", sin_local, product_im, preferred_element_type=jnp.float32)
    ) * (1.0 / row_count)
    back_im = (
        jnp.einsum("mk,jkc->jmc", cos_local, product_im, preferred_element_type=jnp.float32)
        + jnp.einsum("mk,jkc->jmc", sin_local, product_re, preferred_element_type=jnp.float32)
    ) * (1.0 / row_count)
    own_freq = 2 * device + jnp.arange(2, dtype=jnp.int32)
    own_angle = turning(
        own_freq[:, None] * jnp.arange(row_count, dtype=jnp.int32)[None, :], length
    )[:, :, None]
    own_cos = jnp.cos(own_angle)
    own_sin = jnp.sin(own_angle)
    inverse_re = (back_re * own_cos - back_im * own_sin).astype(jnp.bfloat16)
    inverse_im = (back_im * own_cos + back_re * own_sin).astype(jnp.bfloat16)
    spread_re, spread_im = (
        lax.all_to_all(inverse_re, "seq", split_axis=1, concat_axis=0, tiled=True),
        lax.all_to_all(inverse_im, "seq", split_axis=1, concat_axis=0, tiled=True),
    )
    spread_re32 = spread_re.astype(jnp.float32)
    spread_im32 = spread_im.astype(jnp.float32)
    conv_part = (
        jnp.einsum("bf,fmc->mbc", cos_narrow, spread_re32, precision=lax.Precision.HIGHEST)
        - jnp.einsum("bf,fmc->mbc", sin_narrow, spread_im32, precision=lax.Precision.HIGHEST)
    ) * (1.0 / (2 * blocks))
    conv = lax.all_to_all(
        conv_part.astype(jnp.bfloat16), "seq", split_axis=1, concat_axis=0, tiled=True
    ).reshape(row_count, channels)
    mixed = (
        gate_in.astype(jnp.float32)
        * (conv.astype(jnp.float32) + skip_scale * value.astype(jnp.float32))
    ).astype(jnp.bfloat16)
    result = matmul(mixed, lax.all_gather(output_weight, "seq", axis=0, tiled=True))
    return result.astype(jnp.bfloat16)


def solution(mesh):
    placed = (
        P(("groups", "seq"), None),
        P(("groups", "seq"), None),
        P("seq", None),
        P(),
        P("seq", None),
        P(),
        P("seq", None),
    )
    return jax.shard_map(
        local, mesh=mesh, in_specs=placed, out_specs=P(("groups", "seq"), None), check_vma=False
    )
```

profile of v0, /device:TPU:0, one launch (start us, length us, event | category | flops | bytes accessed | tf_op | source)
XLA Modules:
  0.0 411.7 jit_solution(11367074337710142915)
XLA Ops:
  7.8 2.0 reduce.1
  9.8 1.4 reshape.117
  11.2 7.4 %all-to-all-start.3 = ((bf16[16,2,8192]{2,1,0:T(2,128)(2,1)}), bf16[16,2,8192]{2,1,0:T(2,128)(2,1)S(1)}, u32[]{:S(2)}, u32[]{:S(2)}) async-start(bf16[16,2,8192]{2,1,0:T(2,128)(2,1)} %reshape.117), calls=%async_computation.3 | async-start | bytes 1048576 | tf_op jit(solution)/shard_map/all_to_all | solution.py:86
  18.6 77.7 %all-gather.3.cloned.1.call-done = bf16[2048,2048]{1,0:T(8,128)(2,1)} async-done(((bf16[128,2048]{1,0:T(8,128)(2,1)}), bf16[2048,2048]{1,0:T(8,128)(2,1)}) %all-gather.3.cloned.1.call-update) | async-done | bytes 8388624 | tf_op jit(solution)/shard_map/all_gather | solution.py:67
  96.3 4.6 %convolution_convert_fusion.1 = bf16[128,2048]{1,0:T(8,128)(2,1)S(1)} fusion(bf16[128,2048]{1,0:T(8,128)(2,1)S(1)} %copy-done, bf16[2048,2048]{1,0:T(8,128)(2,1)} %all-gather.3.cloned.1.call-done), kind=kOutput, calls=%fused_computation.19 | convolution fusion | flops 1074003968 | bytes 9437184 | tf_op jit(solution)/shard_map/dot_general | solution.py:31
  101.0 2.2 collective-permute-start
  105.4 1.3 reshape.119
  106.7 5.9 %all-to-all-start = ((bf16[16,2,8192]{2,1,0:T(2,128)(2,1)}), bf16[16,2,8192]{2,1,0:T(2,128)(2,1)}, u32[]{:S(2)}, u32[]{:S(2)}) async-start(bf16[16,2,8192]{2,1,0:T(2,128)(2,1)} %reshape.119), calls=%async_computation | async-start | bytes 1048576 | tf_op jit(solution)/shard_map/all_to_all | solution.py:86
  113.7 1.3 convolution_negate_fusion
  115.0 2.6 fusion.41
  117.6 9.6 %all-to-all-done = bf16[16,2,8192]{2,1,0:T(2,128)(2,1)} async-done(((bf16[16,2,8192]{2,1,0:T(2,128)(2,1)}), bf16[16,2,8192]{2,1,0:T(2,128)(2,1)}, u32[]{:S(2)}, u32[]{:S(2)}) %all-to-all-start) | async-done | bytes 524320 | tf_op jit(solution)/shard_map/all_to_all | solution.py:86
  127.1 3.5 reshape.120
  130.6 1.7 copy.164
  132.3 1.3 fusion.44
  133.6 4.0 add_convert_fusion.2
  137.6 1.6 copy.64
  139.2 4.0 all-to-all-start.1
  144.0 1.5 copy.67
  145.5 25.9 %all-to-all-done.1 = bf16[32,8,2048]{2,1,0:T(8,128)(2,1)S(1)} async-done(((bf16[32,8,2048]{2,1,0:T(8,128)(2,1)}), bf16[32,8,2048]{2,1,0:T(8,128)(2,1)S(1)}, u32[]{:S(2)}, u32[]{:S(2)}) %all-to-all-start.1) | async-done | bytes 1048608 | tf_op jit(solution)/shard_map/all_to_all | solution.py:91
  171.4 16.9 %all-to-all-start.2 = ((bf16[32,8,2048]{2,1,0:T(8,128)(2,1)}), bf16[32,8,2048]{2,1,0:T(8,128)(2,1)S(1)}, u32[]{:S(2)}, u32[]{:S(2)}) async-start(bf16[32,8,2048]{2,1,0:T(8,128)(2,1)} %copy.67), calls=%async_computation.2 | async-start | bytes 2097152 | tf_op jit(solution)/shard_map/all_to_all | solution.py:92
  188.3 2.8 copy.72
  191.0 35.2 %all-to-all-done.2 = bf16[32,8,2048]{2,1,0:T(8,128)(2,1)S(1)} async-done(((bf16[32,8,2048]{2,1,0:T(8,128)(2,1)}), bf16[32,8,2048]{2,1,0:T(8,128)(2,1)S(1)}, u32[]{:S(2)}, u32[]{:S(2)}) %all-to-all-start.2) | async-done | bytes 1048608 | tf_op jit(solution)/shard_map/all_to_all | solution.py:92
  226.3 17.0 %all-to-all-start.4 = ((bf16[32,8,2048]{2,1,0:T(8,128)(2,1)}), bf16[32,8,2048]{2,1,0:T(8,128)(2,1)}, u32[]{:S(2)}, u32[]{:S(2)}) async-start(bf16[32,8,2048]{2,1,0:T(8,128)(2,1)} %copy.72), calls=%async_computation.4 | async-start | bytes 2097152 | tf_op jit(solution)/shard_map/all_to_all | solution.py:91
  243.3 2.9 copy.75
  246.2 21.5 %all-to-all-done.4 = bf16[32,8,2048]{2,1,0:T(8,128)(2,1)} async-done(((bf16[32,8,2048]{2,1,0:T(8,128)(2,1)}), bf16[32,8,2048]{2,1,0:T(8,128)(2,1)}, u32[]{:S(2)}, u32[]{:S(2)}) %all-to-all-start.4) | async-done | bytes 1048608 | tf_op jit(solution)/shard_map/all_to_all | solution.py:91
  267.7 7.1 %all-to-all-start.5 = ((bf16[32,8,2048]{2,1,0:T(8,128)(2,1)}), bf16[32,8,2048]{2,1,0:T(8,128)(2,1)}, u32[]{:S(2)}, u32[]{:S(2)}) async-start(bf16[32,8,2048]{2,1,0:T(8,128)(2,1)} %copy.75), calls=%async_computation.5 | async-start | bytes 2097152 | tf_op jit(solution)/shard_map/all_to_all | solution.py:92
  274.9 2.0 fusion.27
  276.9 3.3 fusion.21
  280.2 2.1 fusion.23
  282.3 15.5 %all-to-all-done.5 = bf16[32,8,2048]{2,1,0:T(8,128)(2,1)} async-done(((bf16[32,8,2048]{2,1,0:T(8,128)(2,1)}), bf16[32,8,2048]{2,1,0:T(8,128)(2,1)}, u32[]{:S(2)}, u32[]{:S(2)}) %all-to-all-start.5) | async-done | bytes 1048608 | tf_op jit(solution)/shard_map/all_to_all | solution.py:92
  297.8 2.1 fusion.17
  301.5 2.1 fusion.1
  304.3 2.5 fusion.14
  308.8 1.1 fusion.12
  309.9 2.1 copy.82
  312.0 6.9 %all-to-all-start.6 = ((bf16[2,128,2048]{2,0,1:T(2,128)(2,1)}), bf16[2,128,2048]{2,0,1:T(2,128)(2,1)S(1)}, u32[]{:S(2)}, u32[]{:S(2)}) async-start(bf16[2,128,2048]{2,0,1:T(2,128)(2,1)} %copy.82), calls=%async_computation.6 | async-start | bytes 2097152 | tf_op jit(solution)/shard_map/all_to_all | solution.py:117
  318.9 2.1 copy.86
  320.9 20.9 %all-to-all-done.6 = bf16[2,128,2048]{2,0,1:T(2,128)(2,1)S(1)} async-done(((bf16[2,128,2048]{2,0,1:T(2,128)(2,1)}), bf16[2,128,2048]{2,0,1:T(2,128)(2,1)S(1)}, u32[]{:S(2)}, u32[]{:S(2)}) %all-to-all-start.6) | async-done | bytes 1048608 | tf_op jit(solution)/shard_map/all_to_all | solution.py:117
  341.8 6.9 %all-to-all-start.7 = ((bf16[2,128,2048]{2,0,1:T(2,128)(2,1)}), bf16[2,128,2048]{2,0,1:T(2,128)(2,1)S(1)}, u32[]{:S(2)}, u32[]{:S(2)}) async-start(bf16[2,128,2048]{2,0,1:T(2,128)(2,1)} %copy.86), calls=%async_computation.7 | async-start | bytes 2097152 | tf_op jit(solution)/shard_map/all_to_all | solution.py:118
  349.0 2.1 copy.84
  351.1 1.5 all_to_all.138
  352.6 19.0 %all-to-all-done.7 = bf16[2,128,2048]{2,0,1:T(2,128)(2,1)S(1)} async-done(((bf16[2,128,2048]{2,0,1:T(2,128)(2,1)}), bf16[2,128,2048]{2,0,1:T(2,128)(2,1)S(1)}, u32[]{:S(2)}, u32[]{:S(2)}) %all-to-all-start.7) | async-done | bytes 1048608 | tf_op jit(solution)/shard_map/all_to_all | solution.py:118
  372.0 2.1 copy.88
  374.1 1.5 all_to_all.142
  376.9 1.1 copy.90
  378.0 6.9 %all-to-all-start.8 = ((bf16[8,16,2048]{2,0,1:T(8,128)(2,1)}), bf16[8,16,2048]{2,0,1:T(8,128)(2,1)S(1)}, u32[]{:S(2)}, u32[]{:S(2)}) async-start(bf16[8,16,2048]{2,0,1:T(8,128)(2,1)} %copy.90), calls=%async_computation.8 | async-start | bytes 1048576 | tf_op jit(solution)/shard_map/all_to_all | solution.py:126
  384.9 14.4 %all-to-all-done.8 = bf16[8,16,2048]{2,0,1:T(8,128)(2,1)S(1)} async-done(((bf16[8,16,2048]{2,0,1:T(8,128)(2,1)}), bf16[8,16,2048]{2,0,1:T(8,128)(2,1)S(1)}, u32[]{:S(2)}, u32[]{:S(2)}) %all-to-all-start.8) | async-done | bytes 524320 | tf_op jit(solution)/shard_map/all_to_all | solution.py:126
  399.4 5.5 %convolution_convert_fusion = bf16[128,2048]{1,0:T(8,128)(2,1)} fusion(bf16[2048,2048]{1,0:T(8,128)(2,1)} %all-gather.5.cloned.1.call-done, bf16[128,2048]{1,0:T(8,128)(2,1)S(1)} %add_convert_fusion.3, bf16[128,2048]{1,0:T(8,128)(2,1)S(1)} %copy-done.7, bf16[8,16,2048]{2,0,1:T(8,128)(2,1)S(1)} %all-to-all-done.8, f32[2048]{0:T(1024)S(1)} %copy-done.8), kind=kOutput, calls=%fused_computation.18 | convolution fusion | flops 1075838976 | bytes 10493952 | tf_op jit(solution)/shard_map/dot_general | solution.py:31
  (49 shorter events, 11.7 us)
Async XLA Ops:
  6.5 89.8 %copy-start = (bf16[128,2048]{1,0:T(8,128)(2,1)S(1)}, bf16[128,2048]{1,0:T(8,128)(2,1)}, u32[]{:S(2)}) copy-start(bf16[128,2048]{1,0:T(8,128)(2,1)} %param.7) | copy-start | bytes 1572868
  6.5 12.0 %copy-start.9 = (f32[3,2048]{1,0:T(4,128)S(1)}, f32[3,2048]{1,0:T(4,128)}, u32[]{:S(2)}) copy-start(f32[3,2048]{1,0:T(4,128)} %param.10) | copy-start | bytes 73732
  6.5 89.8 %all-gather.3.cloned.1.call-start = ((), (), s32[]{:S(2)}) async-start(), calls=%async_computation.9 | async-start | bytes 8912896 | tf_op jit(solution)/shard_map/all_gather | solution.py:67
  11.2 95.5 %all-to-all-start.3 = ((bf16[16,2,8192]{2,1,0:T(2,128)(2,1)}), bf16[16,2,8192]{2,1,0:T(2,128)(2,1)S(1)}, u32[]{:S(2)}, u32[]{:S(2)}) async-start(bf16[16,2,8192]{2,1,0:T(2,128)(2,1)} %reshape.117), calls=%async_computation.3 | async-start | bytes 1048576 | tf_op jit(solution)/shard_map/all_to_all | solution.py:86
  101.0 3.0 collective-permute-start
  106.7 20.4 %all-to-all-start = ((bf16[16,2,8192]{2,1,0:T(2,128)(2,1)}), bf16[16,2,8192]{2,1,0:T(2,128)(2,1)}, u32[]{:S(2)}, u32[]{:S(2)}) async-start(bf16[16,2,8192]{2,1,0:T(2,128)(2,1)} %reshape.119), calls=%async_computation | async-start | bytes 1048576 | tf_op jit(solution)/shard_map/all_to_all | solution.py:86
  130.6 3.0 copy-start.2
  137.6 6.3 %copy-start.6 = (bf16[32,8,2048]{2,0,1:T(8,128)(2,1)S(1)}, bf16[32,8,2048]{2,0,1:T(8,128)(2,1)}, u32[]{:S(2)}) copy-start(bf16[32,8,2048]{2,0,1:T(8,128)(2,1)} %get-tuple-element.6) | copy-start | bytes 3145732
  139.2 32.2 %all-to-all-start.1 = ((bf16[32,8,2048]{2,1,0:T(8,128)(2,1)}), bf16[32,8,2048]{2,1,0:T(8,128)(2,1)S(1)}, u32[]{:S(2)}, u32[]{:S(2)}) async-start(bf16[32,8,2048]{2,1,0:T(8,128)(2,1)} %copy.64), calls=%async_computation.1 | async-start | bytes 2097152 | tf_op jit(solution)/shard_map/all_to_all | solution.py:91
  143.2 241.7 %all-gather.5.cloned.1.call-start = ((), (), s32[]{:S(2)}) async-start(), calls=%async_computation.10 | async-start | bytes 8912896 | tf_op jit(solution)/shard_map/all_gather | solution.py:133
  171.4 54.9 %all-to-all-start.2 = ((bf16[32,8,2048]{2,1,0:T(8,128)(2,1)}), bf16[32,8,2048]{2,1,0:T(8,128)(2,1)S(1)}, u32[]{:S(2)}, u32[]{:S(2)}) async-start(bf16[32,8,2048]{2,1,0:T(8,128)(2,1)} %copy.67), calls=%async_computation.2 | async-start | bytes 2097152 | tf_op jit(solution)/shard_map/all_to_all | solution.py:92
  226.3 41.4 %all-to-all-start.4 = ((bf16[32,8,2048]{2,1,0:T(8,128)(2,1)}), bf16[32,8,2048]{2,1,0:T(8,128)(2,1)}, u32[]{:S(2)}, u32[]{:S(2)}) async-start(bf16[32,8,2048]{2,1,0:T(8,128)(2,1)} %copy.72), calls=%async_computation.4 | async-start | bytes 2097152 | tf_op jit(solution)/shard_map/all_to_all | solution.py:91
  267.7 30.1 %all-to-all-start.5 = ((bf16[32,8,2048]{2,1,0:T(8,128)(2,1)}), bf16[32,8,2048]{2,1,0:T(8,128)(2,1)}, u32[]{:S(2)}, u32[]{:S(2)}) async-start(bf16[32,8,2048]{2,1,0:T(8,128)(2,1)} %copy.75), calls=%async_computation.5 | async-start | bytes 2097152 | tf_op jit(solution)/shard_map/all_to_all | solution.py:92
  297.8 2.1 copy-start.5
  299.9 1.6 copy-start.4
  301.5 2.1 copy-start.3
  312.0 29.8 %all-to-all-start.6 = ((bf16[2,128,2048]{2,0,1:T(2,128)(2,1)}), bf16[2,128,2048]{2,0,1:T(2,128)(2,1)S(1)}, u32[]{:S(2)}, u32[]{:S(2)}) async-start(bf16[2,128,2048]{2,0,1:T(2,128)(2,1)} %copy.82), calls=%async_computation.6 | async-start | bytes 2097152 | tf_op jit(solution)/shard_map/all_to_all | solution.py:117
  341.8 29.8 %all-to-all-start.7 = ((bf16[2,128,2048]{2,0,1:T(2,128)(2,1)}), bf16[2,128,2048]{2,0,1:T(2,128)(2,1)S(1)}, u32[]{:S(2)}, u32[]{:S(2)}) async-start(bf16[2,128,2048]{2,0,1:T(2,128)(2,1)} %copy.86), calls=%async_computation.7 | async-start | bytes 2097152 | tf_op jit(solution)/shard_map/all_to_all | solution.py:118
  376.2 23.2 %copy-start.7 = (bf16[128,2048]{1,0:T(8,128)(2,1)S(1)}, bf16[128,2048]{1,0:T(8,128)(2,1)}, u32[]{:S(2)}) copy-start(bf16[128,2048]{1,0:T(8,128)(2,1)} %param.8) | copy-start | bytes 1572868
  376.2 23.1 %copy-start.8 = (f32[2048]{0:T(1024)S(1)}, f32[2048]{0:T(1024)}, u32[]{:S(2)}) copy-start(f32[2048]{0:T(1024)} %param.12) | copy-start | bytes 24580
  378.0 21.3 %all-to-all-start.8 = ((bf16[8,16,2048]{2,0,1:T(8,128)(2,1)}), bf16[8,16,2048]{2,0,1:T(8,128)(2,1)S(1)}, u32[]{:S(2)}, u32[]{:S(2)}) async-start(bf16[8,16,2048]{2,0,1:T(8,128)(2,1)} %copy.90), calls=%async_computation.8 | async-start | bytes 1048576 | tf_op jit(solution)/shard_map/all_to_all | solution.py:126
  399.4 5.5 %copy-start.1 = (bf16[128,2048]{1,0:T(8,128)(2,1)S(1)}, bf16[128,2048]{1,0:T(8,128)(2,1)}, u32[]{:S(2)}) copy-start(bf16[128,2048]{1,0:T(8,128)(2,1)} %param.7) | copy-start | bytes 1572868
Sparse Core Ops, SparseCore 0:
  9.5 86.7 all-gather.2
  146.2 111.1 all-gather.4
where the time goes:
time: 413 us; the launch traced here: 412 us
  waiting for transfers between devices  242 us (59%)
  starting transfers between devices  81 us (20%)
  matrix products  39.2 us (9%)
  local copies, waits for them, and re-layouts  32 us (8%)
  between operations  13.8 us (3%)
    all_gather x1, waiting for transfers between devices, local(): lax.all_gather(value_weight, 'seq', axis=0, tiled=True)  77.7 us
    all_to_all x2, waiting for transfers between devices, transform(): lax.all_to_all(partial_im, 'seq', split_axis=0, concat_axis=1, tiled=True)  50.7 us
    all_to_all x2, waiting for transfers between devices, transform(): lax.all_to_all(partial_re, 'seq', split_axis=0, concat_axis=1, tiled=True)  47.4 us
    all_to_all x2, starting transfers between devices, transform(): lax.all_to_all(partial_im, 'seq', split_axis=0, concat_axis=1, tiled=True)  24 us
    all_to_all x2, starting transfers between devices, transform(): lax.all_to_all(partial_re, 'seq', split_axis=0, concat_axis=1, tiled=True)  21 us
    all_to_all x1, waiting for transfers between devices, local(): lax.all_to_all(inverse_re, 'seq', split_axis=1, concat_axis=0, tiled=True)  20.9 us
    all_to_all x1, waiting for transfers between devices, local(): lax.all_to_all(inverse_im, 'seq', split_axis=1, concat_axis=0, tiled=True)  19 us
    all_to_all x1, waiting for transfers between devices, local(): lax.all_to_all(conv_part.astype(jnp.bfloat16), 'seq', split_axis=1, conca...  14.4 us
  transfers between devices with their start and end apart: 12, of which 10 were waited for; matrix products, arithmetic and copies ran while one was open for 13% of the time, Pallas kernels for 0%

commit v1 on v0

v1 whole, which is shorter than its diff:
```python
import functools
import math

import jax
import jax.numpy as jnp
import ml_dtypes
import numpy as np
from jax import lax
from jax.experimental import pallas as pl
from jax.experimental.pallas import tpu as pltpu
from jax.sharding import PartitionSpec as P

PLANE = 4
LANES = 128
ROWS = 16
MIB = 1 << 20


def stage_tables(blocks):
    width = 2 * blocks
    b = np.arange(blocks)
    forward = [np.ones(blocks), np.cos(np.pi * b)]
    backward = [np.ones(blocks), np.cos(np.pi * b)]
    for f in range(1, blocks):
        angle = 2.0 * np.pi * (f * b % width) / width
        forward += [np.cos(angle), -np.sin(angle)]
        backward += [2.0 * np.cos(angle), -2.0 * np.sin(angle)]
    eye = np.eye(ROWS)
    first = np.kron(np.stack(forward, 0), eye)
    last = np.kron(np.stack(backward, 1), eye) / (width * LANES)
    return first.astype(ml_dtypes.bfloat16), last.astype(ml_dtypes.bfloat16)


def turned_tables(blocks, rows):
    width = 2 * blocks
    k = np.arange(rows)[:, None]
    m = np.arange(rows)[None, :]
    out = []
    for f in range(blocks + 1):
        angle = 2.0 * np.pi * ((width * k + f) * m % (width * rows)) / (width * rows)
        cos, sin = np.cos(angle), np.sin(angle)
        out.append(np.block([[cos, sin], [-sin, cos]]))
    forward = np.stack(out, 0)
    return (
        forward.astype(ml_dtypes.bfloat16),
        np.swapaxes(forward, 1, 2).astype(ml_dtypes.bfloat16),
    )


def dot(left, right):
    return jnp.dot(left, right, preferred_element_type=jnp.float32)


def call(kernel, outs, scratch, pos, args, flops):
    in_specs = [pl.BlockSpec(memory_space=pltpu.SMEM)]
    in_specs += [pl.BlockSpec(memory_space=pltpu.VMEM)] * len(args)
    moved = sum(a.size * a.dtype.itemsize for a in args)
    moved += sum(math.prod(o.shape) * o.dtype.itemsize for o in outs)
    return pl.pallas_call(
        kernel,
        out_shape=outs,
        in_specs=in_specs,
        out_specs=[pl.BlockSpec(memory_space=pltpu.VMEM)] * len(outs),
        scratch_shapes=scratch,
        compiler_params=pltpu.CompilerParams(vmem_limit_bytes=48 * MIB),
        cost_estimate=pl.CostEstimate(flops=flops, bytes_accessed=moved, transcendentals=0),
    )(pos, *args)


def block_at(pos, s, d, rows):
    block = jnp.bitwise_xor(pos[1], s) * PLANE + jnp.bitwise_xor(pos[2], d)
    return pl.multiple_of(block * rows, rows)


def project_kernel(planes, pos, *refs):
    x = refs[:PLANE]
    own = refs[PLANE]
    mine = refs[PLANE + 1 : PLANE + planes]
    other = refs[PLANE + planes : PLANE + 2 * planes - 1]
    outs = refs[PLANE + 2 * planes - 1 : PLANE + 3 * planes - 1]
    xs, ws, ps = refs[PLANE + 3 * planes - 1 :]
    rows = x[0].shape[0]
    deep = own.shape[1]
    share = outs[0].shape[1]
    half = PLANE // 2
    y = pos[0]
    for d in range(PLANE):
        xs[d * rows : (d + 1) * rows, :] = x[d][...]
        ws[pl.ds(block_at(pos, 0, d, deep), deep), :] = own[d]
    for s in range(1, planes):
        for j in range(half):
            for side, part in ((y, mine[s - 1]), (1 - y, other[s - 1])):
                at = block_at(pos, s, side * half + j, deep)
                ws[pl.ds(at, deep), :] = part[j * deep : (j + 1) * deep, :]
    ps[...] = dot(xs[...], ws[...]).astype(ps.dtype)
    for s in range(planes):
        at = pl.multiple_of(jnp.bitwise_xor(pos[1], s) * share, share)
        outs[s][...] = ps[:, pl.ds(at, share)]


def forward_stage(signal, first, work, blocks, rows):
    share = signal.shape[1]
    for pair in range(rows // (2 * ROWS)):
        halves = []
        for h in range(2):
            at = (2 * pair + h) * ROWS
            halves.append(
                jnp.concatenate(
                    [signal[b * rows + at : b * rows + at + ROWS, :] for b in range(blocks)], 0
                )
            )
        got = dot(first[...], jnp.concatenate(halves, 1)).astype(jnp.bfloat16)
        for h in range(2):
            at = (2 * pair + h) * ROWS
            for f in range(2 * blocks):
                work[f, at : at + ROWS, :] = got[
                    f * ROWS : (f + 1) * ROWS, h * share : (h + 1) * share
                ]


def spectrum_at(f, work, turned, blocks, rows):
    if f == 0 or f == blocks:
        return dot(turned[f, :, :rows], work[0 if f == 0 else 1])
    both = jnp.concatenate([work[2 * f], work[2 * f + 1]], 0)
    return dot(turned[f], both)


def taps_kernel(blocks, planes, pos, *refs):
    parts = refs[:PLANE]
    first, turned, out, signal, work = refs[PLANE:]
    rows = signal.shape[0] // blocks
    for d in range(PLANE):
        for s in range(planes):
            signal[pl.ds(block_at(pos, s, d, rows), rows), :] = parts[d][s]
    forward_stage(signal, first, work, blocks, rows)
    for f in range(blocks + 1):
        out[f] = spectrum_at(f, work, turned, blocks, rows).astype(out.dtype)


def conv_kernel(blocks, planes, pos, *refs):
    parts = refs[:planes]
    taps, skip, response, first, last, turned, back = refs[planes : planes + 7]
    outs = refs[planes + 7 : 2 * planes + 7]
    wide, value, work, result = refs[2 * planes + 7 :]
    rows = value.shape[0] // blocks
    share = value.shape[1]
    lead = wide.shape[0] - value.shape[0]
    wide[:lead, :] = jnp.zeros((lead, share), jnp.float32)
    for s in range(planes):
        for d in range(PLANE):
            at = block_at(pos, s, d, rows)
            wide[pl.ds(pl.multiple_of(lead + at, 8), rows), :] = parts[s][
                d * rows : (d + 1) * rows, :
            ].astype(jnp.float32)
    for b in range(blocks):
        at = lead + b * rows
        value[b * rows : (b + 1) * rows, :] = (
            taps[0:1, :] * wide[at : at + rows, :]
            + taps[1:2, :] * wide[at - 1 : at - 1 + rows, :]
            + taps[2:3, :] * wide[at - 2 : at - 2 + rows, :]
        ).astype(value.dtype)
    forward_stage(value, first, work, blocks, rows)
    for f in range(blocks + 1):
        got = spectrum_at(f, work, turned, blocks, rows)
        re, im = got[:rows], got[rows:]
        response_re = response[f, :rows, :].astype(jnp.float32)
        response_im = response[f, rows:, :].astype(jnp.float32)
        product = jnp.concatenate(
            [re * response_re - im * response_im, re * response_im + im * response_re], 0
        ).astype(jnp.bfloat16)
        if f == 0 or f == blocks:
            work[0 if f == 0 else 1] = dot(back[f, :rows, :], product).astype(work.dtype)
        else:
            inverse = dot(back[f], product).astype(work.dtype)
            work[2 * f] = inverse[:rows]
            work[2 * f + 1] = inverse[rows:]
    for pair in range(rows // (2 * ROWS)):
        halves = []
        for h in range(2):
            at = (2 * pair + h) * ROWS
            halves.append(
                jnp.concatenate([work[f, at : at + ROWS, :] for f in range(2 * blocks)], 0)
            )
        got = dot(last[...], jnp.concatenate(halves, 1))
        for h in range(2):
            at = (2 * pair + h) * ROWS
            for b in range(blocks):
                here = slice(b * rows + at, b * rows + at + ROWS)
                conv = got[b * ROWS : (b + 1) * ROWS, h * share : (h + 1) * share]
                result[here, :] = (
                    conv + skip[...] * value[here, :].astype(jnp.float32)
                ).astype(result.dtype)
    for s in range(planes):
        for d in range(PLANE):
            outs[s][d * rows : (d + 1) * rows, :] = result[
                pl.ds(block_at(pos, s, d, rows), rows), :
            ]


def output_kernel(planes, pos, *refs):
    u = refs[:planes]
    gate = refs[planes]
    own = refs[planes + 1]
    mine = refs[planes + 2 : 2 * planes + 1]
    other = refs[2 * planes + 1 : 3 * planes]
    outs = refs[3 * planes : 3 * planes + PLANE]
    mixed, ws = refs[3 * planes + PLANE :]
    share = u[0].shape[1]
    rows = gate.shape[1]
    half = mine[0].shape[1]
    y = pos[0]
    for s in range(planes):
        at = pl.multiple_of(jnp.bitwise_xor(pos[1], s) * share, share)
        for d in range(PLANE):
            mixed[d * rows : (d + 1) * rows, s * share : (s + 1) * share] = (
                gate[d, :, pl.ds(at, share)].astype(jnp.float32)
                * u[s][d * rows : (d + 1) * rows, :].astype(jnp.float32)
            ).astype(mixed.dtype)
        if s == 0:
            ws[:share, :] = own[...]
        else:
            here = slice(s * share, (s + 1) * share)
            ws[here, pl.ds(pl.multiple_of(y * half, half), half)] = mine[s - 1][...]
            ws[here, pl.ds(pl.multiple_of((1 - y) * half, half), half)] = other[s - 1][...]
    for d in range(PLANE):
        outs[d][...] = dot(mixed[d * rows : (d + 1) * rows, :], ws[...]).astype(outs[d].dtype)


def local(inputs, gate_in, value_weight, short_taps, filter_taps, skip_scale, output_weight):
    rows, features = inputs.shape
    deep, channels = value_weight.shape
    devices = lax.axis_size("seq")
    planes = devices // PLANE
    share = channels // devices
    wide = planes * share
    blocks = devices
    index = lax.axis_index("seq")
    y = lax.axis_index("groups")
    z, place = index // PLANE, index % PLANE
    pos = jnp.stack([y, z, place]).astype(jnp.int32)

    def to_place(block, d):
        return lax.ppermute(block, "seq", [(i, i ^ d) for i in range(devices)])

    def to_plane(block, s):
        return lax.ppermute(block, "seq", [(i, i ^ (s * PLANE)) for i in range(devices)])

    def to_group(block):
        return lax.ppermute(block, "groups", [(0, 1), (1, 0)])

    def of_place(array, d):
        cut = array.reshape(array.shape[0], planes, PLANE, share)
        at = jnp.bitwise_xor(place, d)
        return lax.dynamic_index_in_dim(cut, at, 2, keepdims=False).reshape(-1, wide)

    def around(array):
        parts = [of_place(array, 0)]
        return parts + [to_place(of_place(array, d), d) for d in range(1, PLANE)]

    first, last = stage_tables(blocks)
    turned, back = turned_tables(blocks, rows)

    value_parts = around(value_weight)
    stacked = jnp.stack(value_parts)
    half = PLANE // 2
    sent = lax.dynamic_slice_in_dim(stacked, y * half, half, 0).reshape(half * deep, wide)
    mine = [to_plane(sent, s) for s in range(1, planes)]
    other = [to_group(block) for block in mine]
    from_x = to_place(inputs, 2)
    x_parts = [inputs, to_place(inputs, 1), from_x, to_place(from_x, 1)]

    cut = filter_taps.reshape(rows, planes, PLANE * share)
    part = rows // 2

    def taps_for(s):
        block = lax.dynamic_index_in_dim(cut, jnp.bitwise_xor(z, s), 1, keepdims=False)
        return block if s == 0 else lax.dynamic_slice_in_dim(block, y * part, part, 0)

    taps_mine = jnp.stack([to_plane(taps_for(s), s) for s in range(1, planes)])
    taps_other = to_group(taps_mine)
    taps_all = jnp.where(
        y == 0,
        jnp.concatenate([taps_mine, taps_other], 1),
        jnp.concatenate([taps_other, taps_mine], 1),
    )
    taps_all = jnp.concatenate([taps_for(0)[None], taps_all], 0)
    taps_all = taps_all.reshape(planes, rows, PLANE, share)
    taps_parts = []
    for d in range(PLANE):
        block = lax.dynamic_index_in_dim(taps_all, jnp.bitwise_xor(place, d), 2, keepdims=False)
        taps_parts.append(to_place(block, d) if d else block)
    positions = blocks * rows
    response = call(
        functools.partial(taps_kernel, blocks, planes),
        [jax.ShapeDtypeStruct((blocks + 1, 2 * rows, share), jnp.bfloat16)],
        [
            pltpu.VMEM((positions, share), jnp.bfloat16),
            pltpu.VMEM((2 * blocks, rows, share), jnp.bfloat16),
        ],
        pos,
        [*taps_parts, jnp.asarray(first), jnp.asarray(turned)],
        2 * positions * share * (32 * ROWS + 4 * rows),
    )[0]

    gate = jnp.stack(around(gate_in))
    width = output_weight.shape[1] // 2
    out_half = lax.dynamic_slice_in_dim(output_weight, y * width, width, 1)
    out_mine = [to_plane(out_half, s) for s in range(1, planes)]
    out_other = [to_group(block) for block in out_mine]

    projected = call(
        functools.partial(project_kernel, planes),
        [jax.ShapeDtypeStruct((PLANE * rows, share), jnp.bfloat16)] * planes,
        [
            pltpu.VMEM((PLANE * rows, features), jnp.bfloat16),
            pltpu.VMEM((features, wide), jnp.bfloat16),
            pltpu.VMEM((PLANE * rows, wide), jnp.bfloat16),
        ],
        pos,
        [*x_parts, stacked, *mine, *other],
        2 * PLANE * rows * features * wide,
    )
    signal = [projected[0]] + [to_plane(projected[s], s) for s in range(1, planes)]
    taps = lax.dynamic_slice_in_dim(short_taps, index * share, share, 1)
    skip = lax.dynamic_slice_in_dim(skip_scale, index * share, share, 0)[None]
    mixed = call(
        functools.partial(conv_kernel, blocks, planes),
        [jax.ShapeDtypeStruct((PLANE * rows, share), jnp.bfloat16)] * planes,
        [
            pltpu.VMEM((positions + 8, share), jnp.float32),
            pltpu.VMEM((positions, share), jnp.bfloat16),
            pltpu.VMEM((2 * blocks, rows, share), jnp.bfloat16),
            pltpu.VMEM((positions, share), jnp.bfloat16),
        ],
        pos,
        [
            *signal,
            taps,
            skip,
            response,
            jnp.asarray(first),
            jnp.asarray(last),
            jnp.asarray(turned),
            jnp.asarray(back),
        ],
        4 * positions * share * (32 * ROWS + 4 * rows),
    )
    spread = [mixed[0]] + [to_plane(mixed[s], s) for s in range(1, planes)]
    partial = call(
        functools.partial(output_kernel, planes),
        [
            jax.ShapeDtypeStruct((rows, features), jnp.bfloat16 if d % 2 else jnp.float32)
            for d in range(PLANE)
        ],
        [
            pltpu.VMEM((PLANE * rows, wide), jnp.bfloat16),
            pltpu.VMEM((wide, features), jnp.bfloat16),
        ],
        pos,
        [*spread, gate, output_weight, *out_mine, *out_other],
        2 * PLANE * rows * features * wide,
    )
    across = partial[2] + to_place(partial[3], 1).astype(jnp.float32)
    across = to_place(across.astype(jnp.bfloat16), 2).astype(jnp.float32)
    beside = to_place(partial[1], 1).astype(jnp.float32)
    return (partial[0] + beside + across).astype(jnp.bfloat16)


def passed_along(block, axis, distance):
    devices = range(lax.axis_size(axis))
    route = [(i - distance, i) for i in devices if i - distance in devices]
    return lax.ppermute(block, axis, route)


def local_narrow(inputs, gate_in, value_weight, short_taps, filter_taps, skip_scale, output_weight):
    rows, features = inputs.shape
    channels = value_weight.shape[1]
    blocks = lax.axis_size("seq")
    share = channels // blocks
    index = lax.axis_index("seq")
    projected = dot(inputs, lax.all_gather(value_weight, "seq", axis=0, tiled=True)).astype(
        jnp.bfloat16
    )
    earlier = passed_along(projected[rows - 2 :], "seq", 1)
    extended = jnp.concatenate([earlier, projected], 0).astype(jnp.float32)
    value = (
        short_taps[0] * extended[2:]
        + short_taps[1] * extended[1:-1]
        + short_taps[2] * extended[:-2]
    ).astype(jnp.bfloat16)

    def by_channel(signal):
        cut = signal.reshape(rows, blocks, share)
        got = lax.all_to_all(cut, "seq", split_axis=1, concat_axis=0, tiled=True)
        return got.reshape(blocks, rows, share)

    grid = np.arange(2 * blocks)
    angle = 2.0 * np.pi * (grid[:, None] * grid[None, :] % (2 * blocks)) / (2 * blocks)
    wide = np.exp(-1j * angle)[: blocks + 1, :blocks]
    turned, back = (jnp.asarray(t) for t in turned_tables(blocks, rows))
    weight = np.full((blocks + 1, 1), 2.0)
    weight[0] = weight[-1] = 1.0
    narrow = weight * np.conj(wide) / (2 * blocks * rows)

    def einsum(form, table, data):
        return jnp.einsum(form, table, data, preferred_element_type=jnp.float32)

    def table(values):
        return jnp.asarray(values.astype(ml_dtypes.bfloat16))

    def forward(signal):
        re = einsum("fb,bmc->fmc", table(np.real(wide)), signal)
        im = einsum("fb,bmc->fmc", table(np.imag(wide)), signal)
        both = jnp.concatenate([re, im], 1).astype(jnp.bfloat16)
        return einsum("fkm,fmc->fkc", turned, both)

    response = forward(by_channel(filter_taps))
    got = forward(by_channel(value))
    re, im = got[:, :rows], got[:, rows:]
    response_re, response_im = response[:, :rows], response[:, rows:]
    product = jnp.concatenate(
        [re * response_re - im * response_im, re * response_im + im * response_re], 1
    ).astype(jnp.bfloat16)
    inverse = einsum("fmk,fkc->fmc", back, product).astype(jnp.bfloat16)
    conv = einsum("fb,fmc->bmc", table(np.real(narrow)), inverse[:, :rows]) - einsum(
        "fb,fmc->bmc", table(np.imag(narrow)), inverse[:, rows:]
    )
    conv = lax.all_to_all(
        conv.astype(jnp.bfloat16), "seq", split_axis=0, concat_axis=2, tiled=True
    ).reshape(rows, channels)
    mixed = (
        gate_in.astype(jnp.float32)
        * (conv.astype(jnp.float32) + skip_scale * value.astype(jnp.float32))
    ).astype(jnp.bfloat16)
    result = dot(mixed, lax.all_gather(output_weight, "seq", axis=0, tiled=True))
    return result.astype(jnp.bfloat16)


def solution(mesh):
    split = P(("groups", "seq"), None)
    placed = (split, split, P("seq", None), P(), P("seq", None), P(), P("seq", None))

    def run(*args):
        devices = mesh.shape["seq"]
        share = args[2].shape[1] // devices
        tiled = share % LANES == 0 and args[0].shape[0] // mesh.size == LANES
        paired = devices % PLANE == 0 and mesh.shape["groups"] == 2
        body = local if tiled and paired and devices & (devices - 1) == 0 else local_narrow
        return jax.shard_map(body, mesh=mesh, in_specs=placed, out_specs=split, check_vma=False)(
            *args
        )

    return run
```

time: 413 us -> 137 us (0.33)
  waiting for transfers between devices: 242 us -> 42 us
  matrix products: 39.2 us -> 0 us
  starting transfers between devices: 81 us -> 50.7 us
  between operations: 13.8 us -> 0.45 us
  Pallas kernels: 0 us -> 11.9 us
  local copies, waits for them, and re-layouts: 32 us -> 22.1 us
  other arithmetic: 3.78 us -> 9.38 us
    all_to_all x9 -> x0, waiting for transfers between devices: 162 us -> none  [the longest x2 50.7 us: transform(): lax.all_to_all(partial_im, 'seq', split_axis=0, concat_axis=1, tiled=True)]
    all_to_all x9 -> x0, starting transfers between devices: 78.8 us -> none  [the longest x2 24 us: transform(): lax.all_to_all(partial_im, 'seq', split_axis=0, concat_axis=1, tiled=True)]
    all_gather x2 -> x0, waiting for transfers between devices: 77.8 us -> none  [the longest x1 77.7 us: local(): lax.all_gather(value_weight, 'seq', axis=0, tiled=True)]
    ppermute x1 -> x37, starting transfers between devices: 2.16 us -> 50.7 us  [the longest x15 33 us: to_plane(): lax.ppermute(block, 'seq', [(i, i ^ s * PLANE) for i in range(devices)])]
    ppermute x1 -> x37, waiting for transfers between devices: 0.72 us -> 42 us  [the longest x15 19.7 us: to_plane(): lax.ppermute(block, 'seq', [(i, i ^ s * PLANE) for i in range(devices)])]
    dot_general x20 -> x0, matrix products: 39.2 us -> none  [the longest x2 10.2 us: matmul(): return jnp.dot(left, right, preferred_element_type=jnp.float32)]
    convert_element_type x7 -> x0, local copies, waits for them, and re-layouts: 14.1 us -> none  [the longest x2 4.46 us: first_section(): (first_im * cos_turn - first_re * sin_turn).astype(jnp.bfloat16)]
    pallas_call x0 -> x4, Pallas kernels: none -> 11.9 us  [call(): pl.pallas_call(kernel, out_shape=outs, in_specs=in_specs, out_specs=[pl.B...]
  transfers between devices with their start and end apart: 12 -> 37, of which waited for: 10 -> 12; matrix products, arithmetic and copies ran while one was open for 13% -> 21% of each run, Pallas kernels for 0% -> 6%
where the time goes in v1:
time: 137 us
  starting transfers between devices  50.7 us (37%)
  waiting for transfers between devices  42 us (31%)
  local copies, waits for them, and re-layouts  22.1 us (16%)
  Pallas kernels  11.9 us (9%)
  other arithmetic  9.38 us (7%)
    ppermute x15, starting transfers between devices, to_plane(): lax.ppermute(block, 'seq', [(i, i ^ s * PLANE) for i in range(devices)])  33 us
    ppermute x15, waiting for transfers between devices, to_plane(): lax.ppermute(block, 'seq', [(i, i ^ s * PLANE) for i in range(devices)])  19.7 us
    ppermute x15, waiting for transfers between devices, to_place(): return lax.ppermute(block, 'seq', [(i, i ^ d) for i in range(devices)])  14.4 us
    pallas_call x4, Pallas kernels, call(): pl.pallas_call(kernel, out_shape=outs, in_specs=in_specs, out_specs=[pl.B...  11.9 us
    ppermute x15, starting transfers between devices, to_place(): return lax.ppermute(block, 'seq', [(i, i ^ d) for i in range(devices)])  11 us
    ppermute x7, waiting for transfers between devices, to_group(): return lax.ppermute(block, 'groups', [(0, 1), (1, 0)])  7.87 us
    dynamic_slice x1, local copies, waits for them, and re-layouts, of_place(): lax.dynamic_index_in_dim(cut, at, 2, keepdims=False).reshape(-1, wide)  7 us
    ppermute x7, starting transfers between devices, to_group(): return lax.ppermute(block, 'groups', [(0, 1), (1, 0)])  6.72 us
  transfers between devices with their start and end apart: 37, of which 12 were waited for; matrix products, arithmetic and copies ran while one was open for 21% of the time, Pallas kernels for 6%

profile of v1, /device:TPU:0, one launch (start us, length us, event | category | flops | bytes accessed | tf_op | source)
XLA Modules:
  0.0 136.5 jit_solution(8558836343547632666)
XLA Ops:
  0.0 2.9 %collective-permute-start.1 = (bf16[128,2048]{1,0:T(8,128)(2,1)}, bf16[128,2048]{1,0:T(8,128)(2,1)S(1)}, u32[]{:S(2)}, u32[]{:S(2)}) collective-permute-start(bf16[128,2048]{1,0:T(8,128)(2,1)} %refs_0_.1), channel_id=1, source_target_pairs={{0,2},{1,3},{2,0},{3,1},{4,6},{5,7},{6,4},{7,5},{8,10},{9,11},{10,... | collective-permute-start | bytes 1572872 | tf_op jit(solution)/shard_map/ppermute | solution.py:243
  2.9 1.4 %reshape.74 = bf16[128,4,4,128]{3,2,1,0:T(4,128)(2,1)S(1)} reshape(bf16[128,2048]{1,0:T(8,128)(2,1)} %param.12) | data formatting | bytes 1048576 | tf_op jit(solution)/shard_map/reshape | solution.py:252
  4.3 1.4 %reshape.68 = bf16[128,4,4,128]{3,2,1,0:T(4,128)(2,1)S(1)} reshape(bf16[128,2048]{1,0:T(8,128)(2,1)} %param.13) | data formatting | bytes 1048576 | tf_op jit(solution)/shard_map/reshape | solution.py:252
  5.8 7.0 %dynamic-slice_reduce_fusion.3 = (bf16[128,4,128]{2,1,0:T(4,128)(2,1)}, bf16[128,4,128]{2,1,0:T(4,128)(2,1)}, bf16[128,4,128]{2,1,0:T(4,128)(2,1)}, bf16[128,4,1...) fusion(bf16[128,4,4,128]{3,2,1,0:T(4,128)(2,1)S(1)} %reshape.74, ...), kind=kLoop, calls=%fused_computation.20 | loop fusion | bytes 2097168 | tf_op jit(solution)/shard_map/jit(dynamic_index_in_dim)/dynamic_slice | solution.py:254
  12.9 1.2 collective-permute-start.4
  15.5 3.7 %collective-permute-start.17 = (bf16[64,512]{1,0:T(8,128)(2,1)S(1)}, bf16[64,512]{1,0:T(8,128)(2,1)S(1)}, u32[]{:S(2)}, u32[]{:S(2)}) collective-permute-start(bf16[64,512]{1,0:T(8,128)(2,1)S(1)} %bitcast.80), channel_id=1, source_target_pairs={{0,12},{1,13},{2,14},{3,15},{4,8},{5,9},{6,10},{7,11},{8,4},{9,5},... | collective-permute-start | bytes 196616 | tf_op jit(solution)/shard_map/ppermute | solution.py:246
  20.1 0.8 copy.41
  21.4 1.6 %collective-permute-start.15 = (bf16[64,512]{1,0:T(8,128)(2,1)}, bf16[64,512]{1,0:T(8,128)(2,1)S(1)}, u32[]{:S(2)}, u32[]{:S(2)}) collective-permute-start(bf16[64,512]{1,0:T(8,128)(2,1)} %bitcast.10), channel_id=1, source_target_pairs={{0,4},{1,5},{2,6},{3,7},{4,0},{5,1},{6,2},{7,3},{8,12},{9,13},{10,... | collective-permute-start | bytes 196616 | tf_op jit(solution)/shard_map/ppermute | solution.py:246
  23.2 1.1 pad_maximum_fusion.refs_4_
  25.1 1.1 collective-permute-start
  27.0 2.2 %collective-permute-start.7 = (bf16[256,512]{1,0:T(8,128)(2,1)}, bf16[256,512]{1,0:T(8,128)(2,1)S(1)}, u32[]{:S(2)}, u32[]{:S(2)}) collective-permute-start(bf16[256,512]{1,0:T(8,128)(2,1)} %bitcast.6), channel_id=1, source_target_pairs={{0,8},{1,9},{2,10},{3,11},{4,12},{5,13},{6,14},{7,15},{8,0},{9,1},... | collective-permute-start | bytes 786440 | tf_op jit(solution)/shard_map/ppermute | solution.py:246
  29.9 1.5 %collective-permute-start.18 = (bf16[3,64,512]{2,1,0:T(8,128)(2,1)}, bf16[3,64,512]{2,1,0:T(8,128)(2,1)}, u32[]{:S(2)}, u32[]{:S(2)}) collective-permute-start(bf16[3,64,512]{2,1,0:T(8,128)(2,1)} %pad_maximum_fusion.2), channel_id=1, source_target_pairs={{0,16},{16,0},{1,17},{17,1},{2,18},{18,2},{3,19},{19,3},{4,20},{20... | collective-permute-start | bytes 589832 | tf_op jit(solution)/shard_map/ppermute | solution.py:249
  32.2 4.3 %collective-permute-done.18 = bf16[3,64,512]{2,1,0:T(8,128)(2,1)} collective-permute-done((bf16[3,64,512]{2,1,0:T(8,128)(2,1)}, bf16[3,64,512]{2,1,0:T(8,128)(2,1)}, u32[]{:S(2)}, u32[]{:S(2)}) %collective-permute-start.18) | collective-permute-done | bytes 196640 | tf_op jit(solution)/shard_map/ppermute | solution.py:249
  36.5 1.4 %collective-permute-start.8 = (bf16[256,512]{1,0:T(8,128)(2,1)}, bf16[256,512]{1,0:T(8,128)(2,1)S(1)}, u32[]{:S(2)}, u32[]{:S(2)}) collective-permute-start(bf16[256,512]{1,0:T(8,128)(2,1)} %bitcast.6), channel_id=1, source_target_pairs={{0,12},{1,13},{2,14},{3,15},{4,8},{5,9},{6,10},{7,11},{8,4},{9,5},... | collective-permute-start | bytes 786440 | tf_op jit(solution)/shard_map/ppermute | solution.py:246
  38.0 2.3 %collective-permute-done.6.refs_5_ = bf16[256,512]{1,0:T(8,128)(2,1)S(1)} collective-permute-done((bf16[256,512]{1,0:T(8,128)(2,1)}, bf16[256,512]{1,0:T(8,128)(2,1)S(1)}, u32[]{:S(2)}, u32[]{:S(2)}) %collective-permute-start.6) | collective-permute-done | bytes 262176 | tf_op jit(solution)/shard_map/ppermute | solution.py:246
  40.3 1.5 %collective-permute-start.9 = (bf16[256,512]{1,0:T(8,128)(2,1)S(1)}, bf16[256,512]{1,0:T(8,128)(2,1)}, u32[]{:S(2)}, u32[]{:S(2)}) collective-permute-start(bf16[256,512]{1,0:T(8,128)(2,1)S(1)} %collective-permute-done.6.refs_5_), channel_id=1, source_target_pairs={{0,16},{16,0},{1,17},{17,1},{2,18},{18,2},{3,19},{19,3},{4,20},{20... | collective-permute-start | bytes 786440 | tf_op jit(solution)/shard_map/ppermute | solution.py:249
  42.3 0.9 stack.66
  44.0 1.7 %concatenate.19 = bf16[3,64,4,128]{3,2,1,0:T(4,128)(2,1)} reshape(bf16[3,64,512]{2,1,0:T(8,128)(2,1)} %collective-permute-done.18) | data formatting | bytes 393216 | tf_op jit(solution)/shard_map/concatenate | solution.py:283
  45.6 1.7 %maximum_select_fusion = bf16[3,128,4,128]{3,2,1,0:T(4,128)(2,1)S(1)} fusion(bf16[3,64,4,128]{3,2,1,0:T(4,128)(2,1)} %concatenate.19, bf16[3,64,4,128]{3,2,1,0:T(4,128)(2,1)} %constant_dynamic-update-slice_fusion, pred[]{:T(512)S(6)} %eq.5), kind=kLoop, calls=%fused_computation.8 | loop fusion | flops 589824 | bytes 786433 | tf_op jit(solution)/shard_map/jit(_where)/select_n | solution.py:281
  48.0 7.6 %collective-permute-start.28 = (bf16[128,1024]{1,0:T(8,128)(2,1)}, bf16[128,1024]{1,0:T(8,128)(2,1)}, u32[]{:S(2)}, u32[]{:S(2)}) collective-permute-start(bf16[128,1024]{1,0:T(8,128)(2,1)} %constant_dynamic-slice_fusion), channel_id=1, source_target_pairs={{0,4},{1,5},{2,6},{3,7},{4,0},{5,1},{6,2},{7,3},{8,12},{9,13},{10,... | collective-permute-start | bytes 786440 | tf_op jit(solution)/shard_map/ppermute | solution.py:246
  55.6 3.3 %collective-permute-start.29 = (bf16[128,1024]{1,0:T(8,128)(2,1)}, bf16[128,1024]{1,0:T(8,128)(2,1)}, u32[]{:S(2)}, u32[]{:S(2)}) collective-permute-start(bf16[128,1024]{1,0:T(8,128)(2,1)} %constant_dynamic-slice_fusion), channel_id=1, source_target_pairs={{0,8},{1,9},{2,10},{3,11},{4,12},{5,13},{6,14},{7,15},{8,0},{9,1},... | collective-permute-start | bytes 786440 | tf_op jit(solution)/shard_map/ppermute | solution.py:246
  59.5 3.4 %fusion = (bf16[4,128,1,128]{3,2,1,0:T(2,128)(2,1)}, bf16[4,128,1,128]{3,2,1,0:T(2,128)(2,1)}, bf16[4,128,1,128]{3,2,1,0:T(2,128)(2,1)S(1)}, bf16[4,128,1,128]{3,2,1,0:T(2,128)(2,1)}) fusion(s32[]{:T(128)S(6)} %select_n.83, bf16[3,128,4,128]{3,2,1,0:T(4,128)(2,1)S(1)} %maximum_select_fusion, bf16[1,128,4,128]{3,2,1,0:T(4,128)(2,1)} %copy.41, ...), kind=kLoop, calls=%fused_computation.13 | loop fusion | flops 1048576 | bytes 1048592 | tf_op jit(solution)/shard_map/concatenate | solution.py:286
  63.6 3.5 %collective-permute-done.11.refs_10_ = bf16[256,512]{1,0:T(8,128)(2,1)S(1)} collective-permute-done((bf16[256,512]{1,0:T(8,128)(2,1)S(1)}, bf16[256,512]{1,0:T(8,128)(2,1)S(1)}, u32[]{:S(2)}, u32[]{:S(2)}) %collective-permute-start.11) | collective-permute-done | bytes 262176 | tf_op jit(solution)/shard_map/ppermute | solution.py:249
  67.9 1.0 copy.81
  68.9 1.0 copy.80
  69.9 1.1 collective-permute-start.20
  71.0 0.9 copy-done.5
  72.0 2.6 %shard_map.109 = (bf16[512,128]{1,0:T(8,128)(2,1)S(1)}, bf16[512,128]{1,0:T(8,128)(2,1)S(1)}, bf16[512,128]{1,0:T(8,128)(2,1)S(1)}, bf16[512,128]{1,0:T(8,128)(2,1)S(1)}) custom-call(s32[3]{0:T(128)S(1)} %pad_add_fusion.pos, bf16[128,2048]{1,0:T(8,128)(2,1)S(1)} %copy-done.3, bf16[128,2048]{1,0:T(8,128)(2,1)S(1)} %collective-permute-done.refs_1_, ...), custom_call_target="tpu_custom_call" | custom-call | flops 1073741824 | bytes 4718592 | tf_op jit(solution)/shard_map/pallas_call | solution.py:59
  74.6 0.9 collective-permute-start.21
  75.5 2.1 %collective-permute-done.29.refs_7_ = bf16[128,1024]{1,0:T(8,128)(2,1)} collective-permute-done((bf16[128,1024]{1,0:T(8,128)(2,1)}, bf16[128,1024]{1,0:T(8,128)(2,1)}, u32[]{:S(2)}, u32[]{:S(2)}) %collective-permute-start.29) | collective-permute-done | bytes 262176 | tf_op jit(solution)/shard_map/ppermute | solution.py:246
  77.6 6.7 %collective-permute-start.13 = (bf16[512,128]{1,0:T(8,128)(2,1)S(1)}, bf16[512,128]{1,0:T(8,128)(2,1)S(1)}, u32[]{:S(2)}, u32[]{:S(2)}) collective-permute-start(bf16[512,128]{1,0:T(8,128)(2,1)S(1)} %get-tuple-element.19), channel_id=1, source_target_pairs={{0,8},{1,9},{2,10},{3,11},{4,12},{5,13},{6,14},{7,15},{8,0},{9,1},... | collective-permute-start | bytes 393224 | tf_op jit(solution)/shard_map/ppermute | solution.py:246
  84.4 1.4 %collective-permute-start.14 = (bf16[512,128]{1,0:T(8,128)(2,1)S(1)}, bf16[512,128]{1,0:T(8,128)(2,1)S(1)}, u32[]{:S(2)}, u32[]{:S(2)}) collective-permute-start(bf16[512,128]{1,0:T(8,128)(2,1)S(1)} %get-tuple-element.20), channel_id=1, source_target_pairs={{0,12},{1,13},{2,14},{3,15},{4,8},{5,9},{6,10},{7,11},{8,4},{9,5},... | collective-permute-start | bytes 393224 | tf_op jit(solution)/shard_map/ppermute | solution.py:246
  87.2 1.1 collective-permute-start.26
  88.3 6.0 %collective-permute-done.13.refs_2_ = bf16[512,128]{1,0:T(8,128)(2,1)S(1)} collective-permute-done((bf16[512,128]{1,0:T(8,128)(2,1)S(1)}, bf16[512,128]{1,0:T(8,128)(2,1)S(1)}, u32[]{:S(2)}, u32[]{:S(2)}) %collective-permute-start.13) | collective-permute-done | bytes 131104 | tf_op jit(solution)/shard_map/ppermute | solution.py:246
  94.8 1.5 %collective-permute-start.33 = (bf16[128,1024]{1,0:T(8,128)(2,1)}, bf16[128,1024]{1,0:T(8,128)(2,1)S(1)}, u32[]{:S(2)}, u32[]{:S(2)}) collective-permute-start(bf16[128,1024]{1,0:T(8,128)(2,1)} %collective-permute-done.30.refs_8_), channel_id=1, source_target_pairs={{0,16},{16,0},{1,17},{17,1},{2,18},{18,2},{3,19},{19,3},{4,20},{20... | collective-permute-start | bytes 786440 | tf_op jit(solution)/shard_map/ppermute | solution.py:249
  96.3 2.0 %shard_map.110.refs_6_ = bf16[17,256,128]{2,1,0:T(8,128)(2,1)S(1)} custom-call(s32[3]{0:T(128)S(1)} %pad_add_fusion.pos, bf16[4,128,128]{2,1,0:T(8,128)(2,1)S(1)} %bitcast.56, bf16[4,128,128]{2,1,0:T(8,128)(2,1)} %collective-permute-done.19.refs_1_, bf16[4,128,128]{2,1,0:T(8,128)(2,1)S(1)} %collective-permute-done.20.refs_2_, ...), custom_call_target="tpu_custom_call" | custom-call | flops 536870912 | bytes 4128768 | tf_op jit(solution)/shard_map/pallas_call | solution.py:59
  98.4 4.2 %shard_map.111 = (bf16[512,128]{1,0:T(8,128)(2,1)S(1)}, bf16[512,128]{1,0:T(8,128)(2,1)S(1)}, bf16[512,128]{1,0:T(8,128)(2,1)S(1)}, bf16[512,128]{1,0:T(8,128)(2,1)S(1)}) custom-call(s32[3]{0:T(128)S(1)} %pad_add_fusion.pos, bf16[512,128]{1,0:T(8,128)(2,1)S(1)} %get-tuple-element.17.refs_0_, bf16[512,128]{1,0:T(8,128)(2,1)S(1)} %collective-permute-done.12.refs_1_, ...), custom_call_target="tpu_custom_call" | custom-call | flops 1073741824 | bytes 7145472 | tf_op jit(solution)/shard_map/pallas_call | solution.py:59
  102.5 0.9 collective-permute-start.22
  103.5 1.1 collective-permute-start.23
  104.6 2.4 %collective-permute-start.24 = (bf16[512,128]{1,0:T(8,128)(2,1)S(1)}, bf16[512,128]{1,0:T(8,128)(2,1)S(1)}, u32[]{:S(2)}, u32[]{:S(2)}) collective-permute-start(bf16[512,128]{1,0:T(8,128)(2,1)S(1)} %get-tuple-element.24), channel_id=1, source_target_pairs={{0,12},{1,13},{2,14},{3,15},{4,8},{5,9},{6,10},{7,11},{8,4},{9,5},... | collective-permute-start | bytes 393224 | tf_op jit(solution)/shard_map/ppermute | solution.py:246
  107.2 2.7 %collective-permute-done.22.refs_1_ = bf16[512,128]{1,0:T(8,128)(2,1)S(1)} collective-permute-done((bf16[512,128]{1,0:T(8,128)(2,1)S(1)}, bf16[512,128]{1,0:T(8,128)(2,1)S(1)}, u32[]{:S(2)}, u32[]{:S(2)}) %collective-permute-start.22) | collective-permute-done | bytes 131104 | tf_op jit(solution)/shard_map/ppermute | solution.py:246
  109.9 5.1 %collective-permute-done.23.refs_2_ = bf16[512,128]{1,0:T(8,128)(2,1)S(1)} collective-permute-done((bf16[512,128]{1,0:T(8,128)(2,1)S(1)}, bf16[512,128]{1,0:T(8,128)(2,1)S(1)}, u32[]{:S(2)}, u32[]{:S(2)}) %collective-permute-start.23) | collective-permute-done | bytes 131104 | tf_op jit(solution)/shard_map/ppermute | solution.py:246
  115.0 3.2 %shard_map.112 = (f32[128,2048]{1,0:T(8,128)S(1)}, bf16[128,2048]{1,0:T(8,128)(2,1)S(1)}, f32[128,2048]{1,0:T(8,128)}, bf16[128,2048]{1,0:T(8,128)(2,1)S(1)}) custom-call(s32[3]{0:T(128)S(1)} %pad_add_fusion.pos, bf16[512,128]{1,0:T(8,128)(2,1)S(1)} %get-tuple-element.21.refs_0_, bf16[512,128]{1,0:T(8,128)(2,1)S(1)} %collective-permute-done.22.refs_1_, ...), custom_call_target="tpu_custom_call" | custom-call | flops 1073741824 | bytes 6291456 | tf_op jit(solution)/shard_map/pallas_call | solution.py:59
  118.8 1.4 %collective-permute-done.35 = bf16[128,2048]{1,0:T(8,128)(2,1)S(1)} collective-permute-done((bf16[128,2048]{1,0:T(8,128)(2,1)S(1)}, bf16[128,2048]{1,0:T(8,128)(2,1)S(1)}, u32[]{:S(2)}, u32[]{:S(2)}) %collective-permute-start.35) | collective-permute-done | bytes 524320 | tf_op jit(solution)/shard_map/ppermute | solution.py:243
  120.2 1.3 add_convert_fusion.1
  121.5 1.1 collective-permute-start.36
  122.6 13.0 %collective-permute-done.36 = bf16[128,2048]{1,0:T(8,128)(2,1)S(1)} collective-permute-done((bf16[128,2048]{1,0:T(8,128)(2,1)S(1)}, bf16[128,2048]{1,0:T(8,128)(2,1)S(1)}, u32[]{:S(2)}, u32[]{:S(2)}) %collective-permute-start.36) | collective-permute-done | bytes 524320 | tf_op jit(solution)/shard_map/ppermute | solution.py:243
  135.5 1.0 add_convert_fusion
  (107 shorter events, 12.7 us)
Async XLA Ops:
  0.0 85.8 %copy-start = (f32[3,2048]{1,0:T(4,128)S(1)}, f32[3,2048]{1,0:T(4,128)}, u32[]{:S(2)}) copy-start(f32[3,2048]{1,0:T(4,128)} %param.14) | copy-start | bytes 73732
  0.0 43.3 %collective-permute-start.1 = (bf16[128,2048]{1,0:T(8,128)(2,1)}, bf16[128,2048]{1,0:T(8,128)(2,1)S(1)}, u32[]{:S(2)}, u32[]{:S(2)}) collective-permute-start(bf16[128,2048]{1,0:T(8,128)(2,1)} %refs_0_.1), channel_id=1, source_target_pairs={{0,2},{1,3},{2,0},{3,1},{4,6},{5,7},{6,4},{7,5},{8,10},{9,11},{10,... | collective-permute-start | bytes 1572872 | tf_op jit(solution)/shard_map/ppermute | solution.py:243
  5.8 9.2 %copy-start.10 = (bf16[128,2048]{1,0:T(8,128)(2,1)S(1)}, bf16[128,2048]{1,0:T(8,128)(2,1)}, u32[]{:S(2)}) copy-start(bf16[128,2048]{1,0:T(8,128)(2,1)} %param.15) | copy-start | bytes 1572868
  12.8 8.1 %collective-permute-start.5 = (bf16[128,512]{1,0:T(8,128)(2,1)S(1)}, bf16[128,512]{1,0:T(8,128)(2,1)}, u32[]{:S(2)}, u32[]{:S(2)}) collective-permute-start(bf16[128,512]{1,0:T(8,128)(2,1)S(1)} %bitcast.73), channel_id=1, source_target_pairs={{0,3},{1,2},{2,1},{3,0},{4,7},{5,6},{6,5},{7,4},{8,11},{9,10},{10,... | collective-permute-start | bytes 393224 | tf_op jit(solution)/shard_map/ppermute | solution.py:243
  12.9 8.4 %collective-permute-start.4 = (bf16[128,512]{1,0:T(8,128)(2,1)S(1)}, bf16[128,512]{1,0:T(8,128)(2,1)}, u32[]{:S(2)}, u32[]{:S(2)}) collective-permute-start(bf16[128,512]{1,0:T(8,128)(2,1)S(1)} %bitcast.72), channel_id=1, source_target_pairs={{0,2},{1,3},{2,0},{3,1},{4,6},{5,7},{6,4},{7,5},{8,10},{9,11},{10,... | collective-permute-start | bytes 393224 | tf_op jit(solution)/shard_map/ppermute | solution.py:243
  14.2 8.8 %collective-permute-start.3 = (bf16[128,512]{1,0:T(8,128)(2,1)S(1)}, bf16[128,512]{1,0:T(8,128)(2,1)}, u32[]{:S(2)}, u32[]{:S(2)}) collective-permute-start(bf16[128,512]{1,0:T(8,128)(2,1)S(1)} %bitcast.71), channel_id=1, source_target_pairs={{0,1},{1,0},{2,3},{3,2},{4,5},{5,4},{6,7},{7,6},{8,9},{9,8},{10,11... | collective-permute-start | bytes 393224 | tf_op jit(solution)/shard_map/ppermute | solution.py:243
  15.2 9.9 %copy-start.3 = (bf16[128,2048]{1,0:T(8,128)(2,1)S(1)}, bf16[128,2048]{1,0:T(8,128)(2,1)}, u32[]{:S(2)}) copy-start(bf16[128,2048]{1,0:T(8,128)(2,1)} %refs_0_.1) | copy-start | bytes 1572868
  15.2 16.2 %copy-start.7 = (bf16[128,2048]{1,0:T(8,128)(2,1)S(1)}, bf16[128,2048]{1,0:T(8,128)(2,1)}, u32[]{:S(2)}) copy-start(bf16[128,2048]{1,0:T(8,128)(2,1)} %refs_5_.2) | copy-start | bytes 1572868
  15.5 9.5 %collective-permute-start.17 = (bf16[64,512]{1,0:T(8,128)(2,1)S(1)}, bf16[64,512]{1,0:T(8,128)(2,1)S(1)}, u32[]{:S(2)}, u32[]{:S(2)}) collective-permute-start(bf16[64,512]{1,0:T(8,128)(2,1)S(1)} %bitcast.80), channel_id=1, source_target_pairs={{0,12},{1,13},{2,14},{3,15},{4,8},{5,9},{6,10},{7,11},{8,4},{9,5},... | collective-permute-start | bytes 196616 | tf_op jit(solution)/shard_map/ppermute | solution.py:246
  20.9 5.5 %collective-permute-start.16 = (bf16[64,512]{1,0:T(8,128)(2,1)S(1)}, bf16[64,512]{1,0:T(8,128)(2,1)S(1)}, u32[]{:S(2)}, u32[]{:S(2)}) collective-permute-start(bf16[64,512]{1,0:T(8,128)(2,1)S(1)} %bitcast.81), channel_id=1, source_target_pairs={{0,8},{1,9},{2,10},{3,11},{4,12},{5,13},{6,14},{7,15},{8,0},{9,1},... | collective-permute-start | bytes 196616 | tf_op jit(solution)/shard_map/ppermute | solution.py:246
  21.4 5.6 %collective-permute-start.15 = (bf16[64,512]{1,0:T(8,128)(2,1)}, bf16[64,512]{1,0:T(8,128)(2,1)S(1)}, u32[]{:S(2)}, u32[]{:S(2)}) collective-permute-start(bf16[64,512]{1,0:T(8,128)(2,1)} %bitcast.10), channel_id=1, source_target_pairs={{0,4},{1,5},{2,6},{3,7},{4,0},{5,1},{6,2},{7,3},{8,12},{9,13},{10,... | collective-permute-start | bytes 196616 | tf_op jit(solution)/shard_map/ppermute | solution.py:246
  23.0 6.9 %collective-permute-start.27 = (bf16[128,512]{1,0:T(8,128)(2,1)S(1)}, bf16[128,512]{1,0:T(8,128)(2,1)S(1)}, u32[]{:S(2)}, u32[]{:S(2)}) collective-permute-start(bf16[128,512]{1,0:T(8,128)(2,1)S(1)} %bitcast.76), channel_id=1, source_target_pairs={{0,3},{1,2},{2,1},{3,0},{4,7},{5,6},{6,5},{7,4},{8,11},{9,10},{10,... | collective-permute-start | bytes 393224 | tf_op jit(solution)/shard_map/ppermute | solution.py:243
  25.1 30.6 %collective-permute-start = (bf16[128,2048]{1,0:T(8,128)(2,1)S(1)}, bf16[128,2048]{1,0:T(8,128)(2,1)S(1)}, u32[]{:S(2)}, u32[]{:S(2)}) collective-permute-start(bf16[128,2048]{1,0:T(8,128)(2,1)S(1)} %copy-done.3), channel_id=1, source_target_pairs={{0,1},{1,0},{2,3},{3,2},{4,5},{5,4},{6,7},{7,6},{8,9},{9,8},{10,11... | collective-permute-start | bytes 1572872 | tf_op jit(solution)/shard_map/ppermute | solution.py:243
  26.5 13.8 %collective-permute-start.6 = (bf16[256,512]{1,0:T(8,128)(2,1)}, bf16[256,512]{1,0:T(8,128)(2,1)S(1)}, u32[]{:S(2)}, u32[]{:S(2)}) collective-permute-start(bf16[256,512]{1,0:T(8,128)(2,1)} %bitcast.6), channel_id=1, source_target_pairs={{0,4},{1,5},{2,6},{3,7},{4,0},{5,1},{6,2},{7,3},{8,12},{9,13},{10,... | collective-permute-start | bytes 786440 | tf_op jit(solution)/shard_map/ppermute | solution.py:246
  27.0 14.8 %collective-permute-start.7 = (bf16[256,512]{1,0:T(8,128)(2,1)}, bf16[256,512]{1,0:T(8,128)(2,1)S(1)}, u32[]{:S(2)}, u32[]{:S(2)}) collective-permute-start(bf16[256,512]{1,0:T(8,128)(2,1)} %bitcast.6), channel_id=1, source_target_pairs={{0,8},{1,9},{2,10},{3,11},{4,12},{5,13},{6,14},{7,15},{8,0},{9,1},... | collective-permute-start | bytes 786440 | tf_op jit(solution)/shard_map/ppermute | solution.py:246
  29.9 6.6 %collective-permute-start.18 = (bf16[3,64,512]{2,1,0:T(8,128)(2,1)}, bf16[3,64,512]{2,1,0:T(8,128)(2,1)}, u32[]{:S(2)}, u32[]{:S(2)}) collective-permute-start(bf16[3,64,512]{2,1,0:T(8,128)(2,1)} %pad_maximum_fusion.2), channel_id=1, source_target_pairs={{0,16},{16,0},{1,17},{17,1},{2,18},{18,2},{3,19},{19,3},{4,20},{20... | collective-permute-start | bytes 589832 | tf_op jit(solution)/shard_map/ppermute | solution.py:249
  36.5 11.5 %collective-permute-start.8 = (bf16[256,512]{1,0:T(8,128)(2,1)}, bf16[256,512]{1,0:T(8,128)(2,1)S(1)}, u32[]{:S(2)}, u32[]{:S(2)}) collective-permute-start(bf16[256,512]{1,0:T(8,128)(2,1)} %bitcast.6), channel_id=1, source_target_pairs={{0,12},{1,13},{2,14},{3,15},{4,8},{5,9},{6,10},{7,11},{8,4},{9,5},... | collective-permute-start | bytes 786440 | tf_op jit(solution)/shard_map/ppermute | solution.py:246
  40.3 18.6 %collective-permute-start.9 = (bf16[256,512]{1,0:T(8,128)(2,1)S(1)}, bf16[256,512]{1,0:T(8,128)(2,1)}, u32[]{:S(2)}, u32[]{:S(2)}) collective-permute-start(bf16[256,512]{1,0:T(8,128)(2,1)S(1)} %collective-permute-done.6.refs_5_), channel_id=1, source_target_pairs={{0,16},{16,0},{1,17},{17,1},{2,18},{18,2},{3,19},{19,3},{4,20},{20... | collective-permute-start | bytes 786440 | tf_op jit(solution)/shard_map/ppermute | solution.py:249
  41.8 17.1 %collective-permute-start.10 = (bf16[256,512]{1,0:T(8,128)(2,1)S(1)}, bf16[256,512]{1,0:T(8,128)(2,1)}, u32[]{:S(2)}, u32[]{:S(2)}) collective-permute-start(bf16[256,512]{1,0:T(8,128)(2,1)S(1)} %collective-permute-done.7.refs_6_), channel_id=1, source_target_pairs={{0,16},{16,0},{1,17},{17,1},{2,18},{18,2},{3,19},{19,3},{4,20},{20... | collective-permute-start | bytes 786440 | tf_op jit(solution)/shard_map/ppermute | solution.py:249
  43.3 26.6 %collective-permute-start.2 = (bf16[128,2048]{1,0:T(8,128)(2,1)S(1)}, bf16[128,2048]{1,0:T(8,128)(2,1)S(1)}, u32[]{:S(2)}, u32[]{:S(2)}) collective-permute-start(bf16[128,2048]{1,0:T(8,128)(2,1)S(1)} %collective-permute-done.1.refs_2_), channel_id=1, source_target_pairs={{0,1},{1,0},{2,3},{3,2},{4,5},{5,4},{6,7},{7,6},{8,9},{9,8},{10,11... | collective-permute-start | bytes 1572872 | tf_op jit(solution)/shard_map/ppermute | solution.py:243
  48.0 26.5 %collective-permute-start.28 = (bf16[128,1024]{1,0:T(8,128)(2,1)}, bf16[128,1024]{1,0:T(8,128)(2,1)}, u32[]{:S(2)}, u32[]{:S(2)}) collective-permute-start(bf16[128,1024]{1,0:T(8,128)(2,1)} %constant_dynamic-slice_fusion), channel_id=1, source_target_pairs={{0,4},{1,5},{2,6},{3,7},{4,0},{5,1},{6,2},{7,3},{8,12},{9,13},{10,... | collective-permute-start | bytes 786440 | tf_op jit(solution)/shard_map/ppermute | solution.py:246
  55.6 22.0 %collective-permute-start.29 = (bf16[128,1024]{1,0:T(8,128)(2,1)}, bf16[128,1024]{1,0:T(8,128)(2,1)}, u32[]{:S(2)}, u32[]{:S(2)}) collective-permute-start(bf16[128,1024]{1,0:T(8,128)(2,1)} %constant_dynamic-slice_fusion), channel_id=1, source_target_pairs={{0,8},{1,9},{2,10},{3,11},{4,12},{5,13},{6,14},{7,15},{8,0},{9,1},... | collective-permute-start | bytes 786440 | tf_op jit(solution)/shard_map/ppermute | solution.py:246
  58.9 18.7 %collective-permute-start.30 = (bf16[128,1024]{1,0:T(8,128)(2,1)}, bf16[128,1024]{1,0:T(8,128)(2,1)}, u32[]{:S(2)}, u32[]{:S(2)}) collective-permute-start(bf16[128,1024]{1,0:T(8,128)(2,1)} %constant_dynamic-slice_fusion), channel_id=1, source_target_pairs={{0,12},{1,13},{2,14},{3,15},{4,8},{5,9},{6,10},{7,11},{8,4},{9,5},... | collective-permute-start | bytes 786440 | tf_op jit(solution)/shard_map/ppermute | solution.py:246
  58.9 8.2 %collective-permute-start.11 = (bf16[256,512]{1,0:T(8,128)(2,1)S(1)}, bf16[256,512]{1,0:T(8,128)(2,1)S(1)}, u32[]{:S(2)}, u32[]{:S(2)}) collective-permute-start(bf16[256,512]{1,0:T(8,128)(2,1)S(1)} %collective-permute-done.8.refs_7_), channel_id=1, source_target_pairs={{0,16},{16,0},{1,17},{17,1},{2,18},{18,2},{3,19},{19,3},{4,20},{20... | collective-permute-start | bytes 786440 | tf_op jit(solution)/shard_map/ppermute | solution.py:249
  67.8 16.5 %collective-permute-start.19 = (bf16[4,128,128]{2,1,0:T(8,128)(2,1)}, bf16[4,128,128]{2,1,0:T(8,128)(2,1)}, u32[]{:S(2)}, u32[]{:S(2)}) collective-permute-start(bf16[4,128,128]{2,1,0:T(8,128)(2,1)} %bitcast.54), channel_id=1, source_target_pairs={{0,1},{1,0},{2,3},{3,2},{4,5},{5,4},{6,7},{7,6},{8,9},{9,8},{10,11... | collective-permute-start | bytes 393224 | tf_op jit(solution)/shard_map/ppermute | solution.py:243
  68.9 16.9 %copy-start.13 = (bf16[128,4,128]{2,1,0:T(4,128)(2,1)S(1)}, bf16[128,4,128]{2,1,0:T(4,128)(2,1)}, u32[]{:S(2)}) copy-start(bf16[128,4,128]{2,1,0:T(4,128)(2,1)} %get-tuple-element.30) | copy-start | bytes 393220
  69.9 26.4 %copy-start.1 = (bf16[17,256,256]{2,1,0:T(8,128)(2,1)S(1)}, bf16[17,256,256]{2,1,0:T(8,128)(2,1)}, u32[]{:S(2)}) copy-start(bf16[17,256,256]{2,1,0:T(8,128)(2,1)} %constant.142.clone.refs_5_.refs_9_) | copy-start | bytes 6684676
  69.9 26.4 %copy-start.2 = (bf16[512,256]{1,0:T(8,128)(2,1)S(1)}, bf16[512,256]{1,0:T(8,128)(2,1)}, u32[]{:S(2)}) copy-start(bf16[512,256]{1,0:T(8,128)(2,1)} %constant.141.clone.refs_4_.refs_7_) | copy-start | bytes 786436
  69.9 15.9 %collective-permute-start.20 = (bf16[4,128,128]{2,1,0:T(8,128)(2,1)S(1)}, bf16[4,128,128]{2,1,0:T(8,128)(2,1)S(1)}, u32[]{:S(2)}, u32[]{:S(2)}) collective-permute-start(bf16[4,128,128]{2,1,0:T(8,128)(2,1)S(1)} %bitcast.70), channel_id=1, source_target_pairs={{0,2},{1,3},{2,0},{3,1},{4,6},{5,7},{6,4},{7,5},{8,10},{9,11},{10,... | collective-permute-start | bytes 393224 | tf_op jit(solution)/shard_map/ppermute | solution.py:243
  72.0 13.8 %copy-start.12 = (bf16[128,4,128]{2,1,0:T(4,128)(2,1)S(1)}, bf16[128,4,128]{2,1,0:T(4,128)(2,1)}, u32[]{:S(2)}) copy-start(bf16[128,4,128]{2,1,0:T(4,128)(2,1)} %get-tuple-element.31) | copy-start | bytes 393220
  72.0 15.2 %copy-start.9 = (bf16[4,128,1,128]{3,2,1,0:T(2,128)(2,1)S(1)}, bf16[4,128,1,128]{3,2,1,0:T(2,128)(2,1)}, u32[]{:S(2)}) copy-start(bf16[4,128,1,128]{3,2,1,0:T(2,128)(2,1)} %get-tuple-element.38) | copy-start | bytes 393220
  74.6 12.7 %collective-permute-start.21 = (bf16[4,128,128]{2,1,0:T(8,128)(2,1)S(1)}, bf16[4,128,128]{2,1,0:T(8,128)(2,1)S(1)}, u32[]{:S(2)}, u32[]{:S(2)}) collective-permute-start(bf16[4,128,128]{2,1,0:T(8,128)(2,1)S(1)} %bitcast.69), channel_id=1, source_target_pairs={{0,3},{1,2},{2,1},{3,0},{4,7},{5,6},{6,5},{7,4},{8,11},{9,10},{10,... | collective-permute-start | bytes 393224 | tf_op jit(solution)/shard_map/ppermute | solution.py:243
  77.6 10.7 %collective-permute-start.12 = (bf16[512,128]{1,0:T(8,128)(2,1)S(1)}, bf16[512,128]{1,0:T(8,128)(2,1)S(1)}, u32[]{:S(2)}, u32[]{:S(2)}) collective-permute-start(bf16[512,128]{1,0:T(8,128)(2,1)S(1)} %get-tuple-element.18), channel_id=1, source_target_pairs={{0,4},{1,5},{2,6},{3,7},{4,0},{5,1},{6,2},{7,3},{8,12},{9,13},{10,... | collective-permute-start | bytes 393224 | tf_op jit(solution)/shard_map/ppermute | solution.py:246
  77.6 16.7 %collective-permute-start.13 = (bf16[512,128]{1,0:T(8,128)(2,1)S(1)}, bf16[512,128]{1,0:T(8,128)(2,1)S(1)}, u32[]{:S(2)}, u32[]{:S(2)}) collective-permute-start(bf16[512,128]{1,0:T(8,128)(2,1)S(1)} %get-tuple-element.19), channel_id=1, source_target_pairs={{0,8},{1,9},{2,10},{3,11},{4,12},{5,13},{6,14},{7,15},{8,0},{9,1},... | collective-permute-start | bytes 393224 | tf_op jit(solution)/shard_map/ppermute | solution.py:246
  84.4 10.5 %collective-permute-start.14 = (bf16[512,128]{1,0:T(8,128)(2,1)S(1)}, bf16[512,128]{1,0:T(8,128)(2,1)S(1)}, u32[]{:S(2)}, u32[]{:S(2)}) collective-permute-start(bf16[512,128]{1,0:T(8,128)(2,1)S(1)} %get-tuple-element.20), channel_id=1, source_target_pairs={{0,12},{1,13},{2,14},{3,15},{4,8},{5,9},{6,10},{7,11},{8,4},{9,5},... | collective-permute-start | bytes 393224 | tf_op jit(solution)/shard_map/ppermute | solution.py:246
  85.8 18.7 %collective-permute-start.31 = (bf16[128,1024]{1,0:T(8,128)(2,1)}, bf16[128,1024]{1,0:T(8,128)(2,1)S(1)}, u32[]{:S(2)}, u32[]{:S(2)}) collective-permute-start(bf16[128,1024]{1,0:T(8,128)(2,1)} %collective-permute-done.28.refs_6_), channel_id=1, source_target_pairs={{0,16},{16,0},{1,17},{17,1},{2,18},{18,2},{3,19},{19,3},{4,20},{20... | collective-permute-start | bytes 786440 | tf_op jit(solution)/shard_map/ppermute | solution.py:249
  87.2 11.1 %copy-start.6 = (bf16[256,512]{1,0:T(8,128)(2,1)S(1)}, bf16[256,512]{1,0:T(8,128)(2,1)}, u32[]{:S(2)}) copy-start(bf16[256,512]{1,0:T(8,128)(2,1)} %constant.143.clone.refs_8_) | copy-start | bytes 786436
  87.2 15.3 %collective-permute-start.26 = (bf16[128,512]{1,0:T(8,128)(2,1)S(1)}, bf16[128,512]{1,0:T(8,128)(2,1)S(1)}, u32[]{:S(2)}, u32[]{:S(2)}) collective-permute-start(bf16[128,512]{1,0:T(8,128)(2,1)S(1)} %bitcast.75), channel_id=1, source_target_pairs={{0,2},{1,3},{2,0},{3,1},{4,6},{5,7},{6,4},{7,5},{8,10},{9,11},{10,... | collective-permute-start | bytes 393224 | tf_op jit(solution)/shard_map/ppermute | solution.py:243
  88.3 15.2 %collective-permute-start.25 = (bf16[128,512]{1,0:T(8,128)(2,1)S(1)}, bf16[128,512]{1,0:T(8,128)(2,1)S(1)}, u32[]{:S(2)}, u32[]{:S(2)}) collective-permute-start(bf16[128,512]{1,0:T(8,128)(2,1)S(1)} %bitcast.74), channel_id=1, source_target_pairs={{0,1},{1,0},{2,3},{3,2},{4,5},{5,4},{6,7},{7,6},{8,9},{9,8},{10,11... | collective-permute-start | bytes 393224 | tf_op jit(solution)/shard_map/ppermute | solution.py:243
  94.3 12.8 %collective-permute-start.32 = (bf16[128,1024]{1,0:T(8,128)(2,1)}, bf16[128,1024]{1,0:T(8,128)(2,1)S(1)}, u32[]{:S(2)}, u32[]{:S(2)}) collective-permute-start(bf16[128,1024]{1,0:T(8,128)(2,1)} %collective-permute-done.29.refs_7_), channel_id=1, source_target_pairs={{0,16},{16,0},{1,17},{17,1},{2,18},{18,2},{3,19},{19,3},{4,20},{20... | collective-permute-start | bytes 786440 | tf_op jit(solution)/shard_map/ppermute | solution.py:249
  94.8 12.3 %collective-permute-start.33 = (bf16[128,1024]{1,0:T(8,128)(2,1)}, bf16[128,1024]{1,0:T(8,128)(2,1)S(1)}, u32[]{:S(2)}, u32[]{:S(2)}) collective-permute-start(bf16[128,1024]{1,0:T(8,128)(2,1)} %collective-permute-done.30.refs_8_), channel_id=1, source_target_pairs={{0,16},{16,0},{1,17},{17,1},{2,18},{18,2},{3,19},{19,3},{4,20},{20... | collective-permute-start | bytes 786440 | tf_op jit(solution)/shard_map/ppermute | solution.py:249
  98.3 16.7 %copy-start.8 = (bf16[128,2048]{1,0:T(8,128)(2,1)S(1)}, bf16[128,2048]{1,0:T(8,128)(2,1)}, u32[]{:S(2)}) copy-start(bf16[128,2048]{1,0:T(8,128)(2,1)} %refs_5_.2) | copy-start | bytes 1572868
  102.5 7.3 %collective-permute-start.22 = (bf16[512,128]{1,0:T(8,128)(2,1)S(1)}, bf16[512,128]{1,0:T(8,128)(2,1)S(1)}, u32[]{:S(2)}, u32[]{:S(2)}) collective-permute-start(bf16[512,128]{1,0:T(8,128)(2,1)S(1)} %get-tuple-element.22), channel_id=1, source_target_pairs={{0,4},{1,5},{2,6},{3,7},{4,0},{5,1},{6,2},{7,3},{8,12},{9,13},{10,... | collective-permute-start | bytes 393224 | tf_op jit(solution)/shard_map/ppermute | solution.py:246
  103.5 11.5 %collective-permute-start.23 = (bf16[512,128]{1,0:T(8,128)(2,1)S(1)}, bf16[512,128]{1,0:T(8,128)(2,1)S(1)}, u32[]{:S(2)}, u32[]{:S(2)}) collective-permute-start(bf16[512,128]{1,0:T(8,128)(2,1)S(1)} %get-tuple-element.23), channel_id=1, source_target_pairs={{0,8},{1,9},{2,10},{3,11},{4,12},{5,13},{6,14},{7,15},{8,0},{9,1},... | collective-permute-start | bytes 393224 | tf_op jit(solution)/shard_map/ppermute | solution.py:246
  104.6 10.4 %collective-permute-start.24 = (bf16[512,128]{1,0:T(8,128)(2,1)S(1)}, bf16[512,128]{1,0:T(8,128)(2,1)S(1)}, u32[]{:S(2)}, u32[]{:S(2)}) collective-permute-start(bf16[512,128]{1,0:T(8,128)(2,1)S(1)} %get-tuple-element.24), channel_id=1, source_target_pairs={{0,12},{1,13},{2,14},{3,15},{4,8},{5,9},{6,10},{7,11},{8,4},{9,5},... | collective-permute-start | bytes 393224 | tf_op jit(solution)/shard_map/ppermute | solution.py:246
  118.2 1.9 %collective-permute-start.35 = (bf16[128,2048]{1,0:T(8,128)(2,1)S(1)}, bf16[128,2048]{1,0:T(8,128)(2,1)S(1)}, u32[]{:S(2)}, u32[]{:S(2)}) collective-permute-start(bf16[128,2048]{1,0:T(8,128)(2,1)S(1)} %get-tuple-element.28), channel_id=1, source_target_pairs={{0,1},{1,0},{2,3},{3,2},{4,5},{5,4},{6,7},{7,6},{8,9},{9,8},{10,11... | collective-permute-start | bytes 1572872 | tf_op jit(solution)/shard_map/ppermute | solution.py:243
  118.2 4.3 %collective-permute-start.34 = (bf16[128,2048]{1,0:T(8,128)(2,1)S(1)}, bf16[128,2048]{1,0:T(8,128)(2,1)S(1)}, u32[]{:S(2)}, u32[]{:S(2)}) collective-permute-start(bf16[128,2048]{1,0:T(8,128)(2,1)S(1)} %get-tuple-element.26), channel_id=1, source_target_pairs={{0,1},{1,0},{2,3},{3,2},{4,5},{5,4},{6,7},{7,6},{8,9},{9,8},{10,11... | collective-permute-start | bytes 1572872 | tf_op jit(solution)/shard_map/ppermute | solution.py:243
  121.5 14.0 %collective-permute-start.36 = (bf16[128,2048]{1,0:T(8,128)(2,1)S(1)}, bf16[128,2048]{1,0:T(8,128)(2,1)S(1)}, u32[]{:S(2)}, u32[]{:S(2)}) collective-permute-start(bf16[128,2048]{1,0:T(8,128)(2,1)S(1)} %add_convert_fusion.1), channel_id=1, source_target_pairs={{0,2},{1,3},{2,0},{3,1},{4,6},{5,7},{6,4},{7,5},{8,10},{9,11},{10,... | collective-permute-start | bytes 1572872 | tf_op jit(solution)/shard_map/ppermute | solution.py:243
  (7 other events, 28.6 us)

commit v2 on v1

--- a/solution.py
+++ b/solution.py
@@ -51,7 +51,7 @@
     return jnp.dot(left, right, preferred_element_type=jnp.float32)
 
 
-def call(kernel, outs, scratch, pos, args, flops):
+def call(kernel, outs, scratch, pos, args, flops, vmem=4):
     in_specs = [pl.BlockSpec(memory_space=pltpu.SMEM)]
     in_specs += [pl.BlockSpec(memory_space=pltpu.VMEM)] * len(args)
     moved = sum(a.size * a.dtype.itemsize for a in args)
@@ -62,7 +62,7 @@
         in_specs=in_specs,
         out_specs=[pl.BlockSpec(memory_space=pltpu.VMEM)] * len(outs),
         scratch_shapes=scratch,
-        compiler_params=pltpu.CompilerParams(vmem_limit_bytes=48 * MIB),
+        compiler_params=pltpu.CompilerParams(vmem_limit_bytes=vmem * MIB),
         cost_estimate=pl.CostEstimate(flops=flops, bytes_accessed=moved, transcendentals=0),
     )(pos, *args)
 
@@ -72,30 +72,107 @@
     return pl.multiple_of(block * rows, rows)
 
 
+def split_kernel(share, pos, src, *outs):
+    rows = src.shape[0]
+    for d in range(PLANE):
+        out = outs[min(d, len(outs) - 1)]
+        first = (d - len(outs) + 1) * rows if d >= len(outs) else 0
+        place = jnp.bitwise_xor(pos[2], d)
+        for p in range(out.shape[1] // share):
+            at = pl.multiple_of((p * PLANE + place) * share, share)
+            out[first : first + rows, p * share : (p + 1) * share] = src[:, pl.ds(at, share)]
+
+
+def filter_kernel(pos, taps, own, whole, half):
+    wide = own.shape[1]
+    part = half.shape[0]
+
+    def columns(s):
+        return pl.ds(pl.multiple_of(jnp.bitwise_xor(pos[1], s) * wide, wide), wide)
+
+    own[...] = taps[:, columns(0)]
+    whole[...] = taps[:, columns(1 + pos[0])]
+    half[...] = taps[pl.ds(pl.multiple_of(pos[0] * part, part), part), columns(3)]
+
+
+def half_kernel(pos, *refs):
+    parts, (whole, half), (out, lower, upper, joined) = refs[:PLANE], refs[PLANE:-4], refs[-4:]
+    deep = parts[0].shape[0]
+    for y in range(2):
+
+        @pl.when(pos[0] == y)
+        def _():
+            for j, far in enumerate((lower, upper)):
+                out[j * deep : (j + 1) * deep, :] = parts[2 * y + j][...]
+                far[...] = parts[2 * y + j][...]
+
+    joined[: whole.shape[0], :] = whole[...]
+    joined[whole.shape[0] :, :] = half[...]
+
+
+def join(out, parts):
+    at = 0
+    for part in parts:
+        out[at : at + part.shape[0], :] = part[...]
+        at += part.shape[0]
+
+
+def join_kernel(pos, near, far_a, far_b, x, from_x, weight, *outs):
+    got, passed, both_x, out_a, out_b, out_half = outs
+    join(got, (near, far_a, far_b))
+    join(passed, (far_a, far_b))
+    join(both_x, (x, from_x))
+    part, width = out_a.shape
+    columns = pl.ds(pl.multiple_of(pos[0] * width, width), width)
+    out_a[...] = weight[:part, columns]
+    out_b[...] = weight[part:, columns]
+    out_half[...] = weight[:, columns]
+
+
+def pair_kernel(pos, first, second, out):
+    join(out, (first, second))
+
+
+def places_kernel(pos, own, mine, other, *outs):
+    planes, rows, share = outs[0].shape
+    part = rows // 2
+    for d, out in enumerate(outs):
+        columns = pl.ds(pl.multiple_of(jnp.bitwise_xor(pos[2], d) * share, share), share)
+        out[0] = own[:, columns]
+        for side, block in ((pos[0], mine), (1 - pos[0], other)):
+            out[1 + side] = block[:rows, columns]
+            out[3, pl.ds(pl.multiple_of(side * part, part), part), :] = block[rows:, columns]
+
+
 def project_kernel(planes, pos, *refs):
-    x = refs[:PLANE]
-    own = refs[PLANE]
-    mine = refs[PLANE + 1 : PLANE + planes]
-    other = refs[PLANE + planes : PLANE + 2 * planes - 1]
-    outs = refs[PLANE + 2 * planes - 1 : PLANE + 3 * planes - 1]
-    xs, ws, ps = refs[PLANE + 3 * planes - 1 :]
-    rows = x[0].shape[0]
-    deep = own.shape[1]
+    x, from_x, beside = refs[:3]
+    own, halves = refs[3 : 3 + PLANE], refs[3 + PLANE : 7 + PLANE]
+    out_near, out_a, out_b = refs[7 + PLANE : 10 + PLANE]
+    outs, (out_got, out_passed) = refs[10 + PLANE : 10 + PLANE + planes], refs[-5:-3]
+    xs, ws, ps = refs[-3:]
+    rows = x.shape[0]
+    deep = own[0].shape[0]
     share = outs[0].shape[1]
-    half = PLANE // 2
-    y = pos[0]
+
+    def put(s, d, block):
+        ws[pl.ds(block_at(pos, s, d, deep), deep), :] = block
+
+    join(xs, (x, beside.at[:rows], from_x, beside.at[rows:]))
     for d in range(PLANE):
-        xs[d * rows : (d + 1) * rows, :] = x[d][...]
-        ws[pl.ds(block_at(pos, 0, d, deep), deep), :] = own[d]
-    for s in range(1, planes):
-        for j in range(half):
-            for side, part in ((y, mine[s - 1]), (1 - y, other[s - 1])):
-                at = block_at(pos, s, side * half + j, deep)
-                ws[pl.ds(at, deep), :] = part[j * deep : (j + 1) * deep, :]
+        put(0, d, own[d][...])
+    for k in range(2):
+        got, passed = halves[2 * k : 2 * k + 2]
+        d = 2 * (pos[0] if k == 0 else 1 - pos[0])
+        for i, (s, j) in enumerate(((1, 0), (1, 1), (2, 0), (3, 1))):
+            put(s, d + j, got[i * deep : (i + 1) * deep, :])
+        put(3, d, passed[:deep, :])
+        put(2, d + 1, passed[deep:, :])
     ps[...] = dot(xs[...], ws[...]).astype(ps.dtype)
     for s in range(planes):
         at = pl.multiple_of(jnp.bitwise_xor(pos[1], s) * share, share)
         outs[s][...] = ps[:, pl.ds(at, share)]
+    join(out_got, (out_near, out_a, out_b))
+    join(out_passed, (out_a, out_b))
 
 
 def forward_stage(signal, first, work, blocks, rows):
@@ -140,8 +217,8 @@
 def conv_kernel(blocks, planes, pos, *refs):
     parts = refs[:planes]
     taps, skip, response, first, last, turned, back = refs[planes : planes + 7]
-    outs = refs[planes + 7 : 2 * planes + 7]
-    wide, value, work, result = refs[2 * planes + 7 :]
+    outs = refs[planes + 7 : 3 * planes + 7]
+    wide, value, work, result = refs[3 * planes + 7 :]
     rows = value.shape[0] // blocks
     share = value.shape[1]
     lead = wide.shape[0] - value.shape[0]
@@ -192,38 +269,50 @@
                 ).astype(result.dtype)
     for s in range(planes):
         for d in range(PLANE):
-            outs[s][d * rows : (d + 1) * rows, :] = result[
+            half, at = d // 2, d % 2 * rows
+            outs[half * planes + s][at : at + rows, :] = result[
                 pl.ds(block_at(pos, s, d, rows), rows), :
             ]
 
 
-def output_kernel(planes, pos, *refs):
-    u = refs[:planes]
-    gate = refs[planes]
-    own = refs[planes + 1]
-    mine = refs[planes + 2 : 2 * planes + 1]
-    other = refs[2 * planes + 1 : 3 * planes]
-    outs = refs[3 * planes : 3 * planes + PLANE]
-    mixed, ws = refs[3 * planes + PLANE :]
+def mixed_dots(planes, pos, u, gate, ws, mixed, outs):
     share = u[0].shape[1]
-    rows = gate.shape[1]
-    half = mine[0].shape[1]
-    y = pos[0]
+    rows = gate[0].shape[0]
     for s in range(planes):
         at = pl.multiple_of(jnp.bitwise_xor(pos[1], s) * share, share)
-        for d in range(PLANE):
+        for d in range(2):
             mixed[d * rows : (d + 1) * rows, s * share : (s + 1) * share] = (
-                gate[d, :, pl.ds(at, share)].astype(jnp.float32)
+                gate[d][:, pl.ds(at, share)].astype(jnp.float32)
                 * u[s][d * rows : (d + 1) * rows, :].astype(jnp.float32)
             ).astype(mixed.dtype)
-        if s == 0:
-            ws[:share, :] = own[...]
-        else:
-            here = slice(s * share, (s + 1) * share)
-            ws[here, pl.ds(pl.multiple_of(y * half, half), half)] = mine[s - 1][...]
-            ws[here, pl.ds(pl.multiple_of((1 - y) * half, half), half)] = other[s - 1][...]
-    for d in range(PLANE):
-        outs[d][...] = dot(mixed[d * rows : (d + 1) * rows, :], ws[...]).astype(outs[d].dtype)
+    got = dot(mixed[...], ws[...])
+    for d in range(2):
+        outs[d][...] = got[d * rows : (d + 1) * rows].astype(outs[d].dtype)
+
+
+def upper_kernel(planes, pos, *refs):
+    u, gate = refs[:planes], refs[planes : planes + 2]
+    own, halves = refs[planes + 2], refs[planes + 3 : planes + 7]
+    outs, ws, mixed = refs[planes + 7 : planes + 9], refs[planes + 9], refs[planes + 10]
+    share = u[0].shape[1]
+    width = halves[0].shape[1]
+    part = share // 2
+    ws[:share, :] = own[...]
+    for k in range(2):
+        got, passed = halves[2 * k : 2 * k + 2]
+        side = pos[0] if k == 0 else 1 - pos[0]
+        columns = pl.ds(pl.multiple_of(side * width, width), width)
+        ws[share : 2 * share, columns] = got[:share, :]
+        ws[2 * share : 2 * share + part, columns] = got[share : share + part, :]
+        ws[2 * share + part : 3 * share, columns] = passed[part:, :]
+        ws[3 * share : 3 * share + part, columns] = passed[:part, :]
+        ws[3 * share + part :, columns] = got[share + part :, :]
+    mixed_dots(planes, pos, u, gate, ws, mixed, outs)
+
+
+def lower_kernel(planes, pos, *refs):
+    u, gate, ws = refs[:planes], refs[planes : planes + 2], refs[planes + 2]
+    mixed_dots(planes, pos, u, gate, ws, refs[planes + 5], refs[planes + 3 : planes + 5])
 
 
 def local(inputs, gate_in, value_weight, short_taps, filter_taps, skip_scale, output_weight):
@@ -248,84 +337,125 @@
     def to_group(block):
         return lax.ppermute(block, "groups", [(0, 1), (1, 0)])
 
-    def of_place(array, d):
-        cut = array.reshape(array.shape[0], planes, PLANE, share)
-        at = jnp.bitwise_xor(place, d)
-        return lax.dynamic_index_in_dim(cut, at, 2, keepdims=False).reshape(-1, wide)
-
-    def around(array):
-        parts = [of_place(array, 0)]
-        return parts + [to_place(of_place(array, d), d) for d in range(1, PLANE)]
-
-    first, last = stage_tables(blocks)
-    turned, back = turned_tables(blocks, rows)
-
-    value_parts = around(value_weight)
-    stacked = jnp.stack(value_parts)
-    half = PLANE // 2
-    sent = lax.dynamic_slice_in_dim(stacked, y * half, half, 0).reshape(half * deep, wide)
-    mine = [to_plane(sent, s) for s in range(1, planes)]
-    other = [to_group(block) for block in mine]
-    from_x = to_place(inputs, 2)
-    x_parts = [inputs, to_place(inputs, 1), from_x, to_place(from_x, 1)]
-
-    cut = filter_taps.reshape(rows, planes, PLANE * share)
-    part = rows // 2
-
-    def taps_for(s):
-        block = lax.dynamic_index_in_dim(cut, jnp.bitwise_xor(z, s), 1, keepdims=False)
-        return block if s == 0 else lax.dynamic_slice_in_dim(block, y * part, part, 0)
-
-    taps_mine = jnp.stack([to_plane(taps_for(s), s) for s in range(1, planes)])
+    def shaped(*shape, dtype=jnp.bfloat16):
+        return jax.ShapeDtypeStruct(shape, dtype)
+
+    def small(kernel, outs, *args):
+        return list(call(kernel, outs, [], pos, args, 0, vmem=2))
+
+    def split(array, *heights):
+        kernel = functools.partial(split_kernel, share)
+        return small(kernel, [shaped(rows * h, wide) for h in heights], array)
+
+    stage = lax.optimization_barrier
+    first, last, turned, back = (
+        jnp.asarray(t) for t in (*stage_tables(blocks), *turned_tables(blocks, rows))
+    )
+    part, width, positions = rows // 2, features // 2, blocks * rows
+
+    cut = split(value_weight, 1, 1, 1, 1)
+    taps_in, cut[0] = stage((filter_taps, cut[0]))
+    taps_own, taps_whole, taps_half = small(
+        filter_kernel, [shaped(rows, wide), shaped(rows, wide), shaped(part, wide)], taps_in
+    )
+    cut = [cut[0]] + [to_place(cut[d], d) for d in range(1, PLANE)]
+    route = [
+        (y0 * devices + i, y0 * devices + (i ^ (1 + y0) * PLANE))
+        for y0 in range(2)
+        for i in range(devices)
+    ]
+    taps_whole = lax.ppermute(taps_whole, ("groups", "seq"), route)
+    taps_half = to_plane(taps_half, 3)
+    cut, taps_whole, taps_half, late = stage((cut, taps_whole, taps_half, inputs))
+
+    sent, lower, upper, taps_mine = small(
+        half_kernel,
+        [shaped(2 * deep, wide), shaped(deep, wide), shaped(deep, wide), shaped(rows + part, wide)],
+        *cut,
+        taps_whole,
+        taps_half,
+    )
+    near, far_a, far_b = to_plane(sent, 1), to_plane(lower, 2), to_plane(upper, 3)
+    from_x = to_place(late, 2)
     taps_other = to_group(taps_mine)
-    taps_all = jnp.where(
-        y == 0,
-        jnp.concatenate([taps_mine, taps_other], 1),
-        jnp.concatenate([taps_other, taps_mine], 1),
-    )
-    taps_all = jnp.concatenate([taps_for(0)[None], taps_all], 0)
-    taps_all = taps_all.reshape(planes, rows, PLANE, share)
-    taps_parts = []
-    for d in range(PLANE):
-        block = lax.dynamic_index_in_dim(taps_all, jnp.bitwise_xor(place, d), 2, keepdims=False)
-        taps_parts.append(to_place(block, d) if d else block)
-    positions = blocks * rows
-    response = call(
-        functools.partial(taps_kernel, blocks, planes),
-        [jax.ShapeDtypeStruct((blocks + 1, 2 * rows, share), jnp.bfloat16)],
-        [
-            pltpu.VMEM((positions, share), jnp.bfloat16),
-            pltpu.VMEM((2 * blocks, rows, share), jnp.bfloat16),
-        ],
-        pos,
-        [*taps_parts, jnp.asarray(first), jnp.asarray(turned)],
-        2 * positions * share * (32 * ROWS + 4 * rows),
-    )[0]
-
-    gate = jnp.stack(around(gate_in))
-    width = output_weight.shape[1] // 2
-    out_half = lax.dynamic_slice_in_dim(output_weight, y * width, width, 1)
-    out_mine = [to_plane(out_half, s) for s in range(1, planes)]
-    out_other = [to_group(block) for block in out_mine]
-
-    projected = call(
+    near, far_a, far_b, from_x, taps_other, late = stage(
+        (near, far_a, far_b, from_x, taps_other, output_weight)
+    )
+
+    got, passed, both_x, out_a, out_b, out_half = small(
+        join_kernel,
+        [shaped(4 * deep, wide), shaped(2 * deep, wide), shaped(2 * rows, features)]
+        + [shaped(deep // 2, width), shaped(deep // 2, width), shaped(deep, width)],
+        near,
+        far_a,
+        far_b,
+        inputs,
+        from_x,
+        late,
+    )
+    passed = to_plane(passed, 1)
+    got_other = to_group(got)
+    out_a, out_b = to_plane(out_a, 2), to_plane(out_b, 3)
+    beside = to_place(both_x, 1)
+    taps_parts = small(
+        places_kernel, [shaped(planes, rows, share)] * PLANE, taps_own, taps_mine, taps_other
+    )
+    passed, got_other, out_a, out_b, beside, taps_parts, out_half = stage(
+        (passed, got_other, out_a, out_b, beside, taps_parts, out_half)
+    )
+
+    passed_other = to_group(passed)
+    out_near = to_plane(out_half, 1)
+    taps_parts = [taps_parts[0]] + [to_place(taps_parts[d], d) for d in range(1, PLANE)]
+    passed, passed_other, out_near, taps_parts, late = stage(
+        (passed, passed_other, out_near, taps_parts, gate_in)
+    )
+
+    gate_own, gate_beside, gate_x = split(late, 1, 1, 2)
+    *projected, out_got, out_passed = call(
         functools.partial(project_kernel, planes),
-        [jax.ShapeDtypeStruct((PLANE * rows, share), jnp.bfloat16)] * planes,
+        [shaped(PLANE * rows, share)] * planes + [shaped(2 * deep, width), shaped(deep, width)],
         [
             pltpu.VMEM((PLANE * rows, features), jnp.bfloat16),
             pltpu.VMEM((features, wide), jnp.bfloat16),
             pltpu.VMEM((PLANE * rows, wide), jnp.bfloat16),
         ],
         pos,
-        [*x_parts, stacked, *mine, *other],
+        [inputs, from_x, beside, *cut, got, passed, got_other, passed_other]
+        + [out_near, out_a, out_b],
         2 * PLANE * rows * features * wide,
-    )
-    signal = [projected[0]] + [to_plane(projected[s], s) for s in range(1, planes)]
+        vmem=12,
+    )
+    projected, out_got, out_passed, gate_x = stage((projected, out_got, out_passed, gate_x))
+
+    def spread(parts):
+        return [parts[0]] + [to_plane(parts[s], s) for s in range(1, planes)]
+
+    signal = spread(projected)
+    out_other = to_group(out_got)
+    gate_x = to_place(gate_x, 2)
+    response = call(
+        functools.partial(taps_kernel, blocks, planes),
+        [shaped(blocks + 1, 2 * rows, share)],
+        [
+            pltpu.VMEM((positions, share), jnp.bfloat16),
+            pltpu.VMEM((2 * blocks, rows, share), jnp.bfloat16),
+        ],
+        pos,
+        [*taps_parts, first, turned],
+        2 * positions * share * (32 * ROWS + 4 * rows),
+        vmem=8,
+    )[0]
     taps = lax.dynamic_slice_in_dim(short_taps, index * share, share, 1)
     skip = lax.dynamic_slice_in_dim(skip_scale, index * share, share, 0)[None]
+    signal, out_other, gate_x, response, taps, skip, out_passed = stage(
+        (signal, out_other, gate_x, response, taps, skip, out_passed)
+    )
+
+    out_passed = to_plane(out_passed, 1)
     mixed = call(
         functools.partial(conv_kernel, blocks, planes),
-        [jax.ShapeDtypeStruct((PLANE * rows, share), jnp.bfloat16)] * planes,
+        [shaped(2 * rows, share)] * (2 * planes),
         [
             pltpu.VMEM((positions + 8, share), jnp.float32),
             pltpu.VMEM((positions, share), jnp.bfloat16),
@@ -333,37 +463,48 @@
             pltpu.VMEM((positions, share), jnp.bfloat16),
         ],
         pos,
-        [
-            *signal,
-            taps,
-            skip,
-            response,
-            jnp.asarray(first),
-            jnp.asarray(last),
-            jnp.asarray(turned),
-            jnp.asarray(back),
-        ],
+        [*signal, taps, skip, response, first, last, turned, back],
         4 * positions * share * (32 * ROWS + 4 * rows),
-    )
-    spread = [mixed[0]] + [to_plane(mixed[s], s) for s in range(1, planes)]
-    partial = call(
-        functools.partial(output_kernel, planes),
-        [
-            jax.ShapeDtypeStruct((rows, features), jnp.bfloat16 if d % 2 else jnp.float32)
-            for d in range(PLANE)
-        ],
-        [
-            pltpu.VMEM((PLANE * rows, wide), jnp.bfloat16),
-            pltpu.VMEM((wide, features), jnp.bfloat16),
-        ],
+        vmem=12,
+    )
+    gate_beside = small(pair_kernel, [shaped(2 * rows, wide)], gate_beside, gate_x[rows:])[0]
+    mixed, out_passed, gate_beside = stage((mixed, out_passed, gate_beside))
+
+    upper = spread(mixed[planes:])
+    passed_other = to_group(out_passed)
+    gate_beside = to_place(gate_beside, 1)
+    upper, passed_other, gate_beside, lower = stage(
+        (upper, passed_other, gate_beside, mixed[:planes])
+    )
+    scratch = [pltpu.VMEM((2 * rows, wide), jnp.bfloat16)]
+    flops = 4 * rows * features * wide
+    partial_two, partial_three, gathered = call(
+        functools.partial(upper_kernel, planes),
+        [shaped(rows, features, dtype=jnp.float32), shaped(rows, features)]
+        + [shaped(wide, features)],
+        scratch,
         pos,
-        [*spread, gate, output_weight, *out_mine, *out_other],
-        2 * PLANE * rows * features * wide,
-    )
-    across = partial[2] + to_place(partial[3], 1).astype(jnp.float32)
-    across = to_place(across.astype(jnp.bfloat16), 2).astype(jnp.float32)
-    beside = to_place(partial[1], 1).astype(jnp.float32)
-    return (partial[0] + beside + across).astype(jnp.bfloat16)
+        [*upper, gate_x[:rows], gate_beside[rows:], output_weight]
+        + [out_got, out_passed, out_other, passed_other],
+        flops,
+        vmem=12,
+    )
+    across = partial_two + to_place(partial_three, 1).astype(jnp.float32)
+    across, lower = stage((across.astype(jnp.bfloat16), lower))
+
+    across = to_place(across, 2)
+    lower = spread(lower)
+    partial_zero, partial_one = call(
+        functools.partial(lower_kernel, planes),
+        [shaped(rows, features, dtype=jnp.float32), shaped(rows, features)],
+        scratch,
+        pos,
+        [*lower, gate_own, gate_beside[:rows], gathered],
+        flops,
+        vmem=12,
+    )
+    result = partial_zero + to_place(partial_one, 1).astype(jnp.float32)
+    return (result + across.astype(jnp.float32)).astype(jnp.bfloat16)
 
 
 def passed_along(block, axis, distance):
@@ -444,8 +585,8 @@
         devices = mesh.shape["seq"]
         share = args[2].shape[1] // devices
         tiled = share % LANES == 0 and args[0].shape[0] // mesh.size == LANES
-        paired = devices % PLANE == 0 and mesh.shape["groups"] == 2
-        body = local if tiled and paired and devices & (devices - 1) == 0 else local_narrow
+        paired = devices == 4 * PLANE and mesh.shape["groups"] == 2
+        body = local if tiled and paired else local_narrow
         return jax.shard_map(body, mesh=mesh, in_specs=placed, out_specs=split, check_vma=False)(
             *args
         )

time: 137 us -> 131 us (0.956)
  waiting for transfers between devices: 42 us -> 54.9 us
  local copies, waits for them, and re-layouts: 22.1 us -> 11.7 us
  other arithmetic: 9.38 us -> 1.16 us
  Pallas kernels: 11.9 us -> 14.3 us
  starting transfers between devices: 50.7 us -> 48.4 us
    ppermute x15 -> x18, waiting for transfers between devices: 19.7 us -> 40 us  [to_plane(): lax.ppermute(block, 'seq', [(i, i ^ s * PLANE) for i in range(devices)])]
    dynamic_slice x8 -> x0, local copies, waits for them, and re-layouts: 9.55 us -> none  [the longest x1 7 us: of_place(): lax.dynamic_index_in_dim(cut, at, 2, keepdims=False).reshape(-1, wide)]
    ppermute x7 -> x5, waiting for transfers between devices: 7.87 us -> 0.01 us  [to_group(): return lax.ppermute(block, 'groups', [(0, 1), (1, 0)])]
    ppermute x15 -> x18, starting transfers between devices: 33 us -> 25.9 us  [to_plane(): lax.ppermute(block, 'seq', [(i, i ^ s * PLANE) for i in range(devices)])]
    unnamed x49 -> x52, local copies, waits for them, and re-layouts: 4.84 us -> 10.9 us
    ppermute x7 -> x5, starting transfers between devices: 6.72 us -> 11.8 us  [to_group(): return lax.ppermute(block, 'groups', [(0, 1), (1, 0)])]
    concatenate x1 -> x0, other arithmetic: 3.45 us -> none  [local(): taps_all = jnp.concatenate([taps_for(0)[None], taps_all], 0)]
    reshape x2 -> x0, local copies, waits for them, and re-layouts: 2.8 us -> none  [of_place(): cut = array.reshape(array.shape[0], planes, PLANE, share)]
  transfers between devices with their start and end apart: 37 -> 37, of which waited for: 12 -> 12; matrix products, arithmetic and copies ran while one was open for 21% -> 1% of each run, Pallas kernels for 6% -> 6%
where the time goes in v2:
time: 131 us
  waiting for transfers between devices  54.9 us (42%)
  starting transfers between devices  48.4 us (37%)
  Pallas kernels  14.3 us (11%)
  local copies, waits for them, and re-layouts  11.7 us (9%)
    ppermute x18, waiting for transfers between devices, to_plane(): lax.ppermute(block, 'seq', [(i, i ^ s * PLANE) for i in range(devices)])  40 us
    ppermute x18, starting transfers between devices, to_plane(): lax.ppermute(block, 'seq', [(i, i ^ s * PLANE) for i in range(devices)])  25.9 us
    ppermute x13, waiting for transfers between devices, to_place(): return lax.ppermute(block, 'seq', [(i, i ^ d) for i in range(devices)])  14.9 us
    pallas_call x12, Pallas kernels, call(): pl.pallas_call(kernel, out_shape=outs, in_specs=in_specs, out_specs=[pl.B...  14.3 us
    ppermute x5, starting transfers between devices, to_group(): return lax.ppermute(block, 'groups', [(0, 1), (1, 0)])  11.8 us
    unnamed x52, local copies, waits for them, and re-layouts  10.9 us
    ppermute x13, starting transfers between devices, to_place(): return lax.ppermute(block, 'seq', [(i, i ^ d) for i in range(devices)])  8.82 us
  transfers between devices with their start and end apart: 37, of which 12 were waited for; matrix products, arithmetic and copies ran while one was open for 1% of the time, Pallas kernels for 6%

profile of v2, /device:TPU:0, one launch (start us, length us, event | category | flops | bytes accessed | tf_op | source)
XLA Modules:
  0.0 130.9 jit_solution(16540408108319570245)
XLA Ops:
  0.1 1.0 copy-done.8
  2.3 2.6 %collective-permute-start.1 = (bf16[128,512]{1,0:T(8,128)(2,1)S(1)}, bf16[128,512]{1,0:T(8,128)(2,1)S(1)}, u32[]{:S(2)}, u32[]{:S(2)}) collective-permute-start(bf16[128,512]{1,0:T(8,128)(2,1)S(1)} %get-tuple-element.126), channel_id=1, source_target_pairs={{0,2},{1,3},{2,0},{3,1},{4,6},{5,7},{6,4},{7,5},{8,10},{9,11},{10,... | collective-permute-start | bytes 393224 | tf_op jit(solution)/shard_map/ppermute | solution.py:332
  5.0 1.0 copy-done.9
  6.6 1.9 %collective-permute-start.3 = (bf16[128,512]{1,0:T(8,128)(2,1)S(1)}, bf16[128,512]{1,0:T(8,128)(2,1)S(1)}, u32[]{:S(2)}, u32[]{:S(2)}) collective-permute-start(bf16[128,512]{1,0:T(8,128)(2,1)S(1)} %get-tuple-element.129), channel_id=1, source_target_pairs={{0,4},{1,5},{2,6},{3,7},{4,0},{5,1},{6,2},{7,3},{8,12},{9,13},{10,... | collective-permute-start | bytes 393224 | tf_op jit(solution)/shard_map/ppermute | solution.py:367
  8.5 2.5 %collective-permute-start.4 = (bf16[64,512]{1,0:T(8,128)(2,1)S(1)}, bf16[64,512]{1,0:T(8,128)(2,1)S(1)}, u32[]{:S(2)}, u32[]{:S(2)}) collective-permute-start(bf16[64,512]{1,0:T(8,128)(2,1)S(1)} %get-tuple-element.130), channel_id=1, source_target_pairs={{0,12},{1,13},{2,14},{3,15},{4,8},{5,9},{6,10},{7,11},{8,4},{9,5},... | collective-permute-start | bytes 196616 | tf_op jit(solution)/shard_map/ppermute | solution.py:335
  10.9 5.1 %collective-permute-done.4.refs_5_ = bf16[64,512]{1,0:T(8,128)(2,1)S(1)} collective-permute-done((bf16[64,512]{1,0:T(8,128)(2,1)S(1)}, bf16[64,512]{1,0:T(8,128)(2,1)S(1)}, u32[]{:S(2)}, u32[]{:S(2)}) %collective-permute-start.4) | collective-permute-done | bytes 65568 | tf_op jit(solution)/shard_map/ppermute | solution.py:335
  16.1 1.6 %collective-permute-start.8 = (bf16[128,2048]{1,0:T(8,128)(2,1)}, bf16[128,2048]{1,0:T(8,128)(2,1)S(1)}, u32[]{:S(2)}, u32[]{:S(2)}) collective-permute-start(bf16[128,2048]{1,0:T(8,128)(2,1)} %refs_0_.1), channel_id=1, source_target_pairs={{0,2},{1,3},{2,0},{3,1},{4,6},{5,7},{6,4},{7,5},{8,10},{9,11},{10,... | collective-permute-start | bytes 1572872 | tf_op jit(solution)/shard_map/ppermute | solution.py:332
  18.3 5.3 %collective-permute-start.9 = (bf16[192,512]{1,0:T(8,128)(2,1)S(1)}, bf16[192,512]{1,0:T(8,128)(2,1)S(1)}, u32[]{:S(2)}, u32[]{:S(2)}) collective-permute-start(bf16[192,512]{1,0:T(8,128)(2,1)S(1)} %get-tuple-element.141.mine), channel_id=1, source_target_pairs={{0,16},{16,0},{1,17},{17,1},{2,18},{18,2},{3,19},{19,3},{4,20},{20... | collective-permute-start | bytes 589832 | tf_op jit(solution)/shard_map/ppermute | solution.py:338
  23.6 2.0 %collective-permute-start.6 = (bf16[128,512]{1,0:T(8,128)(2,1)S(1)}, bf16[128,512]{1,0:T(8,128)(2,1)S(1)}, u32[]{:S(2)}, u32[]{:S(2)}) collective-permute-start(bf16[128,512]{1,0:T(8,128)(2,1)S(1)} %get-tuple-element.138), channel_id=1, source_target_pairs={{0,8},{1,9},{2,10},{3,11},{4,12},{5,13},{6,14},{7,15},{8,0},{9,1},... | collective-permute-start | bytes 393224 | tf_op jit(solution)/shard_map/ppermute | solution.py:335
  25.6 1.4 %collective-permute-start.7 = (bf16[128,512]{1,0:T(8,128)(2,1)S(1)}, bf16[128,512]{1,0:T(8,128)(2,1)S(1)}, u32[]{:S(2)}, u32[]{:S(2)}) collective-permute-start(bf16[128,512]{1,0:T(8,128)(2,1)S(1)} %get-tuple-element.139), channel_id=1, source_target_pairs={{0,12},{1,13},{2,14},{3,15},{4,8},{5,9},{6,10},{7,11},{8,4},{9,5},... | collective-permute-start | bytes 393224 | tf_op jit(solution)/shard_map/ppermute | solution.py:335
  27.0 8.7 %collective-permute-done.6.far_a = bf16[128,512]{1,0:T(8,128)(2,1)S(1)} collective-permute-done((bf16[128,512]{1,0:T(8,128)(2,1)S(1)}, bf16[128,512]{1,0:T(8,128)(2,1)S(1)}, u32[]{:S(2)}, u32[]{:S(2)}) %collective-permute-start.6) | collective-permute-done | bytes 131104 | tf_op jit(solution)/shard_map/ppermute | solution.py:335
  35.7 1.0 copy-done.3
  36.7 1.0 copy-done.5
  38.5 3.0 %collective-permute-start.11 = (bf16[512,512]{1,0:T(8,128)(2,1)S(1)}, bf16[512,512]{1,0:T(8,128)(2,1)S(1)}, u32[]{:S(2)}, u32[]{:S(2)}) collective-permute-start(bf16[512,512]{1,0:T(8,128)(2,1)S(1)} %get-tuple-element.148.refs_7_), channel_id=1, source_target_pairs={{0,16},{16,0},{1,17},{17,1},{2,18},{18,2},{3,19},{19,3},{4,20},{20... | collective-permute-start | bytes 1572872 | tf_op jit(solution)/shard_map/ppermute | solution.py:338
  41.5 1.9 %collective-permute-start.12 = (bf16[64,1024]{1,0:T(8,128)(2,1)S(1)}, bf16[64,1024]{1,0:T(8,128)(2,1)S(1)}, u32[]{:S(2)}, u32[]{:S(2)}) collective-permute-start(bf16[64,1024]{1,0:T(8,128)(2,1)S(1)} %get-tuple-element.149), channel_id=1, source_target_pairs={{0,8},{1,9},{2,10},{3,11},{4,12},{5,13},{6,14},{7,15},{8,0},{9,1},... | collective-permute-start | bytes 393224 | tf_op jit(solution)/shard_map/ppermute | solution.py:335
  43.4 2.5 %collective-permute-start.13 = (bf16[64,1024]{1,0:T(8,128)(2,1)S(1)}, bf16[64,1024]{1,0:T(8,128)(2,1)S(1)}, u32[]{:S(2)}, u32[]{:S(2)}) collective-permute-start(bf16[64,1024]{1,0:T(8,128)(2,1)S(1)} %get-tuple-element.150), channel_id=1, source_target_pairs={{0,12},{1,13},{2,14},{3,15},{4,8},{5,9},{6,10},{7,11},{8,4},{9,5},... | collective-permute-start | bytes 393224 | tf_op jit(solution)/shard_map/ppermute | solution.py:335
  46.5 4.4 %collective-permute-done.12.refs_12_ = bf16[64,1024]{1,0:T(8,128)(2,1)S(1)} collective-permute-done((bf16[64,1024]{1,0:T(8,128)(2,1)S(1)}, bf16[64,1024]{1,0:T(8,128)(2,1)S(1)}, u32[]{:S(2)}, u32[]{:S(2)}) %collective-permute-start.12) | collective-permute-done | bytes 131104 | tf_op jit(solution)/shard_map/ppermute | solution.py:335
  51.0 5.7 %collective-permute-done.13.refs_13_ = bf16[64,1024]{1,0:T(8,128)(2,1)S(1)} collective-permute-done((bf16[64,1024]{1,0:T(8,128)(2,1)S(1)}, bf16[64,1024]{1,0:T(8,128)(2,1)S(1)}, u32[]{:S(2)}, u32[]{:S(2)}) %collective-permute-start.13) | collective-permute-done | bytes 131104 | tf_op jit(solution)/shard_map/ppermute | solution.py:335
  56.8 1.6 %collective-permute-start.15 = (bf16[256,512]{1,0:T(8,128)(2,1)S(1)}, bf16[256,512]{1,0:T(8,128)(2,1)S(1)}, u32[]{:S(2)}, u32[]{:S(2)}) collective-permute-start(bf16[256,512]{1,0:T(8,128)(2,1)S(1)} %collective-permute-done.10.refs_8_), channel_id=1, source_target_pairs={{0,16},{16,0},{1,17},{17,1},{2,18},{18,2},{3,19},{19,3},{4,20},{20... | collective-permute-start | bytes 786440 | tf_op jit(solution)/shard_map/ppermute | solution.py:338
  58.9 1.3 %collective-permute-start.19 = (bf16[4,128,128]{2,1,0:T(8,128)(2,1)S(1)}, bf16[4,128,128]{2,1,0:T(8,128)(2,1)S(1)}, u32[]{:S(2)}, u32[]{:S(2)}) collective-permute-start(bf16[4,128,128]{2,1,0:T(8,128)(2,1)S(1)} %get-tuple-element.165), channel_id=1, source_target_pairs={{0,3},{1,2},{2,1},{3,0},{4,7},{5,6},{6,5},{7,4},{8,11},{9,10},{10,... | collective-permute-start | bytes 393224 | tf_op jit(solution)/shard_map/ppermute | solution.py:332
  60.2 4.4 %collective-permute-done.18.refs_2_ = bf16[4,128,128]{2,1,0:T(8,128)(2,1)S(1)} collective-permute-done((bf16[4,128,128]{2,1,0:T(8,128)(2,1)S(1)}, bf16[4,128,128]{2,1,0:T(8,128)(2,1)S(1)}, u32[]{:S(2)}, u32[]{:S(2)}) %collective-permute-start.18) | collective-permute-done | bytes 131104 | tf_op jit(solution)/shard_map/ppermute | solution.py:332
  64.7 2.0 %collective-permute-done.19.refs_3_ = bf16[4,128,128]{2,1,0:T(8,128)(2,1)S(1)} collective-permute-done((bf16[4,128,128]{2,1,0:T(8,128)(2,1)S(1)}, bf16[4,128,128]{2,1,0:T(8,128)(2,1)S(1)}, u32[]{:S(2)}, u32[]{:S(2)}) %collective-permute-start.19) | collective-permute-done | bytes 131104 | tf_op jit(solution)/shard_map/ppermute | solution.py:332
  68.1 2.0 %shard_map.114 = (bf16[512,128]{1,0:T(8,128)(2,1)S(1)}, bf16[512,128]{1,0:T(8,128)(2,1)S(1)}, bf16[512,128]{1,0:T(8,128)(2,1)S(1)}, bf16[512,128]{1,0:T(8,128)(2...) custom-call(s32[3]{0:T(128)S(1)} %pad_add_fusion.pos, bf16[128,2048]{1,0:T(8,128)(2,1)S(1)} %copy-done.4, ...), custom_call_target="tpu_custom_call" | custom-call | flops 1073741824 | bytes 6029312 | tf_op jit(solution)/shard_map/pallas_call | solution.py:59
  74.6 1.9 %collective-permute-start.20 = (bf16[512,128]{1,0:T(8,128)(2,1)}, bf16[512,128]{1,0:T(8,128)(2,1)S(1)}, u32[]{:S(2)}, u32[]{:S(2)}) collective-permute-start(bf16[512,128]{1,0:T(8,128)(2,1)} %copy-done.25), channel_id=1, source_target_pairs={{0,4},{1,5},{2,6},{3,7},{4,0},{5,1},{6,2},{7,3},{8,12},{9,13},{10,... | collective-permute-start | bytes 393224 | tf_op jit(solution)/shard_map/ppermute | solution.py:335
  76.6 1.8 %collective-permute-start.21 = (bf16[512,128]{1,0:T(8,128)(2,1)}, bf16[512,128]{1,0:T(8,128)(2,1)S(1)}, u32[]{:S(2)}, u32[]{:S(2)}) collective-permute-start(bf16[512,128]{1,0:T(8,128)(2,1)} %copy-done.24), channel_id=1, source_target_pairs={{0,8},{1,9},{2,10},{3,11},{4,12},{5,13},{6,14},{7,15},{8,0},{9,1},... | collective-permute-start | bytes 393224 | tf_op jit(solution)/shard_map/ppermute | solution.py:335
  79.0 0.8 dynamic-slice_bitcast_fusion.refs_5_
  79.8 0.9 copy-done.13
  80.7 0.9 copy-done.15
  81.6 0.9 copy-done.17
  82.5 1.6 %shard_map.116.refs_6_ = bf16[17,256,128]{2,1,0:T(8,128)(2,1)S(1)} custom-call(s32[3]{0:T(128)S(1)} %pad_add_fusion.pos, bf16[4,128,128]{2,1,0:T(8,128)(2,1)S(1)} %get-tuple-element.186.refs_0_, bf16[4,128,128]{2,1,0:T(8,128)(2,1)S(1)} %copy-done.13, bf16[4,128,128]{2,1,0:T(8,128)(2,1)S(1)} %copy-done.15, bf16[4,128,128]{2,1,0:T(8,128)(2,1)S(1)} %copy-done.17, ...), custom_call_target="tpu_custom_call" | custom-call | flops 536870912 | bytes 4128768 | tf_op jit(solution)/shard_map/pallas_call | solution.py:59
  84.1 5.1 %collective-permute-done.21.refs_2_ = bf16[512,128]{1,0:T(8,128)(2,1)S(1)} collective-permute-done((bf16[512,128]{1,0:T(8,128)(2,1)}, bf16[512,128]{1,0:T(8,128)(2,1)S(1)}, u32[]{:S(2)}, u32[]{:S(2)}) %collective-permute-start.21) | collective-permute-done | bytes 131104 | tf_op jit(solution)/shard_map/ppermute | solution.py:335
  89.2 2.3 %collective-permute-start.25 = (bf16[128,1024]{1,0:T(8,128)(2,1)S(1)}, bf16[128,1024]{1,0:T(8,128)(2,1)S(1)}, u32[]{:S(2)}, u32[]{:S(2)}) collective-permute-start(bf16[128,1024]{1,0:T(8,128)(2,1)S(1)} %copy-done.21), channel_id=1, source_target_pairs={{0,4},{1,5},{2,6},{3,7},{4,0},{5,1},{6,2},{7,3},{8,12},{9,13},{10,... | collective-permute-start | bytes 786440 | tf_op jit(solution)/shard_map/ppermute | solution.py:335
  92.2 3.0 %shard_map.117 = (bf16[256,128]{1,0:T(8,128)(2,1)S(1)}, bf16[256,128]{1,0:T(8,128)(2,1)S(1)}, bf16[256,128]{1,0:T(8,128)(2,1)S(1)}, bf16[256,128]{1,0:T(8,128)(2...) custom-call(s32[3]{0:T(128)S(1)} %pad_add_fusion.pos, ...), custom_call_target="tpu_custom_call" | custom-call | flops 1073741824 | bytes 7145472 | tf_op jit(solution)/shard_map/pallas_call | solution.py:59
  95.2 1.8 %collective-permute-done.25.refs_8_ = bf16[128,1024]{1,0:T(8,128)(2,1)S(1)} collective-permute-done((bf16[128,1024]{1,0:T(8,128)(2,1)S(1)}, bf16[128,1024]{1,0:T(8,128)(2,1)S(1)}, u32[]{:S(2)}, u32[]{:S(2)}) %collective-permute-start.25) | collective-permute-done | bytes 262176 | tf_op jit(solution)/shard_map/ppermute | solution.py:335
  97.0 1.5 %collective-permute-start.29 = (bf16[128,1024]{1,0:T(8,128)(2,1)S(1)}, bf16[128,1024]{1,0:T(8,128)(2,1)S(1)}, u32[]{:S(2)}, u32[]{:S(2)}) collective-permute-start(bf16[128,1024]{1,0:T(8,128)(2,1)S(1)} %collective-permute-done.25.refs_8_), channel_id=1, source_target_pairs={{0,16},{16,0},{1,17},{17,1},{2,18},{18,2},{3,19},{19,3},{4,20},{20... | collective-permute-start | bytes 786440 | tf_op jit(solution)/shard_map/ppermute | solution.py:338
  98.5 1.7 %collective-permute-start.26 = (bf16[256,128]{1,0:T(8,128)(2,1)S(1)}, bf16[256,128]{1,0:T(8,128)(2,1)S(1)}, u32[]{:S(2)}, u32[]{:S(2)}) collective-permute-start(bf16[256,128]{1,0:T(8,128)(2,1)S(1)} %get-tuple-element.210), channel_id=1, source_target_pairs={{0,4},{1,5},{2,6},{3,7},{4,0},{5,1},{6,2},{7,3},{8,12},{9,13},{10,... | collective-permute-start | bytes 196616 | tf_op jit(solution)/shard_map/ppermute | solution.py:335
  100.6 2.3 %collective-permute-start.28 = (bf16[256,128]{1,0:T(8,128)(2,1)S(1)}, bf16[256,128]{1,0:T(8,128)(2,1)S(1)}, u32[]{:S(2)}, u32[]{:S(2)}) collective-permute-start(bf16[256,128]{1,0:T(8,128)(2,1)S(1)} %get-tuple-element.212), channel_id=1, source_target_pairs={{0,12},{1,13},{2,14},{3,15},{4,8},{5,9},{6,10},{7,11},{8,4},{9,5},... | collective-permute-start | bytes 196616 | tf_op jit(solution)/shard_map/ppermute | solution.py:335
  102.9 5.4 %collective-permute-done.27.refs_2_ = bf16[256,128]{1,0:T(8,128)(2,1)S(1)} collective-permute-done((bf16[256,128]{1,0:T(8,128)(2,1)S(1)}, bf16[256,128]{1,0:T(8,128)(2,1)S(1)}, u32[]{:S(2)}, u32[]{:S(2)}) %collective-permute-start.27) | collective-permute-done | bytes 65568 | tf_op jit(solution)/shard_map/ppermute | solution.py:335
  108.3 1.9 %shard_map.119 = (f32[128,2048]{1,0:T(8,128)S(1)}, bf16[128,2048]{1,0:T(8,128)(2,1)S(1)}, bf16[512,2048]{1,0:T(8,128)(2,1)S(1)}) custom-call(s32[3]{0:T(128)S(1)} %pad_add_fusion.pos, bf16[256,128]{1,0:T(8,128)(2,1)S(1)} %get-tuple-element.219.refs_0_, bf16[256,128]{1,0:T(8,128)(2,1)S(1)} %collective-permute-done.26.refs_1_, ...), custom_call_target="tpu_custom_call" | custom-call | flops 536870912 | bytes 6291456 | tf_op jit(solution)/shard_map/pallas_call | solution.py:59
  110.3 1.9 %collective-permute-done.31 = bf16[128,2048]{1,0:T(8,128)(2,1)S(1)} collective-permute-done((bf16[128,2048]{1,0:T(8,128)(2,1)S(1)}, bf16[128,2048]{1,0:T(8,128)(2,1)S(1)}, u32[]{:S(2)}, u32[]{:S(2)}) %collective-permute-start.31) | collective-permute-done | bytes 524320 | tf_op jit(solution)/shard_map/ppermute | solution.py:332
  112.3 1.5 %collective-permute-start.32 = (bf16[256,128]{1,0:T(8,128)(2,1)S(1)}, bf16[256,128]{1,0:T(8,128)(2,1)S(1)}, u32[]{:S(2)}, u32[]{:S(2)}) collective-permute-start(bf16[256,128]{1,0:T(8,128)(2,1)S(1)} %get-tuple-element.233), channel_id=1, source_target_pairs={{0,4},{1,5},{2,6},{3,7},{4,0},{5,1},{6,2},{7,3},{8,12},{9,13},{10,... | collective-permute-start | bytes 196616 | tf_op jit(solution)/shard_map/ppermute | solution.py:335
  113.8 0.9 collective-permute-start.33
  114.8 2.0 %collective-permute-start.34 = (bf16[256,128]{1,0:T(8,128)(2,1)S(1)}, bf16[256,128]{1,0:T(8,128)(2,1)S(1)}, u32[]{:S(2)}, u32[]{:S(2)}) collective-permute-start(bf16[256,128]{1,0:T(8,128)(2,1)S(1)} %get-tuple-element.235), channel_id=1, source_target_pairs={{0,12},{1,13},{2,14},{3,15},{4,8},{5,9},{6,10},{7,11},{8,4},{9,5},... | collective-permute-start | bytes 196616 | tf_op jit(solution)/shard_map/ppermute | solution.py:335
  116.8 1.5 %collective-permute-start.36 = (bf16[128,2048]{1,0:T(8,128)(2,1)S(1)}, bf16[128,2048]{1,0:T(8,128)(2,1)S(1)}, u32[]{:S(2)}, u32[]{:S(2)}) collective-permute-start(bf16[128,2048]{1,0:T(8,128)(2,1)S(1)} %add_convert_fusion.1), channel_id=1, source_target_pairs={{0,2},{1,3},{2,0},{3,1},{4,6},{5,7},{6,4},{7,5},{8,10},{9,11},{10,... | collective-permute-start | bytes 1572872 | tf_op jit(solution)/shard_map/ppermute | solution.py:332
  118.3 3.7 %collective-permute-done.33.refs_2_ = bf16[256,128]{1,0:T(8,128)(2,1)S(1)} collective-permute-done((bf16[256,128]{1,0:T(8,128)(2,1)S(1)}, bf16[256,128]{1,0:T(8,128)(2,1)S(1)}, u32[]{:S(2)}, u32[]{:S(2)}) %collective-permute-start.33) | collective-permute-done | bytes 65568 | tf_op jit(solution)/shard_map/ppermute | solution.py:335
  122.0 1.3 shard_map.120
  123.4 6.6 %collective-permute-done.36 = bf16[128,2048]{1,0:T(8,128)(2,1)S(1)} collective-permute-done((bf16[128,2048]{1,0:T(8,128)(2,1)S(1)}, bf16[128,2048]{1,0:T(8,128)(2,1)S(1)}, u32[]{:S(2)}, u32[]{:S(2)}) %collective-permute-start.36) | collective-permute-done | bytes 524320 | tf_op jit(solution)/shard_map/ppermute | solution.py:332
  129.9 1.0 add_convert_fusion
  (97 shorter events, 12.3 us)
Async XLA Ops:
  0.0 74.6 %copy-start = (f32[3,2048]{1,0:T(4,128)S(1)}, f32[3,2048]{1,0:T(4,128)}, u32[]{:S(2)}) copy-start(f32[3,2048]{1,0:T(4,128)} %param.14) | copy-start | bytes 73732
  1.1 65.6 %copy-start.10 = (bf16[128,2048]{1,0:T(8,128)(2,1)S(1)}, bf16[128,2048]{1,0:T(8,128)(2,1)}, u32[]{:S(2)}) copy-start(bf16[128,2048]{1,0:T(8,128)(2,1)} %src.2) | copy-start | bytes 1572868
  1.8 66.3 %copy-start.4 = (bf16[128,2048]{1,0:T(8,128)(2,1)S(1)}, bf16[128,2048]{1,0:T(8,128)(2,1)}, u32[]{:S(2)}) copy-start(bf16[128,2048]{1,0:T(8,128)(2,1)} %refs_0_.1) | copy-start | bytes 1572868
  1.8 14.3 %collective-permute-start = (bf16[128,512]{1,0:T(8,128)(2,1)S(1)}, bf16[128,512]{1,0:T(8,128)(2,1)S(1)}, u32[]{:S(2)}, u32[]{:S(2)}) collective-permute-start(bf16[128,512]{1,0:T(8,128)(2,1)S(1)} %get-tuple-element.125), channel_id=1, source_target_pairs={{0,1},{1,0},{2,3},{3,2},{4,5},{5,4},{6,7},{7,6},{8,9},{9,8},{10,11... | collective-permute-start | bytes 393224 | tf_op jit(solution)/shard_map/ppermute | solution.py:332
  2.3 13.7 %collective-permute-start.1 = (bf16[128,512]{1,0:T(8,128)(2,1)S(1)}, bf16[128,512]{1,0:T(8,128)(2,1)S(1)}, u32[]{:S(2)}, u32[]{:S(2)}) collective-permute-start(bf16[128,512]{1,0:T(8,128)(2,1)S(1)} %get-tuple-element.126), channel_id=1, source_target_pairs={{0,2},{1,3},{2,0},{3,1},{4,6},{5,7},{6,4},{7,5},{8,10},{9,11},{10,... | collective-permute-start | bytes 393224 | tf_op jit(solution)/shard_map/ppermute | solution.py:332
  4.9 11.2 %collective-permute-start.2 = (bf16[128,512]{1,0:T(8,128)(2,1)S(1)}, bf16[128,512]{1,0:T(8,128)(2,1)S(1)}, u32[]{:S(2)}, u32[]{:S(2)}) collective-permute-start(bf16[128,512]{1,0:T(8,128)(2,1)S(1)} %get-tuple-element.127), channel_id=1, source_target_pairs={{0,3},{1,2},{2,1},{3,0},{4,7},{5,6},{6,5},{7,4},{8,11},{9,10},{10,... | collective-permute-start | bytes 393224 | tf_op jit(solution)/shard_map/ppermute | solution.py:332
  6.6 9.5 %collective-permute-start.3 = (bf16[128,512]{1,0:T(8,128)(2,1)S(1)}, bf16[128,512]{1,0:T(8,128)(2,1)S(1)}, u32[]{:S(2)}, u32[]{:S(2)}) collective-permute-start(bf16[128,512]{1,0:T(8,128)(2,1)S(1)} %get-tuple-element.129), channel_id=1, source_target_pairs={{0,4},{1,5},{2,6},{3,7},{4,0},{5,1},{6,2},{7,3},{8,12},{9,13},{10,... | collective-permute-start | bytes 393224 | tf_op jit(solution)/shard_map/ppermute | solution.py:367
  8.5 7.6 %collective-permute-start.4 = (bf16[64,512]{1,0:T(8,128)(2,1)S(1)}, bf16[64,512]{1,0:T(8,128)(2,1)S(1)}, u32[]{:S(2)}, u32[]{:S(2)}) collective-permute-start(bf16[64,512]{1,0:T(8,128)(2,1)S(1)} %get-tuple-element.130), channel_id=1, source_target_pairs={{0,12},{1,13},{2,14},{3,15},{4,8},{5,9},{6,10},{7,11},{8,4},{9,5},... | collective-permute-start | bytes 196616 | tf_op jit(solution)/shard_map/ppermute | solution.py:335
  16.1 19.6 %collective-permute-start.8 = (bf16[128,2048]{1,0:T(8,128)(2,1)}, bf16[128,2048]{1,0:T(8,128)(2,1)S(1)}, u32[]{:S(2)}, u32[]{:S(2)}) collective-permute-start(bf16[128,2048]{1,0:T(8,128)(2,1)} %refs_0_.1), channel_id=1, source_target_pairs={{0,2},{1,3},{2,0},{3,1},{4,6},{5,7},{6,4},{7,5},{8,10},{9,11},{10,... | collective-permute-start | bytes 1572872 | tf_op jit(solution)/shard_map/ppermute | solution.py:332
  18.3 17.4 %collective-permute-start.5 = (bf16[256,512]{1,0:T(8,128)(2,1)S(1)}, bf16[256,512]{1,0:T(8,128)(2,1)S(1)}, u32[]{:S(2)}, u32[]{:S(2)}) collective-permute-start(bf16[256,512]{1,0:T(8,128)(2,1)S(1)} %get-tuple-element.137), channel_id=1, source_target_pairs={{0,4},{1,5},{2,6},{3,7},{4,0},{5,1},{6,2},{7,3},{8,12},{9,13},{10,... | collective-permute-start | bytes 786440 | tf_op jit(solution)/shard_map/ppermute | solution.py:335
  18.3 17.3 %collective-permute-start.9 = (bf16[192,512]{1,0:T(8,128)(2,1)S(1)}, bf16[192,512]{1,0:T(8,128)(2,1)S(1)}, u32[]{:S(2)}, u32[]{:S(2)}) collective-permute-start(bf16[192,512]{1,0:T(8,128)(2,1)S(1)} %get-tuple-element.141.mine), channel_id=1, source_target_pairs={{0,16},{16,0},{1,17},{17,1},{2,18},{18,2},{3,19},{19,3},{4,20},{20... | collective-permute-start | bytes 589832 | tf_op jit(solution)/shard_map/ppermute | solution.py:338
  23.6 12.0 %collective-permute-start.6 = (bf16[128,512]{1,0:T(8,128)(2,1)S(1)}, bf16[128,512]{1,0:T(8,128)(2,1)S(1)}, u32[]{:S(2)}, u32[]{:S(2)}) collective-permute-start(bf16[128,512]{1,0:T(8,128)(2,1)S(1)} %get-tuple-element.138), channel_id=1, source_target_pairs={{0,8},{1,9},{2,10},{3,11},{4,12},{5,13},{6,14},{7,15},{8,0},{9,1},... | collective-permute-start | bytes 393224 | tf_op jit(solution)/shard_map/ppermute | solution.py:335
  25.6 10.0 %collective-permute-start.7 = (bf16[128,512]{1,0:T(8,128)(2,1)S(1)}, bf16[128,512]{1,0:T(8,128)(2,1)S(1)}, u32[]{:S(2)}, u32[]{:S(2)}) collective-permute-start(bf16[128,512]{1,0:T(8,128)(2,1)S(1)} %get-tuple-element.139), channel_id=1, source_target_pairs={{0,12},{1,13},{2,14},{3,15},{4,8},{5,9},{6,10},{7,11},{8,4},{9,5},... | collective-permute-start | bytes 393224 | tf_op jit(solution)/shard_map/ppermute | solution.py:335
  38.4 18.3 %collective-permute-start.14 = (bf16[256,2048]{1,0:T(8,128)(2,1)S(1)}, bf16[256,2048]{1,0:T(8,128)(2,1)S(1)}, u32[]{:S(2)}, u32[]{:S(2)}) collective-permute-start(bf16[256,2048]{1,0:T(8,128)(2,1)S(1)} %get-tuple-element.151), channel_id=1, source_target_pairs={{0,1},{1,0},{2,3},{3,2},{4,5},{5,4},{6,7},{7,6},{8,9},{9,8},{10,11... | collective-permute-start | bytes 3145736 | tf_op jit(solution)/shard_map/ppermute | solution.py:332
  38.5 18.2 %collective-permute-start.11 = (bf16[512,512]{1,0:T(8,128)(2,1)S(1)}, bf16[512,512]{1,0:T(8,128)(2,1)S(1)}, u32[]{:S(2)}, u32[]{:S(2)}) collective-permute-start(bf16[512,512]{1,0:T(8,128)(2,1)S(1)} %get-tuple-element.148.refs_7_), channel_id=1, source_target_pairs={{0,16},{16,0},{1,17},{17,1},{2,18},{18,2},{3,19},{19,3},{4,20},{20... | collective-permute-start | bytes 1572872 | tf_op jit(solution)/shard_map/ppermute | solution.py:338
  41.5 15.2 %collective-permute-start.10 = (bf16[256,512]{1,0:T(8,128)(2,1)S(1)}, bf16[256,512]{1,0:T(8,128)(2,1)S(1)}, u32[]{:S(2)}, u32[]{:S(2)}) collective-permute-start(bf16[256,512]{1,0:T(8,128)(2,1)S(1)} %get-tuple-element.147), channel_id=1, source_target_pairs={{0,4},{1,5},{2,6},{3,7},{4,0},{5,1},{6,2},{7,3},{8,12},{9,13},{10,... | collective-permute-start | bytes 786440 | tf_op jit(solution)/shard_map/ppermute | solution.py:335
  41.5 9.5 %collective-permute-start.12 = (bf16[64,1024]{1,0:T(8,128)(2,1)S(1)}, bf16[64,1024]{1,0:T(8,128)(2,1)S(1)}, u32[]{:S(2)}, u32[]{:S(2)}) collective-permute-start(bf16[64,1024]{1,0:T(8,128)(2,1)S(1)} %get-tuple-element.149), channel_id=1, source_target_pairs={{0,8},{1,9},{2,10},{3,11},{4,12},{5,13},{6,14},{7,15},{8,0},{9,1},... | collective-permute-start | bytes 393224 | tf_op jit(solution)/shard_map/ppermute | solution.py:335
  43.4 13.4 %collective-permute-start.13 = (bf16[64,1024]{1,0:T(8,128)(2,1)S(1)}, bf16[64,1024]{1,0:T(8,128)(2,1)S(1)}, u32[]{:S(2)}, u32[]{:S(2)}) collective-permute-start(bf16[64,1024]{1,0:T(8,128)(2,1)S(1)} %get-tuple-element.150), channel_id=1, source_target_pairs={{0,12},{1,13},{2,14},{3,15},{4,8},{5,9},{6,10},{7,11},{8,4},{9,5},... | collective-permute-start | bytes 393224 | tf_op jit(solution)/shard_map/ppermute | solution.py:335
  56.7 10.0 %collective-permute-start.16 = (bf16[128,1024]{1,0:T(8,128)(2,1)S(1)}, bf16[128,1024]{1,0:T(8,128)(2,1)S(1)}, u32[]{:S(2)}, u32[]{:S(2)}) collective-permute-start(bf16[128,1024]{1,0:T(8,128)(2,1)S(1)} %get-tuple-element.161), channel_id=1, source_target_pairs={{0,4},{1,5},{2,6},{3,7},{4,0},{5,1},{6,2},{7,3},{8,12},{9,13},{10,... | collective-permute-start | bytes 786440 | tf_op jit(solution)/shard_map/ppermute | solution.py:335
  56.8 9.9 %collective-permute-start.15 = (bf16[256,512]{1,0:T(8,128)(2,1)S(1)}, bf16[256,512]{1,0:T(8,128)(2,1)S(1)}, u32[]{:S(2)}, u32[]{:S(2)}) collective-permute-start(bf16[256,512]{1,0:T(8,128)(2,1)S(1)} %collective-permute-done.10.refs_8_), channel_id=1, source_target_pairs={{0,16},{16,0},{1,17},{17,1},{2,18},{18,2},{3,19},{19,3},{4,20},{20... | collective-permute-start | bytes 786440 | tf_op jit(solution)/shard_map/ppermute | solution.py:338
  58.4 1.9 %collective-permute-start.17 = (bf16[4,128,128]{2,1,0:T(8,128)(2,1)S(1)}, bf16[4,128,128]{2,1,0:T(8,128)(2,1)S(1)}, u32[]{:S(2)}, u32[]{:S(2)}) collective-permute-start(bf16[4,128,128]{2,1,0:T(8,128)(2,1)S(1)} %get-tuple-element.163), channel_id=1, source_target_pairs={{0,1},{1,0},{2,3},{3,2},{4,5},{5,4},{6,7},{7,6},{8,9},{9,8},{10,11... | collective-permute-start | bytes 393224 | tf_op jit(solution)/shard_map/ppermute | solution.py:332
  58.4 6.3 %collective-permute-start.18 = (bf16[4,128,128]{2,1,0:T(8,128)(2,1)S(1)}, bf16[4,128,128]{2,1,0:T(8,128)(2,1)S(1)}, u32[]{:S(2)}, u32[]{:S(2)}) collective-permute-start(bf16[4,128,128]{2,1,0:T(8,128)(2,1)S(1)} %get-tuple-element.164), channel_id=1, source_target_pairs={{0,2},{1,3},{2,0},{3,1},{4,6},{5,7},{6,4},{7,5},{8,10},{9,11},{10,... | collective-permute-start | bytes 393224 | tf_op jit(solution)/shard_map/ppermute | solution.py:332
  58.9 7.8 %collective-permute-start.19 = (bf16[4,128,128]{2,1,0:T(8,128)(2,1)S(1)}, bf16[4,128,128]{2,1,0:T(8,128)(2,1)S(1)}, u32[]{:S(2)}, u32[]{:S(2)}) collective-permute-start(bf16[4,128,128]{2,1,0:T(8,128)(2,1)S(1)} %get-tuple-element.165), channel_id=1, source_target_pairs={{0,3},{1,2},{2,1},{3,0},{4,7},{5,6},{6,5},{7,4},{8,11},{9,10},{10,... | collective-permute-start | bytes 393224 | tf_op jit(solution)/shard_map/ppermute | solution.py:332
  60.2 9.9 %copy-start.12 = (bf16[4,128,128]{2,1,0:T(8,128)(2,1)}, bf16[4,128,128]{2,1,0:T(8,128)(2,1)S(1)}, u32[]{:S(2)}) copy-start(bf16[4,128,128]{2,1,0:T(8,128)(2,1)S(1)} %collective-permute-done.17.refs_1_) | copy-start | bytes 393220
  68.1 11.6 %copy-start.1 = (bf16[17,256,256]{2,1,0:T(8,128)(2,1)S(1)}, bf16[17,256,256]{2,1,0:T(8,128)(2,1)}, u32[]{:S(2)}) copy-start(bf16[17,256,256]{2,1,0:T(8,128)(2,1)} %constant.50.clone.refs_5_.refs_9_) | copy-start | bytes 6684676
  68.1 11.6 %copy-start.7 = (bf16[512,256]{1,0:T(8,128)(2,1)S(1)}, bf16[512,256]{1,0:T(8,128)(2,1)}, u32[]{:S(2)}) copy-start(bf16[512,256]{1,0:T(8,128)(2,1)} %constant.48.clone.refs_4_.refs_7_) | copy-start | bytes 786436
  73.5 15.7 %collective-permute-start.23 = (bf16[256,1024]{1,0:T(8,128)(2,1)S(1)}, bf16[256,1024]{1,0:T(8,128)(2,1)}, u32[]{:S(2)}, u32[]{:S(2)}) collective-permute-start(bf16[256,1024]{1,0:T(8,128)(2,1)S(1)} %get-tuple-element.184.refs_7_), channel_id=1, source_target_pairs={{0,16},{16,0},{1,17},{17,1},{2,18},{18,2},{3,19},{19,3},{4,20},{20... | collective-permute-start | bytes 1572872 | tf_op jit(solution)/shard_map/ppermute | solution.py:338
  74.1 15.1 %collective-permute-start.24 = (bf16[256,512]{1,0:T(8,128)(2,1)}, bf16[256,512]{1,0:T(8,128)(2,1)S(1)}, u32[]{:S(2)}, u32[]{:S(2)}) collective-permute-start(bf16[256,512]{1,0:T(8,128)(2,1)} %copy-done.22), channel_id=1, source_target_pairs={{0,2},{1,3},{2,0},{3,1},{4,6},{5,7},{6,4},{7,5},{8,10},{9,11},{10,... | collective-permute-start | bytes 786440 | tf_op jit(solution)/shard_map/ppermute | solution.py:332
  74.6 9.5 %collective-permute-start.20 = (bf16[512,128]{1,0:T(8,128)(2,1)}, bf16[512,128]{1,0:T(8,128)(2,1)S(1)}, u32[]{:S(2)}, u32[]{:S(2)}) collective-permute-start(bf16[512,128]{1,0:T(8,128)(2,1)} %copy-done.25), channel_id=1, source_target_pairs={{0,4},{1,5},{2,6},{3,7},{4,0},{5,1},{6,2},{7,3},{8,12},{9,13},{10,... | collective-permute-start | bytes 393224 | tf_op jit(solution)/shard_map/ppermute | solution.py:335
  76.6 12.6 %collective-permute-start.21 = (bf16[512,128]{1,0:T(8,128)(2,1)}, bf16[512,128]{1,0:T(8,128)(2,1)S(1)}, u32[]{:S(2)}, u32[]{:S(2)}) collective-permute-start(bf16[512,128]{1,0:T(8,128)(2,1)} %copy-done.24), channel_id=1, source_target_pairs={{0,8},{1,9},{2,10},{3,11},{4,12},{5,13},{6,14},{7,15},{8,0},{9,1},... | collective-permute-start | bytes 393224 | tf_op jit(solution)/shard_map/ppermute | solution.py:335
  78.4 10.8 %collective-permute-start.22 = (bf16[512,128]{1,0:T(8,128)(2,1)}, bf16[512,128]{1,0:T(8,128)(2,1)S(1)}, u32[]{:S(2)}, u32[]{:S(2)}) collective-permute-start(bf16[512,128]{1,0:T(8,128)(2,1)} %copy-done.23), channel_id=1, source_target_pairs={{0,12},{1,13},{2,14},{3,15},{4,8},{5,9},{6,10},{7,11},{8,4},{9,5},... | collective-permute-start | bytes 393224 | tf_op jit(solution)/shard_map/ppermute | solution.py:335
  82.5 6.7 %copy-start.21 = (bf16[128,1024]{1,0:T(8,128)(2,1)S(1)}, bf16[128,1024]{1,0:T(8,128)(2,1)}, u32[]{:S(2)}) copy-start(bf16[128,1024]{1,0:T(8,128)(2,1)} %copy-done.20) | copy-start | bytes 786436
  82.5 9.6 %copy-start.2 = (bf16[17,256,256]{2,1,0:T(8,128)(2,1)S(1)}, bf16[17,256,256]{2,1,0:T(8,128)(2,1)}, u32[]{:S(2)}) copy-start(bf16[17,256,256]{2,1,0:T(8,128)(2,1)} %constant.51.clone.refs_10_) | copy-start | bytes 6684676
  82.5 9.6 %copy-start.11 = (bf16[256,512]{1,0:T(8,128)(2,1)S(1)}, bf16[256,512]{1,0:T(8,128)(2,1)}, u32[]{:S(2)}) copy-start(bf16[256,512]{1,0:T(8,128)(2,1)} %constant.49.clone.refs_8_) | copy-start | bytes 786436
  82.5 9.6 %copy-start.19 = (bf16[512,128]{1,0:T(8,128)(2,1)S(1)}, bf16[512,128]{1,0:T(8,128)(2,1)}, u32[]{:S(2)}) copy-start(bf16[512,128]{1,0:T(8,128)(2,1)} %copy-done.18) | copy-start | bytes 393220
  89.2 7.7 %collective-permute-start.25 = (bf16[128,1024]{1,0:T(8,128)(2,1)S(1)}, bf16[128,1024]{1,0:T(8,128)(2,1)S(1)}, u32[]{:S(2)}, u32[]{:S(2)}) collective-permute-start(bf16[128,1024]{1,0:T(8,128)(2,1)S(1)} %copy-done.21), channel_id=1, source_target_pairs={{0,4},{1,5},{2,6},{3,7},{4,0},{5,1},{6,2},{7,3},{8,12},{9,13},{10,... | collective-permute-start | bytes 786440 | tf_op jit(solution)/shard_map/ppermute | solution.py:335
  92.1 16.2 %copy-start.6 = (bf16[128,2048]{1,0:T(8,128)(2,1)S(1)}, bf16[128,2048]{1,0:T(8,128)(2,1)}, u32[]{:S(2)}) copy-start(bf16[128,2048]{1,0:T(8,128)(2,1)} %refs_6_.1) | copy-start | bytes 1572868
  97.0 11.3 %collective-permute-start.30 = (bf16[256,512]{1,0:T(8,128)(2,1)S(1)}, bf16[256,512]{1,0:T(8,128)(2,1)S(1)}, u32[]{:S(2)}, u32[]{:S(2)}) collective-permute-start(bf16[256,512]{1,0:T(8,128)(2,1)S(1)} %shard_map.118), channel_id=1, source_target_pairs={{0,1},{1,0},{2,3},{3,2},{4,5},{5,4},{6,7},{7,6},{8,9},{9,8},{10,11... | collective-permute-start | bytes 786440 | tf_op jit(solution)/shard_map/ppermute | solution.py:332
  97.0 11.3 %collective-permute-start.29 = (bf16[128,1024]{1,0:T(8,128)(2,1)S(1)}, bf16[128,1024]{1,0:T(8,128)(2,1)S(1)}, u32[]{:S(2)}, u32[]{:S(2)}) collective-permute-start(bf16[128,1024]{1,0:T(8,128)(2,1)S(1)} %collective-permute-done.25.refs_8_), channel_id=1, source_target_pairs={{0,16},{16,0},{1,17},{17,1},{2,18},{18,2},{3,19},{19,3},{4,20},{20... | collective-permute-start | bytes 786440 | tf_op jit(solution)/shard_map/ppermute | solution.py:338
  98.5 4.4 %collective-permute-start.26 = (bf16[256,128]{1,0:T(8,128)(2,1)S(1)}, bf16[256,128]{1,0:T(8,128)(2,1)S(1)}, u32[]{:S(2)}, u32[]{:S(2)}) collective-permute-start(bf16[256,128]{1,0:T(8,128)(2,1)S(1)} %get-tuple-element.210), channel_id=1, source_target_pairs={{0,4},{1,5},{2,6},{3,7},{4,0},{5,1},{6,2},{7,3},{8,12},{9,13},{10,... | collective-permute-start | bytes 196616 | tf_op jit(solution)/shard_map/ppermute | solution.py:335
  100.2 8.1 %collective-permute-start.27 = (bf16[256,128]{1,0:T(8,128)(2,1)S(1)}, bf16[256,128]{1,0:T(8,128)(2,1)S(1)}, u32[]{:S(2)}, u32[]{:S(2)}) collective-permute-start(bf16[256,128]{1,0:T(8,128)(2,1)S(1)} %get-tuple-element.211), channel_id=1, source_target_pairs={{0,8},{1,9},{2,10},{3,11},{4,12},{5,13},{6,14},{7,15},{8,0},{9,1},... | collective-permute-start | bytes 196616 | tf_op jit(solution)/shard_map/ppermute | solution.py:335
  100.6 7.7 %collective-permute-start.28 = (bf16[256,128]{1,0:T(8,128)(2,1)S(1)}, bf16[256,128]{1,0:T(8,128)(2,1)S(1)}, u32[]{:S(2)}, u32[]{:S(2)}) collective-permute-start(bf16[256,128]{1,0:T(8,128)(2,1)S(1)} %get-tuple-element.212), channel_id=1, source_target_pairs={{0,12},{1,13},{2,14},{3,15},{4,8},{5,9},{6,10},{7,11},{8,4},{9,5},... | collective-permute-start | bytes 196616 | tf_op jit(solution)/shard_map/ppermute | solution.py:335
  110.3 2.0 %collective-permute-start.31 = (bf16[128,2048]{1,0:T(8,128)(2,1)S(1)}, bf16[128,2048]{1,0:T(8,128)(2,1)S(1)}, u32[]{:S(2)}, u32[]{:S(2)}) collective-permute-start(bf16[128,2048]{1,0:T(8,128)(2,1)S(1)} %get-tuple-element.227), channel_id=1, source_target_pairs={{0,1},{1,0},{2,3},{3,2},{4,5},{5,4},{6,7},{7,6},{8,9},{9,8},{10,11... | collective-permute-start | bytes 1572872 | tf_op jit(solution)/shard_map/ppermute | solution.py:332
  112.3 6.0 %collective-permute-start.32 = (bf16[256,128]{1,0:T(8,128)(2,1)S(1)}, bf16[256,128]{1,0:T(8,128)(2,1)S(1)}, u32[]{:S(2)}, u32[]{:S(2)}) collective-permute-start(bf16[256,128]{1,0:T(8,128)(2,1)S(1)} %get-tuple-element.233), channel_id=1, source_target_pairs={{0,4},{1,5},{2,6},{3,7},{4,0},{5,1},{6,2},{7,3},{8,12},{9,13},{10,... | collective-permute-start | bytes 196616 | tf_op jit(solution)/shard_map/ppermute | solution.py:335
  113.8 8.2 %collective-permute-start.33 = (bf16[256,128]{1,0:T(8,128)(2,1)S(1)}, bf16[256,128]{1,0:T(8,128)(2,1)S(1)}, u32[]{:S(2)}, u32[]{:S(2)}) collective-permute-start(bf16[256,128]{1,0:T(8,128)(2,1)S(1)} %get-tuple-element.234), channel_id=1, source_target_pairs={{0,8},{1,9},{2,10},{3,11},{4,12},{5,13},{6,14},{7,15},{8,0},{9,1},... | collective-permute-start | bytes 196616 | tf_op jit(solution)/shard_map/ppermute | solution.py:335
  114.8 7.2 %collective-permute-start.34 = (bf16[256,128]{1,0:T(8,128)(2,1)S(1)}, bf16[256,128]{1,0:T(8,128)(2,1)S(1)}, u32[]{:S(2)}, u32[]{:S(2)}) collective-permute-start(bf16[256,128]{1,0:T(8,128)(2,1)S(1)} %get-tuple-element.235), channel_id=1, source_target_pairs={{0,12},{1,13},{2,14},{3,15},{4,8},{5,9},{6,10},{7,11},{8,4},{9,5},... | collective-permute-start | bytes 196616 | tf_op jit(solution)/shard_map/ppermute | solution.py:335
  116.8 13.1 %collective-permute-start.36 = (bf16[128,2048]{1,0:T(8,128)(2,1)S(1)}, bf16[128,2048]{1,0:T(8,128)(2,1)S(1)}, u32[]{:S(2)}, u32[]{:S(2)}) collective-permute-start(bf16[128,2048]{1,0:T(8,128)(2,1)S(1)} %add_convert_fusion.1), channel_id=1, source_target_pairs={{0,2},{1,3},{2,0},{3,1},{4,6},{5,7},{6,4},{7,5},{8,10},{9,11},{10,... | collective-permute-start | bytes 1572872 | tf_op jit(solution)/shard_map/ppermute | solution.py:332
  123.3 6.6 %collective-permute-start.35 = (bf16[128,2048]{1,0:T(8,128)(2,1)S(1)}, bf16[128,2048]{1,0:T(8,128)(2,1)S(1)}, u32[]{:S(2)}, u32[]{:S(2)}) collective-permute-start(bf16[128,2048]{1,0:T(8,128)(2,1)S(1)} %get-tuple-element.239), channel_id=1, source_target_pairs={{0,1},{1,0},{2,3},{3,2},{4,5},{5,4},{6,7},{7,6},{8,9},{9,8},{10,11... | collective-permute-start | bytes 1572872 | tf_op jit(solution)/shard_map/ppermute | solution.py:332
  (15 other events, 19.9 us)

commit v3 on v2

--- a/solution.py
+++ b/solution.py
@@ -51,11 +51,12 @@
     return jnp.dot(left, right, preferred_element_type=jnp.float32)
 
 
-def call(kernel, outs, scratch, pos, args, flops, vmem=4):
+def call(kernel, outs, scratch, pos, args, flops, vmem=4, fetched=0):
     in_specs = [pl.BlockSpec(memory_space=pltpu.SMEM)]
-    in_specs += [pl.BlockSpec(memory_space=pltpu.VMEM)] * len(args)
-    moved = sum(a.size * a.dtype.itemsize for a in args)
-    moved += sum(math.prod(o.shape) * o.dtype.itemsize for o in outs)
+    in_specs += [pl.BlockSpec(memory_space=pltpu.HBM)] * fetched
+    in_specs += [pl.BlockSpec(memory_space=pltpu.VMEM)] * (len(args) - fetched)
+    moved = sum(a.size * a.dtype.itemsize for a in args) if flops else 0
+    moved += sum(math.prod(o.shape) * o.dtype.itemsize for o in outs) if flops else 0
     return pl.pallas_call(
         kernel,
         out_shape=outs,
@@ -72,42 +73,77 @@
     return pl.multiple_of(block * rows, rows)
 
 
-def split_kernel(share, pos, src, *outs):
-    rows = src.shape[0]
-    for d in range(PLANE):
-        out = outs[min(d, len(outs) - 1)]
-        first = (d - len(outs) + 1) * rows if d >= len(outs) else 0
+def fetch(pairs, sems):
+    copies = [pltpu.make_async_copy(src, dst, sems.at[i]) for i, (src, dst) in enumerate(pairs)]
+    for copy in copies:
+        copy.start()
+    return copies
+
+
+def start_kernel(share, pos, weight, taps, out_weight, *refs):
+    outs, (own, whole, near, out_half) = refs[:PLANE], refs[PLANE : PLANE + 4]
+    weight_here, taps_here, sems = refs[PLANE + 4 :]
+    rows, wide = own.shape
+    deep, width = out_half.shape
+    quarter = rows // 4
+    side = pl.ds(pl.multiple_of(pos[0] * width, width), width)
+    pairs = []
+    for source, here in ((weight, weight_here), (taps, taps_here)):
+        for q in range(4):
+            cut = pl.ds(q * quarter, quarter)
+            pairs.append((source.at[cut], here.at[cut]))
+    pairs.append((out_weight.at[:, side], out_half))
+    copies = fetch(pairs, sems)
+    for copy in copies[:4]:
+        copy.wait()
+    for d, out in enumerate(outs):
         place = jnp.bitwise_xor(pos[2], d)
-        for p in range(out.shape[1] // share):
+        for p in range(wide // share):
             at = pl.multiple_of((p * PLANE + place) * share, share)
-            out[first : first + rows, p * share : (p + 1) * share] = src[:, pl.ds(at, share)]
-
-
-def filter_kernel(pos, taps, own, whole, half):
-    wide = own.shape[1]
-    part = half.shape[0]
+            out[:, p * share : (p + 1) * share] = weight_here[:, pl.ds(at, share)]
+    for copy in copies[4:]:
+        copy.wait()
 
     def columns(s):
         return pl.ds(pl.multiple_of(jnp.bitwise_xor(pos[1], s) * wide, wide), wide)
 
-    own[...] = taps[:, columns(0)]
-    whole[...] = taps[:, columns(1 + pos[0])]
-    half[...] = taps[pl.ds(pl.multiple_of(pos[0] * part, part), part), columns(3)]
-
-
-def half_kernel(pos, *refs):
-    parts, (whole, half), (out, lower, upper, joined) = refs[:PLANE], refs[PLANE:-4], refs[-4:]
-    deep = parts[0].shape[0]
-    for y in range(2):
-
-        @pl.when(pos[0] == y)
-        def _():
-            for j, far in enumerate((lower, upper)):
-                out[j * deep : (j + 1) * deep, :] = parts[2 * y + j][...]
-                far[...] = parts[2 * y + j][...]
-
-    joined[: whole.shape[0], :] = whole[...]
-    joined[whole.shape[0] :, :] = half[...]
+    own[...] = taps_here[:, columns(0)]
+    whole[...] = taps_here[:, columns(2 + pos[0])]
+    near[:deep, :] = out_half[...]
+    for q in range(2):
+        first = pl.multiple_of(pos[0] * (rows // 2) + q * quarter, quarter)
+        near[deep:, q * wide : (q + 1) * wide] = taps_here[pl.ds(first, quarter), columns(1)]
+
+
+def across_kernel(share, pos, x, gate, own, core, across, sems):
+    rows = x.shape[0]
+    part, wide = rows // 4, own.shape[1]
+    pairs = [(x, core.at[pl.ds(0, rows)]), (x, across.at[pl.ds(0, rows)])]
+    for d in range(PLANE):
+        place = jnp.bitwise_xor(pos[2], d)
+        for p in range(wide // share):
+            at = pl.multiple_of((p * PLANE + place) * share, share)
+            if d == 0:
+                here = pl.ds(p * share, share)
+                pairs.append((gate.at[:, pl.ds(at, share)], own.at[:, here]))
+                continue
+            out, first = (core, rows) if d == 1 else (across, rows + (d - 2) * part)
+            for q in range(4):
+                columns = pl.ds(q * wide + p * share, share)
+                source = gate.at[pl.ds(q * part, part), pl.ds(at, share)]
+                pairs.append((source, out.at[pl.ds(first, part), columns]))
+    for copy in fetch(pairs, sems):
+        copy.wait()
+
+
+def unfold_kernel(pos, core, from_x, both, *outs):
+    rows, wide = outs[0].shape
+    part = rows // 4
+    for source, first, out in zip((core, from_x, both), (0, 0, part), outs):
+        for q in range(4):
+            out[q * part : (q + 1) * part, :] = source[
+                rows + first : rows + first + part, q * wide : (q + 1) * wide
+            ]
 
 
 def join(out, parts):
@@ -117,20 +153,26 @@
         at += part.shape[0]
 
 
-def join_kernel(pos, near, far_a, far_b, x, from_x, weight, *outs):
-    got, passed, both_x, out_a, out_b, out_half = outs
-    join(got, (near, far_a, far_b))
-    join(passed, (far_a, far_b))
-    join(both_x, (x, from_x))
-    part, width = out_a.shape
-    columns = pl.ds(pl.multiple_of(pos[0] * width, width), width)
-    out_a[...] = weight[:part, columns]
-    out_b[...] = weight[part:, columns]
-    out_half[...] = weight[:, columns]
-
-
-def pair_kernel(pos, first, second, out):
-    join(out, (first, second))
+def half_kernel(pos, *refs):
+    parts, (whole, near), (out, joined) = refs[:PLANE], refs[PLANE:-2], refs[-2:]
+    deep = parts[0].shape[0]
+    rows, wide = whole.shape
+    quarter = rows // 4
+    for y in range(2):
+
+        @pl.when(pos[0] == y)
+        def _():
+            for j in range(2):
+                out[j * deep : (j + 1) * deep, :] = parts[2 * y + j][...]
+
+    joined[:rows, :] = whole[...]
+    for q in range(2):
+        here = slice(rows + q * quarter, rows + (q + 1) * quarter)
+        joined[here, :] = near[deep:, q * wide : (q + 1) * wide]
+
+
+def join_kernel(pos, *refs):
+    join(refs[-1], refs[:-1])
 
 
 def places_kernel(pos, own, mine, other, *outs):
@@ -140,39 +182,28 @@
         columns = pl.ds(pl.multiple_of(jnp.bitwise_xor(pos[2], d) * share, share), share)
         out[0] = own[:, columns]
         for side, block in ((pos[0], mine), (1 - pos[0], other)):
-            out[1 + side] = block[:rows, columns]
-            out[3, pl.ds(pl.multiple_of(side * part, part), part), :] = block[rows:, columns]
-
-
-def project_kernel(planes, pos, *refs):
-    x, from_x, beside = refs[:3]
-    own, halves = refs[3 : 3 + PLANE], refs[3 + PLANE : 7 + PLANE]
-    out_near, out_a, out_b = refs[7 + PLANE : 10 + PLANE]
-    outs, (out_got, out_passed) = refs[10 + PLANE : 10 + PLANE + planes], refs[-5:-3]
+            out[2 + side] = block[:rows, columns]
+            out[1, pl.ds(pl.multiple_of(side * part, part), part), :] = block[rows:, columns]
+
+
+def project_kernel(planes, pos, x, core, from_x, both, own, *refs):
+    halves, outs = refs[: 2 * planes - 2], refs[2 * planes - 2 : -3]
     xs, ws, ps = refs[-3:]
     rows = x.shape[0]
-    deep = own[0].shape[0]
+    deep = own.shape[0] // PLANE
     share = outs[0].shape[1]
-
-    def put(s, d, block):
-        ws[pl.ds(block_at(pos, s, d, deep), deep), :] = block
-
-    join(xs, (x, beside.at[:rows], from_x, beside.at[rows:]))
+    join(xs, [block.at[:rows] for block in (x, core, from_x, both)])
     for d in range(PLANE):
-        put(0, d, own[d][...])
-    for k in range(2):
-        got, passed = halves[2 * k : 2 * k + 2]
-        d = 2 * (pos[0] if k == 0 else 1 - pos[0])
-        for i, (s, j) in enumerate(((1, 0), (1, 1), (2, 0), (3, 1))):
-            put(s, d + j, got[i * deep : (i + 1) * deep, :])
-        put(3, d, passed[:deep, :])
-        put(2, d + 1, passed[deep:, :])
+        ws[pl.ds(block_at(pos, 0, d, deep), deep), :] = own[d * deep : (d + 1) * deep, :]
+    for i, half in enumerate(halves):
+        side = pos[0] if i < planes - 1 else 1 - pos[0]
+        for j in range(2):
+            at = block_at(pos, 1 + i % (planes - 1), 2 * side + j, deep)
+            ws[pl.ds(at, deep), :] = half[j * deep : (j + 1) * deep, :]
     ps[...] = dot(xs[...], ws[...]).astype(ps.dtype)
     for s in range(planes):
         at = pl.multiple_of(jnp.bitwise_xor(pos[1], s) * share, share)
         outs[s][...] = ps[:, pl.ds(at, share)]
-    join(out_got, (out_near, out_a, out_b))
-    join(out_passed, (out_a, out_b))
 
 
 def forward_stage(signal, first, work, blocks, rows):
@@ -222,6 +253,9 @@
     rows = value.shape[0] // blocks
     share = value.shape[1]
     lead = wide.shape[0] - value.shape[0]
+    own = pos[1] * PLANE + pos[2]
+    columns = pl.ds(pl.multiple_of(own * share, share), share)
+    taps, skip = taps[:, columns], skip[:, columns]
     wide[:lead, :] = jnp.zeros((lead, share), jnp.float32)
     for s in range(planes):
         for d in range(PLANE):
@@ -265,7 +299,7 @@
                 here = slice(b * rows + at, b * rows + at + ROWS)
                 conv = got[b * ROWS : (b + 1) * ROWS, h * share : (h + 1) * share]
                 result[here, :] = (
-                    conv + skip[...] * value[here, :].astype(jnp.float32)
+                    conv + skip * value[here, :].astype(jnp.float32)
                 ).astype(result.dtype)
     for s in range(planes):
         for d in range(PLANE):
@@ -286,33 +320,30 @@
                 * u[s][d * rows : (d + 1) * rows, :].astype(jnp.float32)
             ).astype(mixed.dtype)
     got = dot(mixed[...], ws[...])
-    for d in range(2):
-        outs[d][...] = got[d * rows : (d + 1) * rows].astype(outs[d].dtype)
+    outs[0][...] = got[:rows].astype(outs[0].dtype)
+    width = outs[1].shape[1]
+    for i, out in enumerate(outs[1:]):
+        out[...] = got[rows:, i * width : (i + 1) * width].astype(out.dtype)
 
 
 def upper_kernel(planes, pos, *refs):
     u, gate = refs[:planes], refs[planes : planes + 2]
-    own, halves = refs[planes + 2], refs[planes + 3 : planes + 7]
-    outs, ws, mixed = refs[planes + 7 : planes + 9], refs[planes + 9], refs[planes + 10]
+    own, halves = refs[planes + 2], refs[planes + 3 : 3 * planes + 1]
+    outs, ws, mixed = refs[3 * planes + 1 : -2], refs[-2], refs[-1]
     share = u[0].shape[1]
     width = halves[0].shape[1]
-    part = share // 2
     ws[:share, :] = own[...]
-    for k in range(2):
-        got, passed = halves[2 * k : 2 * k + 2]
-        side = pos[0] if k == 0 else 1 - pos[0]
+    for i, half in enumerate(halves):
+        side = pos[0] if i < planes - 1 else 1 - pos[0]
         columns = pl.ds(pl.multiple_of(side * width, width), width)
-        ws[share : 2 * share, columns] = got[:share, :]
-        ws[2 * share : 2 * share + part, columns] = got[share : share + part, :]
-        ws[2 * share + part : 3 * share, columns] = passed[part:, :]
-        ws[3 * share : 3 * share + part, columns] = passed[:part, :]
-        ws[3 * share + part :, columns] = got[share + part :, :]
+        s = 1 + i % (planes - 1)
+        ws[s * share : (s + 1) * share, columns] = half[:share, :]
     mixed_dots(planes, pos, u, gate, ws, mixed, outs)
 
 
 def lower_kernel(planes, pos, *refs):
     u, gate, ws = refs[:planes], refs[planes : planes + 2], refs[planes + 2]
-    mixed_dots(planes, pos, u, gate, ws, refs[planes + 5], refs[planes + 3 : planes + 5])
+    mixed_dots(planes, pos, u, gate, ws, refs[-1], refs[planes + 3 : -1])
 
 
 def local(inputs, gate_in, value_weight, short_taps, filter_taps, skip_scale, output_weight):
@@ -340,12 +371,9 @@
     def shaped(*shape, dtype=jnp.bfloat16):
         return jax.ShapeDtypeStruct(shape, dtype)
 
-    def small(kernel, outs, *args):
-        return list(call(kernel, outs, [], pos, args, 0, vmem=2))
-
-    def split(array, *heights):
-        kernel = functools.partial(split_kernel, share)
-        return small(kernel, [shaped(rows * h, wide) for h in heights], array)
+    def small(kernel, outs, *args, copies=0, fetched=0, vmem=2):
+        scratch = [pltpu.SemaphoreType.DMA((copies,))] if copies else []
+        return list(call(kernel, outs, scratch, pos, args, 0, vmem=vmem, fetched=fetched))
 
     stage = lax.optimization_barrier
     first, last, turned, back = (
@@ -353,87 +381,91 @@
     )
     part, width, positions = rows // 2, features // 2, blocks * rows
 
-    cut = split(value_weight, 1, 1, 1, 1)
-    taps_in, cut[0] = stage((filter_taps, cut[0]))
-    taps_own, taps_whole, taps_half = small(
-        filter_kernel, [shaped(rows, wide), shaped(rows, wide), shaped(part, wide)], taps_in
+    *cut, taps_own, taps_whole, out_near, out_half = call(
+        functools.partial(start_kernel, share),
+        [shaped(deep, wide)] * PLANE
+        + [shaped(rows, wide), shaped(rows, wide)]
+        + [shaped(deep + rows // 4, width), shaped(deep, width)],
+        [
+            pltpu.VMEM((deep, channels), jnp.bfloat16),
+            pltpu.VMEM((rows, channels), jnp.bfloat16),
+            pltpu.SemaphoreType.DMA((9,)),
+        ],
+        pos,
+        [value_weight, filter_taps, output_weight],
+        0,
+        vmem=60,
+        fetched=3,
+    )
+    cut = list(cut)
+    out_near = to_plane(out_near, 1)
+    gate_own, core, message = small(
+        functools.partial(across_kernel, share),
+        [shaped(rows, wide), shaped(rows * 5 // 4, features), shaped(rows * 3 // 2, features)],
+        inputs,
+        gate_in,
+        copies=13 * planes + 2,
+        fetched=2,
     )
     cut = [cut[0]] + [to_place(cut[d], d) for d in range(1, PLANE)]
     route = [
-        (y0 * devices + i, y0 * devices + (i ^ (1 + y0) * PLANE))
+        (y0 * devices + i, y0 * devices + (i ^ (2 + y0) * PLANE))
         for y0 in range(2)
         for i in range(devices)
     ]
     taps_whole = lax.ppermute(taps_whole, ("groups", "seq"), route)
-    taps_half = to_plane(taps_half, 3)
-    cut, taps_whole, taps_half, late = stage((cut, taps_whole, taps_half, inputs))
-
-    sent, lower, upper, taps_mine = small(
-        half_kernel,
-        [shaped(2 * deep, wide), shaped(deep, wide), shaped(deep, wide), shaped(rows + part, wide)],
-        *cut,
-        taps_whole,
-        taps_half,
-    )
-    near, far_a, far_b = to_plane(sent, 1), to_plane(lower, 2), to_plane(upper, 3)
-    from_x = to_place(late, 2)
+    cut, taps_whole, message, core, out_near = stage((cut, taps_whole, message, core, out_near))
+
+    sent, taps_mine = small(
+        half_kernel, [shaped(2 * deep, wide), shaped(rows + part, wide)], *cut, taps_whole, out_near
+    )
+    near, far = to_plane(sent, 1), to_plane(sent, 2)
+    from_x = to_place(message, 2)
+    core = to_place(core, 1)
     taps_other = to_group(taps_mine)
-    near, far_a, far_b, from_x, taps_other, late = stage(
-        (near, far_a, far_b, from_x, taps_other, output_weight)
-    )
-
-    got, passed, both_x, out_a, out_b, out_half = small(
-        join_kernel,
-        [shaped(4 * deep, wide), shaped(2 * deep, wide), shaped(2 * rows, features)]
-        + [shaped(deep // 2, width), shaped(deep // 2, width), shaped(deep, width)],
-        near,
-        far_a,
-        far_b,
-        inputs,
-        from_x,
-        late,
-    )
-    passed = to_plane(passed, 1)
-    got_other = to_group(got)
-    out_a, out_b = to_plane(out_a, 2), to_plane(out_b, 3)
-    beside = to_place(both_x, 1)
+    near, far, from_x, taps_other, core, out_half = stage(
+        (near, far, from_x, taps_other, core, out_half)
+    )
+
+    passed = to_plane(far, 1)
+    near_other, far_other = to_group(near), to_group(far)
+    out_far = to_plane(out_half, 2)
+    both = to_place(from_x, 1)
     taps_parts = small(
         places_kernel, [shaped(planes, rows, share)] * PLANE, taps_own, taps_mine, taps_other
     )
-    passed, got_other, out_a, out_b, beside, taps_parts, out_half = stage(
-        (passed, got_other, out_a, out_b, beside, taps_parts, out_half)
+    passed, near_other, far_other, out_far, both, taps_parts = stage(
+        (passed, near_other, far_other, out_far, both, taps_parts)
     )
 
     passed_other = to_group(passed)
-    out_near = to_plane(out_half, 1)
+    out_passed = to_plane(out_far, 1)
     taps_parts = [taps_parts[0]] + [to_place(taps_parts[d], d) for d in range(1, PLANE)]
-    passed, passed_other, out_near, taps_parts, late = stage(
-        (passed, passed_other, out_near, taps_parts, gate_in)
-    )
-
-    gate_own, gate_beside, gate_x = split(late, 1, 1, 2)
-    *projected, out_got, out_passed = call(
+    held = small(join_kernel, [shaped(PLANE * deep, wide)], *cut)[0]
+    passed, passed_other, out_passed, taps_parts, held = stage(
+        (passed, passed_other, out_passed, taps_parts, held)
+    )
+    projected = call(
         functools.partial(project_kernel, planes),
-        [shaped(PLANE * rows, share)] * planes + [shaped(2 * deep, width), shaped(deep, width)],
+        [shaped(PLANE * rows, share)] * planes,
         [
             pltpu.VMEM((PLANE * rows, features), jnp.bfloat16),
             pltpu.VMEM((features, wide), jnp.bfloat16),
             pltpu.VMEM((PLANE * rows, wide), jnp.bfloat16),
         ],
         pos,
-        [inputs, from_x, beside, *cut, got, passed, got_other, passed_other]
-        + [out_near, out_a, out_b],
+        [inputs, core, from_x, both, held, near, far, passed]
+        + [near_other, far_other, passed_other],
         2 * PLANE * rows * features * wide,
-        vmem=12,
-    )
-    projected, out_got, out_passed, gate_x = stage((projected, out_got, out_passed, gate_x))
+        vmem=8,
+    )
+    projected, out_far, out_near = stage((projected, out_far, out_near))
 
     def spread(parts):
         return [parts[0]] + [to_plane(parts[s], s) for s in range(1, planes)]
 
     signal = spread(projected)
-    out_other = to_group(out_got)
-    gate_x = to_place(gate_x, 2)
+    out_other = [to_group(out_near), to_group(out_far)]
     response = call(
         functools.partial(taps_kernel, blocks, planes),
         [shaped(blocks + 1, 2 * rows, share)],
@@ -444,15 +476,11 @@
         pos,
         [*taps_parts, first, turned],
         2 * positions * share * (32 * ROWS + 4 * rows),
-        vmem=8,
+        vmem=4,
     )[0]
-    taps = lax.dynamic_slice_in_dim(short_taps, index * share, share, 1)
-    skip = lax.dynamic_slice_in_dim(skip_scale, index * share, share, 0)[None]
-    signal, out_other, gate_x, response, taps, skip, out_passed = stage(
-        (signal, out_other, gate_x, response, taps, skip, out_passed)
-    )
-
-    out_passed = to_plane(out_passed, 1)
+    gate = [gate_own] + small(unfold_kernel, [shaped(rows, wide)] * 3, core, from_x, both)
+    signal, out_other, response = stage((signal, out_other, response))
+
     mixed = call(
         functools.partial(conv_kernel, blocks, planes),
         [shaped(2 * rows, share)] * (2 * planes),
@@ -463,19 +491,15 @@
             pltpu.VMEM((positions, share), jnp.bfloat16),
         ],
         pos,
-        [*signal, taps, skip, response, first, last, turned, back],
+        [*signal, short_taps, skip_scale[None], response, first, last, turned, back],
         4 * positions * share * (32 * ROWS + 4 * rows),
-        vmem=12,
-    )
-    gate_beside = small(pair_kernel, [shaped(2 * rows, wide)], gate_beside, gate_x[rows:])[0]
-    mixed, out_passed, gate_beside = stage((mixed, out_passed, gate_beside))
+        vmem=8,
+    )
+    mixed, out_passed = stage((mixed, out_passed))
 
     upper = spread(mixed[planes:])
-    passed_other = to_group(out_passed)
-    gate_beside = to_place(gate_beside, 1)
-    upper, passed_other, gate_beside, lower = stage(
-        (upper, passed_other, gate_beside, mixed[:planes])
-    )
+    out_other += [to_group(out_passed)]
+    upper, out_other, lower = stage((upper, out_other, mixed[:planes]))
     scratch = [pltpu.VMEM((2 * rows, wide), jnp.bfloat16)]
     flops = 4 * rows * features * wide
     partial_two, partial_three, gathered = call(
@@ -484,27 +508,28 @@
         + [shaped(wide, features)],
         scratch,
         pos,
-        [*upper, gate_x[:rows], gate_beside[rows:], output_weight]
-        + [out_got, out_passed, out_other, passed_other],
+        [*upper, *gate[2:], output_weight]
+        + [out_near, out_far, out_passed, *out_other],
         flops,
-        vmem=12,
+        vmem=8,
     )
     across = partial_two + to_place(partial_three, 1).astype(jnp.float32)
     across, lower = stage((across.astype(jnp.bfloat16), lower))
 
     across = to_place(across, 2)
     lower = spread(lower)
-    partial_zero, partial_one = call(
+    partial_zero, *partial_one = call(
         functools.partial(lower_kernel, planes),
-        [shaped(rows, features, dtype=jnp.float32), shaped(rows, features)],
+        [shaped(rows, features, dtype=jnp.float32)] + [shaped(rows, features // 4)] * 4,
         scratch,
         pos,
-        [*lower, gate_own, gate_beside[:rows], gathered],
-        flops,
-        vmem=12,
-    )
-    result = partial_zero + to_place(partial_one, 1).astype(jnp.float32)
-    return (result + across.astype(jnp.float32)).astype(jnp.bfloat16)
+        [*lower, *gate[:2], gathered],
+        0,
+        vmem=8,
+    )
+    partial_one = jnp.concatenate([to_place(block, 1) for block in partial_one], 1)
+    result = partial_zero + partial_one.astype(jnp.float32) + across.astype(jnp.float32)
+    return result.astype(jnp.bfloat16)
 
 
 def passed_along(block, axis, distance):

time: 131 us -> 115 us (0.88)
  waiting for transfers between devices: 54.9 us -> 46.7 us
  local copies, waits for them, and re-layouts: 11.7 us -> 4.62 us
  starting transfers between devices: 48.4 us -> 44.6 us
  Pallas kernels: 14.3 us -> 16.4 us
    ppermute x18 -> x15, waiting for transfers between devices: 40 us -> 30.1 us  [to_plane(): lax.ppermute(block, 'seq', [(i, i ^ s * PLANE) for i in range(devices)])]
    unnamed x52 -> x30, local copies, waits for them, and re-layouts: 10.9 us -> 4.62 us
    ppermute x5 -> x7, waiting for transfers between devices: 0.01 us -> 6.12 us  [to_group(): return lax.ppermute(block, 'groups', [(0, 1), (1, 0)])]
    ppermute x13 -> x15, waiting for transfers between devices: 14.9 us -> 9.08 us  [to_place(): return lax.ppermute(block, 'seq', [(i, i ^ d) for i in range(devices)])]
    ppermute x5 -> x7, starting transfers between devices: 11.8 us -> 8.75 us  [to_group(): return lax.ppermute(block, 'groups', [(0, 1), (1, 0)])]
    pallas_call x12 -> x11, Pallas kernels: 14.3 us -> 16.4 us  [call(): pl.pallas_call(kernel, out_shape=outs, in_specs=in_specs, out_specs=[pl.B...]
    ppermute x1, waiting for transfers between devices: 0.01 us -> 1.46 us  [local(): taps_whole = lax.ppermute(taps_whole, ('groups', 'seq'), route)]
    ppermute x13 -> x15, starting transfers between devices: 8.82 us -> 8.09 us  [to_place(): return lax.ppermute(block, 'seq', [(i, i ^ d) for i in range(devices)])]
  transfers between devices with their start and end apart: 37 -> 38, of which waited for: 12 -> 20; matrix products, arithmetic and copies ran while one was open for 1% -> 0% of each run, Pallas kernels for 6% -> 6%
where the time goes in v3:
time: 115 us; the launch traced here: 114 us
  waiting for transfers between devices  46.7 us (41%)
  starting transfers between devices  44.6 us (39%)
  Pallas kernels  16.4 us (14%)
  local copies, waits for them, and re-layouts  4.62 us (4%)
  other arithmetic  1.74 us (2%)
    ppermute x15, waiting for transfers between devices, to_plane(): lax.ppermute(block, 'seq', [(i, i ^ s * PLANE) for i in range(devices)])  30.1 us
    ppermute x15, starting transfers between devices, to_plane(): lax.ppermute(block, 'seq', [(i, i ^ s * PLANE) for i in range(devices)])  25.2 us
    pallas_call x11, Pallas kernels, call(): pl.pallas_call(kernel, out_shape=outs, in_specs=in_specs, out_specs=[pl.B...  16.4 us
    ppermute x15, waiting for transfers between devices, to_place(): return lax.ppermute(block, 'seq', [(i, i ^ d) for i in range(devices)])  9.08 us
    ppermute x7, starting transfers between devices, to_group(): return lax.ppermute(block, 'groups', [(0, 1), (1, 0)])  8.75 us
    ppermute x15, starting transfers between devices, to_place(): return lax.ppermute(block, 'seq', [(i, i ^ d) for i in range(devices)])  8.09 us
    ppermute x7, waiting for transfers between devices, to_group(): return lax.ppermute(block, 'groups', [(0, 1), (1, 0)])  6.12 us
    unnamed x30, local copies, waits for them, and re-layouts  4.62 us
  transfers between devices with their start and end apart: 38, of which 20 were waited for; matrix products, arithmetic and copies ran while one was open for 0% of the time, Pallas kernels for 6%

profile of v3, /device:TPU:0, one launch (start us, length us, event | category | flops | bytes accessed | tf_op | source)
XLA Modules:
  0.0 114.3 jit_solution(166085642013629052)
XLA Ops:
  0.7 3.3 %shard_map.109 = (bf16[128,512]{1,0:T(8,128)(2,1)}, bf16[128,512]{1,0:T(8,128)(2,1)}, bf16[128,512]{1,0:T(8,128)(2,1)}, bf16[128,512]{1,0:T(8,128)(2,1)}, bf16[1...) custom-call(s32[3]{0:T(128)} %pad_add_fusion.pos, ...), custom_call_target="tpu_custom_call" | custom-call | tf_op jit(solution)/shard_map/pallas_call | solution.py:60
  4.0 3.1 %collective-permute-start.4 = (bf16[160,1024]{1,0:T(8,128)(2,1)}, bf16[160,1024]{1,0:T(8,128)(2,1)S(1)}, u32[]{:S(2)}, u32[]{:S(2)}) collective-permute-start(bf16[160,1024]{1,0:T(8,128)(2,1)} %get-tuple-element.121), channel_id=1, source_target_pairs={{0,4},{1,5},{2,6},{3,7},{4,0},{5,1},{6,2},{7,3},{8,12},{9,13},{10,... | collective-permute-start | bytes 983048 | tf_op jit(solution)/shard_map/ppermute | solution.py:366
  7.1 1.5 %collective-permute-start.1 = (bf16[128,512]{1,0:T(8,128)(2,1)}, bf16[128,512]{1,0:T(8,128)(2,1)S(1)}, u32[]{:S(2)}, u32[]{:S(2)}) collective-permute-start(bf16[128,512]{1,0:T(8,128)(2,1)} %get-tuple-element.116), channel_id=1, source_target_pairs={{0,2},{1,3},{2,0},{3,1},{4,6},{5,7},{6,4},{7,5},{8,10},{9,11},{10,... | collective-permute-start | bytes 393224 | tf_op jit(solution)/shard_map/ppermute | solution.py:363
  8.9 2.6 %collective-permute-start.3 = (bf16[128,512]{1,0:T(8,128)(2,1)}, bf16[128,512]{1,0:T(8,128)(2,1)S(1)}, u32[]{:S(2)}, u32[]{:S(2)}) collective-permute-start(bf16[128,512]{1,0:T(8,128)(2,1)} %get-tuple-element.118), channel_id=1, source_target_pairs={{0,8},{1,9},{2,10},{3,11},{4,12},{5,13},{6,14},{7,15},{8,0},{9,1},... | collective-permute-start | bytes 393224 | tf_op jit(solution)/shard_map/ppermute | solution.py:416
  11.5 1.0 copy-done.2
  12.6 1.0 copy-done.6
  14.3 1.4 %shard_map.110 = (bf16[128,512]{1,0:T(8,128)(2,1)S(1)}, bf16[160,2048]{1,0:T(8,128)(2,1)S(1)}, bf16[192,2048]{1,0:T(8,128)(2,1)S(1)}) custom-call(s32[3]{0:T(128)S(1)} %copy-done.11, bf16[128,2048]{1,0:T(8,128)(2,1)S(1)} %copy-done.2, bf16[128,2048]{1,0:T(8,128)(2,1)S(1)} %copy-done.6), custom_call_target="tpu_custom_call" | custom-call | tf_op jit(solution)/shard_map/pallas_call | solution.py:60
  15.7 1.5 %collective-permute-done.3.refs_4_ = bf16[128,512]{1,0:T(8,128)(2,1)S(1)} collective-permute-done((bf16[128,512]{1,0:T(8,128)(2,1)}, bf16[128,512]{1,0:T(8,128)(2,1)S(1)}, u32[]{:S(2)}, u32[]{:S(2)}) %collective-permute-start.3) | collective-permute-done | bytes 131104 | tf_op jit(solution)/shard_map/ppermute | solution.py:416
  17.8 1.7 %collective-permute-start.7 = (bf16[192,2048]{1,0:T(8,128)(2,1)S(1)}, bf16[192,2048]{1,0:T(8,128)(2,1)S(1)}, u32[]{:S(2)}, u32[]{:S(2)}) collective-permute-start(bf16[192,2048]{1,0:T(8,128)(2,1)S(1)} %get-tuple-element.129), channel_id=1, source_target_pairs={{0,2},{1,3},{2,0},{3,1},{4,6},{5,7},{6,4},{7,5},{8,10},{9,11},{10,... | collective-permute-start | bytes 2359304 | tf_op jit(solution)/shard_map/ppermute | solution.py:363
  19.5 0.9 copy-done.7
  21.0 2.5 %collective-permute-start.6 = (bf16[256,512]{1,0:T(8,128)(2,1)S(1)}, bf16[256,512]{1,0:T(8,128)(2,1)S(1)}, u32[]{:S(2)}, u32[]{:S(2)}) collective-permute-start(bf16[256,512]{1,0:T(8,128)(2,1)S(1)} %get-tuple-element.128), channel_id=1, source_target_pairs={{0,8},{1,9},{2,10},{3,11},{4,12},{5,13},{6,14},{7,15},{8,0},{9,1},... | collective-permute-start | bytes 786440 | tf_op jit(solution)/shard_map/ppermute | solution.py:366
  23.5 1.7 %collective-permute-start.5 = (bf16[256,512]{1,0:T(8,128)(2,1)S(1)}, bf16[256,512]{1,0:T(8,128)(2,1)S(1)}, u32[]{:S(2)}, u32[]{:S(2)}) collective-permute-start(bf16[256,512]{1,0:T(8,128)(2,1)S(1)} %get-tuple-element.128), channel_id=1, source_target_pairs={{0,4},{1,5},{2,6},{3,7},{4,0},{5,1},{6,2},{7,3},{8,12},{9,13},{10,... | collective-permute-start | bytes 786440 | tf_op jit(solution)/shard_map/ppermute | solution.py:366
  25.2 1.5 %collective-permute-start.8 = (bf16[192,512]{1,0:T(8,128)(2,1)S(1)}, bf16[192,512]{1,0:T(8,128)(2,1)S(1)}, u32[]{:S(2)}, u32[]{:S(2)}) collective-permute-start(bf16[192,512]{1,0:T(8,128)(2,1)S(1)} %get-tuple-element.130.mine), channel_id=1, source_target_pairs={{0,16},{16,0},{1,17},{17,1},{2,18},{18,2},{3,19},{19,3},{4,20},{20... | collective-permute-start | bytes 589832 | tf_op jit(solution)/shard_map/ppermute | solution.py:369
  26.7 5.2 %collective-permute-done.8.other = bf16[192,512]{1,0:T(8,128)(2,1)S(1)} collective-permute-done((bf16[192,512]{1,0:T(8,128)(2,1)S(1)}, bf16[192,512]{1,0:T(8,128)(2,1)S(1)}, u32[]{:S(2)}, u32[]{:S(2)}) %collective-permute-start.8) | collective-permute-done | bytes 196640 | tf_op jit(solution)/shard_map/ppermute | solution.py:369
  31.9 4.3 %collective-permute-done.6.refs_1_ = bf16[256,512]{1,0:T(8,128)(2,1)S(1)} collective-permute-done((bf16[256,512]{1,0:T(8,128)(2,1)S(1)}, bf16[256,512]{1,0:T(8,128)(2,1)S(1)}, u32[]{:S(2)}, u32[]{:S(2)}) %collective-permute-start.6) | collective-permute-done | bytes 262176 | tf_op jit(solution)/shard_map/ppermute | solution.py:366
  36.5 2.4 %collective-permute-start.13 = (bf16[128,1024]{1,0:T(8,128)(2,1)}, bf16[128,1024]{1,0:T(8,128)(2,1)S(1)}, u32[]{:S(2)}, u32[]{:S(2)}) collective-permute-start(bf16[128,1024]{1,0:T(8,128)(2,1)} %get-tuple-element.137), channel_id=1, source_target_pairs={{0,8},{1,9},{2,10},{3,11},{4,12},{5,13},{6,14},{7,15},{8,0},{9,1},... | collective-permute-start | bytes 786440 | tf_op jit(solution)/shard_map/ppermute | solution.py:366
  39.0 1.0 collective-permute-start.11
  39.9 1.1 collective-permute-start.12
  41.0 1.7 %collective-permute-start.10 = (bf16[256,512]{1,0:T(8,128)(2,1)S(1)}, bf16[256,512]{1,0:T(8,128)(2,1)S(1)}, u32[]{:S(2)}, u32[]{:S(2)}) collective-permute-start(bf16[256,512]{1,0:T(8,128)(2,1)S(1)} %collective-permute-done.6.refs_1_), channel_id=1, source_target_pairs={{0,4},{1,5},{2,6},{3,7},{4,0},{5,1},{6,2},{7,3},{8,12},{9,13},{10,... | collective-permute-start | bytes 786440 | tf_op jit(solution)/shard_map/ppermute | solution.py:366
  42.7 0.9 copy-done.10
  44.2 7.8 %collective-permute-done.13.refs_8_ = bf16[128,1024]{1,0:T(8,128)(2,1)S(1)} collective-permute-done((bf16[128,1024]{1,0:T(8,128)(2,1)}, bf16[128,1024]{1,0:T(8,128)(2,1)S(1)}, u32[]{:S(2)}, u32[]{:S(2)}) %collective-permute-start.13) | collective-permute-done | bytes 262176 | tf_op jit(solution)/shard_map/ppermute | solution.py:366
  52.1 0.9 collective-permute-done.12.refs_4_
  53.0 2.7 %collective-permute-start.15 = (bf16[256,512]{1,0:T(8,128)(2,1)S(1)}, bf16[256,512]{1,0:T(8,128)(2,1)S(1)}, u32[]{:S(2)}, u32[]{:S(2)}) collective-permute-start(bf16[256,512]{1,0:T(8,128)(2,1)S(1)} %collective-permute-done.10.refs_2_), channel_id=1, source_target_pairs={{0,16},{16,0},{1,17},{17,1},{2,18},{18,2},{3,19},{19,3},{4,20},{20... | collective-permute-start | bytes 786440 | tf_op jit(solution)/shard_map/ppermute | solution.py:369
  55.9 1.5 %collective-permute-start.18 = (bf16[4,128,128]{2,1,0:T(8,128)(2,1)S(1)}, bf16[4,128,128]{2,1,0:T(8,128)(2,1)S(1)}, u32[]{:S(2)}, u32[]{:S(2)}) collective-permute-start(bf16[4,128,128]{2,1,0:T(8,128)(2,1)S(1)} %get-tuple-element.149), channel_id=1, source_target_pairs={{0,2},{1,3},{2,0},{3,1},{4,6},{5,7},{6,4},{7,5},{8,10},{9,11},{10,... | collective-permute-start | bytes 393224 | tf_op jit(solution)/shard_map/ppermute | solution.py:363
  58.4 3.8 %collective-permute-done.18.refs_2_ = bf16[4,128,128]{2,1,0:T(8,128)(2,1)S(1)} collective-permute-done((bf16[4,128,128]{2,1,0:T(8,128)(2,1)S(1)}, bf16[4,128,128]{2,1,0:T(8,128)(2,1)S(1)}, u32[]{:S(2)}, u32[]{:S(2)}) %collective-permute-start.18) | collective-permute-done | bytes 131104 | tf_op jit(solution)/shard_map/ppermute | solution.py:363
  62.2 2.0 %collective-permute-done.19.refs_3_ = bf16[4,128,128]{2,1,0:T(8,128)(2,1)S(1)} collective-permute-done((bf16[4,128,128]{2,1,0:T(8,128)(2,1)S(1)}, bf16[4,128,128]{2,1,0:T(8,128)(2,1)S(1)}, u32[]{:S(2)}, u32[]{:S(2)}) %collective-permute-start.19) | collective-permute-done | bytes 131104 | tf_op jit(solution)/shard_map/ppermute | solution.py:363
  64.3 2.0 %shard_map.114 = (bf16[512,128]{1,0:T(8,128)(2,1)S(1)}, bf16[512,128]{1,0:T(8,128)(2,1)S(1)}, bf16[512,128]{1,0:T(8,128)(2,1)S(1)}, bf16[512,128]{1,0:T(8,128)(2,1)S(1)}) custom-call(s32[3]{0:T(128)S(1)} %copy-done.12, bf16[128,2048]{1,0:T(8,128)(2,1)S(1)} %copy-done.3, bf16[160,2048]{1,0:T(8,128)(2,1)S(1)} %collective-permute-done.9.core, ...), custom_call_target="tpu_custom_call" | custom-call | flops 1073741824 | bytes 5373952 | tf_op jit(solution)/shard_map/pallas_call | solution.py:60
  67.2 1.3 %collective-permute-start.24 = (bf16[128,1024]{1,0:T(8,128)(2,1)S(1)}, bf16[128,1024]{1,0:T(8,128)(2,1)S(1)}, u32[]{:S(2)}, u32[]{:S(2)}) collective-permute-start(bf16[128,1024]{1,0:T(8,128)(2,1)S(1)} %collective-permute-done.13.refs_8_), channel_id=1, source_target_pairs={{0,16},{16,0},{1,17},{17,1},{2,18},{18,2},{3,19},{19,3},{4,20},{20... | collective-permute-start | bytes 786440 | tf_op jit(solution)/shard_map/ppermute | solution.py:369
  68.5 1.8 %collective-permute-start.20 = (bf16[512,128]{1,0:T(8,128)(2,1)S(1)}, bf16[512,128]{1,0:T(8,128)(2,1)S(1)}, u32[]{:S(2)}, u32[]{:S(2)}) collective-permute-start(bf16[512,128]{1,0:T(8,128)(2,1)S(1)} %get-tuple-element.161), channel_id=1, source_target_pairs={{0,4},{1,5},{2,6},{3,7},{4,0},{5,1},{6,2},{7,3},{8,12},{9,13},{10,... | collective-permute-start | bytes 393224 | tf_op jit(solution)/shard_map/ppermute | solution.py:366
  70.3 1.2 %collective-permute-start.21 = (bf16[512,128]{1,0:T(8,128)(2,1)S(1)}, bf16[512,128]{1,0:T(8,128)(2,1)S(1)}, u32[]{:S(2)}, u32[]{:S(2)}) collective-permute-start(bf16[512,128]{1,0:T(8,128)(2,1)S(1)} %get-tuple-element.162), channel_id=1, source_target_pairs={{0,8},{1,9},{2,10},{3,11},{4,12},{5,13},{6,14},{7,15},{8,0},{9,1},... | collective-permute-start | bytes 393224 | tf_op jit(solution)/shard_map/ppermute | solution.py:366
  71.5 1.4 %collective-permute-start.22 = (bf16[512,128]{1,0:T(8,128)(2,1)S(1)}, bf16[512,128]{1,0:T(8,128)(2,1)S(1)}, u32[]{:S(2)}, u32[]{:S(2)}) collective-permute-start(bf16[512,128]{1,0:T(8,128)(2,1)S(1)} %get-tuple-element.163), channel_id=1, source_target_pairs={{0,12},{1,13},{2,14},{3,15},{4,8},{5,9},{6,10},{7,11},{8,4},{9,5},... | collective-permute-start | bytes 393224 | tf_op jit(solution)/shard_map/ppermute | solution.py:366
  72.8 1.6 %shard_map.115.refs_6_ = bf16[17,256,128]{2,1,0:T(8,128)(2,1)S(1)} custom-call(s32[3]{0:T(128)S(1)} %copy-done.12, bf16[4,128,128]{2,1,0:T(8,128)(2,1)S(1)} %get-tuple-element.166.refs_0_, bf16[4,128,128]{2,1,0:T(8,128)(2,1)S(1)} %collective-permute-done.17.refs_1_, bf16[4,128,128]{2,1,0:T(8,128)(2,1)S(1)} %collective-permute-done.18.refs_2_, ...), custom_call_target="tpu_custom_call" | custom-call | flops 536870912 | bytes 4128768 | tf_op jit(solution)/shard_map/pallas_call | solution.py:60
  75.0 7.9 %collective-permute-done.21.refs_2_ = bf16[512,128]{1,0:T(8,128)(2,1)S(1)} collective-permute-done((bf16[512,128]{1,0:T(8,128)(2,1)S(1)}, bf16[512,128]{1,0:T(8,128)(2,1)S(1)}, u32[]{:S(2)}, u32[]{:S(2)}) %collective-permute-start.21) | collective-permute-done | bytes 131104 | tf_op jit(solution)/shard_map/ppermute | solution.py:366
  83.0 3.0 %shard_map.116 = (bf16[256,128]{1,0:T(8,128)(2,1)S(1)}, bf16[256,128]{1,0:T(8,128)(2,1)S(1)}, bf16[256,128]{1,0:T(8,128)(2,1)S(1)}, bf16[256,128]{1,0:T(8,128)(2...) custom-call(s32[3]{0:T(128)S(1)} %copy-done.12, ...), custom_call_target="tpu_custom_call" | custom-call | flops 1073741824 | bytes 7176192 | tf_op jit(solution)/shard_map/pallas_call | solution.py:60
  86.4 2.1 %collective-permute-start.25 = (bf16[256,128]{1,0:T(8,128)(2,1)S(1)}, bf16[256,128]{1,0:T(8,128)(2,1)S(1)}, u32[]{:S(2)}, u32[]{:S(2)}) collective-permute-start(bf16[256,128]{1,0:T(8,128)(2,1)S(1)} %get-tuple-element.185), channel_id=1, source_target_pairs={{0,4},{1,5},{2,6},{3,7},{4,0},{5,1},{6,2},{7,3},{8,12},{9,13},{10,... | collective-permute-start | bytes 196616 | tf_op jit(solution)/shard_map/ppermute | solution.py:366
  88.5 1.2 %collective-permute-start.26 = (bf16[256,128]{1,0:T(8,128)(2,1)S(1)}, bf16[256,128]{1,0:T(8,128)(2,1)S(1)}, u32[]{:S(2)}, u32[]{:S(2)}) collective-permute-start(bf16[256,128]{1,0:T(8,128)(2,1)S(1)} %get-tuple-element.186), channel_id=1, source_target_pairs={{0,8},{1,9},{2,10},{3,11},{4,12},{5,13},{6,14},{7,15},{8,0},{9,1},... | collective-permute-start | bytes 196616 | tf_op jit(solution)/shard_map/ppermute | solution.py:366
  89.7 1.5 %collective-permute-start.27 = (bf16[256,128]{1,0:T(8,128)(2,1)S(1)}, bf16[256,128]{1,0:T(8,128)(2,1)S(1)}, u32[]{:S(2)}, u32[]{:S(2)}) collective-permute-start(bf16[256,128]{1,0:T(8,128)(2,1)S(1)} %get-tuple-element.187), channel_id=1, source_target_pairs={{0,12},{1,13},{2,14},{3,15},{4,8},{5,9},{6,10},{7,11},{8,4},{9,5},... | collective-permute-start | bytes 196616 | tf_op jit(solution)/shard_map/ppermute | solution.py:366
  91.7 3.2 %collective-permute-done.26.refs_2_ = bf16[256,128]{1,0:T(8,128)(2,1)S(1)} collective-permute-done((bf16[256,128]{1,0:T(8,128)(2,1)S(1)}, bf16[256,128]{1,0:T(8,128)(2,1)S(1)}, u32[]{:S(2)}, u32[]{:S(2)}) %collective-permute-start.26) | collective-permute-done | bytes 65568 | tf_op jit(solution)/shard_map/ppermute | solution.py:366
  94.9 0.9 collective-permute-done.27.refs_3_
  95.8 1.4 %shard_map.118 = (f32[128,2048]{1,0:T(8,128)S(1)}, bf16[128,2048]{1,0:T(8,128)(2,1)S(1)}, bf16[512,2048]{1,0:T(8,128)(2,1)S(1)}) custom-call(s32[3]{0:T(128)S(1)} %copy-done.12, bf16[256,128]{1,0:T(8,128)(2,1)S(1)} %get-tuple-element.195.refs_0_, bf16[256,128]{1,0:T(8,128)(2,1)S(1)} %collective-permute-done.25.refs_1_, ...), custom_call_target="tpu_custom_call" | custom-call | flops 536870912 | bytes 6422528 | tf_op jit(solution)/shard_map/pallas_call | solution.py:60
  97.3 1.9 %collective-permute-done.29 = bf16[128,2048]{1,0:T(8,128)(2,1)S(1)} collective-permute-done((bf16[128,2048]{1,0:T(8,128)(2,1)S(1)}, bf16[128,2048]{1,0:T(8,128)(2,1)S(1)}, u32[]{:S(2)}, u32[]{:S(2)}) %collective-permute-start.29) | collective-permute-done | bytes 524320 | tf_op jit(solution)/shard_map/ppermute | solution.py:363
  99.3 1.6 %collective-permute-start.37 = (bf16[128,2048]{1,0:T(8,128)(2,1)S(1)}, bf16[128,2048]{1,0:T(8,128)(2,1)S(1)}, u32[]{:S(2)}, u32[]{:S(2)}) collective-permute-start(bf16[128,2048]{1,0:T(8,128)(2,1)S(1)} %add_convert_fusion.1), channel_id=1, source_target_pairs={{0,2},{1,3},{2,0},{3,1},{4,6},{5,7},{6,4},{7,5},{8,10},{9,11},{10,... | collective-permute-start | bytes 1572872 | tf_op jit(solution)/shard_map/ppermute | solution.py:363
  100.9 1.1 collective-permute-start.30
  101.9 1.6 %collective-permute-start.31 = (bf16[256,128]{1,0:T(8,128)(2,1)S(1)}, bf16[256,128]{1,0:T(8,128)(2,1)S(1)}, u32[]{:S(2)}, u32[]{:S(2)}) collective-permute-start(bf16[256,128]{1,0:T(8,128)(2,1)S(1)} %get-tuple-element.212), channel_id=1, source_target_pairs={{0,8},{1,9},{2,10},{3,11},{4,12},{5,13},{6,14},{7,15},{8,0},{9,1},... | collective-permute-start | bytes 196616 | tf_op jit(solution)/shard_map/ppermute | solution.py:366
  103.5 1.8 %collective-permute-start.32 = (bf16[256,128]{1,0:T(8,128)(2,1)S(1)}, bf16[256,128]{1,0:T(8,128)(2,1)S(1)}, u32[]{:S(2)}, u32[]{:S(2)}) collective-permute-start(bf16[256,128]{1,0:T(8,128)(2,1)S(1)} %get-tuple-element.213), channel_id=1, source_target_pairs={{0,12},{1,13},{2,14},{3,15},{4,8},{5,9},{6,10},{7,11},{8,4},{9,5},... | collective-permute-start | bytes 196616 | tf_op jit(solution)/shard_map/ppermute | solution.py:366
  105.6 4.3 %collective-permute-done.31.refs_2_ = bf16[256,128]{1,0:T(8,128)(2,1)S(1)} collective-permute-done((bf16[256,128]{1,0:T(8,128)(2,1)S(1)}, bf16[256,128]{1,0:T(8,128)(2,1)S(1)}, u32[]{:S(2)}, u32[]{:S(2)}) %collective-permute-start.31) | collective-permute-done | bytes 65568 | tf_op jit(solution)/shard_map/ppermute | solution.py:366
  109.9 1.3 %shard_map.119 = (f32[128,2048]{1,0:T(8,128)S(1)}, bf16[128,512]{1,0:T(8,128)(2,1)S(1)}, bf16[128,512]{1,0:T(8,128)(2,1)S(1)}, bf16[128,512]{1,0:T(8,128)(2,1)S(1)}, bf16[128,512]{1,0:T(8,128)(2,1)S(1)}) custom-call(s32[3]{0:T(128)S(1)} %copy-done.12, bf16[256,128]{1,0:T(8,128)(2,1)S(1)} %get-tuple-element.210.refs_0_, ...), custom_call_target="tpu_custom_call" | custom-call | tf_op jit(solution)/shard_map/pallas_call | solution.py:60
  113.3 1.0 add_convert_fusion
  (72 shorter events, 10.1 us)
Async XLA Ops:
  0.7 63.6 %copy-start.3 = (bf16[128,2048]{1,0:T(8,128)(2,1)S(1)}, bf16[128,2048]{1,0:T(8,128)(2,1)}, u32[]{:S(2)}) copy-start(bf16[128,2048]{1,0:T(8,128)(2,1)} %x.3) | copy-start | bytes 1572868
  0.7 63.6 %copy-start.12 = (s32[3]{0:T(128)S(1)}, s32[3]{0:T(128)}, u32[]{:S(2)}) copy-start(s32[3]{0:T(128)} %pad_add_fusion.pos) | copy-start | bytes 40
  4.0 13.8 %collective-permute-start.4 = (bf16[160,1024]{1,0:T(8,128)(2,1)}, bf16[160,1024]{1,0:T(8,128)(2,1)S(1)}, u32[]{:S(2)}, u32[]{:S(2)}) collective-permute-start(bf16[160,1024]{1,0:T(8,128)(2,1)} %get-tuple-element.121), channel_id=1, source_target_pairs={{0,4},{1,5},{2,6},{3,7},{4,0},{5,1},{6,2},{7,3},{8,12},{9,13},{10,... | collective-permute-start | bytes 983048 | tf_op jit(solution)/shard_map/ppermute | solution.py:366
  7.1 8.6 %collective-permute-start = (bf16[128,512]{1,0:T(8,128)(2,1)}, bf16[128,512]{1,0:T(8,128)(2,1)S(1)}, u32[]{:S(2)}, u32[]{:S(2)}) collective-permute-start(bf16[128,512]{1,0:T(8,128)(2,1)} %get-tuple-element.115), channel_id=1, source_target_pairs={{0,1},{1,0},{2,3},{3,2},{4,5},{5,4},{6,7},{7,6},{8,9},{9,8},{10,11... | collective-permute-start | bytes 393224 | tf_op jit(solution)/shard_map/ppermute | solution.py:363
  7.1 8.6 %collective-permute-start.1 = (bf16[128,512]{1,0:T(8,128)(2,1)}, bf16[128,512]{1,0:T(8,128)(2,1)S(1)}, u32[]{:S(2)}, u32[]{:S(2)}) collective-permute-start(bf16[128,512]{1,0:T(8,128)(2,1)} %get-tuple-element.116), channel_id=1, source_target_pairs={{0,2},{1,3},{2,0},{3,1},{4,6},{5,7},{6,4},{7,5},{8,10},{9,11},{10,... | collective-permute-start | bytes 393224 | tf_op jit(solution)/shard_map/ppermute | solution.py:363
  8.6 7.1 %collective-permute-start.2 = (bf16[128,512]{1,0:T(8,128)(2,1)}, bf16[128,512]{1,0:T(8,128)(2,1)S(1)}, u32[]{:S(2)}, u32[]{:S(2)}) collective-permute-start(bf16[128,512]{1,0:T(8,128)(2,1)} %get-tuple-element.117), channel_id=1, source_target_pairs={{0,3},{1,2},{2,1},{3,0},{4,7},{5,6},{6,5},{7,4},{8,11},{9,10},{10,... | collective-permute-start | bytes 393224 | tf_op jit(solution)/shard_map/ppermute | solution.py:363
  8.9 8.2 %collective-permute-start.3 = (bf16[128,512]{1,0:T(8,128)(2,1)}, bf16[128,512]{1,0:T(8,128)(2,1)S(1)}, u32[]{:S(2)}, u32[]{:S(2)}) collective-permute-start(bf16[128,512]{1,0:T(8,128)(2,1)} %get-tuple-element.118), channel_id=1, source_target_pairs={{0,8},{1,9},{2,10},{3,11},{4,12},{5,13},{6,14},{7,15},{8,0},{9,1},... | collective-permute-start | bytes 393224 | tf_op jit(solution)/shard_map/ppermute | solution.py:416
  14.3 43.5 %copy-start.8 = (bf16[128,512]{1,0:T(8,128)(2,1)S(1)}, bf16[128,512]{1,0:T(8,128)(2,1)}, u32[]{:S(2)}) copy-start(bf16[128,512]{1,0:T(8,128)(2,1)} %get-tuple-element.122.refs_0_) | copy-start | bytes 393220
  17.8 18.7 %collective-permute-start.7 = (bf16[192,2048]{1,0:T(8,128)(2,1)S(1)}, bf16[192,2048]{1,0:T(8,128)(2,1)S(1)}, u32[]{:S(2)}, u32[]{:S(2)}) collective-permute-start(bf16[192,2048]{1,0:T(8,128)(2,1)S(1)} %get-tuple-element.129), channel_id=1, source_target_pairs={{0,2},{1,3},{2,0},{3,1},{4,6},{5,7},{6,4},{7,5},{8,10},{9,11},{10,... | collective-permute-start | bytes 2359304 | tf_op jit(solution)/shard_map/ppermute | solution.py:363
  19.5 16.8 %collective-permute-start.9 = (bf16[160,2048]{1,0:T(8,128)(2,1)S(1)}, bf16[160,2048]{1,0:T(8,128)(2,1)S(1)}, u32[]{:S(2)}, u32[]{:S(2)}) collective-permute-start(bf16[160,2048]{1,0:T(8,128)(2,1)S(1)} %get-tuple-element.131), channel_id=1, source_target_pairs={{0,1},{1,0},{2,3},{3,2},{4,5},{5,4},{6,7},{7,6},{8,9},{9,8},{10,11... | collective-permute-start | bytes 1966088 | tf_op jit(solution)/shard_map/ppermute | solution.py:363
  21.0 15.3 %collective-permute-start.6 = (bf16[256,512]{1,0:T(8,128)(2,1)S(1)}, bf16[256,512]{1,0:T(8,128)(2,1)S(1)}, u32[]{:S(2)}, u32[]{:S(2)}) collective-permute-start(bf16[256,512]{1,0:T(8,128)(2,1)S(1)} %get-tuple-element.128), channel_id=1, source_target_pairs={{0,8},{1,9},{2,10},{3,11},{4,12},{5,13},{6,14},{7,15},{8,0},{9,1},... | collective-permute-start | bytes 786440 | tf_op jit(solution)/shard_map/ppermute | solution.py:366
  23.5 12.8 %collective-permute-start.5 = (bf16[256,512]{1,0:T(8,128)(2,1)S(1)}, bf16[256,512]{1,0:T(8,128)(2,1)S(1)}, u32[]{:S(2)}, u32[]{:S(2)}) collective-permute-start(bf16[256,512]{1,0:T(8,128)(2,1)S(1)} %get-tuple-element.128), channel_id=1, source_target_pairs={{0,4},{1,5},{2,6},{3,7},{4,0},{5,1},{6,2},{7,3},{8,12},{9,13},{10,... | collective-permute-start | bytes 786440 | tf_op jit(solution)/shard_map/ppermute | solution.py:366
  25.2 6.8 %collective-permute-start.8 = (bf16[192,512]{1,0:T(8,128)(2,1)S(1)}, bf16[192,512]{1,0:T(8,128)(2,1)S(1)}, u32[]{:S(2)}, u32[]{:S(2)}) collective-permute-start(bf16[192,512]{1,0:T(8,128)(2,1)S(1)} %get-tuple-element.130.mine), channel_id=1, source_target_pairs={{0,16},{16,0},{1,17},{17,1},{2,18},{18,2},{3,19},{19,3},{4,20},{20... | collective-permute-start | bytes 589832 | tf_op jit(solution)/shard_map/ppermute | solution.py:369
  36.5 16.4 %collective-permute-start.14 = (bf16[192,2048]{1,0:T(8,128)(2,1)S(1)}, bf16[192,2048]{1,0:T(8,128)(2,1)S(1)}, u32[]{:S(2)}, u32[]{:S(2)}) collective-permute-start(bf16[192,2048]{1,0:T(8,128)(2,1)S(1)} %collective-permute-done.7.from_x), channel_id=1, source_target_pairs={{0,1},{1,0},{2,3},{3,2},{4,5},{5,4},{6,7},{7,6},{8,9},{9,8},{10,11... | collective-permute-start | bytes 2359304 | tf_op jit(solution)/shard_map/ppermute | solution.py:363
  36.5 15.6 %collective-permute-start.13 = (bf16[128,1024]{1,0:T(8,128)(2,1)}, bf16[128,1024]{1,0:T(8,128)(2,1)S(1)}, u32[]{:S(2)}, u32[]{:S(2)}) collective-permute-start(bf16[128,1024]{1,0:T(8,128)(2,1)} %get-tuple-element.137), channel_id=1, source_target_pairs={{0,8},{1,9},{2,10},{3,11},{4,12},{5,13},{6,14},{7,15},{8,0},{9,1},... | collective-permute-start | bytes 786440 | tf_op jit(solution)/shard_map/ppermute | solution.py:366
  39.0 13.1 %collective-permute-start.11 = (bf16[256,512]{1,0:T(8,128)(2,1)S(1)}, bf16[256,512]{1,0:T(8,128)(2,1)S(1)}, u32[]{:S(2)}, u32[]{:S(2)}) collective-permute-start(bf16[256,512]{1,0:T(8,128)(2,1)S(1)} %collective-permute-done.5.refs_0_), channel_id=1, source_target_pairs={{0,16},{16,0},{1,17},{17,1},{2,18},{18,2},{3,19},{19,3},{4,20},{20... | collective-permute-start | bytes 786440 | tf_op jit(solution)/shard_map/ppermute | solution.py:369
  39.9 13.0 %collective-permute-start.12 = (bf16[256,512]{1,0:T(8,128)(2,1)S(1)}, bf16[256,512]{1,0:T(8,128)(2,1)S(1)}, u32[]{:S(2)}, u32[]{:S(2)}) collective-permute-start(bf16[256,512]{1,0:T(8,128)(2,1)S(1)} %collective-permute-done.6.refs_1_), channel_id=1, source_target_pairs={{0,16},{16,0},{1,17},{17,1},{2,18},{18,2},{3,19},{19,3},{4,20},{20... | collective-permute-start | bytes 786440 | tf_op jit(solution)/shard_map/ppermute | solution.py:369
  41.0 12.0 %collective-permute-start.10 = (bf16[256,512]{1,0:T(8,128)(2,1)S(1)}, bf16[256,512]{1,0:T(8,128)(2,1)S(1)}, u32[]{:S(2)}, u32[]{:S(2)}) collective-permute-start(bf16[256,512]{1,0:T(8,128)(2,1)S(1)} %collective-permute-done.6.refs_1_), channel_id=1, source_target_pairs={{0,4},{1,5},{2,6},{3,7},{4,0},{5,1},{6,2},{7,3},{8,12},{9,13},{10,... | collective-permute-start | bytes 786440 | tf_op jit(solution)/shard_map/ppermute | solution.py:366
  53.0 11.3 %collective-permute-start.15 = (bf16[256,512]{1,0:T(8,128)(2,1)S(1)}, bf16[256,512]{1,0:T(8,128)(2,1)S(1)}, u32[]{:S(2)}, u32[]{:S(2)}) collective-permute-start(bf16[256,512]{1,0:T(8,128)(2,1)S(1)} %collective-permute-done.10.refs_2_), channel_id=1, source_target_pairs={{0,16},{16,0},{1,17},{17,1},{2,18},{18,2},{3,19},{19,3},{4,20},{20... | collective-permute-start | bytes 786440 | tf_op jit(solution)/shard_map/ppermute | solution.py:369
  55.7 8.5 %collective-permute-start.16 = (bf16[128,1024]{1,0:T(8,128)(2,1)S(1)}, bf16[128,1024]{1,0:T(8,128)(2,1)S(1)}, u32[]{:S(2)}, u32[]{:S(2)}) collective-permute-start(bf16[128,1024]{1,0:T(8,128)(2,1)S(1)} %collective-permute-done.13.refs_8_), channel_id=1, source_target_pairs={{0,4},{1,5},{2,6},{3,7},{4,0},{5,1},{6,2},{7,3},{8,12},{9,13},{10,... | collective-permute-start | bytes 786440 | tf_op jit(solution)/shard_map/ppermute | solution.py:366
  55.9 2.5 %collective-permute-start.17 = (bf16[4,128,128]{2,1,0:T(8,128)(2,1)S(1)}, bf16[4,128,128]{2,1,0:T(8,128)(2,1)S(1)}, u32[]{:S(2)}, u32[]{:S(2)}) collective-permute-start(bf16[4,128,128]{2,1,0:T(8,128)(2,1)S(1)} %get-tuple-element.148), channel_id=1, source_target_pairs={{0,1},{1,0},{2,3},{3,2},{4,5},{5,4},{6,7},{7,6},{8,9},{9,8},{10,11... | collective-permute-start | bytes 393224 | tf_op jit(solution)/shard_map/ppermute | solution.py:363
  55.9 6.3 %collective-permute-start.18 = (bf16[4,128,128]{2,1,0:T(8,128)(2,1)S(1)}, bf16[4,128,128]{2,1,0:T(8,128)(2,1)S(1)}, u32[]{:S(2)}, u32[]{:S(2)}) collective-permute-start(bf16[4,128,128]{2,1,0:T(8,128)(2,1)S(1)} %get-tuple-element.149), channel_id=1, source_target_pairs={{0,2},{1,3},{2,0},{3,1},{4,6},{5,7},{6,4},{7,5},{8,10},{9,11},{10,... | collective-permute-start | bytes 393224 | tf_op jit(solution)/shard_map/ppermute | solution.py:363
  57.4 6.8 %collective-permute-start.19 = (bf16[4,128,128]{2,1,0:T(8,128)(2,1)S(1)}, bf16[4,128,128]{2,1,0:T(8,128)(2,1)S(1)}, u32[]{:S(2)}, u32[]{:S(2)}) collective-permute-start(bf16[4,128,128]{2,1,0:T(8,128)(2,1)S(1)} %get-tuple-element.150), channel_id=1, source_target_pairs={{0,3},{1,2},{2,1},{3,0},{4,7},{5,6},{6,5},{7,4},{8,11},{9,10},{10,... | collective-permute-start | bytes 393224 | tf_op jit(solution)/shard_map/ppermute | solution.py:363
  58.4 14.5 %copy-start = (bf16[17,256,256]{2,1,0:T(8,128)(2,1)S(1)}, bf16[17,256,256]{2,1,0:T(8,128)(2,1)}, u32[]{:S(2)}) copy-start(bf16[17,256,256]{2,1,0:T(8,128)(2,1)} %constant.45.clone.refs_5_.refs_9_) | copy-start | bytes 6684676
  58.4 14.5 %copy-start.5 = (bf16[512,256]{1,0:T(8,128)(2,1)S(1)}, bf16[512,256]{1,0:T(8,128)(2,1)}, u32[]{:S(2)}) copy-start(bf16[512,256]{1,0:T(8,128)(2,1)} %constant.43.clone.refs_4_.refs_7_) | copy-start | bytes 786436
  66.3 16.7 %copy-start.1 = (bf16[17,256,256]{2,1,0:T(8,128)(2,1)S(1)}, bf16[17,256,256]{2,1,0:T(8,128)(2,1)}, u32[]{:S(2)}) copy-start(bf16[17,256,256]{2,1,0:T(8,128)(2,1)} %constant.46.clone.refs_10_) | copy-start | bytes 6684676
  66.3 16.7 %copy-start.9 = (bf16[256,512]{1,0:T(8,128)(2,1)S(1)}, bf16[256,512]{1,0:T(8,128)(2,1)}, u32[]{:S(2)}) copy-start(bf16[256,512]{1,0:T(8,128)(2,1)} %constant.44.clone.refs_8_) | copy-start | bytes 786436
  66.3 16.7 %copy-start.13 = (f32[3,2048]{1,0:T(4,128)S(1)}, f32[3,2048]{1,0:T(4,128)}, u32[]{:S(2)}) copy-start(f32[3,2048]{1,0:T(4,128)} %refs_4_.2) | copy-start | bytes 73732
  66.3 16.7 %copy-start.14 = (f32[2048]{0:T(1024)S(1)}, f32[2048]{0:T(1024)}, u32[]{:S(2)}) copy-start(f32[2048]{0:T(1024)} %param.16) | copy-start | bytes 24580
  66.4 16.6 %collective-permute-start.23 = (bf16[160,1024]{1,0:T(8,128)(2,1)S(1)}, bf16[160,1024]{1,0:T(8,128)(2,1)S(1)}, u32[]{:S(2)}, u32[]{:S(2)}) collective-permute-start(bf16[160,1024]{1,0:T(8,128)(2,1)S(1)} %collective-permute-done.4.refs_5_.refs_7_), channel_id=1, source_target_pairs={{0,16},{16,0},{1,17},{17,1},{2,18},{18,2},{3,19},{19,3},{4,20},{20... | collective-permute-start | bytes 983048 | tf_op jit(solution)/shard_map/ppermute | solution.py:369
  67.2 15.8 %collective-permute-start.24 = (bf16[128,1024]{1,0:T(8,128)(2,1)S(1)}, bf16[128,1024]{1,0:T(8,128)(2,1)S(1)}, u32[]{:S(2)}, u32[]{:S(2)}) collective-permute-start(bf16[128,1024]{1,0:T(8,128)(2,1)S(1)} %collective-permute-done.13.refs_8_), channel_id=1, source_target_pairs={{0,16},{16,0},{1,17},{17,1},{2,18},{18,2},{3,19},{19,3},{4,20},{20... | collective-permute-start | bytes 786440 | tf_op jit(solution)/shard_map/ppermute | solution.py:369
  68.5 6.6 %collective-permute-start.20 = (bf16[512,128]{1,0:T(8,128)(2,1)S(1)}, bf16[512,128]{1,0:T(8,128)(2,1)S(1)}, u32[]{:S(2)}, u32[]{:S(2)}) collective-permute-start(bf16[512,128]{1,0:T(8,128)(2,1)S(1)} %get-tuple-element.161), channel_id=1, source_target_pairs={{0,4},{1,5},{2,6},{3,7},{4,0},{5,1},{6,2},{7,3},{8,12},{9,13},{10,... | collective-permute-start | bytes 393224 | tf_op jit(solution)/shard_map/ppermute | solution.py:366
  70.3 12.7 %collective-permute-start.21 = (bf16[512,128]{1,0:T(8,128)(2,1)S(1)}, bf16[512,128]{1,0:T(8,128)(2,1)S(1)}, u32[]{:S(2)}, u32[]{:S(2)}) collective-permute-start(bf16[512,128]{1,0:T(8,128)(2,1)S(1)} %get-tuple-element.162), channel_id=1, source_target_pairs={{0,8},{1,9},{2,10},{3,11},{4,12},{5,13},{6,14},{7,15},{8,0},{9,1},... | collective-permute-start | bytes 393224 | tf_op jit(solution)/shard_map/ppermute | solution.py:366
  71.5 11.5 %collective-permute-start.22 = (bf16[512,128]{1,0:T(8,128)(2,1)S(1)}, bf16[512,128]{1,0:T(8,128)(2,1)S(1)}, u32[]{:S(2)}, u32[]{:S(2)}) collective-permute-start(bf16[512,128]{1,0:T(8,128)(2,1)S(1)} %get-tuple-element.163), channel_id=1, source_target_pairs={{0,12},{1,13},{2,14},{3,15},{4,8},{5,9},{6,10},{7,11},{8,4},{9,5},... | collective-permute-start | bytes 393224 | tf_op jit(solution)/shard_map/ppermute | solution.py:366
  86.0 9.8 %copy-start.4 = (bf16[128,2048]{1,0:T(8,128)(2,1)S(1)}, bf16[128,2048]{1,0:T(8,128)(2,1)}, u32[]{:S(2)}) copy-start(bf16[128,2048]{1,0:T(8,128)(2,1)} %refs_6_.1) | copy-start | bytes 1572868
  86.0 9.8 %collective-permute-start.28 = (bf16[128,1024]{1,0:T(8,128)(2,1)S(1)}, bf16[128,1024]{1,0:T(8,128)(2,1)S(1)}, u32[]{:S(2)}, u32[]{:S(2)}) collective-permute-start(bf16[128,1024]{1,0:T(8,128)(2,1)S(1)} %collective-permute-done.16.refs_9_), channel_id=1, source_target_pairs={{0,16},{16,0},{1,17},{17,1},{2,18},{18,2},{3,19},{19,3},{4,20},{20... | collective-permute-start | bytes 786440 | tf_op jit(solution)/shard_map/ppermute | solution.py:369
  86.4 5.3 %collective-permute-start.25 = (bf16[256,128]{1,0:T(8,128)(2,1)S(1)}, bf16[256,128]{1,0:T(8,128)(2,1)S(1)}, u32[]{:S(2)}, u32[]{:S(2)}) collective-permute-start(bf16[256,128]{1,0:T(8,128)(2,1)S(1)} %get-tuple-element.185), channel_id=1, source_target_pairs={{0,4},{1,5},{2,6},{3,7},{4,0},{5,1},{6,2},{7,3},{8,12},{9,13},{10,... | collective-permute-start | bytes 196616 | tf_op jit(solution)/shard_map/ppermute | solution.py:366
  88.5 6.4 %collective-permute-start.26 = (bf16[256,128]{1,0:T(8,128)(2,1)S(1)}, bf16[256,128]{1,0:T(8,128)(2,1)S(1)}, u32[]{:S(2)}, u32[]{:S(2)}) collective-permute-start(bf16[256,128]{1,0:T(8,128)(2,1)S(1)} %get-tuple-element.186), channel_id=1, source_target_pairs={{0,8},{1,9},{2,10},{3,11},{4,12},{5,13},{6,14},{7,15},{8,0},{9,1},... | collective-permute-start | bytes 196616 | tf_op jit(solution)/shard_map/ppermute | solution.py:366
  89.7 6.1 %collective-permute-start.27 = (bf16[256,128]{1,0:T(8,128)(2,1)S(1)}, bf16[256,128]{1,0:T(8,128)(2,1)S(1)}, u32[]{:S(2)}, u32[]{:S(2)}) collective-permute-start(bf16[256,128]{1,0:T(8,128)(2,1)S(1)} %get-tuple-element.187), channel_id=1, source_target_pairs={{0,12},{1,13},{2,14},{3,15},{4,8},{5,9},{6,10},{7,11},{8,4},{9,5},... | collective-permute-start | bytes 196616 | tf_op jit(solution)/shard_map/ppermute | solution.py:366
  97.2 2.0 %collective-permute-start.29 = (bf16[128,2048]{1,0:T(8,128)(2,1)S(1)}, bf16[128,2048]{1,0:T(8,128)(2,1)S(1)}, u32[]{:S(2)}, u32[]{:S(2)}) collective-permute-start(bf16[128,2048]{1,0:T(8,128)(2,1)S(1)} %get-tuple-element.205), channel_id=1, source_target_pairs={{0,1},{1,0},{2,3},{3,2},{4,5},{5,4},{6,7},{7,6},{8,9},{9,8},{10,11... | collective-permute-start | bytes 1572872 | tf_op jit(solution)/shard_map/ppermute | solution.py:363
  99.3 14.0 %collective-permute-start.37 = (bf16[128,2048]{1,0:T(8,128)(2,1)S(1)}, bf16[128,2048]{1,0:T(8,128)(2,1)S(1)}, u32[]{:S(2)}, u32[]{:S(2)}) collective-permute-start(bf16[128,2048]{1,0:T(8,128)(2,1)S(1)} %add_convert_fusion.1), channel_id=1, source_target_pairs={{0,2},{1,3},{2,0},{3,1},{4,6},{5,7},{6,4},{7,5},{8,10},{9,11},{10,... | collective-permute-start | bytes 1572872 | tf_op jit(solution)/shard_map/ppermute | solution.py:363
  100.9 4.8 %collective-permute-start.30 = (bf16[256,128]{1,0:T(8,128)(2,1)S(1)}, bf16[256,128]{1,0:T(8,128)(2,1)S(1)}, u32[]{:S(2)}, u32[]{:S(2)}) collective-permute-start(bf16[256,128]{1,0:T(8,128)(2,1)S(1)} %get-tuple-element.211), channel_id=1, source_target_pairs={{0,4},{1,5},{2,6},{3,7},{4,0},{5,1},{6,2},{7,3},{8,12},{9,13},{10,... | collective-permute-start | bytes 196616 | tf_op jit(solution)/shard_map/ppermute | solution.py:366
  101.9 8.0 %collective-permute-start.31 = (bf16[256,128]{1,0:T(8,128)(2,1)S(1)}, bf16[256,128]{1,0:T(8,128)(2,1)S(1)}, u32[]{:S(2)}, u32[]{:S(2)}) collective-permute-start(bf16[256,128]{1,0:T(8,128)(2,1)S(1)} %get-tuple-element.212), channel_id=1, source_target_pairs={{0,8},{1,9},{2,10},{3,11},{4,12},{5,13},{6,14},{7,15},{8,0},{9,1},... | collective-permute-start | bytes 196616 | tf_op jit(solution)/shard_map/ppermute | solution.py:366
  103.5 6.4 %collective-permute-start.32 = (bf16[256,128]{1,0:T(8,128)(2,1)S(1)}, bf16[256,128]{1,0:T(8,128)(2,1)S(1)}, u32[]{:S(2)}, u32[]{:S(2)}) collective-permute-start(bf16[256,128]{1,0:T(8,128)(2,1)S(1)} %get-tuple-element.213), channel_id=1, source_target_pairs={{0,12},{1,13},{2,14},{3,15},{4,8},{5,9},{6,10},{7,11},{8,4},{9,5},... | collective-permute-start | bytes 196616 | tf_op jit(solution)/shard_map/ppermute | solution.py:366
  111.2 1.4 %collective-permute-start.33 = (bf16[128,512]{1,0:T(8,128)(2,1)S(1)}, bf16[128,512]{1,0:T(8,128)(2,1)S(1)}, u32[]{:S(2)}, u32[]{:S(2)}) collective-permute-start(bf16[128,512]{1,0:T(8,128)(2,1)S(1)} %get-tuple-element.218), channel_id=1, source_target_pairs={{0,1},{1,0},{2,3},{3,2},{4,5},{5,4},{6,7},{7,6},{8,9},{9,8},{10,11... | collective-permute-start | bytes 393224 | tf_op jit(solution)/shard_map/ppermute | solution.py:363
  111.3 1.5 %collective-permute-start.34 = (bf16[128,512]{1,0:T(8,128)(2,1)S(1)}, bf16[128,512]{1,0:T(8,128)(2,1)S(1)}, u32[]{:S(2)}, u32[]{:S(2)}) collective-permute-start(bf16[128,512]{1,0:T(8,128)(2,1)S(1)} %get-tuple-element.219), channel_id=1, source_target_pairs={{0,1},{1,0},{2,3},{3,2},{4,5},{5,4},{6,7},{7,6},{8,9},{9,8},{10,11... | collective-permute-start | bytes 393224 | tf_op jit(solution)/shard_map/ppermute | solution.py:363
  111.8 1.3 %collective-permute-start.35 = (bf16[128,512]{1,0:T(8,128)(2,1)S(1)}, bf16[128,512]{1,0:T(8,128)(2,1)S(1)}, u32[]{:S(2)}, u32[]{:S(2)}) collective-permute-start(bf16[128,512]{1,0:T(8,128)(2,1)S(1)} %get-tuple-element.220), channel_id=1, source_target_pairs={{0,1},{1,0},{2,3},{3,2},{4,5},{5,4},{6,7},{7,6},{8,9},{9,8},{10,11... | collective-permute-start | bytes 393224 | tf_op jit(solution)/shard_map/ppermute | solution.py:363
  111.9 1.5 %collective-permute-start.36 = (bf16[128,512]{1,0:T(8,128)(2,1)S(1)}, bf16[128,512]{1,0:T(8,128)(2,1)S(1)}, u32[]{:S(2)}, u32[]{:S(2)}) collective-permute-start(bf16[128,512]{1,0:T(8,128)(2,1)S(1)} %get-tuple-element.221), channel_id=1, source_target_pairs={{0,1},{1,0},{2,3},{3,2},{4,5},{5,4},{6,7},{7,6},{8,9},{9,8},{10,11... | collective-permute-start | bytes 393224 | tf_op jit(solution)/shard_map/ppermute | solution.py:363
  (5 other events, 4.6 us)

commit v4 on v3

--- a/solution.py
+++ b/solution.py
@@ -154,21 +154,20 @@
 
 
 def half_kernel(pos, *refs):
-    parts, (whole, near), (out, joined) = refs[:PLANE], refs[PLANE:-2], refs[-2:]
-    deep = parts[0].shape[0]
+    parts, (whole, near), (out, joined, beside) = refs[:PLANE], refs[PLANE:-3], refs[-3:]
+    for y in range(2):
+
+        @pl.when(pos[0] == y)
+        def _():
+            join(out, parts[2 * y : 2 * y + 2])
+
     rows, wide = whole.shape
     quarter = rows // 4
-    for y in range(2):
-
-        @pl.when(pos[0] == y)
-        def _():
-            for j in range(2):
-                out[j * deep : (j + 1) * deep, :] = parts[2 * y + j][...]
-
     joined[:rows, :] = whole[...]
     for q in range(2):
         here = slice(rows + q * quarter, rows + (q + 1) * quarter)
-        joined[here, :] = near[deep:, q * wide : (q + 1) * wide]
+        joined[here, :] = near[near.shape[0] - quarter :, q * wide : (q + 1) * wide]
+    beside[...] = near[: beside.shape[0], :]
 
 
 def join_kernel(pos, *refs):
@@ -394,7 +393,7 @@
         pos,
         [value_weight, filter_taps, output_weight],
         0,
-        vmem=60,
+        vmem=53,
         fetched=3,
     )
     cut = list(cut)
@@ -407,7 +406,8 @@
         copies=13 * planes + 2,
         fetched=2,
     )
-    cut = [cut[0]] + [to_place(cut[d], d) for d in range(1, PLANE)]
+    own = small(join_kernel, [shaped(deep, wide)], cut[0])
+    cut = own + [to_place(cut[d], d) for d in range(1, PLANE)]
     route = [
         (y0 * devices + i, y0 * devices + (i ^ (2 + y0) * PLANE))
         for y0 in range(2)
@@ -416,15 +416,19 @@
     taps_whole = lax.ppermute(taps_whole, ("groups", "seq"), route)
     cut, taps_whole, message, core, out_near = stage((cut, taps_whole, message, core, out_near))
 
-    sent, taps_mine = small(
-        half_kernel, [shaped(2 * deep, wide), shaped(rows + part, wide)], *cut, taps_whole, out_near
+    sent, taps_mine, out_near = small(
+        half_kernel,
+        [shaped(2 * deep, wide), shaped(rows * 3 // 2, wide), shaped(deep, width)],
+        *cut,
+        taps_whole,
+        out_near,
     )
     near, far = to_plane(sent, 1), to_plane(sent, 2)
     from_x = to_place(message, 2)
     core = to_place(core, 1)
-    taps_other = to_group(taps_mine)
-    near, far, from_x, taps_other, core, out_half = stage(
-        (near, far, from_x, taps_other, core, out_half)
+    taps_other, out_other = to_group(taps_mine), to_group(out_near)
+    near, far, from_x, taps_other, core, out_half, out_other = stage(
+        (near, far, from_x, taps_other, core, out_half, out_other)
     )
 
     passed = to_plane(far, 1)
@@ -434,16 +438,13 @@
     taps_parts = small(
         places_kernel, [shaped(planes, rows, share)] * PLANE, taps_own, taps_mine, taps_other
     )
-    passed, near_other, far_other, out_far, both, taps_parts = stage(
-        (passed, near_other, far_other, out_far, both, taps_parts)
-    )
-
+    taps_parts, passed, both = stage((taps_parts, passed, both))
     passed_other = to_group(passed)
-    out_passed = to_plane(out_far, 1)
     taps_parts = [taps_parts[0]] + [to_place(taps_parts[d], d) for d in range(1, PLANE)]
     held = small(join_kernel, [shaped(PLANE * deep, wide)], *cut)[0]
-    passed, passed_other, out_passed, taps_parts, held = stage(
-        (passed, passed_other, out_passed, taps_parts, held)
+    out_passed = to_plane(out_far, 1)
+    passed, near_other, far_other, out_passed, both, taps_parts, passed_other, held = stage(
+        (passed, near_other, far_other, out_passed, both, taps_parts, passed_other, held)
     )
     projected = call(
         functools.partial(project_kernel, planes),
@@ -459,13 +460,13 @@
         2 * PLANE * rows * features * wide,
         vmem=8,
     )
-    projected, out_far, out_near = stage((projected, out_far, out_near))
+    projected, out_far = stage((projected, out_far))
 
     def spread(parts):
         return [parts[0]] + [to_plane(parts[s], s) for s in range(1, planes)]
 
     signal = spread(projected)
-    out_other = [to_group(out_near), to_group(out_far)]
+    out_other = [out_other, to_group(out_far)]
     response = call(
         functools.partial(taps_kernel, blocks, planes),
         [shaped(blocks + 1, 2 * rows, share)],
@@ -479,7 +480,7 @@
         vmem=4,
     )[0]
     gate = [gate_own] + small(unfold_kernel, [shaped(rows, wide)] * 3, core, from_x, both)
-    signal, out_other, response = stage((signal, out_other, response))
+    signal, response = stage((signal, response))
 
     mixed = call(
         functools.partial(conv_kernel, blocks, planes),
@@ -495,7 +496,7 @@
         4 * positions * share * (32 * ROWS + 4 * rows),
         vmem=8,
     )
-    mixed, out_passed = stage((mixed, out_passed))
+    mixed, out_passed, out_other = stage((mixed, out_passed, out_other))
 
     upper = spread(mixed[planes:])
     out_other += [to_group(out_passed)]

time: 115 us -> 111 us (0.965)
  local copies, waits for them, and re-layouts: 4.62 us -> 0.06 us
  waiting for transfers between devices: 46.7 us -> 50.7 us
  starting transfers between devices: 44.6 us -> 42.6 us
    ppermute x15, waiting for transfers between devices: 30.1 us -> 39.2 us  [to_plane(): lax.ppermute(block, 'seq', [(i, i ^ s * PLANE) for i in range(devices)])]
    unnamed x30 -> x20, local copies, waits for them, and re-layouts: 4.62 us -> 0.06 us
    ppermute x15, starting transfers between devices: 25.2 us -> 21.4 us  [to_plane(): lax.ppermute(block, 'seq', [(i, i ^ s * PLANE) for i in range(devices)])]
    ppermute x15, waiting for transfers between devices: 9.08 us -> 6.39 us  [to_place(): return lax.ppermute(block, 'seq', [(i, i ^ d) for i in range(devices)])]
    ppermute x7, waiting for transfers between devices: 6.12 us -> 3.45 us  [to_group(): return lax.ppermute(block, 'groups', [(0, 1), (1, 0)])]
    ppermute x7, starting transfers between devices: 8.75 us -> 10.5 us  [to_group(): return lax.ppermute(block, 'groups', [(0, 1), (1, 0)])]
    pallas_call x11 -> x12, Pallas kernels: 16.4 us -> 16.4 us  [call(): pl.pallas_call(kernel, out_shape=outs, in_specs=in_specs, out_specs=[pl.B...]
  transfers between devices with their start and end apart: 38 -> 38, of which waited for: 20 -> 19; matrix products, arithmetic and copies ran while one was open for 0% -> 0% of each run, Pallas kernels for 6% -> 9%
where the time goes in v4:
time: 111 us
  waiting for transfers between devices  50.7 us (46%)
  starting transfers between devices  42.6 us (38%)
  Pallas kernels  16.4 us (15%)
  other arithmetic  1.15 us (1%)
    ppermute x15, waiting for transfers between devices, to_plane(): lax.ppermute(block, 'seq', [(i, i ^ s * PLANE) for i in range(devices)])  39.2 us
    ppermute x15, starting transfers between devices, to_plane(): lax.ppermute(block, 'seq', [(i, i ^ s * PLANE) for i in range(devices)])  21.4 us
    pallas_call x12, Pallas kernels, call(): pl.pallas_call(kernel, out_shape=outs, in_specs=in_specs, out_specs=[pl.B...  16.4 us
    ppermute x7, starting transfers between devices, to_group(): return lax.ppermute(block, 'groups', [(0, 1), (1, 0)])  10.5 us
    ppermute x15, starting transfers between devices, to_place(): return lax.ppermute(block, 'seq', [(i, i ^ d) for i in range(devices)])  8.14 us
    ppermute x15, waiting for transfers between devices, to_place(): return lax.ppermute(block, 'seq', [(i, i ^ d) for i in range(devices)])  6.39 us
    ppermute x7, waiting for transfers between devices, to_group(): return lax.ppermute(block, 'groups', [(0, 1), (1, 0)])  3.45 us
    ppermute x1, starting transfers between devices, local(): taps_whole = lax.ppermute(taps_whole, ('groups', 'seq'), route)  2.59 us
  transfers between devices with their start and end apart: 38, of which 19 were waited for; matrix products, arithmetic and copies ran while one was open for 0% of the time, Pallas kernels for 9%

profile of v4, /device:TPU:0, one launch (start us, length us, event | category | flops | bytes accessed | tf_op | source)
XLA Modules:
  0.0 111.3 jit_solution(2551914821421643295)
XLA Ops:
  0.1 2.8 %shard_map.109 = (bf16[128,512]{1,0:T(8,128)(2,1)S(1)}, bf16[128,512]{1,0:T(8,128)(2,1)S(1)}, bf16[128,512]{1,0:T(8,128)(2,1)S(1)}, bf16[128,512]{1,0:T(8,128)(2...) custom-call(s32[3]{0:T(128)S(1)} %pad_add_fusion.pos, ...), custom_call_target="tpu_custom_call" | custom-call | tf_op jit(solution)/shard_map/pallas_call | solution.py:60
  2.9 3.1 %collective-permute-start.4 = (bf16[160,1024]{1,0:T(8,128)(2,1)}, bf16[160,1024]{1,0:T(8,128)(2,1)S(1)}, u32[]{:S(2)}, u32[]{:S(2)}) collective-permute-start(bf16[160,1024]{1,0:T(8,128)(2,1)} %get-tuple-element.122), channel_id=1, source_target_pairs={{0,4},{1,5},{2,6},{3,7},{4,0},{5,1},{6,2},{7,3},{8,12},{9,13},{10,... | collective-permute-start | bytes 983048 | tf_op jit(solution)/shard_map/ppermute | solution.py:365
  6.0 1.5 %collective-permute-start.1 = (bf16[128,512]{1,0:T(8,128)(2,1)S(1)}, bf16[128,512]{1,0:T(8,128)(2,1)S(1)}, u32[]{:S(2)}, u32[]{:S(2)}) collective-permute-start(bf16[128,512]{1,0:T(8,128)(2,1)S(1)} %get-tuple-element.117), channel_id=1, source_target_pairs={{0,2},{1,3},{2,0},{3,1},{4,6},{5,7},{6,4},{7,5},{8,10},{9,11},{10,... | collective-permute-start | bytes 393224 | tf_op jit(solution)/shard_map/ppermute | solution.py:362
  7.8 2.6 %collective-permute-start.3 = (bf16[128,512]{1,0:T(8,128)(2,1)S(1)}, bf16[128,512]{1,0:T(8,128)(2,1)S(1)}, u32[]{:S(2)}, u32[]{:S(2)}) collective-permute-start(bf16[128,512]{1,0:T(8,128)(2,1)S(1)} %get-tuple-element.119), channel_id=1, source_target_pairs={{0,8},{1,9},{2,10},{3,11},{4,12},{5,13},{6,14},{7,15},{8,0},{9,1},... | collective-permute-start | bytes 393224 | tf_op jit(solution)/shard_map/ppermute | solution.py:416
  11.0 1.4 %shard_map.111 = (bf16[128,512]{1,0:T(8,128)(2,1)S(1)}, bf16[160,2048]{1,0:T(8,128)(2,1)S(1)}, bf16[192,2048]{1,0:T(8,128)(2,1)S(1)}) custom-call(s32[3]{0:T(128)S(1)} %pad_add_fusion.pos, bf16[128,2048]{1,0:T(8,128)(2,1)S(1)} %copy-done.2, bf16[128,2048]{1,0:T(8,128)(2,1)S(1)} %copy-done.5), custom_call_target="tpu_custom_call" | custom-call | tf_op jit(solution)/shard_map/pallas_call | solution.py:60
  12.4 1.9 %collective-permute-done.2.refs_3_ = bf16[128,512]{1,0:T(8,128)(2,1)S(1)} collective-permute-done((bf16[128,512]{1,0:T(8,128)(2,1)S(1)}, bf16[128,512]{1,0:T(8,128)(2,1)S(1)}, u32[]{:S(2)}, u32[]{:S(2)}) %collective-permute-start.2) | collective-permute-done | bytes 131104 | tf_op jit(solution)/shard_map/ppermute | solution.py:362
  14.3 1.7 %collective-permute-done.3.refs_4_ = bf16[128,512]{1,0:T(8,128)(2,1)S(1)} collective-permute-done((bf16[128,512]{1,0:T(8,128)(2,1)S(1)}, bf16[128,512]{1,0:T(8,128)(2,1)S(1)}, u32[]{:S(2)}, u32[]{:S(2)}) %collective-permute-start.3) | collective-permute-done | bytes 131104 | tf_op jit(solution)/shard_map/ppermute | solution.py:416
  16.0 0.7 collective-permute-done.4.refs_5_
  16.7 1.7 %collective-permute-start.7 = (bf16[192,2048]{1,0:T(8,128)(2,1)S(1)}, bf16[192,2048]{1,0:T(8,128)(2,1)S(1)}, u32[]{:S(2)}, u32[]{:S(2)}) collective-permute-start(bf16[192,2048]{1,0:T(8,128)(2,1)S(1)} %get-tuple-element.130), channel_id=1, source_target_pairs={{0,2},{1,3},{2,0},{3,1},{4,6},{5,7},{6,4},{7,5},{8,10},{9,11},{10,... | collective-permute-start | bytes 2359304 | tf_op jit(solution)/shard_map/ppermute | solution.py:362
  19.0 3.6 %collective-permute-start.8 = (bf16[192,512]{1,0:T(8,128)(2,1)S(1)}, bf16[192,512]{1,0:T(8,128)(2,1)S(1)}, u32[]{:S(2)}, u32[]{:S(2)}) collective-permute-start(bf16[192,512]{1,0:T(8,128)(2,1)S(1)} %get-tuple-element.131.mine), channel_id=1, source_target_pairs={{0,16},{16,0},{1,17},{17,1},{2,18},{18,2},{3,19},{19,3},{4,20},{20... | collective-permute-start | bytes 589832 | tf_op jit(solution)/shard_map/ppermute | solution.py:368
  22.6 2.1 %collective-permute-start.5 = (bf16[256,512]{1,0:T(8,128)(2,1)S(1)}, bf16[256,512]{1,0:T(8,128)(2,1)S(1)}, u32[]{:S(2)}, u32[]{:S(2)}) collective-permute-start(bf16[256,512]{1,0:T(8,128)(2,1)S(1)} %get-tuple-element.129), channel_id=1, source_target_pairs={{0,4},{1,5},{2,6},{3,7},{4,0},{5,1},{6,2},{7,3},{8,12},{9,13},{10,... | collective-permute-start | bytes 786440 | tf_op jit(solution)/shard_map/ppermute | solution.py:365
  24.7 3.4 %collective-permute-done.8.other = bf16[192,512]{1,0:T(8,128)(2,1)S(1)} collective-permute-done((bf16[192,512]{1,0:T(8,128)(2,1)S(1)}, bf16[192,512]{1,0:T(8,128)(2,1)S(1)}, u32[]{:S(2)}, u32[]{:S(2)}) %collective-permute-start.8) | collective-permute-done | bytes 196640 | tf_op jit(solution)/shard_map/ppermute | solution.py:368
  28.2 1.7 %collective-permute-start.10 = (bf16[128,1024]{1,0:T(8,128)(2,1)S(1)}, bf16[128,1024]{1,0:T(8,128)(2,1)S(1)}, u32[]{:S(2)}, u32[]{:S(2)}) collective-permute-start(bf16[128,1024]{1,0:T(8,128)(2,1)S(1)} %get-tuple-element.134.refs_7_), channel_id=1, source_target_pairs={{0,16},{16,0},{1,17},{17,1},{2,18},{18,2},{3,19},{19,3},{4,20},{20... | collective-permute-start | bytes 786440 | tf_op jit(solution)/shard_map/ppermute | solution.py:368
  29.9 6.7 %collective-permute-done.6.refs_1_ = bf16[256,512]{1,0:T(8,128)(2,1)S(1)} collective-permute-done((bf16[256,512]{1,0:T(8,128)(2,1)S(1)}, bf16[256,512]{1,0:T(8,128)(2,1)S(1)}, u32[]{:S(2)}, u32[]{:S(2)}) %collective-permute-start.6) | collective-permute-done | bytes 262176 | tf_op jit(solution)/shard_map/ppermute | solution.py:365
  36.9 0.9 collective-permute-start.15
  37.8 2.0 %collective-permute-start.11 = (bf16[256,512]{1,0:T(8,128)(2,1)S(1)}, bf16[256,512]{1,0:T(8,128)(2,1)S(1)}, u32[]{:S(2)}, u32[]{:S(2)}) collective-permute-start(bf16[256,512]{1,0:T(8,128)(2,1)S(1)} %collective-permute-done.6.refs_1_), channel_id=1, source_target_pairs={{0,4},{1,5},{2,6},{3,7},{4,0},{5,1},{6,2},{7,3},{8,12},{9,13},{10,... | collective-permute-start | bytes 786440 | tf_op jit(solution)/shard_map/ppermute | solution.py:365
  39.7 1.0 collective-permute-start.13
  40.8 1.0 collective-permute-start.14
  41.8 0.6 shard_map.113
  42.4 9.7 %collective-permute-done.15.refs_8_ = bf16[128,1024]{1,0:T(8,128)(2,1)S(1)} collective-permute-done((bf16[128,1024]{1,0:T(8,128)(2,1)S(1)}, bf16[128,1024]{1,0:T(8,128)(2,1)S(1)}, u32[]{:S(2)}, u32[]{:S(2)}) %collective-permute-start.15) | collective-permute-done | bytes 262176 | tf_op jit(solution)/shard_map/ppermute | solution.py:365
  52.1 1.1 collective-permute-start.20
  53.2 1.5 %collective-permute-start.18 = (bf16[4,128,128]{2,1,0:T(8,128)(2,1)S(1)}, bf16[4,128,128]{2,1,0:T(8,128)(2,1)S(1)}, u32[]{:S(2)}, u32[]{:S(2)}) collective-permute-start(bf16[4,128,128]{2,1,0:T(8,128)(2,1)S(1)} %get-tuple-element.150), channel_id=1, source_target_pairs={{0,2},{1,3},{2,0},{3,1},{4,6},{5,7},{6,4},{7,5},{8,10},{9,11},{10,... | collective-permute-start | bytes 393224 | tf_op jit(solution)/shard_map/ppermute | solution.py:362
  55.7 4.3 %collective-permute-done.16.refs_9_ = bf16[128,1024]{1,0:T(8,128)(2,1)S(1)} collective-permute-done((bf16[128,1024]{1,0:T(8,128)(2,1)S(1)}, bf16[128,1024]{1,0:T(8,128)(2,1)S(1)}, u32[]{:S(2)}, u32[]{:S(2)}) %collective-permute-start.16) | collective-permute-done | bytes 262176 | tf_op jit(solution)/shard_map/ppermute | solution.py:365
  60.0 1.5 %collective-permute-done.19.refs_3_ = bf16[4,128,128]{2,1,0:T(8,128)(2,1)S(1)} collective-permute-done((bf16[4,128,128]{2,1,0:T(8,128)(2,1)S(1)}, bf16[4,128,128]{2,1,0:T(8,128)(2,1)S(1)}, u32[]{:S(2)}, u32[]{:S(2)}) %collective-permute-start.19) | collective-permute-done | bytes 131104 | tf_op jit(solution)/shard_map/ppermute | solution.py:362
  61.5 2.0 %shard_map.115 = (bf16[512,128]{1,0:T(8,128)(2,1)S(1)}, bf16[512,128]{1,0:T(8,128)(2,1)S(1)}, bf16[512,128]{1,0:T(8,128)(2,1)S(1)}, bf16[512,128]{1,0:T(8,128)(2,1)S(1)}) custom-call(s32[3]{0:T(128)S(1)} %pad_add_fusion.pos, bf16[128,2048]{1,0:T(8,128)(2,1)S(1)} %copy-done.2, bf16[160,2048]{1,0:T(8,128)(2,1)S(1)} %collective-permute-done.9.core, ...), custom_call_target="tpu_custom_call" | custom-call | flops 1073741824 | bytes 5373952 | tf_op jit(solution)/shard_map/pallas_call | solution.py:60
  63.6 1.1 collective-permute-start.24
  64.7 2.0 %collective-permute-start.21 = (bf16[512,128]{1,0:T(8,128)(2,1)S(1)}, bf16[512,128]{1,0:T(8,128)(2,1)S(1)}, u32[]{:S(2)}, u32[]{:S(2)}) collective-permute-start(bf16[512,128]{1,0:T(8,128)(2,1)S(1)} %get-tuple-element.163), channel_id=1, source_target_pairs={{0,4},{1,5},{2,6},{3,7},{4,0},{5,1},{6,2},{7,3},{8,12},{9,13},{10,... | collective-permute-start | bytes 393224 | tf_op jit(solution)/shard_map/ppermute | solution.py:365
  66.6 0.7 collective-permute-start.22
  67.4 1.7 %collective-permute-start.23 = (bf16[512,128]{1,0:T(8,128)(2,1)S(1)}, bf16[512,128]{1,0:T(8,128)(2,1)S(1)}, u32[]{:S(2)}, u32[]{:S(2)}) collective-permute-start(bf16[512,128]{1,0:T(8,128)(2,1)S(1)} %get-tuple-element.165), channel_id=1, source_target_pairs={{0,12},{1,13},{2,14},{3,15},{4,8},{5,9},{6,10},{7,11},{8,4},{9,5},... | collective-permute-start | bytes 393224 | tf_op jit(solution)/shard_map/ppermute | solution.py:365
  69.1 1.6 %shard_map.116.refs_6_ = bf16[17,256,128]{2,1,0:T(8,128)(2,1)S(1)} custom-call(s32[3]{0:T(128)S(1)} %pad_add_fusion.pos, bf16[4,128,128]{2,1,0:T(8,128)(2,1)S(1)} %get-tuple-element.166.refs_0_, bf16[4,128,128]{2,1,0:T(8,128)(2,1)S(1)} %collective-permute-done.17.refs_1_, bf16[4,128,128]{2,1,0:T(8,128)(2,1)S(1)} %collective-permute-done.18.refs_2_, ...), custom_call_target="tpu_custom_call" | custom-call | flops 536870912 | bytes 4128768 | tf_op jit(solution)/shard_map/pallas_call | solution.py:60
  70.7 1.0 collective-permute-done.21.refs_1_
  71.6 7.8 %collective-permute-done.22.refs_2_ = bf16[512,128]{1,0:T(8,128)(2,1)S(1)} collective-permute-done((bf16[512,128]{1,0:T(8,128)(2,1)S(1)}, bf16[512,128]{1,0:T(8,128)(2,1)S(1)}, u32[]{:S(2)}, u32[]{:S(2)}) %collective-permute-start.22) | collective-permute-done | bytes 131104 | tf_op jit(solution)/shard_map/ppermute | solution.py:365
  79.5 3.0 %shard_map.117 = (bf16[256,128]{1,0:T(8,128)(2,1)S(1)}, bf16[256,128]{1,0:T(8,128)(2,1)S(1)}, bf16[256,128]{1,0:T(8,128)(2,1)S(1)}, bf16[256,128]{1,0:T(8,128)(2...) custom-call(s32[3]{0:T(128)S(1)} %pad_add_fusion.pos, ...), custom_call_target="tpu_custom_call" | custom-call | flops 1073741824 | bytes 7176192 | tf_op jit(solution)/shard_map/pallas_call | solution.py:60
  82.5 1.0 collective-permute-start.28
  83.5 2.0 %collective-permute-start.25 = (bf16[256,128]{1,0:T(8,128)(2,1)S(1)}, bf16[256,128]{1,0:T(8,128)(2,1)S(1)}, u32[]{:S(2)}, u32[]{:S(2)}) collective-permute-start(bf16[256,128]{1,0:T(8,128)(2,1)S(1)} %get-tuple-element.187), channel_id=1, source_target_pairs={{0,4},{1,5},{2,6},{3,7},{4,0},{5,1},{6,2},{7,3},{8,12},{9,13},{10,... | collective-permute-start | bytes 196616 | tf_op jit(solution)/shard_map/ppermute | solution.py:365
  85.5 1.0 collective-permute-start.26
  86.5 1.5 %collective-permute-start.27 = (bf16[256,128]{1,0:T(8,128)(2,1)S(1)}, bf16[256,128]{1,0:T(8,128)(2,1)S(1)}, u32[]{:S(2)}, u32[]{:S(2)}) collective-permute-start(bf16[256,128]{1,0:T(8,128)(2,1)S(1)} %get-tuple-element.189), channel_id=1, source_target_pairs={{0,12},{1,13},{2,14},{3,15},{4,8},{5,9},{6,10},{7,11},{8,4},{9,5},... | collective-permute-start | bytes 196616 | tf_op jit(solution)/shard_map/ppermute | solution.py:365
  88.6 3.3 %collective-permute-done.26.refs_2_ = bf16[256,128]{1,0:T(8,128)(2,1)S(1)} collective-permute-done((bf16[256,128]{1,0:T(8,128)(2,1)S(1)}, bf16[256,128]{1,0:T(8,128)(2,1)S(1)}, u32[]{:S(2)}, u32[]{:S(2)}) %collective-permute-start.26) | collective-permute-done | bytes 65568 | tf_op jit(solution)/shard_map/ppermute | solution.py:365
  91.9 0.8 collective-permute-done.27.refs_3_
  92.6 1.4 %shard_map.119 = (f32[128,2048]{1,0:T(8,128)S(1)}, bf16[128,2048]{1,0:T(8,128)(2,1)S(1)}, bf16[512,2048]{1,0:T(8,128)(2,1)S(1)}) custom-call(s32[3]{0:T(128)S(1)} %pad_add_fusion.pos, bf16[256,128]{1,0:T(8,128)(2,1)S(1)} %get-tuple-element.197.refs_0_, bf16[256,128]{1,0:T(8,128)(2,1)S(1)} %collective-permute-done.25.refs_1_, ...), custom_call_target="tpu_custom_call" | custom-call | flops 536870912 | bytes 6291456 | tf_op jit(solution)/shard_map/pallas_call | solution.py:60
  94.1 1.9 %collective-permute-done.29 = bf16[128,2048]{1,0:T(8,128)(2,1)S(1)} collective-permute-done((bf16[128,2048]{1,0:T(8,128)(2,1)S(1)}, bf16[128,2048]{1,0:T(8,128)(2,1)S(1)}, u32[]{:S(2)}, u32[]{:S(2)}) %collective-permute-start.29) | collective-permute-done | bytes 524320 | tf_op jit(solution)/shard_map/ppermute | solution.py:362
  96.2 1.5 %collective-permute-start.37 = (bf16[128,2048]{1,0:T(8,128)(2,1)S(1)}, bf16[128,2048]{1,0:T(8,128)(2,1)S(1)}, u32[]{:S(2)}, u32[]{:S(2)}) collective-permute-start(bf16[128,2048]{1,0:T(8,128)(2,1)S(1)} %add_convert_fusion.1), channel_id=1, source_target_pairs={{0,2},{1,3},{2,0},{3,1},{4,6},{5,7},{6,4},{7,5},{8,10},{9,11},{10,... | collective-permute-start | bytes 1572872 | tf_op jit(solution)/shard_map/ppermute | solution.py:362
  97.7 1.2 %collective-permute-start.30 = (bf16[256,128]{1,0:T(8,128)(2,1)S(1)}, bf16[256,128]{1,0:T(8,128)(2,1)S(1)}, u32[]{:S(2)}, u32[]{:S(2)}) collective-permute-start(bf16[256,128]{1,0:T(8,128)(2,1)S(1)} %get-tuple-element.213), channel_id=1, source_target_pairs={{0,4},{1,5},{2,6},{3,7},{4,0},{5,1},{6,2},{7,3},{8,12},{9,13},{10,... | collective-permute-start | bytes 196616 | tf_op jit(solution)/shard_map/ppermute | solution.py:365
  98.9 1.5 %collective-permute-start.31 = (bf16[256,128]{1,0:T(8,128)(2,1)S(1)}, bf16[256,128]{1,0:T(8,128)(2,1)S(1)}, u32[]{:S(2)}, u32[]{:S(2)}) collective-permute-start(bf16[256,128]{1,0:T(8,128)(2,1)S(1)} %get-tuple-element.214), channel_id=1, source_target_pairs={{0,8},{1,9},{2,10},{3,11},{4,12},{5,13},{6,14},{7,15},{8,0},{9,1},... | collective-permute-start | bytes 196616 | tf_op jit(solution)/shard_map/ppermute | solution.py:365
  100.4 1.7 %collective-permute-start.32 = (bf16[256,128]{1,0:T(8,128)(2,1)S(1)}, bf16[256,128]{1,0:T(8,128)(2,1)S(1)}, u32[]{:S(2)}, u32[]{:S(2)}) collective-permute-start(bf16[256,128]{1,0:T(8,128)(2,1)S(1)} %get-tuple-element.215), channel_id=1, source_target_pairs={{0,12},{1,13},{2,14},{3,15},{4,8},{5,9},{6,10},{7,11},{8,4},{9,5},... | collective-permute-start | bytes 196616 | tf_op jit(solution)/shard_map/ppermute | solution.py:365
  102.1 4.8 %collective-permute-done.31.refs_2_ = bf16[256,128]{1,0:T(8,128)(2,1)S(1)} collective-permute-done((bf16[256,128]{1,0:T(8,128)(2,1)S(1)}, bf16[256,128]{1,0:T(8,128)(2,1)S(1)}, u32[]{:S(2)}, u32[]{:S(2)}) %collective-permute-start.31) | collective-permute-done | bytes 65568 | tf_op jit(solution)/shard_map/ppermute | solution.py:365
  106.9 1.3 %shard_map.120 = (f32[128,2048]{1,0:T(8,128)S(1)}, bf16[128,512]{1,0:T(8,128)(2,1)S(1)}, bf16[128,512]{1,0:T(8,128)(2,1)S(1)}, bf16[128,512]{1,0:T(8,128)(2,1)S(1)}, bf16[128,512]{1,0:T(8,128)(2,1)S(1)}) custom-call(s32[3]{0:T(128)S(1)} %pad_add_fusion.pos, bf16[256,128]{1,0:T(8,128)(2,1)S(1)} %get-tuple-element.212.refs_0_, ...), custom_call_target="tpu_custom_call" | custom-call | tf_op jit(solution)/shard_map/pallas_call | solution.py:60
  110.3 1.0 add_convert_fusion
  (63 shorter events, 5.7 us)
Async XLA Ops:
  0.0 11.0 %copy-start.2 = (bf16[128,2048]{1,0:T(8,128)(2,1)S(1)}, bf16[128,2048]{1,0:T(8,128)(2,1)}, u32[]{:S(2)}) copy-start(bf16[128,2048]{1,0:T(8,128)(2,1)} %x.3) | copy-start | bytes 1572868
  0.0 11.0 %copy-start.5 = (bf16[128,2048]{1,0:T(8,128)(2,1)S(1)}, bf16[128,2048]{1,0:T(8,128)(2,1)}, u32[]{:S(2)}) copy-start(bf16[128,2048]{1,0:T(8,128)(2,1)} %gate.1) | copy-start | bytes 1572868
  2.9 34.0 %copy-start.9 = (bf16[128,1024]{1,0:T(8,128)(2,1)S(1)}, bf16[128,1024]{1,0:T(8,128)(2,1)}, u32[]{:S(2)}) copy-start(bf16[128,1024]{1,0:T(8,128)(2,1)} %get-tuple-element.146) | copy-start | bytes 786436
  2.9 13.8 %collective-permute-start.4 = (bf16[160,1024]{1,0:T(8,128)(2,1)}, bf16[160,1024]{1,0:T(8,128)(2,1)S(1)}, u32[]{:S(2)}, u32[]{:S(2)}) collective-permute-start(bf16[160,1024]{1,0:T(8,128)(2,1)} %get-tuple-element.122), channel_id=1, source_target_pairs={{0,4},{1,5},{2,6},{3,7},{4,0},{5,1},{6,2},{7,3},{8,12},{9,13},{10,... | collective-permute-start | bytes 983048 | tf_op jit(solution)/shard_map/ppermute | solution.py:365
  6.0 6.4 %collective-permute-start = (bf16[128,512]{1,0:T(8,128)(2,1)S(1)}, bf16[128,512]{1,0:T(8,128)(2,1)S(1)}, u32[]{:S(2)}, u32[]{:S(2)}) collective-permute-start(bf16[128,512]{1,0:T(8,128)(2,1)S(1)} %get-tuple-element.116), channel_id=1, source_target_pairs={{0,1},{1,0},{2,3},{3,2},{4,5},{5,4},{6,7},{7,6},{8,9},{9,8},{10,11... | collective-permute-start | bytes 393224 | tf_op jit(solution)/shard_map/ppermute | solution.py:362
  6.0 6.4 %collective-permute-start.1 = (bf16[128,512]{1,0:T(8,128)(2,1)S(1)}, bf16[128,512]{1,0:T(8,128)(2,1)S(1)}, u32[]{:S(2)}, u32[]{:S(2)}) collective-permute-start(bf16[128,512]{1,0:T(8,128)(2,1)S(1)} %get-tuple-element.117), channel_id=1, source_target_pairs={{0,2},{1,3},{2,0},{3,1},{4,6},{5,7},{6,4},{7,5},{8,10},{9,11},{10,... | collective-permute-start | bytes 393224 | tf_op jit(solution)/shard_map/ppermute | solution.py:362
  7.5 6.8 %collective-permute-start.2 = (bf16[128,512]{1,0:T(8,128)(2,1)S(1)}, bf16[128,512]{1,0:T(8,128)(2,1)S(1)}, u32[]{:S(2)}, u32[]{:S(2)}) collective-permute-start(bf16[128,512]{1,0:T(8,128)(2,1)S(1)} %get-tuple-element.118), channel_id=1, source_target_pairs={{0,3},{1,2},{2,1},{3,0},{4,7},{5,6},{6,5},{7,4},{8,11},{9,10},{10,... | collective-permute-start | bytes 393224 | tf_op jit(solution)/shard_map/ppermute | solution.py:362
  7.8 8.1 %collective-permute-start.3 = (bf16[128,512]{1,0:T(8,128)(2,1)S(1)}, bf16[128,512]{1,0:T(8,128)(2,1)S(1)}, u32[]{:S(2)}, u32[]{:S(2)}) collective-permute-start(bf16[128,512]{1,0:T(8,128)(2,1)S(1)} %get-tuple-element.119), channel_id=1, source_target_pairs={{0,8},{1,9},{2,10},{3,11},{4,12},{5,13},{6,14},{7,15},{8,0},{9,1},... | collective-permute-start | bytes 393224 | tf_op jit(solution)/shard_map/ppermute | solution.py:416
  16.7 20.1 %collective-permute-start.7 = (bf16[192,2048]{1,0:T(8,128)(2,1)S(1)}, bf16[192,2048]{1,0:T(8,128)(2,1)S(1)}, u32[]{:S(2)}, u32[]{:S(2)}) collective-permute-start(bf16[192,2048]{1,0:T(8,128)(2,1)S(1)} %get-tuple-element.130), channel_id=1, source_target_pairs={{0,2},{1,3},{2,0},{3,1},{4,6},{5,7},{6,4},{7,5},{8,10},{9,11},{10,... | collective-permute-start | bytes 2359304 | tf_op jit(solution)/shard_map/ppermute | solution.py:362
  18.4 18.4 %collective-permute-start.9 = (bf16[160,2048]{1,0:T(8,128)(2,1)S(1)}, bf16[160,2048]{1,0:T(8,128)(2,1)S(1)}, u32[]{:S(2)}, u32[]{:S(2)}) collective-permute-start(bf16[160,2048]{1,0:T(8,128)(2,1)S(1)} %get-tuple-element.132), channel_id=1, source_target_pairs={{0,1},{1,0},{2,3},{3,2},{4,5},{5,4},{6,7},{7,6},{8,9},{9,8},{10,11... | collective-permute-start | bytes 1966088 | tf_op jit(solution)/shard_map/ppermute | solution.py:362
  19.0 9.2 %collective-permute-start.8 = (bf16[192,512]{1,0:T(8,128)(2,1)S(1)}, bf16[192,512]{1,0:T(8,128)(2,1)S(1)}, u32[]{:S(2)}, u32[]{:S(2)}) collective-permute-start(bf16[192,512]{1,0:T(8,128)(2,1)S(1)} %get-tuple-element.131.mine), channel_id=1, source_target_pairs={{0,16},{16,0},{1,17},{17,1},{2,18},{18,2},{3,19},{19,3},{4,20},{20... | collective-permute-start | bytes 589832 | tf_op jit(solution)/shard_map/ppermute | solution.py:368
  22.6 14.0 %collective-permute-start.6 = (bf16[256,512]{1,0:T(8,128)(2,1)S(1)}, bf16[256,512]{1,0:T(8,128)(2,1)S(1)}, u32[]{:S(2)}, u32[]{:S(2)}) collective-permute-start(bf16[256,512]{1,0:T(8,128)(2,1)S(1)} %get-tuple-element.129), channel_id=1, source_target_pairs={{0,8},{1,9},{2,10},{3,11},{4,12},{5,13},{6,14},{7,15},{8,0},{9,1},... | collective-permute-start | bytes 786440 | tf_op jit(solution)/shard_map/ppermute | solution.py:365
  22.6 14.2 %collective-permute-start.5 = (bf16[256,512]{1,0:T(8,128)(2,1)S(1)}, bf16[256,512]{1,0:T(8,128)(2,1)S(1)}, u32[]{:S(2)}, u32[]{:S(2)}) collective-permute-start(bf16[256,512]{1,0:T(8,128)(2,1)S(1)} %get-tuple-element.129), channel_id=1, source_target_pairs={{0,4},{1,5},{2,6},{3,7},{4,0},{5,1},{6,2},{7,3},{8,12},{9,13},{10,... | collective-permute-start | bytes 786440 | tf_op jit(solution)/shard_map/ppermute | solution.py:365
  28.2 8.6 %collective-permute-start.10 = (bf16[128,1024]{1,0:T(8,128)(2,1)S(1)}, bf16[128,1024]{1,0:T(8,128)(2,1)S(1)}, u32[]{:S(2)}, u32[]{:S(2)}) collective-permute-start(bf16[128,1024]{1,0:T(8,128)(2,1)S(1)} %get-tuple-element.134.refs_7_), channel_id=1, source_target_pairs={{0,16},{16,0},{1,17},{17,1},{2,18},{18,2},{3,19},{19,3},{4,20},{20... | collective-permute-start | bytes 786440 | tf_op jit(solution)/shard_map/ppermute | solution.py:368
  36.8 15.3 %collective-permute-start.12 = (bf16[192,2048]{1,0:T(8,128)(2,1)S(1)}, bf16[192,2048]{1,0:T(8,128)(2,1)S(1)}, u32[]{:S(2)}, u32[]{:S(2)}) collective-permute-start(bf16[192,2048]{1,0:T(8,128)(2,1)S(1)} %collective-permute-done.7.from_x), channel_id=1, source_target_pairs={{0,1},{1,0},{2,3},{3,2},{4,5},{5,4},{6,7},{7,6},{8,9},{9,8},{10,11... | collective-permute-start | bytes 2359304 | tf_op jit(solution)/shard_map/ppermute | solution.py:362
  36.9 15.2 %collective-permute-start.15 = (bf16[128,1024]{1,0:T(8,128)(2,1)S(1)}, bf16[128,1024]{1,0:T(8,128)(2,1)S(1)}, u32[]{:S(2)}, u32[]{:S(2)}) collective-permute-start(bf16[128,1024]{1,0:T(8,128)(2,1)S(1)} %copy-done.9), channel_id=1, source_target_pairs={{0,8},{1,9},{2,10},{3,11},{4,12},{5,13},{6,14},{7,15},{8,0},{9,1},... | collective-permute-start | bytes 786440 | tf_op jit(solution)/shard_map/ppermute | solution.py:365
  37.8 14.3 %collective-permute-start.11 = (bf16[256,512]{1,0:T(8,128)(2,1)S(1)}, bf16[256,512]{1,0:T(8,128)(2,1)S(1)}, u32[]{:S(2)}, u32[]{:S(2)}) collective-permute-start(bf16[256,512]{1,0:T(8,128)(2,1)S(1)} %collective-permute-done.6.refs_1_), channel_id=1, source_target_pairs={{0,4},{1,5},{2,6},{3,7},{4,0},{5,1},{6,2},{7,3},{8,12},{9,13},{10,... | collective-permute-start | bytes 786440 | tf_op jit(solution)/shard_map/ppermute | solution.py:365
  39.7 13.4 %collective-permute-start.13 = (bf16[256,512]{1,0:T(8,128)(2,1)S(1)}, bf16[256,512]{1,0:T(8,128)(2,1)S(1)}, u32[]{:S(2)}, u32[]{:S(2)}) collective-permute-start(bf16[256,512]{1,0:T(8,128)(2,1)S(1)} %collective-permute-done.5.refs_0_), channel_id=1, source_target_pairs={{0,16},{16,0},{1,17},{17,1},{2,18},{18,2},{3,19},{19,3},{4,20},{20... | collective-permute-start | bytes 786440 | tf_op jit(solution)/shard_map/ppermute | solution.py:368
  40.8 13.9 %collective-permute-start.14 = (bf16[256,512]{1,0:T(8,128)(2,1)S(1)}, bf16[256,512]{1,0:T(8,128)(2,1)S(1)}, u32[]{:S(2)}, u32[]{:S(2)}) collective-permute-start(bf16[256,512]{1,0:T(8,128)(2,1)S(1)} %collective-permute-done.6.refs_1_), channel_id=1, source_target_pairs={{0,16},{16,0},{1,17},{17,1},{2,18},{18,2},{3,19},{19,3},{4,20},{20... | collective-permute-start | bytes 786440 | tf_op jit(solution)/shard_map/ppermute | solution.py:368
  52.1 7.9 %collective-permute-start.16 = (bf16[128,1024]{1,0:T(8,128)(2,1)S(1)}, bf16[128,1024]{1,0:T(8,128)(2,1)S(1)}, u32[]{:S(2)}, u32[]{:S(2)}) collective-permute-start(bf16[128,1024]{1,0:T(8,128)(2,1)S(1)} %collective-permute-done.15.refs_8_), channel_id=1, source_target_pairs={{0,4},{1,5},{2,6},{3,7},{4,0},{5,1},{6,2},{7,3},{8,12},{9,13},{10,... | collective-permute-start | bytes 786440 | tf_op jit(solution)/shard_map/ppermute | solution.py:365
  52.1 9.4 %collective-permute-start.20 = (bf16[256,512]{1,0:T(8,128)(2,1)S(1)}, bf16[256,512]{1,0:T(8,128)(2,1)S(1)}, u32[]{:S(2)}, u32[]{:S(2)}) collective-permute-start(bf16[256,512]{1,0:T(8,128)(2,1)S(1)} %collective-permute-done.11.refs_2_), channel_id=1, source_target_pairs={{0,16},{16,0},{1,17},{17,1},{2,18},{18,2},{3,19},{19,3},{4,20},{20... | collective-permute-start | bytes 786440 | tf_op jit(solution)/shard_map/ppermute | solution.py:368
  53.2 6.8 %collective-permute-start.17 = (bf16[4,128,128]{2,1,0:T(8,128)(2,1)S(1)}, bf16[4,128,128]{2,1,0:T(8,128)(2,1)S(1)}, u32[]{:S(2)}, u32[]{:S(2)}) collective-permute-start(bf16[4,128,128]{2,1,0:T(8,128)(2,1)S(1)} %get-tuple-element.149), channel_id=1, source_target_pairs={{0,1},{1,0},{2,3},{3,2},{4,5},{5,4},{6,7},{7,6},{8,9},{9,8},{10,11... | collective-permute-start | bytes 393224 | tf_op jit(solution)/shard_map/ppermute | solution.py:362
  53.2 6.8 %collective-permute-start.18 = (bf16[4,128,128]{2,1,0:T(8,128)(2,1)S(1)}, bf16[4,128,128]{2,1,0:T(8,128)(2,1)S(1)}, u32[]{:S(2)}, u32[]{:S(2)}) collective-permute-start(bf16[4,128,128]{2,1,0:T(8,128)(2,1)S(1)} %get-tuple-element.150), channel_id=1, source_target_pairs={{0,2},{1,3},{2,0},{3,1},{4,6},{5,7},{6,4},{7,5},{8,10},{9,11},{10,... | collective-permute-start | bytes 393224 | tf_op jit(solution)/shard_map/ppermute | solution.py:362
  54.7 6.8 %collective-permute-start.19 = (bf16[4,128,128]{2,1,0:T(8,128)(2,1)S(1)}, bf16[4,128,128]{2,1,0:T(8,128)(2,1)S(1)}, u32[]{:S(2)}, u32[]{:S(2)}) collective-permute-start(bf16[4,128,128]{2,1,0:T(8,128)(2,1)S(1)} %get-tuple-element.151), channel_id=1, source_target_pairs={{0,3},{1,2},{2,1},{3,0},{4,7},{5,6},{6,5},{7,4},{8,11},{9,10},{10,... | collective-permute-start | bytes 393224 | tf_op jit(solution)/shard_map/ppermute | solution.py:362
  55.6 13.4 %copy-start = (bf16[17,256,256]{2,1,0:T(8,128)(2,1)S(1)}, bf16[17,256,256]{2,1,0:T(8,128)(2,1)}, u32[]{:S(2)}) copy-start(bf16[17,256,256]{2,1,0:T(8,128)(2,1)} %constant.45.clone.refs_5_.refs_9_) | copy-start | bytes 6684676
  55.7 13.4 %copy-start.4 = (bf16[512,256]{1,0:T(8,128)(2,1)S(1)}, bf16[512,256]{1,0:T(8,128)(2,1)}, u32[]{:S(2)}) copy-start(bf16[512,256]{1,0:T(8,128)(2,1)} %constant.43.clone.refs_4_.refs_7_) | copy-start | bytes 786436
  63.6 15.9 %copy-start.1 = (bf16[17,256,256]{2,1,0:T(8,128)(2,1)S(1)}, bf16[17,256,256]{2,1,0:T(8,128)(2,1)}, u32[]{:S(2)}) copy-start(bf16[17,256,256]{2,1,0:T(8,128)(2,1)} %constant.46.clone.refs_10_) | copy-start | bytes 6684676
  63.6 15.9 %copy-start.6 = (bf16[256,512]{1,0:T(8,128)(2,1)S(1)}, bf16[256,512]{1,0:T(8,128)(2,1)}, u32[]{:S(2)}) copy-start(bf16[256,512]{1,0:T(8,128)(2,1)} %constant.44.clone.refs_8_) | copy-start | bytes 786436
  63.6 15.9 %copy-start.7 = (f32[3,2048]{1,0:T(4,128)S(1)}, f32[3,2048]{1,0:T(4,128)}, u32[]{:S(2)}) copy-start(f32[3,2048]{1,0:T(4,128)} %refs_4_.2) | copy-start | bytes 73732
  63.6 15.9 %copy-start.8 = (f32[2048]{0:T(1024)S(1)}, f32[2048]{0:T(1024)}, u32[]{:S(2)}) copy-start(f32[2048]{0:T(1024)} %param.16) | copy-start | bytes 24580
  63.6 18.9 %collective-permute-start.24 = (bf16[128,1024]{1,0:T(8,128)(2,1)S(1)}, bf16[128,1024]{1,0:T(8,128)(2,1)S(1)}, u32[]{:S(2)}, u32[]{:S(2)}) collective-permute-start(bf16[128,1024]{1,0:T(8,128)(2,1)S(1)} %collective-permute-done.15.refs_8_), channel_id=1, source_target_pairs={{0,16},{16,0},{1,17},{17,1},{2,18},{18,2},{3,19},{19,3},{4,20},{20... | collective-permute-start | bytes 786440 | tf_op jit(solution)/shard_map/ppermute | solution.py:368
  64.7 6.9 %collective-permute-start.21 = (bf16[512,128]{1,0:T(8,128)(2,1)S(1)}, bf16[512,128]{1,0:T(8,128)(2,1)S(1)}, u32[]{:S(2)}, u32[]{:S(2)}) collective-permute-start(bf16[512,128]{1,0:T(8,128)(2,1)S(1)} %get-tuple-element.163), channel_id=1, source_target_pairs={{0,4},{1,5},{2,6},{3,7},{4,0},{5,1},{6,2},{7,3},{8,12},{9,13},{10,... | collective-permute-start | bytes 393224 | tf_op jit(solution)/shard_map/ppermute | solution.py:365
  66.6 12.8 %collective-permute-start.22 = (bf16[512,128]{1,0:T(8,128)(2,1)S(1)}, bf16[512,128]{1,0:T(8,128)(2,1)S(1)}, u32[]{:S(2)}, u32[]{:S(2)}) collective-permute-start(bf16[512,128]{1,0:T(8,128)(2,1)S(1)} %get-tuple-element.164), channel_id=1, source_target_pairs={{0,8},{1,9},{2,10},{3,11},{4,12},{5,13},{6,14},{7,15},{8,0},{9,1},... | collective-permute-start | bytes 393224 | tf_op jit(solution)/shard_map/ppermute | solution.py:365
  67.4 12.0 %collective-permute-start.23 = (bf16[512,128]{1,0:T(8,128)(2,1)S(1)}, bf16[512,128]{1,0:T(8,128)(2,1)S(1)}, u32[]{:S(2)}, u32[]{:S(2)}) collective-permute-start(bf16[512,128]{1,0:T(8,128)(2,1)S(1)} %get-tuple-element.165), channel_id=1, source_target_pairs={{0,12},{1,13},{2,14},{3,15},{4,8},{5,9},{6,10},{7,11},{8,4},{9,5},... | collective-permute-start | bytes 393224 | tf_op jit(solution)/shard_map/ppermute | solution.py:365
  82.5 10.2 %copy-start.3 = (bf16[128,2048]{1,0:T(8,128)(2,1)S(1)}, bf16[128,2048]{1,0:T(8,128)(2,1)}, u32[]{:S(2)}) copy-start(bf16[128,2048]{1,0:T(8,128)(2,1)} %refs_6_.1) | copy-start | bytes 1572868
  82.5 10.1 %collective-permute-start.28 = (bf16[128,1024]{1,0:T(8,128)(2,1)S(1)}, bf16[128,1024]{1,0:T(8,128)(2,1)S(1)}, u32[]{:S(2)}, u32[]{:S(2)}) collective-permute-start(bf16[128,1024]{1,0:T(8,128)(2,1)S(1)} %collective-permute-done.16.refs_9_), channel_id=1, source_target_pairs={{0,16},{16,0},{1,17},{17,1},{2,18},{18,2},{3,19},{19,3},{4,20},{20... | collective-permute-start | bytes 786440 | tf_op jit(solution)/shard_map/ppermute | solution.py:368
  83.5 5.1 %collective-permute-start.25 = (bf16[256,128]{1,0:T(8,128)(2,1)S(1)}, bf16[256,128]{1,0:T(8,128)(2,1)S(1)}, u32[]{:S(2)}, u32[]{:S(2)}) collective-permute-start(bf16[256,128]{1,0:T(8,128)(2,1)S(1)} %get-tuple-element.187), channel_id=1, source_target_pairs={{0,4},{1,5},{2,6},{3,7},{4,0},{5,1},{6,2},{7,3},{8,12},{9,13},{10,... | collective-permute-start | bytes 196616 | tf_op jit(solution)/shard_map/ppermute | solution.py:365
  85.5 6.3 %collective-permute-start.26 = (bf16[256,128]{1,0:T(8,128)(2,1)S(1)}, bf16[256,128]{1,0:T(8,128)(2,1)S(1)}, u32[]{:S(2)}, u32[]{:S(2)}) collective-permute-start(bf16[256,128]{1,0:T(8,128)(2,1)S(1)} %get-tuple-element.188), channel_id=1, source_target_pairs={{0,8},{1,9},{2,10},{3,11},{4,12},{5,13},{6,14},{7,15},{8,0},{9,1},... | collective-permute-start | bytes 196616 | tf_op jit(solution)/shard_map/ppermute | solution.py:365
  86.5 6.1 %collective-permute-start.27 = (bf16[256,128]{1,0:T(8,128)(2,1)S(1)}, bf16[256,128]{1,0:T(8,128)(2,1)S(1)}, u32[]{:S(2)}, u32[]{:S(2)}) collective-permute-start(bf16[256,128]{1,0:T(8,128)(2,1)S(1)} %get-tuple-element.189), channel_id=1, source_target_pairs={{0,12},{1,13},{2,14},{3,15},{4,8},{5,9},{6,10},{7,11},{8,4},{9,5},... | collective-permute-start | bytes 196616 | tf_op jit(solution)/shard_map/ppermute | solution.py:365
  94.1 2.0 %collective-permute-start.29 = (bf16[128,2048]{1,0:T(8,128)(2,1)S(1)}, bf16[128,2048]{1,0:T(8,128)(2,1)S(1)}, u32[]{:S(2)}, u32[]{:S(2)}) collective-permute-start(bf16[128,2048]{1,0:T(8,128)(2,1)S(1)} %get-tuple-element.207), channel_id=1, source_target_pairs={{0,1},{1,0},{2,3},{3,2},{4,5},{5,4},{6,7},{7,6},{8,9},{9,8},{10,11... | collective-permute-start | bytes 1572872 | tf_op jit(solution)/shard_map/ppermute | solution.py:362
  96.2 14.1 %collective-permute-start.37 = (bf16[128,2048]{1,0:T(8,128)(2,1)S(1)}, bf16[128,2048]{1,0:T(8,128)(2,1)S(1)}, u32[]{:S(2)}, u32[]{:S(2)}) collective-permute-start(bf16[128,2048]{1,0:T(8,128)(2,1)S(1)} %add_convert_fusion.1), channel_id=1, source_target_pairs={{0,2},{1,3},{2,0},{3,1},{4,6},{5,7},{6,4},{7,5},{8,10},{9,11},{10,... | collective-permute-start | bytes 1572872 | tf_op jit(solution)/shard_map/ppermute | solution.py:362
  97.7 4.4 %collective-permute-start.30 = (bf16[256,128]{1,0:T(8,128)(2,1)S(1)}, bf16[256,128]{1,0:T(8,128)(2,1)S(1)}, u32[]{:S(2)}, u32[]{:S(2)}) collective-permute-start(bf16[256,128]{1,0:T(8,128)(2,1)S(1)} %get-tuple-element.213), channel_id=1, source_target_pairs={{0,4},{1,5},{2,6},{3,7},{4,0},{5,1},{6,2},{7,3},{8,12},{9,13},{10,... | collective-permute-start | bytes 196616 | tf_op jit(solution)/shard_map/ppermute | solution.py:365
  98.9 8.0 %collective-permute-start.31 = (bf16[256,128]{1,0:T(8,128)(2,1)S(1)}, bf16[256,128]{1,0:T(8,128)(2,1)S(1)}, u32[]{:S(2)}, u32[]{:S(2)}) collective-permute-start(bf16[256,128]{1,0:T(8,128)(2,1)S(1)} %get-tuple-element.214), channel_id=1, source_target_pairs={{0,8},{1,9},{2,10},{3,11},{4,12},{5,13},{6,14},{7,15},{8,0},{9,1},... | collective-permute-start | bytes 196616 | tf_op jit(solution)/shard_map/ppermute | solution.py:365
  100.4 6.5 %collective-permute-start.32 = (bf16[256,128]{1,0:T(8,128)(2,1)S(1)}, bf16[256,128]{1,0:T(8,128)(2,1)S(1)}, u32[]{:S(2)}, u32[]{:S(2)}) collective-permute-start(bf16[256,128]{1,0:T(8,128)(2,1)S(1)} %get-tuple-element.215), channel_id=1, source_target_pairs={{0,12},{1,13},{2,14},{3,15},{4,8},{5,9},{6,10},{7,11},{8,4},{9,5},... | collective-permute-start | bytes 196616 | tf_op jit(solution)/shard_map/ppermute | solution.py:365
  108.2 1.4 %collective-permute-start.33 = (bf16[128,512]{1,0:T(8,128)(2,1)S(1)}, bf16[128,512]{1,0:T(8,128)(2,1)S(1)}, u32[]{:S(2)}, u32[]{:S(2)}) collective-permute-start(bf16[128,512]{1,0:T(8,128)(2,1)S(1)} %get-tuple-element.220), channel_id=1, source_target_pairs={{0,1},{1,0},{2,3},{3,2},{4,5},{5,4},{6,7},{7,6},{8,9},{9,8},{10,11... | collective-permute-start | bytes 393224 | tf_op jit(solution)/shard_map/ppermute | solution.py:362
  108.2 1.5 %collective-permute-start.34 = (bf16[128,512]{1,0:T(8,128)(2,1)S(1)}, bf16[128,512]{1,0:T(8,128)(2,1)S(1)}, u32[]{:S(2)}, u32[]{:S(2)}) collective-permute-start(bf16[128,512]{1,0:T(8,128)(2,1)S(1)} %get-tuple-element.221), channel_id=1, source_target_pairs={{0,1},{1,0},{2,3},{3,2},{4,5},{5,4},{6,7},{7,6},{8,9},{9,8},{10,11... | collective-permute-start | bytes 393224 | tf_op jit(solution)/shard_map/ppermute | solution.py:362
  108.7 1.3 %collective-permute-start.35 = (bf16[128,512]{1,0:T(8,128)(2,1)S(1)}, bf16[128,512]{1,0:T(8,128)(2,1)S(1)}, u32[]{:S(2)}, u32[]{:S(2)}) collective-permute-start(bf16[128,512]{1,0:T(8,128)(2,1)S(1)} %get-tuple-element.222), channel_id=1, source_target_pairs={{0,1},{1,0},{2,3},{3,2},{4,5},{5,4},{6,7},{7,6},{8,9},{9,8},{10,11... | collective-permute-start | bytes 393224 | tf_op jit(solution)/shard_map/ppermute | solution.py:362
  108.8 1.5 %collective-permute-start.36 = (bf16[128,512]{1,0:T(8,128)(2,1)S(1)}, bf16[128,512]{1,0:T(8,128)(2,1)S(1)}, u32[]{:S(2)}, u32[]{:S(2)}) collective-permute-start(bf16[128,512]{1,0:T(8,128)(2,1)S(1)} %get-tuple-element.223), channel_id=1, source_target_pairs={{0,1},{1,0},{2,3},{3,2},{4,5},{5,4},{6,7},{7,6},{8,9},{9,8},{10,11... | collective-permute-start | bytes 393224 | tf_op jit(solution)/shard_map/ppermute | solution.py:362

commit v5 on v4

--- a/solution.py
+++ b/solution.py
@@ -115,35 +115,17 @@
         near[deep:, q * wide : (q + 1) * wide] = taps_here[pl.ds(first, quarter), columns(1)]
 
 
-def across_kernel(share, pos, x, gate, own, core, across, sems):
-    rows = x.shape[0]
-    part, wide = rows // 4, own.shape[1]
-    pairs = [(x, core.at[pl.ds(0, rows)]), (x, across.at[pl.ds(0, rows)])]
-    for d in range(PLANE):
+def gate_kernel(share, pos, gate, own, beside, across, sems):
+    rows, wide = own.shape
+    pairs = []
+    for d, (out, first) in enumerate(((own, 0), (beside, 0), (across, 0), (across, rows))):
         place = jnp.bitwise_xor(pos[2], d)
         for p in range(wide // share):
             at = pl.multiple_of((p * PLANE + place) * share, share)
-            if d == 0:
-                here = pl.ds(p * share, share)
-                pairs.append((gate.at[:, pl.ds(at, share)], own.at[:, here]))
-                continue
-            out, first = (core, rows) if d == 1 else (across, rows + (d - 2) * part)
-            for q in range(4):
-                columns = pl.ds(q * wide + p * share, share)
-                source = gate.at[pl.ds(q * part, part), pl.ds(at, share)]
-                pairs.append((source, out.at[pl.ds(first, part), columns]))
+            here = out.at[pl.ds(first, rows), pl.ds(p * share, share)]
+            pairs.append((gate.at[:, pl.ds(at, share)], here))
     for copy in fetch(pairs, sems):
         copy.wait()
-
-
-def unfold_kernel(pos, core, from_x, both, *outs):
-    rows, wide = outs[0].shape
-    part = rows // 4
-    for source, first, out in zip((core, from_x, both), (0, 0, part), outs):
-        for q in range(4):
-            out[q * part : (q + 1) * part, :] = source[
-                rows + first : rows + first + part, q * wide : (q + 1) * wide
-            ]
 
 
 def join(out, parts):
@@ -154,13 +136,15 @@
 
 
 def half_kernel(pos, *refs):
-    parts, (whole, near), (out, joined, beside) = refs[:PLANE], refs[PLANE:-3], refs[-3:]
+    parts, out = refs[:PLANE], refs[PLANE]
     for y in range(2):
 
         @pl.when(pos[0] == y)
         def _():
             join(out, parts[2 * y : 2 * y + 2])
 
+
+def trade_kernel(pos, whole, near, joined, beside):
     rows, wide = whole.shape
     quarter = rows // 4
     joined[:rows, :] = whole[...]
@@ -174,7 +158,7 @@
     join(refs[-1], refs[:-1])
 
 
-def places_kernel(pos, own, mine, other, *outs):
+def places_kernel(pos, own, mine, other, gate, *outs):
     planes, rows, share = outs[0].shape
     part = rows // 2
     for d, out in enumerate(outs):
@@ -183,21 +167,23 @@
         for side, block in ((pos[0], mine), (1 - pos[0], other)):
             out[2 + side] = block[:rows, columns]
             out[1, pl.ds(pl.multiple_of(side * part, part), part), :] = block[rows:, columns]
+    for p in range(planes):
+        outs[1][planes + p] = gate[:, p * share : (p + 1) * share]
 
 
 def project_kernel(planes, pos, x, core, from_x, both, own, *refs):
-    halves, outs = refs[: 2 * planes - 2], refs[2 * planes - 2 : -3]
+    halves, outs = refs[:5], refs[5:-3]
     xs, ws, ps = refs[-3:]
     rows = x.shape[0]
     deep = own.shape[0] // PLANE
     share = outs[0].shape[1]
-    join(xs, [block.at[:rows] for block in (x, core, from_x, both)])
+    join(xs, (x, core, from_x, both))
     for d in range(PLANE):
         ws[pl.ds(block_at(pos, 0, d, deep), deep), :] = own[d * deep : (d + 1) * deep, :]
-    for i, half in enumerate(halves):
-        side = pos[0] if i < planes - 1 else 1 - pos[0]
-        for j in range(2):
-            at = block_at(pos, 1 + i % (planes - 1), 2 * side + j, deep)
+    for half, k, first in zip(halves, (0, 0, 0, 1, 1), (1, 2, 3, 1, 3)):
+        side = pos[0] if k == 0 else 1 - pos[0]
+        for j in range(half.shape[0] // deep):
+            at = block_at(pos, first + j // 2, 2 * side + j % 2, deep)
             ws[pl.ds(at, deep), :] = half[j * deep : (j + 1) * deep, :]
     ps[...] = dot(xs[...], ws[...]).astype(ps.dtype)
     for s in range(planes):
@@ -310,12 +296,16 @@
 
 def mixed_dots(planes, pos, u, gate, ws, mixed, outs):
     share = u[0].shape[1]
-    rows = gate[0].shape[0]
+    rows = u[0].shape[0] // 2
     for s in range(planes):
-        at = pl.multiple_of(jnp.bitwise_xor(pos[1], s) * share, share)
+        plane = jnp.bitwise_xor(pos[1], s)
         for d in range(2):
+            if len(gate[d].shape) == 3:
+                columns = gate[d][planes + plane]
+            else:
+                columns = gate[d][:rows, pl.ds(pl.multiple_of(plane * share, share), share)]
             mixed[d * rows : (d + 1) * rows, s * share : (s + 1) * share] = (
-                gate[d][:, pl.ds(at, share)].astype(jnp.float32)
+                columns.astype(jnp.float32)
                 * u[s][d * rows : (d + 1) * rows, :].astype(jnp.float32)
             ).astype(mixed.dtype)
     got = dot(mixed[...], ws[...])
@@ -327,16 +317,16 @@
 
 def upper_kernel(planes, pos, *refs):
     u, gate = refs[:planes], refs[planes : planes + 2]
-    own, halves = refs[planes + 2], refs[planes + 3 : 3 * planes + 1]
-    outs, ws, mixed = refs[3 * planes + 1 : -2], refs[-2], refs[-1]
+    own, halves = refs[planes + 2], refs[planes + 3 : planes + 7]
+    outs, ws, mixed = refs[planes + 7 : -2], refs[-2], refs[-1]
     share = u[0].shape[1]
     width = halves[0].shape[1]
     ws[:share, :] = own[...]
-    for i, half in enumerate(halves):
-        side = pos[0] if i < planes - 1 else 1 - pos[0]
+    for k in range(2):
+        side = pos[0] if k == 0 else 1 - pos[0]
         columns = pl.ds(pl.multiple_of(side * width, width), width)
-        s = 1 + i % (planes - 1)
-        ws[s * share : (s + 1) * share, columns] = half[:share, :]
+        ws[share : 2 * share, columns] = halves[2 * k][...]
+        ws[2 * share :, columns] = halves[2 * k + 1][...]
     mixed_dots(planes, pos, u, gate, ws, mixed, outs)
 
 
@@ -370,9 +360,9 @@
     def shaped(*shape, dtype=jnp.bfloat16):
         return jax.ShapeDtypeStruct(shape, dtype)
 
-    def small(kernel, outs, *args, copies=0, fetched=0, vmem=2):
+    def small(kernel, outs, *args, copies=0, fetched=0, vmem=2, flops=0):
         scratch = [pltpu.SemaphoreType.DMA((copies,))] if copies else []
-        return list(call(kernel, outs, scratch, pos, args, 0, vmem=vmem, fetched=fetched))
+        return list(call(kernel, outs, scratch, pos, args, flops, vmem=vmem, fetched=fetched))
 
     stage = lax.optimization_barrier
     first, last, turned, back = (
@@ -398,14 +388,14 @@
     )
     cut = list(cut)
     out_near = to_plane(out_near, 1)
-    gate_own, core, message = small(
-        functools.partial(across_kernel, share),
-        [shaped(rows, wide), shaped(rows * 5 // 4, features), shaped(rows * 3 // 2, features)],
-        inputs,
+    gate_own, gate_beside, gate_x = small(
+        functools.partial(gate_kernel, share),
+        [shaped(rows, wide), shaped(rows, wide), shaped(2 * rows, wide)],
         gate_in,
-        copies=13 * planes + 2,
-        fetched=2,
-    )
+        copies=4 * planes,
+        fetched=1,
+    )
+    core = to_place(inputs, 1)
     own = small(join_kernel, [shaped(deep, wide)], cut[0])
     cut = own + [to_place(cut[d], d) for d in range(1, PLANE)]
     route = [
@@ -414,37 +404,45 @@
         for i in range(devices)
     ]
     taps_whole = lax.ppermute(taps_whole, ("groups", "seq"), route)
-    cut, taps_whole, message, core, out_near = stage((cut, taps_whole, message, core, out_near))
-
-    sent, taps_mine, out_near = small(
-        half_kernel,
-        [shaped(2 * deep, wide), shaped(rows * 3 // 2, wide), shaped(deep, width)],
-        *cut,
+    sent = small(half_kernel, [shaped(2 * deep, wide)], *cut, flops=1)[0]
+    cut, taps_whole, late, core, out_near, sent, gate_own, gate_beside, gate_x = stage(
+        (cut, taps_whole, inputs, core, out_near, sent, gate_own, gate_beside, gate_x)
+    )
+
+    taps_mine, out_near = small(
+        trade_kernel,
+        [shaped(rows * 3 // 2, wide), shaped(deep, width)],
         taps_whole,
         out_near,
     )
     near, far = to_plane(sent, 1), to_plane(sent, 2)
-    from_x = to_place(message, 2)
-    core = to_place(core, 1)
+    from_x = to_place(late, 2)
     taps_other, out_other = to_group(taps_mine), to_group(out_near)
-    near, far, from_x, taps_other, core, out_half, out_other = stage(
-        (near, far, from_x, taps_other, core, out_half, out_other)
+    near, far, from_x, taps_other, out_half, out_other = stage(
+        (near, far, from_x, taps_other, out_half, out_other)
     )
 
     passed = to_plane(far, 1)
-    near_other, far_other = to_group(near), to_group(far)
+    other = small(
+        join_kernel, [shaped(4 * deep, wide)], to_group(near), to_group(far), flops=1073741824
+    )[0]
     out_far = to_plane(out_half, 2)
     both = to_place(from_x, 1)
     taps_parts = small(
-        places_kernel, [shaped(planes, rows, share)] * PLANE, taps_own, taps_mine, taps_other
-    )
-    taps_parts, passed, both = stage((taps_parts, passed, both))
+        places_kernel,
+        [shaped(planes * (2 if d == 1 else 1), rows, share) for d in range(PLANE)],
+        taps_own,
+        taps_mine,
+        taps_other,
+        gate_beside,
+    )
+    other, passed, both = stage((other, passed, both))
     passed_other = to_group(passed)
     taps_parts = [taps_parts[0]] + [to_place(taps_parts[d], d) for d in range(1, PLANE)]
     held = small(join_kernel, [shaped(PLANE * deep, wide)], *cut)[0]
-    out_passed = to_plane(out_far, 1)
-    passed, near_other, far_other, out_passed, both, taps_parts, passed_other, held = stage(
-        (passed, near_other, far_other, out_passed, both, taps_parts, passed_other, held)
+    weights = small(join_kernel, [shaped(2 * deep, width)], out_far, to_plane(out_far, 1))[0]
+    passed, other, both, taps_parts, passed_other, held = stage(
+        (passed, other, both, taps_parts, passed_other, held)
     )
     projected = call(
         functools.partial(project_kernel, planes),
@@ -455,18 +453,19 @@
             pltpu.VMEM((PLANE * rows, wide), jnp.bfloat16),
         ],
         pos,
-        [inputs, core, from_x, both, held, near, far, passed]
-        + [near_other, far_other, passed_other],
+        [inputs, core, from_x, both, held, near, far, passed, other, passed_other],
         2 * PLANE * rows * features * wide,
         vmem=8,
     )
-    projected, out_far = stage((projected, out_far))
+    projected, weights, gate_x = stage((projected, weights, gate_x))
 
     def spread(parts):
-        return [parts[0]] + [to_plane(parts[s], s) for s in range(1, planes)]
+        sent = [to_plane(parts[s], s) for s in reversed(range(1, planes))]
+        return [parts[0]] + sent[::-1]
 
     signal = spread(projected)
-    out_other = [out_other, to_group(out_far)]
+    weights_other = to_group(weights)
+    gate_x = to_place(gate_x, 2)
     response = call(
         functools.partial(taps_kernel, blocks, planes),
         [shaped(blocks + 1, 2 * rows, share)],
@@ -479,8 +478,8 @@
         2 * positions * share * (32 * ROWS + 4 * rows),
         vmem=4,
     )[0]
-    gate = [gate_own] + small(unfold_kernel, [shaped(rows, wide)] * 3, core, from_x, both)
-    signal, response = stage((signal, response))
+    signal, response = stage((signal[::-1], response))
+    signal = signal[::-1]
 
     mixed = call(
         functools.partial(conv_kernel, blocks, planes),
@@ -493,14 +492,15 @@
         ],
         pos,
         [*signal, short_taps, skip_scale[None], response, first, last, turned, back],
-        4 * positions * share * (32 * ROWS + 4 * rows),
+        16 * positions * share * (32 * ROWS + 4 * rows),
         vmem=8,
     )
-    mixed, out_passed, out_other = stage((mixed, out_passed, out_other))
+    mixed, weights_other, gate_x = stage((mixed, weights_other, gate_x))
 
     upper = spread(mixed[planes:])
-    out_other += [to_group(out_passed)]
-    upper, out_other, lower = stage((upper, out_other, mixed[:planes]))
+    gate_three = to_place(gate_x[rows:], 1)
+    upper, lower, gate_three = stage((upper[::-1], mixed[:planes], gate_three))
+    upper = upper[::-1]
     scratch = [pltpu.VMEM((2 * rows, wide), jnp.bfloat16)]
     flops = 4 * rows * features * wide
     partial_two, partial_three, gathered = call(
@@ -509,8 +509,8 @@
         + [shaped(wide, features)],
         scratch,
         pos,
-        [*upper, *gate[2:], output_weight]
-        + [out_near, out_far, out_passed, *out_other],
+        [*upper, gate_x, gate_three, output_weight]
+        + [out_near, weights, out_other, weights_other],
         flops,
         vmem=8,
     )
@@ -524,7 +524,7 @@
         [shaped(rows, features, dtype=jnp.float32)] + [shaped(rows, features // 4)] * 4,
         scratch,
         pos,
-        [*lower, *gate[:2], gathered],
+        [*lower, gate_own, taps_parts[1], gathered],
         0,
         vmem=8,
     )

time: 111 us -> 109 us (0.982)
  starting transfers between devices: 42.6 us -> 39.5 us
    ppermute x7 -> x6, waiting for transfers between devices: 3.45 us -> 9.39 us  [to_group(): return lax.ppermute(block, 'groups', [(0, 1), (1, 0)])]
    ppermute x15, waiting for transfers between devices: 39.2 us -> 33.4 us  [to_plane(): lax.ppermute(block, 'seq', [(i, i ^ s * PLANE) for i in range(devices)])]
    ppermute x7 -> x6, starting transfers between devices: 10.5 us -> 6.71 us  [to_group(): return lax.ppermute(block, 'groups', [(0, 1), (1, 0)])]
    ppermute x15, starting transfers between devices: 21.4 us -> 22.8 us  [to_plane(): lax.ppermute(block, 'seq', [(i, i ^ s * PLANE) for i in range(devices)])]
    ppermute x15 -> x17, waiting for transfers between devices: 6.39 us -> 4.97 us  [to_place(): return lax.ppermute(block, 'seq', [(i, i ^ d) for i in range(devices)])]
    ppermute x15 -> x17, starting transfers between devices: 8.14 us -> 7.37 us  [to_place(): return lax.ppermute(block, 'seq', [(i, i ^ d) for i in range(devices)])]
    pallas_call x12 -> x14, Pallas kernels: 16.4 us -> 17 us  [call(): pl.pallas_call(kernel, out_shape=outs, in_specs=in_specs, out_specs=[pl.B...]
  transfers between devices with their start and end apart: 38 -> 39, of which waited for: 19 -> 21; matrix products, arithmetic and copies ran while one was open for 0% -> 0% of each run, Pallas kernels for 9% -> 13%
where the time goes in v5:
time: 109 us
  waiting for transfers between devices  49.8 us (46%)
  starting transfers between devices  39.5 us (36%)
  Pallas kernels  17 us (16%)
  other arithmetic  1.14 us (1%)
  local copies, waits for them, and re-layouts  1.1 us (1%)
    ppermute x15, waiting for transfers between devices, to_plane(): lax.ppermute(block, 'seq', [(i, i ^ s * PLANE) for i in range(devices)])  33.4 us
    ppermute x15, starting transfers between devices, to_plane(): lax.ppermute(block, 'seq', [(i, i ^ s * PLANE) for i in range(devices)])  22.8 us
    pallas_call x14, Pallas kernels, call(): pl.pallas_call(kernel, out_shape=outs, in_specs=in_specs, out_specs=[pl.B...  17 us
    ppermute x6, waiting for transfers between devices, to_group(): return lax.ppermute(block, 'groups', [(0, 1), (1, 0)])  9.39 us
    ppermute x17, starting transfers between devices, to_place(): return lax.ppermute(block, 'seq', [(i, i ^ d) for i in range(devices)])  7.37 us
    ppermute x6, starting transfers between devices, to_group(): return lax.ppermute(block, 'groups', [(0, 1), (1, 0)])  6.71 us
    ppermute x17, waiting for transfers between devices, to_place(): return lax.ppermute(block, 'seq', [(i, i ^ d) for i in range(devices)])  4.97 us
    ppermute x1, starting transfers between devices, local(): taps_whole = lax.ppermute(taps_whole, ('groups', 'seq'), route)  2.59 us
  transfers between devices with their start and end apart: 39, of which 21 were waited for; matrix products, arithmetic and copies ran while one was open for 0% of the time, Pallas kernels for 13%

profile of v5, /device:TPU:0, one launch (start us, length us, event | category | flops | bytes accessed | tf_op | source)
XLA Modules:
  0.0 108.9 jit_solution(9207114078173668292)
XLA Ops:
  0.5 2.8 %shard_map.109 = (bf16[128,512]{1,0:T(8,128)(2,1)S(1)}, bf16[128,512]{1,0:T(8,128)(2,1)S(1)}, bf16[128,512]{1,0:T(8,128)(2,1)S(1)}, bf16[128,512]{1,0:T(8,128)(2...) custom-call(s32[3]{0:T(128)S(1)} %pad_add_fusion.pos, ...), custom_call_target="tpu_custom_call" | custom-call | tf_op jit(solution)/shard_map/pallas_call | solution.py:60
  3.3 2.6 %collective-permute-start.5 = (bf16[160,1024]{1,0:T(8,128)(2,1)}, bf16[160,1024]{1,0:T(8,128)(2,1)S(1)}, u32[]{:S(2)}, u32[]{:S(2)}) collective-permute-start(bf16[160,1024]{1,0:T(8,128)(2,1)} %get-tuple-element.112), channel_id=1, source_target_pairs={{0,4},{1,5},{2,6},{3,7},{4,0},{5,1},{6,2},{7,3},{8,12},{9,13},{10,... | collective-permute-start | bytes 983048 | tf_op jit(solution)/shard_map/ppermute | solution.py:355
  6.2 1.5 %collective-permute-start.1 = (bf16[128,512]{1,0:T(8,128)(2,1)S(1)}, bf16[128,512]{1,0:T(8,128)(2,1)S(1)}, u32[]{:S(2)}, u32[]{:S(2)}) collective-permute-start(bf16[128,512]{1,0:T(8,128)(2,1)S(1)} %get-tuple-element.109), channel_id=1, source_target_pairs={{0,2},{1,3},{2,0},{3,1},{4,6},{5,7},{6,4},{7,5},{8,10},{9,11},{10,... | collective-permute-start | bytes 393224 | tf_op jit(solution)/shard_map/ppermute | solution.py:352
  7.8 2.6 %collective-permute-start.3 = (bf16[128,512]{1,0:T(8,128)(2,1)S(1)}, bf16[128,512]{1,0:T(8,128)(2,1)S(1)}, u32[]{:S(2)}, u32[]{:S(2)}) collective-permute-start(bf16[128,512]{1,0:T(8,128)(2,1)S(1)} %get-tuple-element.111), channel_id=1, source_target_pairs={{0,8},{1,9},{2,10},{3,11},{4,12},{5,13},{6,14},{7,15},{8,0},{9,1},... | collective-permute-start | bytes 393224 | tf_op jit(solution)/shard_map/ppermute | solution.py:406
  10.4 1.0 copy-done.3
  11.5 0.9 shard_map.112
  12.9 1.1 %collective-permute-done.2.refs_3_ = bf16[128,512]{1,0:T(8,128)(2,1)S(1)} collective-permute-done((bf16[128,512]{1,0:T(8,128)(2,1)S(1)}, bf16[128,512]{1,0:T(8,128)(2,1)S(1)}, u32[]{:S(2)}, u32[]{:S(2)}) %collective-permute-start.2) | collective-permute-done | bytes 131104 | tf_op jit(solution)/shard_map/ppermute | solution.py:352
  14.6 2.0 %collective-permute-done.3.whole = bf16[128,512]{1,0:T(8,128)(2,1)S(1)} collective-permute-done((bf16[128,512]{1,0:T(8,128)(2,1)S(1)}, bf16[128,512]{1,0:T(8,128)(2,1)S(1)}, u32[]{:S(2)}, u32[]{:S(2)}) %collective-permute-start.3) | collective-permute-done | bytes 131104 | tf_op jit(solution)/shard_map/ppermute | solution.py:406
  16.6 0.7 collective-permute-done.5.near
  17.4 1.7 %collective-permute-start.8 = (bf16[128,2048]{1,0:T(8,128)(2,1)S(1)}, bf16[128,2048]{1,0:T(8,128)(2,1)S(1)}, u32[]{:S(2)}, u32[]{:S(2)}) collective-permute-start(bf16[128,2048]{1,0:T(8,128)(2,1)S(1)} %copy-done.2), channel_id=1, source_target_pairs={{0,2},{1,3},{2,0},{3,1},{4,6},{5,7},{6,4},{7,5},{8,10},{9,11},{10,... | collective-permute-start | bytes 1572872 | tf_op jit(solution)/shard_map/ppermute | solution.py:352
  19.0 2.5 %collective-permute-start.7 = (bf16[256,512]{1,0:T(8,128)(2,1)S(1)}, bf16[256,512]{1,0:T(8,128)(2,1)S(1)}, u32[]{:S(2)}, u32[]{:S(2)}) collective-permute-start(bf16[256,512]{1,0:T(8,128)(2,1)S(1)} %shard_map.111), channel_id=1, source_target_pairs={{0,8},{1,9},{2,10},{3,11},{4,12},{5,13},{6,14},{7,15},{8,0},{9,1},... | collective-permute-start | bytes 786440 | tf_op jit(solution)/shard_map/ppermute | solution.py:355
  21.6 1.6 %collective-permute-start.6 = (bf16[256,512]{1,0:T(8,128)(2,1)S(1)}, bf16[256,512]{1,0:T(8,128)(2,1)S(1)}, u32[]{:S(2)}, u32[]{:S(2)}) collective-permute-start(bf16[256,512]{1,0:T(8,128)(2,1)S(1)} %shard_map.111), channel_id=1, source_target_pairs={{0,4},{1,5},{2,6},{3,7},{4,0},{5,1},{6,2},{7,3},{8,12},{9,13},{10,... | collective-permute-start | bytes 786440 | tf_op jit(solution)/shard_map/ppermute | solution.py:355
  23.8 1.6 %collective-permute-start.10 = (bf16[128,1024]{1,0:T(8,128)(2,1)S(1)}, bf16[128,1024]{1,0:T(8,128)(2,1)S(1)}, u32[]{:S(2)}, u32[]{:S(2)}) collective-permute-start(bf16[128,1024]{1,0:T(8,128)(2,1)S(1)} %get-tuple-element.123.refs_7_), channel_id=1, source_target_pairs={{0,16},{16,0},{1,17},{17,1},{2,18},{18,2},{3,19},{19,3},{4,20},{20... | collective-permute-start | bytes 786440 | tf_op jit(solution)/shard_map/ppermute | solution.py:358
  25.9 9.3 %collective-permute-done.9.other = bf16[192,512]{1,0:T(8,128)(2,1)S(1)} collective-permute-done((bf16[192,512]{1,0:T(8,128)(2,1)S(1)}, bf16[192,512]{1,0:T(8,128)(2,1)S(1)}, u32[]{:S(2)}, u32[]{:S(2)}) %collective-permute-start.9) | collective-permute-done | bytes 196640 | tf_op jit(solution)/shard_map/ppermute | solution.py:358
  35.3 1.5 %collective-permute-start.19 = (bf16[128,1024]{1,0:T(8,128)(2,1)}, bf16[128,1024]{1,0:T(8,128)(2,1)S(1)}, u32[]{:S(2)}, u32[]{:S(2)}) collective-permute-start(bf16[128,1024]{1,0:T(8,128)(2,1)} %get-tuple-element.150), channel_id=1, source_target_pairs={{0,8},{1,9},{2,10},{3,11},{4,12},{5,13},{6,14},{7,15},{8,0},{9,1},... | collective-permute-start | bytes 786440 | tf_op jit(solution)/shard_map/ppermute | solution.py:355
  36.7 1.2 %collective-permute-start.11 = (bf16[256,512]{1,0:T(8,128)(2,1)S(1)}, bf16[256,512]{1,0:T(8,128)(2,1)S(1)}, u32[]{:S(2)}, u32[]{:S(2)}) collective-permute-start(bf16[256,512]{1,0:T(8,128)(2,1)S(1)} %collective-permute-done.6.refs_0_), channel_id=1, source_target_pairs={{0,16},{16,0},{1,17},{17,1},{2,18},{18,2},{3,19},{19,3},{4,20},{20... | collective-permute-start | bytes 786440 | tf_op jit(solution)/shard_map/ppermute | solution.py:358
  38.0 0.8 collective-permute-start.12
  38.8 1.2 %collective-permute-start.13 = (bf16[256,512]{1,0:T(8,128)(2,1)S(1)}, bf16[256,512]{1,0:T(8,128)(2,1)S(1)}, u32[]{:S(2)}, u32[]{:S(2)}) collective-permute-start(bf16[256,512]{1,0:T(8,128)(2,1)S(1)} %collective-permute-done.7.refs_1_), channel_id=1, source_target_pairs={{0,4},{1,5},{2,6},{3,7},{4,0},{5,1},{6,2},{7,3},{8,12},{9,13},{10,... | collective-permute-start | bytes 786440 | tf_op jit(solution)/shard_map/ppermute | solution.py:355
  40.0 0.7 shard_map.115
  40.7 10.0 %collective-permute-done.19.refs_0_ = bf16[128,1024]{1,0:T(8,128)(2,1)S(1)} collective-permute-done((bf16[128,1024]{1,0:T(8,128)(2,1)}, bf16[128,1024]{1,0:T(8,128)(2,1)S(1)}, u32[]{:S(2)}, u32[]{:S(2)}) %collective-permute-start.19) | collective-permute-done | bytes 262176 | tf_op jit(solution)/shard_map/ppermute | solution.py:355
  50.7 0.6 shard_map.114.refs_3_
  51.3 0.8 collective-permute-done.13.refs_2_
  52.1 1.2 %collective-permute-start.18 = (bf16[256,512]{1,0:T(8,128)(2,1)S(1)}, bf16[256,512]{1,0:T(8,128)(2,1)S(1)}, u32[]{:S(2)}, u32[]{:S(2)}) collective-permute-start(bf16[256,512]{1,0:T(8,128)(2,1)S(1)} %collective-permute-done.13.refs_2_), channel_id=1, source_target_pairs={{0,16},{16,0},{1,17},{17,1},{2,18},{18,2},{3,19},{19,3},{4,20},{20... | collective-permute-start | bytes 786440 | tf_op jit(solution)/shard_map/ppermute | solution.py:358
  54.9 4.5 %collective-permute-done.20.refs_1_ = bf16[128,1024]{1,0:T(8,128)(2,1)S(1)} collective-permute-done((bf16[128,1024]{1,0:T(8,128)(2,1)S(1)}, bf16[128,1024]{1,0:T(8,128)(2,1)S(1)}, u32[]{:S(2)}, u32[]{:S(2)}) %collective-permute-start.20) | collective-permute-done | bytes 262176 | tf_op jit(solution)/shard_map/ppermute | solution.py:355
  59.4 0.6 shard_map.118.refs_8_
  60.1 2.0 %shard_map.117 = (bf16[512,128]{1,0:T(8,128)(2,1)S(1)}, bf16[512,128]{1,0:T(8,128)(2,1)S(1)}, bf16[512,128]{1,0:T(8,128)(2,1)S(1)}, bf16[512,128]{1,0:T(8,128)(2,1)S(1)}) custom-call(s32[3]{0:T(128)S(1)} %pad_add_fusion.pos, bf16[128,2048]{1,0:T(8,128)(2,1)S(1)} %copy-done.2, bf16[128,2048]{1,0:T(8,128)(2,1)S(1)} %collective-permute-done.4.core, ...), custom_call_target="tpu_custom_call" | custom-call | flops 1073741824 | bytes 4718592 | tf_op jit(solution)/shard_map/pallas_call | solution.py:60
  62.1 2.8 %collective-permute-start.21 = (bf16[512,128]{1,0:T(8,128)(2,1)S(1)}, bf16[512,128]{1,0:T(8,128)(2,1)S(1)}, u32[]{:S(2)}, u32[]{:S(2)}) collective-permute-start(bf16[512,128]{1,0:T(8,128)(2,1)S(1)} %get-tuple-element.152), channel_id=1, source_target_pairs={{0,12},{1,13},{2,14},{3,15},{4,8},{5,9},{6,10},{7,11},{8,4},{9,5},... | collective-permute-start | bytes 393224 | tf_op jit(solution)/shard_map/ppermute | solution.py:355
  65.5 1.1 %collective-permute-start.23 = (bf16[512,128]{1,0:T(8,128)(2,1)S(1)}, bf16[512,128]{1,0:T(8,128)(2,1)S(1)}, u32[]{:S(2)}, u32[]{:S(2)}) collective-permute-start(bf16[512,128]{1,0:T(8,128)(2,1)S(1)} %get-tuple-element.154), channel_id=1, source_target_pairs={{0,4},{1,5},{2,6},{3,7},{4,0},{5,1},{6,2},{7,3},{8,12},{9,13},{10,... | collective-permute-start | bytes 393224 | tf_op jit(solution)/shard_map/ppermute | solution.py:355
  66.6 1.4 %collective-permute-start.24 = (bf16[256,1024]{1,0:T(8,128)(2,1)S(1)}, bf16[256,1024]{1,0:T(8,128)(2,1)S(1)}, u32[]{:S(2)}, u32[]{:S(2)}) collective-permute-start(bf16[256,1024]{1,0:T(8,128)(2,1)S(1)} %shard_map.118.refs_8_), channel_id=1, source_target_pairs={{0,16},{16,0},{1,17},{17,1},{2,18},{18,2},{3,19},{19,3},{4,20},{20... | collective-permute-start | bytes 1572872 | tf_op jit(solution)/shard_map/ppermute | solution.py:358
  68.5 1.6 %shard_map.119.refs_6_ = bf16[17,256,128]{2,1,0:T(8,128)(2,1)S(1)} custom-call(s32[3]{0:T(128)S(1)} %pad_add_fusion.pos, bf16[4,128,128]{2,1,0:T(8,128)(2,1)S(1)} %get-tuple-element.156.refs_0_, bf16[8,128,128]{2,1,0:T(8,128)(2,1)S(1)} %collective-permute-done.15.refs_1_.refs_5_, bf16[4,128,128]{2,1,0:T(8,128)(2,1)S(1)} %collective-permute-done.16.refs_2_, ...), custom_call_target="tpu_custom_call" | custom-call | flops 536870912 | bytes 4259840 | tf_op jit(solution)/shard_map/pallas_call | solution.py:60
  70.5 7.6 %collective-permute-done.22.refs_2_ = bf16[512,128]{1,0:T(8,128)(2,1)S(1)} collective-permute-done((bf16[512,128]{1,0:T(8,128)(2,1)S(1)}, bf16[512,128]{1,0:T(8,128)(2,1)S(1)}, u32[]{:S(2)}, u32[]{:S(2)}) %collective-permute-start.22) | collective-permute-done | bytes 131104 | tf_op jit(solution)/shard_map/ppermute | solution.py:355
  78.2 3.0 %shard_map.120 = (bf16[256,128]{1,0:T(8,128)(2,1)S(1)}, bf16[256,128]{1,0:T(8,128)(2,1)S(1)}, bf16[256,128]{1,0:T(8,128)(2,1)S(1)}, bf16[256,128]{1,0:T(8,128)(2...) custom-call(s32[3]{0:T(128)S(1)} %pad_add_fusion.pos, ...), custom_call_target="tpu_custom_call" | custom-call | flops 4294967296 | bytes 7176192 | tf_op jit(solution)/shard_map/pallas_call | solution.py:60
  81.3 2.4 %collective-permute-start.26 = (bf16[256,128]{1,0:T(8,128)(2,1)S(1)}, bf16[256,128]{1,0:T(8,128)(2,1)S(1)}, u32[]{:S(2)}, u32[]{:S(2)}) collective-permute-start(bf16[256,128]{1,0:T(8,128)(2,1)S(1)} %get-tuple-element.175), channel_id=1, source_target_pairs={{0,12},{1,13},{2,14},{3,15},{4,8},{5,9},{6,10},{7,11},{8,4},{9,5},... | collective-permute-start | bytes 196616 | tf_op jit(solution)/shard_map/ppermute | solution.py:355
  83.7 2.0 %collective-permute-start.28 = (bf16[256,128]{1,0:T(8,128)(2,1)S(1)}, bf16[256,128]{1,0:T(8,128)(2,1)S(1)}, u32[]{:S(2)}, u32[]{:S(2)}) collective-permute-start(bf16[256,128]{1,0:T(8,128)(2,1)S(1)} %get-tuple-element.177), channel_id=1, source_target_pairs={{0,4},{1,5},{2,6},{3,7},{4,0},{5,1},{6,2},{7,3},{8,12},{9,13},{10,... | collective-permute-start | bytes 196616 | tf_op jit(solution)/shard_map/ppermute | solution.py:355
  85.7 2.4 %collective-permute-done.26.refs_3_ = bf16[256,128]{1,0:T(8,128)(2,1)S(1)} collective-permute-done((bf16[256,128]{1,0:T(8,128)(2,1)S(1)}, bf16[256,128]{1,0:T(8,128)(2,1)S(1)}, u32[]{:S(2)}, u32[]{:S(2)}) %collective-permute-start.26) | collective-permute-done | bytes 65568 | tf_op jit(solution)/shard_map/ppermute | solution.py:355
  88.1 2.3 %collective-permute-done.27.refs_2_ = bf16[256,128]{1,0:T(8,128)(2,1)S(1)} collective-permute-done((bf16[256,128]{1,0:T(8,128)(2,1)S(1)}, bf16[256,128]{1,0:T(8,128)(2,1)S(1)}, u32[]{:S(2)}, u32[]{:S(2)}) %collective-permute-start.27) | collective-permute-done | bytes 65568 | tf_op jit(solution)/shard_map/ppermute | solution.py:355
  90.4 1.4 %shard_map.121 = (f32[128,2048]{1,0:T(8,128)S(1)}, bf16[128,2048]{1,0:T(8,128)(2,1)S(1)}, bf16[512,2048]{1,0:T(8,128)(2,1)S(1)}) custom-call(s32[3]{0:T(128)S(1)} %pad_add_fusion.pos, bf16[256,128]{1,0:T(8,128)(2,1)S(1)} %get-tuple-element.184.refs_0_, bf16[256,128]{1,0:T(8,128)(2,1)S(1)} %collective-permute-done.28.refs_1_, ...), custom_call_target="tpu_custom_call" | custom-call | flops 536870912 | bytes 6422528 | tf_op jit(solution)/shard_map/pallas_call | solution.py:60
  91.9 1.9 %collective-permute-done.30 = bf16[128,2048]{1,0:T(8,128)(2,1)S(1)} collective-permute-done((bf16[128,2048]{1,0:T(8,128)(2,1)S(1)}, bf16[128,2048]{1,0:T(8,128)(2,1)S(1)}, u32[]{:S(2)}, u32[]{:S(2)}) %collective-permute-start.30) | collective-permute-done | bytes 524320 | tf_op jit(solution)/shard_map/ppermute | solution.py:352
  93.9 0.6 collective-permute-start.38
  94.5 0.6 collective-permute-start.31
  95.1 2.3 %collective-permute-start.32 = (bf16[256,128]{1,0:T(8,128)(2,1)S(1)}, bf16[256,128]{1,0:T(8,128)(2,1)S(1)}, u32[]{:S(2)}, u32[]{:S(2)}) collective-permute-start(bf16[256,128]{1,0:T(8,128)(2,1)S(1)} %get-tuple-element.199), channel_id=1, source_target_pairs={{0,8},{1,9},{2,10},{3,11},{4,12},{5,13},{6,14},{7,15},{8,0},{9,1},... | collective-permute-start | bytes 196616 | tf_op jit(solution)/shard_map/ppermute | solution.py:355
  97.5 1.5 %collective-permute-start.33 = (bf16[256,128]{1,0:T(8,128)(2,1)S(1)}, bf16[256,128]{1,0:T(8,128)(2,1)S(1)}, u32[]{:S(2)}, u32[]{:S(2)}) collective-permute-start(bf16[256,128]{1,0:T(8,128)(2,1)S(1)} %get-tuple-element.200), channel_id=1, source_target_pairs={{0,12},{1,13},{2,14},{3,15},{4,8},{5,9},{6,10},{7,11},{8,4},{9,5},... | collective-permute-start | bytes 196616 | tf_op jit(solution)/shard_map/ppermute | solution.py:355
  98.9 0.6 collective-permute-done.31.refs_1_
  99.5 3.1 %collective-permute-done.32.refs_2_ = bf16[256,128]{1,0:T(8,128)(2,1)S(1)} collective-permute-done((bf16[256,128]{1,0:T(8,128)(2,1)S(1)}, bf16[256,128]{1,0:T(8,128)(2,1)S(1)}, u32[]{:S(2)}, u32[]{:S(2)}) %collective-permute-start.32) | collective-permute-done | bytes 65568 | tf_op jit(solution)/shard_map/ppermute | solution.py:355
  102.6 1.1 collective-permute-done.33.refs_3_
  103.6 1.3 %shard_map.122 = (f32[128,2048]{1,0:T(8,128)S(1)}, bf16[128,512]{1,0:T(8,128)(2,1)S(1)}, bf16[128,512]{1,0:T(8,128)(2,1)S(1)}, bf16[128,512]{1,0:T(8,128)(2,1)S(1)}, bf16[128,512]{1,0:T(8,128)(2,1)S(1)}) custom-call(s32[3]{0:T(128)S(1)} %pad_add_fusion.pos, bf16[256,128]{1,0:T(8,128)(2,1)S(1)} %get-tuple-element.197.refs_0_, ...), custom_call_target="tpu_custom_call" | custom-call | tf_op jit(solution)/shard_map/pallas_call | solution.py:60
  107.0 0.9 collective-permute-done.38
  108.0 1.0 add_convert_fusion
  (66 shorter events, 8.8 us)
Async XLA Ops:
  0.0 17.4 %copy-start.2 = (bf16[128,2048]{1,0:T(8,128)(2,1)S(1)}, bf16[128,2048]{1,0:T(8,128)(2,1)}, u32[]{:S(2)}) copy-start(bf16[128,2048]{1,0:T(8,128)(2,1)} %x.1) | copy-start | bytes 1572868
  0.0 17.4 %collective-permute-start.4 = (bf16[128,2048]{1,0:T(8,128)(2,1)}, bf16[128,2048]{1,0:T(8,128)(2,1)S(1)}, u32[]{:S(2)}, u32[]{:S(2)}) collective-permute-start(bf16[128,2048]{1,0:T(8,128)(2,1)} %x.1), channel_id=1, source_target_pairs={{0,1},{1,0},{2,3},{3,2},{4,5},{5,4},{6,7},{7,6},{8,9},{9,8},{10,11... | collective-permute-start | bytes 1572872 | tf_op jit(solution)/shard_map/ppermute | solution.py:352
  3.3 14.0 %collective-permute-start.5 = (bf16[160,1024]{1,0:T(8,128)(2,1)}, bf16[160,1024]{1,0:T(8,128)(2,1)S(1)}, u32[]{:S(2)}, u32[]{:S(2)}) collective-permute-start(bf16[160,1024]{1,0:T(8,128)(2,1)} %get-tuple-element.112), channel_id=1, source_target_pairs={{0,4},{1,5},{2,6},{3,7},{4,0},{5,1},{6,2},{7,3},{8,12},{9,13},{10,... | collective-permute-start | bytes 983048 | tf_op jit(solution)/shard_map/ppermute | solution.py:355
  6.0 1.9 %collective-permute-start = (bf16[128,512]{1,0:T(8,128)(2,1)S(1)}, bf16[128,512]{1,0:T(8,128)(2,1)S(1)}, u32[]{:S(2)}, u32[]{:S(2)}) collective-permute-start(bf16[128,512]{1,0:T(8,128)(2,1)S(1)} %get-tuple-element.108), channel_id=1, source_target_pairs={{0,1},{1,0},{2,3},{3,2},{4,5},{5,4},{6,7},{7,6},{8,9},{9,8},{10,11... | collective-permute-start | bytes 393224 | tf_op jit(solution)/shard_map/ppermute | solution.py:352
  6.2 6.7 %collective-permute-start.1 = (bf16[128,512]{1,0:T(8,128)(2,1)S(1)}, bf16[128,512]{1,0:T(8,128)(2,1)S(1)}, u32[]{:S(2)}, u32[]{:S(2)}) collective-permute-start(bf16[128,512]{1,0:T(8,128)(2,1)S(1)} %get-tuple-element.109), channel_id=1, source_target_pairs={{0,2},{1,3},{2,0},{3,1},{4,6},{5,7},{6,4},{7,5},{8,10},{9,11},{10,... | collective-permute-start | bytes 393224 | tf_op jit(solution)/shard_map/ppermute | solution.py:352
  7.7 6.4 %collective-permute-start.2 = (bf16[128,512]{1,0:T(8,128)(2,1)S(1)}, bf16[128,512]{1,0:T(8,128)(2,1)S(1)}, u32[]{:S(2)}, u32[]{:S(2)}) collective-permute-start(bf16[128,512]{1,0:T(8,128)(2,1)S(1)} %get-tuple-element.110), channel_id=1, source_target_pairs={{0,3},{1,2},{2,1},{3,0},{4,7},{5,6},{6,5},{7,4},{8,11},{9,10},{10,... | collective-permute-start | bytes 393224 | tf_op jit(solution)/shard_map/ppermute | solution.py:352
  7.8 8.8 %collective-permute-start.3 = (bf16[128,512]{1,0:T(8,128)(2,1)S(1)}, bf16[128,512]{1,0:T(8,128)(2,1)S(1)}, u32[]{:S(2)}, u32[]{:S(2)}) collective-permute-start(bf16[128,512]{1,0:T(8,128)(2,1)S(1)} %get-tuple-element.111), channel_id=1, source_target_pairs={{0,8},{1,9},{2,10},{3,11},{4,12},{5,13},{6,14},{7,15},{8,0},{9,1},... | collective-permute-start | bytes 393224 | tf_op jit(solution)/shard_map/ppermute | solution.py:406
  10.4 1.0 copy-start.3
  17.4 17.8 %collective-permute-start.8 = (bf16[128,2048]{1,0:T(8,128)(2,1)S(1)}, bf16[128,2048]{1,0:T(8,128)(2,1)S(1)}, u32[]{:S(2)}, u32[]{:S(2)}) collective-permute-start(bf16[128,2048]{1,0:T(8,128)(2,1)S(1)} %copy-done.2), channel_id=1, source_target_pairs={{0,2},{1,3},{2,0},{3,1},{4,6},{5,7},{6,4},{7,5},{8,10},{9,11},{10,... | collective-permute-start | bytes 1572872 | tf_op jit(solution)/shard_map/ppermute | solution.py:352
  19.0 16.1 %collective-permute-start.7 = (bf16[256,512]{1,0:T(8,128)(2,1)S(1)}, bf16[256,512]{1,0:T(8,128)(2,1)S(1)}, u32[]{:S(2)}, u32[]{:S(2)}) collective-permute-start(bf16[256,512]{1,0:T(8,128)(2,1)S(1)} %shard_map.111), channel_id=1, source_target_pairs={{0,8},{1,9},{2,10},{3,11},{4,12},{5,13},{6,14},{7,15},{8,0},{9,1},... | collective-permute-start | bytes 786440 | tf_op jit(solution)/shard_map/ppermute | solution.py:355
  21.6 13.6 %collective-permute-start.6 = (bf16[256,512]{1,0:T(8,128)(2,1)S(1)}, bf16[256,512]{1,0:T(8,128)(2,1)S(1)}, u32[]{:S(2)}, u32[]{:S(2)}) collective-permute-start(bf16[256,512]{1,0:T(8,128)(2,1)S(1)} %shard_map.111), channel_id=1, source_target_pairs={{0,4},{1,5},{2,6},{3,7},{4,0},{5,1},{6,2},{7,3},{8,12},{9,13},{10,... | collective-permute-start | bytes 786440 | tf_op jit(solution)/shard_map/ppermute | solution.py:355
  23.8 11.4 %collective-permute-start.10 = (bf16[128,1024]{1,0:T(8,128)(2,1)S(1)}, bf16[128,1024]{1,0:T(8,128)(2,1)S(1)}, u32[]{:S(2)}, u32[]{:S(2)}) collective-permute-start(bf16[128,1024]{1,0:T(8,128)(2,1)S(1)} %get-tuple-element.123.refs_7_), channel_id=1, source_target_pairs={{0,16},{16,0},{1,17},{17,1},{2,18},{18,2},{3,19},{19,3},{4,20},{20... | collective-permute-start | bytes 786440 | tf_op jit(solution)/shard_map/ppermute | solution.py:358
  25.4 9.8 %collective-permute-start.9 = (bf16[192,512]{1,0:T(8,128)(2,1)S(1)}, bf16[192,512]{1,0:T(8,128)(2,1)S(1)}, u32[]{:S(2)}, u32[]{:S(2)}) collective-permute-start(bf16[192,512]{1,0:T(8,128)(2,1)S(1)} %get-tuple-element.121.mine), channel_id=1, source_target_pairs={{0,16},{16,0},{1,17},{17,1},{2,18},{18,2},{3,19},{19,3},{4,20},{20... | collective-permute-start | bytes 589832 | tf_op jit(solution)/shard_map/ppermute | solution.py:358
  35.2 16.9 %collective-permute-start.14 = (bf16[128,2048]{1,0:T(8,128)(2,1)S(1)}, bf16[128,2048]{1,0:T(8,128)(2,1)S(1)}, u32[]{:S(2)}, u32[]{:S(2)}) collective-permute-start(bf16[128,2048]{1,0:T(8,128)(2,1)S(1)} %collective-permute-done.8.from_x), channel_id=1, source_target_pairs={{0,1},{1,0},{2,3},{3,2},{4,5},{5,4},{6,7},{7,6},{8,9},{9,8},{10,11... | collective-permute-start | bytes 1572872 | tf_op jit(solution)/shard_map/ppermute | solution.py:352
  35.3 15.4 %collective-permute-start.19 = (bf16[128,1024]{1,0:T(8,128)(2,1)}, bf16[128,1024]{1,0:T(8,128)(2,1)S(1)}, u32[]{:S(2)}, u32[]{:S(2)}) collective-permute-start(bf16[128,1024]{1,0:T(8,128)(2,1)} %get-tuple-element.150), channel_id=1, source_target_pairs={{0,8},{1,9},{2,10},{3,11},{4,12},{5,13},{6,14},{7,15},{8,0},{9,1},... | collective-permute-start | bytes 786440 | tf_op jit(solution)/shard_map/ppermute | solution.py:355
  36.7 13.9 %collective-permute-start.11 = (bf16[256,512]{1,0:T(8,128)(2,1)S(1)}, bf16[256,512]{1,0:T(8,128)(2,1)S(1)}, u32[]{:S(2)}, u32[]{:S(2)}) collective-permute-start(bf16[256,512]{1,0:T(8,128)(2,1)S(1)} %collective-permute-done.6.refs_0_), channel_id=1, source_target_pairs={{0,16},{16,0},{1,17},{17,1},{2,18},{18,2},{3,19},{19,3},{4,20},{20... | collective-permute-start | bytes 786440 | tf_op jit(solution)/shard_map/ppermute | solution.py:358
  38.0 12.8 %collective-permute-start.12 = (bf16[256,512]{1,0:T(8,128)(2,1)S(1)}, bf16[256,512]{1,0:T(8,128)(2,1)S(1)}, u32[]{:S(2)}, u32[]{:S(2)}) collective-permute-start(bf16[256,512]{1,0:T(8,128)(2,1)S(1)} %collective-permute-done.7.refs_1_), channel_id=1, source_target_pairs={{0,16},{16,0},{1,17},{17,1},{2,18},{18,2},{3,19},{19,3},{4,20},{20... | collective-permute-start | bytes 786440 | tf_op jit(solution)/shard_map/ppermute | solution.py:358
  38.8 13.3 %collective-permute-start.13 = (bf16[256,512]{1,0:T(8,128)(2,1)S(1)}, bf16[256,512]{1,0:T(8,128)(2,1)S(1)}, u32[]{:S(2)}, u32[]{:S(2)}) collective-permute-start(bf16[256,512]{1,0:T(8,128)(2,1)S(1)} %collective-permute-done.7.refs_1_), channel_id=1, source_target_pairs={{0,4},{1,5},{2,6},{3,7},{4,0},{5,1},{6,2},{7,3},{8,12},{9,13},{10,... | collective-permute-start | bytes 786440 | tf_op jit(solution)/shard_map/ppermute | solution.py:355
  50.7 9.4 %collective-permute-start.15 = (bf16[8,128,128]{2,1,0:T(8,128)(2,1)S(1)}, bf16[8,128,128]{2,1,0:T(8,128)(2,1)S(1)}, u32[]{:S(2)}, u32[]{:S(2)}) collective-permute-start(bf16[8,128,128]{2,1,0:T(8,128)(2,1)S(1)} %get-tuple-element.134), channel_id=1, source_target_pairs={{0,1},{1,0},{2,3},{3,2},{4,5},{5,4},{6,7},{7,6},{8,9},{9,8},{10,11... | collective-permute-start | bytes 786440 | tf_op jit(solution)/shard_map/ppermute | solution.py:352
  50.7 8.7 %collective-permute-start.20 = (bf16[128,1024]{1,0:T(8,128)(2,1)S(1)}, bf16[128,1024]{1,0:T(8,128)(2,1)S(1)}, u32[]{:S(2)}, u32[]{:S(2)}) collective-permute-start(bf16[128,1024]{1,0:T(8,128)(2,1)S(1)} %collective-permute-done.19.refs_0_), channel_id=1, source_target_pairs={{0,4},{1,5},{2,6},{3,7},{4,0},{5,1},{6,2},{7,3},{8,12},{9,13},{10,... | collective-permute-start | bytes 786440 | tf_op jit(solution)/shard_map/ppermute | solution.py:355
  52.1 8.0 %collective-permute-start.18 = (bf16[256,512]{1,0:T(8,128)(2,1)S(1)}, bf16[256,512]{1,0:T(8,128)(2,1)S(1)}, u32[]{:S(2)}, u32[]{:S(2)}) collective-permute-start(bf16[256,512]{1,0:T(8,128)(2,1)S(1)} %collective-permute-done.13.refs_2_), channel_id=1, source_target_pairs={{0,16},{16,0},{1,17},{17,1},{2,18},{18,2},{3,19},{19,3},{4,20},{20... | collective-permute-start | bytes 786440 | tf_op jit(solution)/shard_map/ppermute | solution.py:358
  53.4 6.6 %collective-permute-start.16 = (bf16[4,128,128]{2,1,0:T(8,128)(2,1)S(1)}, bf16[4,128,128]{2,1,0:T(8,128)(2,1)S(1)}, u32[]{:S(2)}, u32[]{:S(2)}) collective-permute-start(bf16[4,128,128]{2,1,0:T(8,128)(2,1)S(1)} %get-tuple-element.135), channel_id=1, source_target_pairs={{0,2},{1,3},{2,0},{3,1},{4,6},{5,7},{6,4},{7,5},{8,10},{9,11},{10,... | collective-permute-start | bytes 393224 | tf_op jit(solution)/shard_map/ppermute | solution.py:352
  53.9 6.1 %collective-permute-start.17 = (bf16[4,128,128]{2,1,0:T(8,128)(2,1)S(1)}, bf16[4,128,128]{2,1,0:T(8,128)(2,1)S(1)}, u32[]{:S(2)}, u32[]{:S(2)}) collective-permute-start(bf16[4,128,128]{2,1,0:T(8,128)(2,1)S(1)} %get-tuple-element.136), channel_id=1, source_target_pairs={{0,3},{1,2},{2,1},{3,0},{4,7},{5,6},{6,5},{7,4},{8,11},{9,10},{10,... | collective-permute-start | bytes 393224 | tf_op jit(solution)/shard_map/ppermute | solution.py:352
  60.0 8.5 %copy-start = (bf16[17,256,256]{2,1,0:T(8,128)(2,1)S(1)}, bf16[17,256,256]{2,1,0:T(8,128)(2,1)}, u32[]{:S(2)}) copy-start(bf16[17,256,256]{2,1,0:T(8,128)(2,1)} %constant.45.clone.refs_5_.refs_9_) | copy-start | bytes 6684676
  60.0 8.5 %copy-start.4 = (bf16[512,256]{1,0:T(8,128)(2,1)S(1)}, bf16[512,256]{1,0:T(8,128)(2,1)}, u32[]{:S(2)}) copy-start(bf16[512,256]{1,0:T(8,128)(2,1)} %constant.43.clone.refs_4_.refs_7_) | copy-start | bytes 786436
  62.1 16.0 %copy-start.5 = (f32[3,2048]{1,0:T(4,128)S(1)}, f32[3,2048]{1,0:T(4,128)}, u32[]{:S(2)}) copy-start(f32[3,2048]{1,0:T(4,128)} %refs_4_.2) | copy-start | bytes 73732
  62.1 16.0 %copy-start.6 = (f32[2048]{0:T(1024)S(1)}, f32[2048]{0:T(1024)}, u32[]{:S(2)}) copy-start(f32[2048]{0:T(1024)} %param.16) | copy-start | bytes 24580
  62.1 16.0 %copy-start.7 = (bf16[17,256,256]{2,1,0:T(8,128)(2,1)S(1)}, bf16[17,256,256]{2,1,0:T(8,128)(2,1)}, u32[]{:S(2)}) copy-start(bf16[17,256,256]{2,1,0:T(8,128)(2,1)} %constant.46.clone.refs_10_) | copy-start | bytes 6684676
  62.1 16.0 %copy-start.8 = (bf16[256,512]{1,0:T(8,128)(2,1)S(1)}, bf16[256,512]{1,0:T(8,128)(2,1)}, u32[]{:S(2)}) copy-start(bf16[256,512]{1,0:T(8,128)(2,1)} %constant.44.clone.refs_8_) | copy-start | bytes 786436
  62.1 8.4 %collective-permute-start.21 = (bf16[512,128]{1,0:T(8,128)(2,1)S(1)}, bf16[512,128]{1,0:T(8,128)(2,1)S(1)}, u32[]{:S(2)}, u32[]{:S(2)}) collective-permute-start(bf16[512,128]{1,0:T(8,128)(2,1)S(1)} %get-tuple-element.152), channel_id=1, source_target_pairs={{0,12},{1,13},{2,14},{3,15},{4,8},{5,9},{6,10},{7,11},{8,4},{9,5},... | collective-permute-start | bytes 393224 | tf_op jit(solution)/shard_map/ppermute | solution.py:355
  64.9 13.2 %collective-permute-start.22 = (bf16[512,128]{1,0:T(8,128)(2,1)S(1)}, bf16[512,128]{1,0:T(8,128)(2,1)S(1)}, u32[]{:S(2)}, u32[]{:S(2)}) collective-permute-start(bf16[512,128]{1,0:T(8,128)(2,1)S(1)} %get-tuple-element.153), channel_id=1, source_target_pairs={{0,8},{1,9},{2,10},{3,11},{4,12},{5,13},{6,14},{7,15},{8,0},{9,1},... | collective-permute-start | bytes 393224 | tf_op jit(solution)/shard_map/ppermute | solution.py:355
  65.5 12.7 %collective-permute-start.23 = (bf16[512,128]{1,0:T(8,128)(2,1)S(1)}, bf16[512,128]{1,0:T(8,128)(2,1)S(1)}, u32[]{:S(2)}, u32[]{:S(2)}) collective-permute-start(bf16[512,128]{1,0:T(8,128)(2,1)S(1)} %get-tuple-element.154), channel_id=1, source_target_pairs={{0,4},{1,5},{2,6},{3,7},{4,0},{5,1},{6,2},{7,3},{8,12},{9,13},{10,... | collective-permute-start | bytes 393224 | tf_op jit(solution)/shard_map/ppermute | solution.py:355
  66.6 14.6 %collective-permute-start.24 = (bf16[256,1024]{1,0:T(8,128)(2,1)S(1)}, bf16[256,1024]{1,0:T(8,128)(2,1)S(1)}, u32[]{:S(2)}, u32[]{:S(2)}) collective-permute-start(bf16[256,1024]{1,0:T(8,128)(2,1)S(1)} %shard_map.118.refs_8_), channel_id=1, source_target_pairs={{0,16},{16,0},{1,17},{17,1},{2,18},{18,2},{3,19},{19,3},{4,20},{20... | collective-permute-start | bytes 1572872 | tf_op jit(solution)/shard_map/ppermute | solution.py:358
  68.0 13.2 %collective-permute-start.25 = (bf16[256,512]{1,0:T(8,128)(2,1)S(1)}, bf16[256,512]{1,0:T(8,128)(2,1)S(1)}, u32[]{:S(2)}, u32[]{:S(2)}) collective-permute-start(bf16[256,512]{1,0:T(8,128)(2,1)S(1)} %get-tuple-element.174), channel_id=1, source_target_pairs={{0,2},{1,3},{2,0},{3,1},{4,6},{5,7},{6,4},{7,5},{8,10},{9,11},{10,... | collective-permute-start | bytes 786440 | tf_op jit(solution)/shard_map/ppermute | solution.py:352
  78.2 12.3 %copy-start.1 = (bf16[128,2048]{1,0:T(8,128)(2,1)S(1)}, bf16[128,2048]{1,0:T(8,128)(2,1)}, u32[]{:S(2)}) copy-start(bf16[128,2048]{1,0:T(8,128)(2,1)} %refs_6_.1) | copy-start | bytes 1572868
  81.2 9.2 %collective-permute-start.29 = (bf16[128,512]{1,0:T(8,128)(2,1)S(1)}, bf16[128,512]{1,0:T(8,128)(2,1)S(1)}, u32[]{:S(2)}, u32[]{:S(2)}) collective-permute-start(bf16[128,512]{1,0:T(8,128)(2,1)S(1)} %slice.3), channel_id=1, source_target_pairs={{0,1},{1,0},{2,3},{3,2},{4,5},{5,4},{6,7},{7,6},{8,9},{9,8},{10,11... | collective-permute-start | bytes 393224 | tf_op jit(solution)/shard_map/ppermute | solution.py:352
  81.3 6.8 %collective-permute-start.26 = (bf16[256,128]{1,0:T(8,128)(2,1)S(1)}, bf16[256,128]{1,0:T(8,128)(2,1)S(1)}, u32[]{:S(2)}, u32[]{:S(2)}) collective-permute-start(bf16[256,128]{1,0:T(8,128)(2,1)S(1)} %get-tuple-element.175), channel_id=1, source_target_pairs={{0,12},{1,13},{2,14},{3,15},{4,8},{5,9},{6,10},{7,11},{8,4},{9,5},... | collective-permute-start | bytes 196616 | tf_op jit(solution)/shard_map/ppermute | solution.py:355
  83.7 6.7 %collective-permute-start.27 = (bf16[256,128]{1,0:T(8,128)(2,1)S(1)}, bf16[256,128]{1,0:T(8,128)(2,1)S(1)}, u32[]{:S(2)}, u32[]{:S(2)}) collective-permute-start(bf16[256,128]{1,0:T(8,128)(2,1)S(1)} %get-tuple-element.176), channel_id=1, source_target_pairs={{0,8},{1,9},{2,10},{3,11},{4,12},{5,13},{6,14},{7,15},{8,0},{9,1},... | collective-permute-start | bytes 196616 | tf_op jit(solution)/shard_map/ppermute | solution.py:355
  83.7 6.7 %collective-permute-start.28 = (bf16[256,128]{1,0:T(8,128)(2,1)S(1)}, bf16[256,128]{1,0:T(8,128)(2,1)S(1)}, u32[]{:S(2)}, u32[]{:S(2)}) collective-permute-start(bf16[256,128]{1,0:T(8,128)(2,1)S(1)} %get-tuple-element.177), channel_id=1, source_target_pairs={{0,4},{1,5},{2,6},{3,7},{4,0},{5,1},{6,2},{7,3},{8,12},{9,13},{10,... | collective-permute-start | bytes 196616 | tf_op jit(solution)/shard_map/ppermute | solution.py:355
  91.8 2.0 %collective-permute-start.30 = (bf16[128,2048]{1,0:T(8,128)(2,1)S(1)}, bf16[128,2048]{1,0:T(8,128)(2,1)S(1)}, u32[]{:S(2)}, u32[]{:S(2)}) collective-permute-start(bf16[128,2048]{1,0:T(8,128)(2,1)S(1)} %get-tuple-element.192), channel_id=1, source_target_pairs={{0,1},{1,0},{2,3},{3,2},{4,5},{5,4},{6,7},{7,6},{8,9},{9,8},{10,11... | collective-permute-start | bytes 1572872 | tf_op jit(solution)/shard_map/ppermute | solution.py:352
  93.9 14.0 %collective-permute-start.38 = (bf16[128,2048]{1,0:T(8,128)(2,1)S(1)}, bf16[128,2048]{1,0:T(8,128)(2,1)S(1)}, u32[]{:S(2)}, u32[]{:S(2)}) collective-permute-start(bf16[128,2048]{1,0:T(8,128)(2,1)S(1)} %add_convert_fusion.1), channel_id=1, source_target_pairs={{0,2},{1,3},{2,0},{3,1},{4,6},{5,7},{6,4},{7,5},{8,10},{9,11},{10,... | collective-permute-start | bytes 1572872 | tf_op jit(solution)/shard_map/ppermute | solution.py:352
  94.5 5.0 %collective-permute-start.31 = (bf16[256,128]{1,0:T(8,128)(2,1)S(1)}, bf16[256,128]{1,0:T(8,128)(2,1)S(1)}, u32[]{:S(2)}, u32[]{:S(2)}) collective-permute-start(bf16[256,128]{1,0:T(8,128)(2,1)S(1)} %get-tuple-element.198), channel_id=1, source_target_pairs={{0,4},{1,5},{2,6},{3,7},{4,0},{5,1},{6,2},{7,3},{8,12},{9,13},{10,... | collective-permute-start | bytes 196616 | tf_op jit(solution)/shard_map/ppermute | solution.py:355
  95.1 7.4 %collective-permute-start.32 = (bf16[256,128]{1,0:T(8,128)(2,1)S(1)}, bf16[256,128]{1,0:T(8,128)(2,1)S(1)}, u32[]{:S(2)}, u32[]{:S(2)}) collective-permute-start(bf16[256,128]{1,0:T(8,128)(2,1)S(1)} %get-tuple-element.199), channel_id=1, source_target_pairs={{0,8},{1,9},{2,10},{3,11},{4,12},{5,13},{6,14},{7,15},{8,0},{9,1},... | collective-permute-start | bytes 196616 | tf_op jit(solution)/shard_map/ppermute | solution.py:355
  97.5 6.2 %collective-permute-start.33 = (bf16[256,128]{1,0:T(8,128)(2,1)S(1)}, bf16[256,128]{1,0:T(8,128)(2,1)S(1)}, u32[]{:S(2)}, u32[]{:S(2)}) collective-permute-start(bf16[256,128]{1,0:T(8,128)(2,1)S(1)} %get-tuple-element.200), channel_id=1, source_target_pairs={{0,12},{1,13},{2,14},{3,15},{4,8},{5,9},{6,10},{7,11},{8,4},{9,5},... | collective-permute-start | bytes 196616 | tf_op jit(solution)/shard_map/ppermute | solution.py:355
  104.9 1.4 %collective-permute-start.34 = (bf16[128,512]{1,0:T(8,128)(2,1)S(1)}, bf16[128,512]{1,0:T(8,128)(2,1)S(1)}, u32[]{:S(2)}, u32[]{:S(2)}) collective-permute-start(bf16[128,512]{1,0:T(8,128)(2,1)S(1)} %get-tuple-element.204), channel_id=1, source_target_pairs={{0,1},{1,0},{2,3},{3,2},{4,5},{5,4},{6,7},{7,6},{8,9},{9,8},{10,11... | collective-permute-start | bytes 393224 | tf_op jit(solution)/shard_map/ppermute | solution.py:352
  105.0 1.5 %collective-permute-start.35 = (bf16[128,512]{1,0:T(8,128)(2,1)S(1)}, bf16[128,512]{1,0:T(8,128)(2,1)S(1)}, u32[]{:S(2)}, u32[]{:S(2)}) collective-permute-start(bf16[128,512]{1,0:T(8,128)(2,1)S(1)} %get-tuple-element.205), channel_id=1, source_target_pairs={{0,1},{1,0},{2,3},{3,2},{4,5},{5,4},{6,7},{7,6},{8,9},{9,8},{10,11... | collective-permute-start | bytes 393224 | tf_op jit(solution)/shard_map/ppermute | solution.py:352
  105.5 1.3 %collective-permute-start.36 = (bf16[128,512]{1,0:T(8,128)(2,1)S(1)}, bf16[128,512]{1,0:T(8,128)(2,1)S(1)}, u32[]{:S(2)}, u32[]{:S(2)}) collective-permute-start(bf16[128,512]{1,0:T(8,128)(2,1)S(1)} %get-tuple-element.206), channel_id=1, source_target_pairs={{0,1},{1,0},{2,3},{3,2},{4,5},{5,4},{6,7},{7,6},{8,9},{9,8},{10,11... | collective-permute-start | bytes 393224 | tf_op jit(solution)/shard_map/ppermute | solution.py:352
  105.6 1.5 %collective-permute-start.37 = (bf16[128,512]{1,0:T(8,128)(2,1)S(1)}, bf16[128,512]{1,0:T(8,128)(2,1)S(1)}, u32[]{:S(2)}, u32[]{:S(2)}) collective-permute-start(bf16[128,512]{1,0:T(8,128)(2,1)S(1)} %get-tuple-element.207), channel_id=1, source_target_pairs={{0,1},{1,0},{2,3},{3,2},{4,5},{5,4},{6,7},{7,6},{8,9},{9,8},{10,11... | collective-permute-start | bytes 393224 | tf_op jit(solution)/shard_map/ppermute | solution.py:352

commit v6 on v5

--- a/solution.py
+++ b/solution.py
@@ -418,13 +418,13 @@
     near, far = to_plane(sent, 1), to_plane(sent, 2)
     from_x = to_place(late, 2)
     taps_other, out_other = to_group(taps_mine), to_group(out_near)
-    near, far, from_x, taps_other, out_half, out_other = stage(
-        (near, far, from_x, taps_other, out_half, out_other)
+    near, far, taps_other, out_half, out_other = stage(
+        (near, far, taps_other, out_half, out_other)
     )
 
     passed = to_plane(far, 1)
     other = small(
-        join_kernel, [shaped(4 * deep, wide)], to_group(near), to_group(far), flops=1073741824
+        join_kernel, [shaped(4 * deep, wide)], to_group(near), to_group(far), flops=1 << 30
     )[0]
     out_far = to_plane(out_half, 2)
     both = to_place(from_x, 1)

time: 109 us -> 108 us (level)
  waiting for transfers between devices: 49.8 us -> 47.1 us
  starting transfers between devices: 39.5 us -> 40.7 us
    ppermute x17, waiting for transfers between devices: 4.97 us -> 11.2 us  [to_place(): return lax.ppermute(block, 'seq', [(i, i ^ d) for i in range(devices)])]
    ppermute x6, waiting for transfers between devices: 9.39 us -> 4.03 us  [to_group(): return lax.ppermute(block, 'groups', [(0, 1), (1, 0)])]
    ppermute x15, waiting for transfers between devices: 33.4 us -> 29.8 us  [to_plane(): lax.ppermute(block, 'seq', [(i, i ^ s * PLANE) for i in range(devices)])]
    ppermute x6, starting transfers between devices: 6.71 us -> 8.02 us  [to_group(): return lax.ppermute(block, 'groups', [(0, 1), (1, 0)])]
where the time goes in v6:
time: 108 us; the launch traced here: 107 us
  waiting for transfers between devices  47.1 us (44%)
  starting transfers between devices  40.7 us (38%)
  Pallas kernels  17.1 us (16%)
  other arithmetic  1.14 us (1%)
  local copies, waits for them, and re-layouts  1.1 us (1%)
    ppermute x15, waiting for transfers between devices, to_plane(): lax.ppermute(block, 'seq', [(i, i ^ s * PLANE) for i in range(devices)])  29.8 us
    ppermute x15, starting transfers between devices, to_plane(): lax.ppermute(block, 'seq', [(i, i ^ s * PLANE) for i in range(devices)])  22.8 us
    pallas_call x14, Pallas kernels, call(): pl.pallas_call(kernel, out_shape=outs, in_specs=in_specs, out_specs=[pl.B...  17.1 us
    ppermute x17, waiting for transfers between devices, to_place(): return lax.ppermute(block, 'seq', [(i, i ^ d) for i in range(devices)])  11.2 us
    ppermute x6, starting transfers between devices, to_group(): return lax.ppermute(block, 'groups', [(0, 1), (1, 0)])  8.02 us
    ppermute x17, starting transfers between devices, to_place(): return lax.ppermute(block, 'seq', [(i, i ^ d) for i in range(devices)])  7.29 us
    ppermute x6, waiting for transfers between devices, to_group(): return lax.ppermute(block, 'groups', [(0, 1), (1, 0)])  4.03 us
    ppermute x1, starting transfers between devices, local(): taps_whole = lax.ppermute(taps_whole, ('groups', 'seq'), route)  2.59 us
  transfers between devices with their start and end apart: 39, of which 21 were waited for; matrix products, arithmetic and copies ran while one was open for 0% of the time, Pallas kernels for 13%

profile of v6, /device:TPU:0, one launch (start us, length us, event | category | flops | bytes accessed | tf_op | source)
XLA Modules:
  0.0 107.4 jit_solution(17529450860651161770)
XLA Ops:
  0.5 2.8 %shard_map.109 = (bf16[128,512]{1,0:T(8,128)(2,1)S(1)}, bf16[128,512]{1,0:T(8,128)(2,1)S(1)}, bf16[128,512]{1,0:T(8,128)(2,1)S(1)}, bf16[128,512]{1,0:T(8,128)(2...) custom-call(s32[3]{0:T(128)S(1)} %pad_add_fusion.pos, ...), custom_call_target="tpu_custom_call" | custom-call | tf_op jit(solution)/shard_map/pallas_call | solution.py:60
  3.3 2.6 %collective-permute-start.5 = (bf16[160,1024]{1,0:T(8,128)(2,1)}, bf16[160,1024]{1,0:T(8,128)(2,1)S(1)}, u32[]{:S(2)}, u32[]{:S(2)}) collective-permute-start(bf16[160,1024]{1,0:T(8,128)(2,1)} %get-tuple-element.111), channel_id=1, source_target_pairs={{0,4},{1,5},{2,6},{3,7},{4,0},{5,1},{6,2},{7,3},{8,12},{9,13},{10,... | collective-permute-start | bytes 983048 | tf_op jit(solution)/shard_map/ppermute | solution.py:355
  6.2 1.5 %collective-permute-start.1 = (bf16[128,512]{1,0:T(8,128)(2,1)S(1)}, bf16[128,512]{1,0:T(8,128)(2,1)S(1)}, u32[]{:S(2)}, u32[]{:S(2)}) collective-permute-start(bf16[128,512]{1,0:T(8,128)(2,1)S(1)} %get-tuple-element.108), channel_id=1, source_target_pairs={{0,2},{1,3},{2,0},{3,1},{4,6},{5,7},{6,4},{7,5},{8,10},{9,11},{10,... | collective-permute-start | bytes 393224 | tf_op jit(solution)/shard_map/ppermute | solution.py:352
  7.8 2.6 %collective-permute-start.3 = (bf16[128,512]{1,0:T(8,128)(2,1)S(1)}, bf16[128,512]{1,0:T(8,128)(2,1)S(1)}, u32[]{:S(2)}, u32[]{:S(2)}) collective-permute-start(bf16[128,512]{1,0:T(8,128)(2,1)S(1)} %get-tuple-element.110), channel_id=1, source_target_pairs={{0,8},{1,9},{2,10},{3,11},{4,12},{5,13},{6,14},{7,15},{8,0},{9,1},... | collective-permute-start | bytes 393224 | tf_op jit(solution)/shard_map/ppermute | solution.py:406
  10.4 1.0 copy-done.3
  11.5 0.9 shard_map.112
  12.9 1.1 %collective-permute-done.2.refs_3_ = bf16[128,512]{1,0:T(8,128)(2,1)S(1)} collective-permute-done((bf16[128,512]{1,0:T(8,128)(2,1)S(1)}, bf16[128,512]{1,0:T(8,128)(2,1)S(1)}, u32[]{:S(2)}, u32[]{:S(2)}) %collective-permute-start.2) | collective-permute-done | bytes 131104 | tf_op jit(solution)/shard_map/ppermute | solution.py:352
  14.6 2.0 %collective-permute-done.3.whole = bf16[128,512]{1,0:T(8,128)(2,1)S(1)} collective-permute-done((bf16[128,512]{1,0:T(8,128)(2,1)S(1)}, bf16[128,512]{1,0:T(8,128)(2,1)S(1)}, u32[]{:S(2)}, u32[]{:S(2)}) %collective-permute-start.3) | collective-permute-done | bytes 131104 | tf_op jit(solution)/shard_map/ppermute | solution.py:406
  16.6 0.7 collective-permute-done.5.near
  17.4 1.7 %collective-permute-start.6 = (bf16[128,2048]{1,0:T(8,128)(2,1)S(1)}, bf16[128,2048]{1,0:T(8,128)(2,1)S(1)}, u32[]{:S(2)}, u32[]{:S(2)}) collective-permute-start(bf16[128,2048]{1,0:T(8,128)(2,1)S(1)} %copy-done.2), channel_id=1, source_target_pairs={{0,2},{1,3},{2,0},{3,1},{4,6},{5,7},{6,4},{7,5},{8,10},{9,11},{10,... | collective-permute-start | bytes 1572872 | tf_op jit(solution)/shard_map/ppermute | solution.py:352
  19.0 2.5 %collective-permute-start.8 = (bf16[256,512]{1,0:T(8,128)(2,1)S(1)}, bf16[256,512]{1,0:T(8,128)(2,1)S(1)}, u32[]{:S(2)}, u32[]{:S(2)}) collective-permute-start(bf16[256,512]{1,0:T(8,128)(2,1)S(1)} %shard_map.111), channel_id=1, source_target_pairs={{0,8},{1,9},{2,10},{3,11},{4,12},{5,13},{6,14},{7,15},{8,0},{9,1},... | collective-permute-start | bytes 786440 | tf_op jit(solution)/shard_map/ppermute | solution.py:355
  21.6 1.6 %collective-permute-start.7 = (bf16[256,512]{1,0:T(8,128)(2,1)S(1)}, bf16[256,512]{1,0:T(8,128)(2,1)S(1)}, u32[]{:S(2)}, u32[]{:S(2)}) collective-permute-start(bf16[256,512]{1,0:T(8,128)(2,1)S(1)} %shard_map.111), channel_id=1, source_target_pairs={{0,4},{1,5},{2,6},{3,7},{4,0},{5,1},{6,2},{7,3},{8,12},{9,13},{10,... | collective-permute-start | bytes 786440 | tf_op jit(solution)/shard_map/ppermute | solution.py:355
  23.8 1.6 %collective-permute-start.10 = (bf16[128,1024]{1,0:T(8,128)(2,1)S(1)}, bf16[128,1024]{1,0:T(8,128)(2,1)S(1)}, u32[]{:S(2)}, u32[]{:S(2)}) collective-permute-start(bf16[128,1024]{1,0:T(8,128)(2,1)S(1)} %get-tuple-element.122.refs_7_), channel_id=1, source_target_pairs={{0,16},{16,0},{1,17},{17,1},{2,18},{18,2},{3,19},{19,3},{4,20},{20... | collective-permute-start | bytes 786440 | tf_op jit(solution)/shard_map/ppermute | solution.py:358
  25.9 5.3 %collective-permute-done.6.from_x = bf16[128,2048]{1,0:T(8,128)(2,1)S(1)} collective-permute-done((bf16[128,2048]{1,0:T(8,128)(2,1)S(1)}, bf16[128,2048]{1,0:T(8,128)(2,1)S(1)}, u32[]{:S(2)}, u32[]{:S(2)}) %collective-permute-start.6) | collective-permute-done | bytes 524320 | tf_op jit(solution)/shard_map/ppermute | solution.py:352
  31.1 4.0 %collective-permute-done.9.other = bf16[192,512]{1,0:T(8,128)(2,1)S(1)} collective-permute-done((bf16[192,512]{1,0:T(8,128)(2,1)S(1)}, bf16[192,512]{1,0:T(8,128)(2,1)S(1)}, u32[]{:S(2)}, u32[]{:S(2)}) %collective-permute-start.9) | collective-permute-done | bytes 196640 | tf_op jit(solution)/shard_map/ppermute | solution.py:358
  35.2 1.5 %collective-permute-start.19 = (bf16[128,1024]{1,0:T(8,128)(2,1)}, bf16[128,1024]{1,0:T(8,128)(2,1)S(1)}, u32[]{:S(2)}, u32[]{:S(2)}) collective-permute-start(bf16[128,1024]{1,0:T(8,128)(2,1)} %get-tuple-element.148), channel_id=1, source_target_pairs={{0,8},{1,9},{2,10},{3,11},{4,12},{5,13},{6,14},{7,15},{8,0},{9,1},... | collective-permute-start | bytes 786440 | tf_op jit(solution)/shard_map/ppermute | solution.py:355
  36.7 1.2 %collective-permute-start.11 = (bf16[256,512]{1,0:T(8,128)(2,1)S(1)}, bf16[256,512]{1,0:T(8,128)(2,1)S(1)}, u32[]{:S(2)}, u32[]{:S(2)}) collective-permute-start(bf16[256,512]{1,0:T(8,128)(2,1)S(1)} %collective-permute-done.7.refs_0_), channel_id=1, source_target_pairs={{0,16},{16,0},{1,17},{17,1},{2,18},{18,2},{3,19},{19,3},{4,20},{20... | collective-permute-start | bytes 786440 | tf_op jit(solution)/shard_map/ppermute | solution.py:358
  37.9 0.8 collective-permute-start.12
  38.7 1.2 %collective-permute-start.13 = (bf16[256,512]{1,0:T(8,128)(2,1)S(1)}, bf16[256,512]{1,0:T(8,128)(2,1)S(1)}, u32[]{:S(2)}, u32[]{:S(2)}) collective-permute-start(bf16[256,512]{1,0:T(8,128)(2,1)S(1)} %collective-permute-done.8.refs_1_), channel_id=1, source_target_pairs={{0,4},{1,5},{2,6},{3,7},{4,0},{5,1},{6,2},{7,3},{8,12},{9,13},{10,... | collective-permute-start | bytes 786440 | tf_op jit(solution)/shard_map/ppermute | solution.py:355
  39.9 0.7 shard_map.115
  40.6 7.7 %collective-permute-done.19.refs_0_ = bf16[128,1024]{1,0:T(8,128)(2,1)S(1)} collective-permute-done((bf16[128,1024]{1,0:T(8,128)(2,1)}, bf16[128,1024]{1,0:T(8,128)(2,1)S(1)}, u32[]{:S(2)}, u32[]{:S(2)}) %collective-permute-start.19) | collective-permute-done | bytes 262176 | tf_op jit(solution)/shard_map/ppermute | solution.py:355
  48.3 0.6 shard_map.114.refs_3_
  48.9 0.7 collective-permute-done.13.refs_2_
  49.6 2.2 %collective-permute-start.18 = (bf16[256,512]{1,0:T(8,128)(2,1)S(1)}, bf16[256,512]{1,0:T(8,128)(2,1)S(1)}, u32[]{:S(2)}, u32[]{:S(2)}) collective-permute-start(bf16[256,512]{1,0:T(8,128)(2,1)S(1)} %collective-permute-done.13.refs_2_), channel_id=1, source_target_pairs={{0,16},{16,0},{1,17},{17,1},{2,18},{18,2},{3,19},{19,3},{4,20},{20... | collective-permute-start | bytes 786440 | tf_op jit(solution)/shard_map/ppermute | solution.py:358
  53.3 3.6 %collective-permute-done.20.refs_1_ = bf16[128,1024]{1,0:T(8,128)(2,1)S(1)} collective-permute-done((bf16[128,1024]{1,0:T(8,128)(2,1)S(1)}, bf16[128,1024]{1,0:T(8,128)(2,1)S(1)}, u32[]{:S(2)}, u32[]{:S(2)}) %collective-permute-start.20) | collective-permute-done | bytes 262176 | tf_op jit(solution)/shard_map/ppermute | solution.py:355
  57.6 0.6 collective-permute-done.16.refs_2_
  58.2 2.0 %shard_map.117 = (bf16[512,128]{1,0:T(8,128)(2,1)S(1)}, bf16[512,128]{1,0:T(8,128)(2,1)S(1)}, bf16[512,128]{1,0:T(8,128)(2,1)S(1)}, bf16[512,128]{1,0:T(8,128)(2,1)S(1)}) custom-call(s32[3]{0:T(128)S(1)} %pad_add_fusion.pos, bf16[128,2048]{1,0:T(8,128)(2,1)S(1)} %copy-done.2, bf16[128,2048]{1,0:T(8,128)(2,1)S(1)} %collective-permute-done.4.core, ...), custom_call_target="tpu_custom_call" | custom-call | flops 1073741824 | bytes 4718592 | tf_op jit(solution)/shard_map/pallas_call | solution.py:60
  60.3 2.0 %collective-permute-start.21 = (bf16[512,128]{1,0:T(8,128)(2,1)S(1)}, bf16[512,128]{1,0:T(8,128)(2,1)S(1)}, u32[]{:S(2)}, u32[]{:S(2)}) collective-permute-start(bf16[512,128]{1,0:T(8,128)(2,1)S(1)} %get-tuple-element.150), channel_id=1, source_target_pairs={{0,12},{1,13},{2,14},{3,15},{4,8},{5,9},{6,10},{7,11},{8,4},{9,5},... | collective-permute-start | bytes 393224 | tf_op jit(solution)/shard_map/ppermute | solution.py:355
  62.3 1.7 %collective-permute-start.22 = (bf16[512,128]{1,0:T(8,128)(2,1)S(1)}, bf16[512,128]{1,0:T(8,128)(2,1)S(1)}, u32[]{:S(2)}, u32[]{:S(2)}) collective-permute-start(bf16[512,128]{1,0:T(8,128)(2,1)S(1)} %get-tuple-element.151), channel_id=1, source_target_pairs={{0,8},{1,9},{2,10},{3,11},{4,12},{5,13},{6,14},{7,15},{8,0},{9,1},... | collective-permute-start | bytes 393224 | tf_op jit(solution)/shard_map/ppermute | solution.py:355
  63.9 0.8 collective-permute-start.23
  64.8 1.7 %collective-permute-start.24 = (bf16[256,1024]{1,0:T(8,128)(2,1)S(1)}, bf16[256,1024]{1,0:T(8,128)(2,1)S(1)}, u32[]{:S(2)}, u32[]{:S(2)}) collective-permute-start(bf16[256,1024]{1,0:T(8,128)(2,1)S(1)} %shard_map.118.refs_8_), channel_id=1, source_target_pairs={{0,16},{16,0},{1,17},{17,1},{2,18},{18,2},{3,19},{19,3},{4,20},{20... | collective-permute-start | bytes 1572872 | tf_op jit(solution)/shard_map/ppermute | solution.py:358
  67.0 1.6 %shard_map.119.refs_6_ = bf16[17,256,128]{2,1,0:T(8,128)(2,1)S(1)} custom-call(s32[3]{0:T(128)S(1)} %pad_add_fusion.pos, bf16[4,128,128]{2,1,0:T(8,128)(2,1)S(1)} %get-tuple-element.154.refs_0_, bf16[8,128,128]{2,1,0:T(8,128)(2,1)S(1)} %collective-permute-done.15.refs_1_.refs_5_, bf16[4,128,128]{2,1,0:T(8,128)(2,1)S(1)} %collective-permute-done.16.refs_2_, ...), custom_call_target="tpu_custom_call" | custom-call | flops 536870912 | bytes 4259840 | tf_op jit(solution)/shard_map/pallas_call | solution.py:60
  68.6 8.0 %collective-permute-done.22.refs_2_ = bf16[512,128]{1,0:T(8,128)(2,1)S(1)} collective-permute-done((bf16[512,128]{1,0:T(8,128)(2,1)S(1)}, bf16[512,128]{1,0:T(8,128)(2,1)S(1)}, u32[]{:S(2)}, u32[]{:S(2)}) %collective-permute-start.22) | collective-permute-done | bytes 131104 | tf_op jit(solution)/shard_map/ppermute | solution.py:355
  76.6 3.0 %shard_map.120 = (bf16[256,128]{1,0:T(8,128)(2,1)S(1)}, bf16[256,128]{1,0:T(8,128)(2,1)S(1)}, bf16[256,128]{1,0:T(8,128)(2,1)S(1)}, bf16[256,128]{1,0:T(8,128)(2...) custom-call(s32[3]{0:T(128)S(1)} %pad_add_fusion.pos, ...), custom_call_target="tpu_custom_call" | custom-call | flops 4294967296 | bytes 7176192 | tf_op jit(solution)/shard_map/pallas_call | solution.py:60
  79.8 1.7 %collective-permute-start.26 = (bf16[256,128]{1,0:T(8,128)(2,1)S(1)}, bf16[256,128]{1,0:T(8,128)(2,1)S(1)}, u32[]{:S(2)}, u32[]{:S(2)}) collective-permute-start(bf16[256,128]{1,0:T(8,128)(2,1)S(1)} %get-tuple-element.173), channel_id=1, source_target_pairs={{0,12},{1,13},{2,14},{3,15},{4,8},{5,9},{6,10},{7,11},{8,4},{9,5},... | collective-permute-start | bytes 196616 | tf_op jit(solution)/shard_map/ppermute | solution.py:355
  81.4 2.8 %collective-permute-start.28 = (bf16[256,128]{1,0:T(8,128)(2,1)S(1)}, bf16[256,128]{1,0:T(8,128)(2,1)S(1)}, u32[]{:S(2)}, u32[]{:S(2)}) collective-permute-start(bf16[256,128]{1,0:T(8,128)(2,1)S(1)} %get-tuple-element.175), channel_id=1, source_target_pairs={{0,4},{1,5},{2,6},{3,7},{4,0},{5,1},{6,2},{7,3},{8,12},{9,13},{10,... | collective-permute-start | bytes 196616 | tf_op jit(solution)/shard_map/ppermute | solution.py:355
  84.2 2.4 %collective-permute-done.26.refs_3_ = bf16[256,128]{1,0:T(8,128)(2,1)S(1)} collective-permute-done((bf16[256,128]{1,0:T(8,128)(2,1)S(1)}, bf16[256,128]{1,0:T(8,128)(2,1)S(1)}, u32[]{:S(2)}, u32[]{:S(2)}) %collective-permute-start.26) | collective-permute-done | bytes 65568 | tf_op jit(solution)/shard_map/ppermute | solution.py:355
  86.6 2.3 %collective-permute-done.27.refs_2_ = bf16[256,128]{1,0:T(8,128)(2,1)S(1)} collective-permute-done((bf16[256,128]{1,0:T(8,128)(2,1)S(1)}, bf16[256,128]{1,0:T(8,128)(2,1)S(1)}, u32[]{:S(2)}, u32[]{:S(2)}) %collective-permute-start.27) | collective-permute-done | bytes 65568 | tf_op jit(solution)/shard_map/ppermute | solution.py:355
  88.9 1.4 %shard_map.121 = (f32[128,2048]{1,0:T(8,128)S(1)}, bf16[128,2048]{1,0:T(8,128)(2,1)S(1)}, bf16[512,2048]{1,0:T(8,128)(2,1)S(1)}) custom-call(s32[3]{0:T(128)S(1)} %pad_add_fusion.pos, bf16[256,128]{1,0:T(8,128)(2,1)S(1)} %get-tuple-element.182.refs_0_, bf16[256,128]{1,0:T(8,128)(2,1)S(1)} %collective-permute-done.28.refs_1_, ...), custom_call_target="tpu_custom_call" | custom-call | flops 536870912 | bytes 6422528 | tf_op jit(solution)/shard_map/pallas_call | solution.py:60
  90.4 1.9 %collective-permute-done.30 = bf16[128,2048]{1,0:T(8,128)(2,1)S(1)} collective-permute-done((bf16[128,2048]{1,0:T(8,128)(2,1)S(1)}, bf16[128,2048]{1,0:T(8,128)(2,1)S(1)}, u32[]{:S(2)}, u32[]{:S(2)}) %collective-permute-start.30) | collective-permute-done | bytes 524320 | tf_op jit(solution)/shard_map/ppermute | solution.py:352
  92.4 0.6 collective-permute-start.38
  93.2 2.3 %collective-permute-start.32 = (bf16[256,128]{1,0:T(8,128)(2,1)S(1)}, bf16[256,128]{1,0:T(8,128)(2,1)S(1)}, u32[]{:S(2)}, u32[]{:S(2)}) collective-permute-start(bf16[256,128]{1,0:T(8,128)(2,1)S(1)} %get-tuple-element.197), channel_id=1, source_target_pairs={{0,8},{1,9},{2,10},{3,11},{4,12},{5,13},{6,14},{7,15},{8,0},{9,1},... | collective-permute-start | bytes 196616 | tf_op jit(solution)/shard_map/ppermute | solution.py:355
  95.6 1.8 %collective-permute-start.33 = (bf16[256,128]{1,0:T(8,128)(2,1)S(1)}, bf16[256,128]{1,0:T(8,128)(2,1)S(1)}, u32[]{:S(2)}, u32[]{:S(2)}) collective-permute-start(bf16[256,128]{1,0:T(8,128)(2,1)S(1)} %get-tuple-element.198), channel_id=1, source_target_pairs={{0,12},{1,13},{2,14},{3,15},{4,8},{5,9},{6,10},{7,11},{8,4},{9,5},... | collective-permute-start | bytes 196616 | tf_op jit(solution)/shard_map/ppermute | solution.py:355
  97.8 3.0 %collective-permute-done.32.refs_2_ = bf16[256,128]{1,0:T(8,128)(2,1)S(1)} collective-permute-done((bf16[256,128]{1,0:T(8,128)(2,1)S(1)}, bf16[256,128]{1,0:T(8,128)(2,1)S(1)}, u32[]{:S(2)}, u32[]{:S(2)}) %collective-permute-start.32) | collective-permute-done | bytes 65568 | tf_op jit(solution)/shard_map/ppermute | solution.py:355
  100.7 1.1 collective-permute-done.33.refs_3_
  101.8 1.3 %shard_map.122 = (f32[128,2048]{1,0:T(8,128)S(1)}, bf16[128,512]{1,0:T(8,128)(2,1)S(1)}, bf16[128,512]{1,0:T(8,128)(2,1)S(1)}, bf16[128,512]{1,0:T(8,128)(2,1)S(1)}, bf16[128,512]{1,0:T(8,128)(2,1)S(1)}) custom-call(s32[3]{0:T(128)S(1)} %pad_add_fusion.pos, bf16[256,128]{1,0:T(8,128)(2,1)S(1)} %get-tuple-element.195.refs_0_, ...), custom_call_target="tpu_custom_call" | custom-call | tf_op jit(solution)/shard_map/pallas_call | solution.py:60
  105.1 1.3 %collective-permute-done.38 = bf16[128,2048]{1,0:T(8,128)(2,1)S(1)} collective-permute-done((bf16[128,2048]{1,0:T(8,128)(2,1)S(1)}, bf16[128,2048]{1,0:T(8,128)(2,1)S(1)}, u32[]{:S(2)}, u32[]{:S(2)}) %collective-permute-start.38) | collective-permute-done | bytes 524320 | tf_op jit(solution)/shard_map/ppermute | solution.py:352
  106.4 1.0 add_convert_fusion
  (66 shorter events, 8.8 us)
Async XLA Ops:
  0.0 17.4 %copy-start.2 = (bf16[128,2048]{1,0:T(8,128)(2,1)S(1)}, bf16[128,2048]{1,0:T(8,128)(2,1)}, u32[]{:S(2)}) copy-start(bf16[128,2048]{1,0:T(8,128)(2,1)} %x.1) | copy-start | bytes 1572868
  0.0 17.4 %collective-permute-start.4 = (bf16[128,2048]{1,0:T(8,128)(2,1)}, bf16[128,2048]{1,0:T(8,128)(2,1)S(1)}, u32[]{:S(2)}, u32[]{:S(2)}) collective-permute-start(bf16[128,2048]{1,0:T(8,128)(2,1)} %x.1), channel_id=1, source_target_pairs={{0,1},{1,0},{2,3},{3,2},{4,5},{5,4},{6,7},{7,6},{8,9},{9,8},{10,11... | collective-permute-start | bytes 1572872 | tf_op jit(solution)/shard_map/ppermute | solution.py:352
  3.3 14.0 %collective-permute-start.5 = (bf16[160,1024]{1,0:T(8,128)(2,1)}, bf16[160,1024]{1,0:T(8,128)(2,1)S(1)}, u32[]{:S(2)}, u32[]{:S(2)}) collective-permute-start(bf16[160,1024]{1,0:T(8,128)(2,1)} %get-tuple-element.111), channel_id=1, source_target_pairs={{0,4},{1,5},{2,6},{3,7},{4,0},{5,1},{6,2},{7,3},{8,12},{9,13},{10,... | collective-permute-start | bytes 983048 | tf_op jit(solution)/shard_map/ppermute | solution.py:355
  6.0 1.9 %collective-permute-start = (bf16[128,512]{1,0:T(8,128)(2,1)S(1)}, bf16[128,512]{1,0:T(8,128)(2,1)S(1)}, u32[]{:S(2)}, u32[]{:S(2)}) collective-permute-start(bf16[128,512]{1,0:T(8,128)(2,1)S(1)} %get-tuple-element.107), channel_id=1, source_target_pairs={{0,1},{1,0},{2,3},{3,2},{4,5},{5,4},{6,7},{7,6},{8,9},{9,8},{10,11... | collective-permute-start | bytes 393224 | tf_op jit(solution)/shard_map/ppermute | solution.py:352
  6.2 6.7 %collective-permute-start.1 = (bf16[128,512]{1,0:T(8,128)(2,1)S(1)}, bf16[128,512]{1,0:T(8,128)(2,1)S(1)}, u32[]{:S(2)}, u32[]{:S(2)}) collective-permute-start(bf16[128,512]{1,0:T(8,128)(2,1)S(1)} %get-tuple-element.108), channel_id=1, source_target_pairs={{0,2},{1,3},{2,0},{3,1},{4,6},{5,7},{6,4},{7,5},{8,10},{9,11},{10,... | collective-permute-start | bytes 393224 | tf_op jit(solution)/shard_map/ppermute | solution.py:352
  7.7 6.4 %collective-permute-start.2 = (bf16[128,512]{1,0:T(8,128)(2,1)S(1)}, bf16[128,512]{1,0:T(8,128)(2,1)S(1)}, u32[]{:S(2)}, u32[]{:S(2)}) collective-permute-start(bf16[128,512]{1,0:T(8,128)(2,1)S(1)} %get-tuple-element.109), channel_id=1, source_target_pairs={{0,3},{1,2},{2,1},{3,0},{4,7},{5,6},{6,5},{7,4},{8,11},{9,10},{10,... | collective-permute-start | bytes 393224 | tf_op jit(solution)/shard_map/ppermute | solution.py:352
  7.8 8.8 %collective-permute-start.3 = (bf16[128,512]{1,0:T(8,128)(2,1)S(1)}, bf16[128,512]{1,0:T(8,128)(2,1)S(1)}, u32[]{:S(2)}, u32[]{:S(2)}) collective-permute-start(bf16[128,512]{1,0:T(8,128)(2,1)S(1)} %get-tuple-element.110), channel_id=1, source_target_pairs={{0,8},{1,9},{2,10},{3,11},{4,12},{5,13},{6,14},{7,15},{8,0},{9,1},... | collective-permute-start | bytes 393224 | tf_op jit(solution)/shard_map/ppermute | solution.py:406
  10.4 1.0 copy-start.3
  17.4 13.8 %collective-permute-start.6 = (bf16[128,2048]{1,0:T(8,128)(2,1)S(1)}, bf16[128,2048]{1,0:T(8,128)(2,1)S(1)}, u32[]{:S(2)}, u32[]{:S(2)}) collective-permute-start(bf16[128,2048]{1,0:T(8,128)(2,1)S(1)} %copy-done.2), channel_id=1, source_target_pairs={{0,2},{1,3},{2,0},{3,1},{4,6},{5,7},{6,4},{7,5},{8,10},{9,11},{10,... | collective-permute-start | bytes 1572872 | tf_op jit(solution)/shard_map/ppermute | solution.py:352
  19.0 16.1 %collective-permute-start.8 = (bf16[256,512]{1,0:T(8,128)(2,1)S(1)}, bf16[256,512]{1,0:T(8,128)(2,1)S(1)}, u32[]{:S(2)}, u32[]{:S(2)}) collective-permute-start(bf16[256,512]{1,0:T(8,128)(2,1)S(1)} %shard_map.111), channel_id=1, source_target_pairs={{0,8},{1,9},{2,10},{3,11},{4,12},{5,13},{6,14},{7,15},{8,0},{9,1},... | collective-permute-start | bytes 786440 | tf_op jit(solution)/shard_map/ppermute | solution.py:355
  21.6 13.6 %collective-permute-start.7 = (bf16[256,512]{1,0:T(8,128)(2,1)S(1)}, bf16[256,512]{1,0:T(8,128)(2,1)S(1)}, u32[]{:S(2)}, u32[]{:S(2)}) collective-permute-start(bf16[256,512]{1,0:T(8,128)(2,1)S(1)} %shard_map.111), channel_id=1, source_target_pairs={{0,4},{1,5},{2,6},{3,7},{4,0},{5,1},{6,2},{7,3},{8,12},{9,13},{10,... | collective-permute-start | bytes 786440 | tf_op jit(solution)/shard_map/ppermute | solution.py:355
  23.8 11.4 %collective-permute-start.10 = (bf16[128,1024]{1,0:T(8,128)(2,1)S(1)}, bf16[128,1024]{1,0:T(8,128)(2,1)S(1)}, u32[]{:S(2)}, u32[]{:S(2)}) collective-permute-start(bf16[128,1024]{1,0:T(8,128)(2,1)S(1)} %get-tuple-element.122.refs_7_), channel_id=1, source_target_pairs={{0,16},{16,0},{1,17},{17,1},{2,18},{18,2},{3,19},{19,3},{4,20},{20... | collective-permute-start | bytes 786440 | tf_op jit(solution)/shard_map/ppermute | solution.py:358
  25.4 9.8 %collective-permute-start.9 = (bf16[192,512]{1,0:T(8,128)(2,1)S(1)}, bf16[192,512]{1,0:T(8,128)(2,1)S(1)}, u32[]{:S(2)}, u32[]{:S(2)}) collective-permute-start(bf16[192,512]{1,0:T(8,128)(2,1)S(1)} %get-tuple-element.120.mine), channel_id=1, source_target_pairs={{0,16},{16,0},{1,17},{17,1},{2,18},{18,2},{3,19},{19,3},{4,20},{20... | collective-permute-start | bytes 589832 | tf_op jit(solution)/shard_map/ppermute | solution.py:358
  31.1 18.4 %collective-permute-start.14 = (bf16[128,2048]{1,0:T(8,128)(2,1)S(1)}, bf16[128,2048]{1,0:T(8,128)(2,1)S(1)}, u32[]{:S(2)}, u32[]{:S(2)}) collective-permute-start(bf16[128,2048]{1,0:T(8,128)(2,1)S(1)} %collective-permute-done.6.from_x), channel_id=1, source_target_pairs={{0,1},{1,0},{2,3},{3,2},{4,5},{5,4},{6,7},{7,6},{8,9},{9,8},{10,11... | collective-permute-start | bytes 1572872 | tf_op jit(solution)/shard_map/ppermute | solution.py:352
  35.2 13.1 %collective-permute-start.19 = (bf16[128,1024]{1,0:T(8,128)(2,1)}, bf16[128,1024]{1,0:T(8,128)(2,1)S(1)}, u32[]{:S(2)}, u32[]{:S(2)}) collective-permute-start(bf16[128,1024]{1,0:T(8,128)(2,1)} %get-tuple-element.148), channel_id=1, source_target_pairs={{0,8},{1,9},{2,10},{3,11},{4,12},{5,13},{6,14},{7,15},{8,0},{9,1},... | collective-permute-start | bytes 786440 | tf_op jit(solution)/shard_map/ppermute | solution.py:355
  36.7 11.6 %collective-permute-start.11 = (bf16[256,512]{1,0:T(8,128)(2,1)S(1)}, bf16[256,512]{1,0:T(8,128)(2,1)S(1)}, u32[]{:S(2)}, u32[]{:S(2)}) collective-permute-start(bf16[256,512]{1,0:T(8,128)(2,1)S(1)} %collective-permute-done.7.refs_0_), channel_id=1, source_target_pairs={{0,16},{16,0},{1,17},{17,1},{2,18},{18,2},{3,19},{19,3},{4,20},{20... | collective-permute-start | bytes 786440 | tf_op jit(solution)/shard_map/ppermute | solution.py:358
  37.9 10.4 %collective-permute-start.12 = (bf16[256,512]{1,0:T(8,128)(2,1)S(1)}, bf16[256,512]{1,0:T(8,128)(2,1)S(1)}, u32[]{:S(2)}, u32[]{:S(2)}) collective-permute-start(bf16[256,512]{1,0:T(8,128)(2,1)S(1)} %collective-permute-done.8.refs_1_), channel_id=1, source_target_pairs={{0,16},{16,0},{1,17},{17,1},{2,18},{18,2},{3,19},{19,3},{4,20},{20... | collective-permute-start | bytes 786440 | tf_op jit(solution)/shard_map/ppermute | solution.py:358
  38.7 10.9 %collective-permute-start.13 = (bf16[256,512]{1,0:T(8,128)(2,1)S(1)}, bf16[256,512]{1,0:T(8,128)(2,1)S(1)}, u32[]{:S(2)}, u32[]{:S(2)}) collective-permute-start(bf16[256,512]{1,0:T(8,128)(2,1)S(1)} %collective-permute-done.8.refs_1_), channel_id=1, source_target_pairs={{0,4},{1,5},{2,6},{3,7},{4,0},{5,1},{6,2},{7,3},{8,12},{9,13},{10,... | collective-permute-start | bytes 786440 | tf_op jit(solution)/shard_map/ppermute | solution.py:355
  48.2 10.0 %collective-permute-start.15 = (bf16[8,128,128]{2,1,0:T(8,128)(2,1)S(1)}, bf16[8,128,128]{2,1,0:T(8,128)(2,1)S(1)}, u32[]{:S(2)}, u32[]{:S(2)}) collective-permute-start(bf16[8,128,128]{2,1,0:T(8,128)(2,1)S(1)} %get-tuple-element.132), channel_id=1, source_target_pairs={{0,1},{1,0},{2,3},{3,2},{4,5},{5,4},{6,7},{7,6},{8,9},{9,8},{10,11... | collective-permute-start | bytes 786440 | tf_op jit(solution)/shard_map/ppermute | solution.py:352
  48.3 8.7 %collective-permute-start.20 = (bf16[128,1024]{1,0:T(8,128)(2,1)S(1)}, bf16[128,1024]{1,0:T(8,128)(2,1)S(1)}, u32[]{:S(2)}, u32[]{:S(2)}) collective-permute-start(bf16[128,1024]{1,0:T(8,128)(2,1)S(1)} %collective-permute-done.19.refs_0_), channel_id=1, source_target_pairs={{0,4},{1,5},{2,6},{3,7},{4,0},{5,1},{6,2},{7,3},{8,12},{9,13},{10,... | collective-permute-start | bytes 786440 | tf_op jit(solution)/shard_map/ppermute | solution.py:355
  49.6 8.6 %collective-permute-start.18 = (bf16[256,512]{1,0:T(8,128)(2,1)S(1)}, bf16[256,512]{1,0:T(8,128)(2,1)S(1)}, u32[]{:S(2)}, u32[]{:S(2)}) collective-permute-start(bf16[256,512]{1,0:T(8,128)(2,1)S(1)} %collective-permute-done.13.refs_2_), channel_id=1, source_target_pairs={{0,16},{16,0},{1,17},{17,1},{2,18},{18,2},{3,19},{19,3},{4,20},{20... | collective-permute-start | bytes 786440 | tf_op jit(solution)/shard_map/ppermute | solution.py:358
  51.8 6.4 %collective-permute-start.16 = (bf16[4,128,128]{2,1,0:T(8,128)(2,1)S(1)}, bf16[4,128,128]{2,1,0:T(8,128)(2,1)S(1)}, u32[]{:S(2)}, u32[]{:S(2)}) collective-permute-start(bf16[4,128,128]{2,1,0:T(8,128)(2,1)S(1)} %get-tuple-element.133), channel_id=1, source_target_pairs={{0,2},{1,3},{2,0},{3,1},{4,6},{5,7},{6,4},{7,5},{8,10},{9,11},{10,... | collective-permute-start | bytes 393224 | tf_op jit(solution)/shard_map/ppermute | solution.py:352
  52.4 5.8 %collective-permute-start.17 = (bf16[4,128,128]{2,1,0:T(8,128)(2,1)S(1)}, bf16[4,128,128]{2,1,0:T(8,128)(2,1)S(1)}, u32[]{:S(2)}, u32[]{:S(2)}) collective-permute-start(bf16[4,128,128]{2,1,0:T(8,128)(2,1)S(1)} %get-tuple-element.134), channel_id=1, source_target_pairs={{0,3},{1,2},{2,1},{3,0},{4,7},{5,6},{6,5},{7,4},{8,11},{9,10},{10,... | collective-permute-start | bytes 393224 | tf_op jit(solution)/shard_map/ppermute | solution.py:352
  57.6 9.4 %copy-start = (bf16[17,256,256]{2,1,0:T(8,128)(2,1)S(1)}, bf16[17,256,256]{2,1,0:T(8,128)(2,1)}, u32[]{:S(2)}) copy-start(bf16[17,256,256]{2,1,0:T(8,128)(2,1)} %constant.45.clone.refs_5_.refs_9_) | copy-start | bytes 6684676
  57.6 9.4 %copy-start.4 = (bf16[512,256]{1,0:T(8,128)(2,1)S(1)}, bf16[512,256]{1,0:T(8,128)(2,1)}, u32[]{:S(2)}) copy-start(bf16[512,256]{1,0:T(8,128)(2,1)} %constant.43.clone.refs_4_.refs_7_) | copy-start | bytes 786436
  60.3 16.3 %copy-start.5 = (f32[3,2048]{1,0:T(4,128)S(1)}, f32[3,2048]{1,0:T(4,128)}, u32[]{:S(2)}) copy-start(f32[3,2048]{1,0:T(4,128)} %refs_4_.2) | copy-start | bytes 73732
  60.3 16.3 %copy-start.6 = (f32[2048]{0:T(1024)S(1)}, f32[2048]{0:T(1024)}, u32[]{:S(2)}) copy-start(f32[2048]{0:T(1024)} %param.16) | copy-start | bytes 24580
  60.3 16.3 %copy-start.7 = (bf16[17,256,256]{2,1,0:T(8,128)(2,1)S(1)}, bf16[17,256,256]{2,1,0:T(8,128)(2,1)}, u32[]{:S(2)}) copy-start(bf16[17,256,256]{2,1,0:T(8,128)(2,1)} %constant.46.clone.refs_10_) | copy-start | bytes 6684676
  60.3 16.3 %copy-start.8 = (bf16[256,512]{1,0:T(8,128)(2,1)S(1)}, bf16[256,512]{1,0:T(8,128)(2,1)}, u32[]{:S(2)}) copy-start(bf16[256,512]{1,0:T(8,128)(2,1)} %constant.44.clone.refs_8_) | copy-start | bytes 786436
  60.3 8.3 %collective-permute-start.21 = (bf16[512,128]{1,0:T(8,128)(2,1)S(1)}, bf16[512,128]{1,0:T(8,128)(2,1)S(1)}, u32[]{:S(2)}, u32[]{:S(2)}) collective-permute-start(bf16[512,128]{1,0:T(8,128)(2,1)S(1)} %get-tuple-element.150), channel_id=1, source_target_pairs={{0,12},{1,13},{2,14},{3,15},{4,8},{5,9},{6,10},{7,11},{8,4},{9,5},... | collective-permute-start | bytes 393224 | tf_op jit(solution)/shard_map/ppermute | solution.py:355
  62.3 14.3 %collective-permute-start.22 = (bf16[512,128]{1,0:T(8,128)(2,1)S(1)}, bf16[512,128]{1,0:T(8,128)(2,1)S(1)}, u32[]{:S(2)}, u32[]{:S(2)}) collective-permute-start(bf16[512,128]{1,0:T(8,128)(2,1)S(1)} %get-tuple-element.151), channel_id=1, source_target_pairs={{0,8},{1,9},{2,10},{3,11},{4,12},{5,13},{6,14},{7,15},{8,0},{9,1},... | collective-permute-start | bytes 393224 | tf_op jit(solution)/shard_map/ppermute | solution.py:355
  63.9 12.7 %collective-permute-start.23 = (bf16[512,128]{1,0:T(8,128)(2,1)S(1)}, bf16[512,128]{1,0:T(8,128)(2,1)S(1)}, u32[]{:S(2)}, u32[]{:S(2)}) collective-permute-start(bf16[512,128]{1,0:T(8,128)(2,1)S(1)} %get-tuple-element.152), channel_id=1, source_target_pairs={{0,4},{1,5},{2,6},{3,7},{4,0},{5,1},{6,2},{7,3},{8,12},{9,13},{10,... | collective-permute-start | bytes 393224 | tf_op jit(solution)/shard_map/ppermute | solution.py:355
  64.8 14.9 %collective-permute-start.24 = (bf16[256,1024]{1,0:T(8,128)(2,1)S(1)}, bf16[256,1024]{1,0:T(8,128)(2,1)S(1)}, u32[]{:S(2)}, u32[]{:S(2)}) collective-permute-start(bf16[256,1024]{1,0:T(8,128)(2,1)S(1)} %shard_map.118.refs_8_), channel_id=1, source_target_pairs={{0,16},{16,0},{1,17},{17,1},{2,18},{18,2},{3,19},{19,3},{4,20},{20... | collective-permute-start | bytes 1572872 | tf_op jit(solution)/shard_map/ppermute | solution.py:358
  66.4 13.2 %collective-permute-start.25 = (bf16[256,512]{1,0:T(8,128)(2,1)S(1)}, bf16[256,512]{1,0:T(8,128)(2,1)S(1)}, u32[]{:S(2)}, u32[]{:S(2)}) collective-permute-start(bf16[256,512]{1,0:T(8,128)(2,1)S(1)} %get-tuple-element.172), channel_id=1, source_target_pairs={{0,2},{1,3},{2,0},{3,1},{4,6},{5,7},{6,4},{7,5},{8,10},{9,11},{10,... | collective-permute-start | bytes 786440 | tf_op jit(solution)/shard_map/ppermute | solution.py:352
  76.6 12.3 %copy-start.1 = (bf16[128,2048]{1,0:T(8,128)(2,1)S(1)}, bf16[128,2048]{1,0:T(8,128)(2,1)}, u32[]{:S(2)}) copy-start(bf16[128,2048]{1,0:T(8,128)(2,1)} %refs_6_.1) | copy-start | bytes 1572868
  79.7 9.2 %collective-permute-start.29 = (bf16[128,512]{1,0:T(8,128)(2,1)S(1)}, bf16[128,512]{1,0:T(8,128)(2,1)S(1)}, u32[]{:S(2)}, u32[]{:S(2)}) collective-permute-start(bf16[128,512]{1,0:T(8,128)(2,1)S(1)} %slice.3), channel_id=1, source_target_pairs={{0,1},{1,0},{2,3},{3,2},{4,5},{5,4},{6,7},{7,6},{8,9},{9,8},{10,11... | collective-permute-start | bytes 393224 | tf_op jit(solution)/shard_map/ppermute | solution.py:352
  79.8 6.9 %collective-permute-start.26 = (bf16[256,128]{1,0:T(8,128)(2,1)S(1)}, bf16[256,128]{1,0:T(8,128)(2,1)S(1)}, u32[]{:S(2)}, u32[]{:S(2)}) collective-permute-start(bf16[256,128]{1,0:T(8,128)(2,1)S(1)} %get-tuple-element.173), channel_id=1, source_target_pairs={{0,12},{1,13},{2,14},{3,15},{4,8},{5,9},{6,10},{7,11},{8,4},{9,5},... | collective-permute-start | bytes 196616 | tf_op jit(solution)/shard_map/ppermute | solution.py:355
  81.4 7.4 %collective-permute-start.27 = (bf16[256,128]{1,0:T(8,128)(2,1)S(1)}, bf16[256,128]{1,0:T(8,128)(2,1)S(1)}, u32[]{:S(2)}, u32[]{:S(2)}) collective-permute-start(bf16[256,128]{1,0:T(8,128)(2,1)S(1)} %get-tuple-element.174), channel_id=1, source_target_pairs={{0,8},{1,9},{2,10},{3,11},{4,12},{5,13},{6,14},{7,15},{8,0},{9,1},... | collective-permute-start | bytes 196616 | tf_op jit(solution)/shard_map/ppermute | solution.py:355
  81.4 7.4 %collective-permute-start.28 = (bf16[256,128]{1,0:T(8,128)(2,1)S(1)}, bf16[256,128]{1,0:T(8,128)(2,1)S(1)}, u32[]{:S(2)}, u32[]{:S(2)}) collective-permute-start(bf16[256,128]{1,0:T(8,128)(2,1)S(1)} %get-tuple-element.175), channel_id=1, source_target_pairs={{0,4},{1,5},{2,6},{3,7},{4,0},{5,1},{6,2},{7,3},{8,12},{9,13},{10,... | collective-permute-start | bytes 196616 | tf_op jit(solution)/shard_map/ppermute | solution.py:355
  90.3 2.0 %collective-permute-start.30 = (bf16[128,2048]{1,0:T(8,128)(2,1)S(1)}, bf16[128,2048]{1,0:T(8,128)(2,1)S(1)}, u32[]{:S(2)}, u32[]{:S(2)}) collective-permute-start(bf16[128,2048]{1,0:T(8,128)(2,1)S(1)} %get-tuple-element.190), channel_id=1, source_target_pairs={{0,1},{1,0},{2,3},{3,2},{4,5},{5,4},{6,7},{7,6},{8,9},{9,8},{10,11... | collective-permute-start | bytes 1572872 | tf_op jit(solution)/shard_map/ppermute | solution.py:352
  92.4 14.0 %collective-permute-start.38 = (bf16[128,2048]{1,0:T(8,128)(2,1)S(1)}, bf16[128,2048]{1,0:T(8,128)(2,1)S(1)}, u32[]{:S(2)}, u32[]{:S(2)}) collective-permute-start(bf16[128,2048]{1,0:T(8,128)(2,1)S(1)} %add_convert_fusion.1), channel_id=1, source_target_pairs={{0,2},{1,3},{2,0},{3,1},{4,6},{5,7},{6,4},{7,5},{8,10},{9,11},{10,... | collective-permute-start | bytes 1572872 | tf_op jit(solution)/shard_map/ppermute | solution.py:352
  93.0 4.8 %collective-permute-start.31 = (bf16[256,128]{1,0:T(8,128)(2,1)S(1)}, bf16[256,128]{1,0:T(8,128)(2,1)S(1)}, u32[]{:S(2)}, u32[]{:S(2)}) collective-permute-start(bf16[256,128]{1,0:T(8,128)(2,1)S(1)} %get-tuple-element.196), channel_id=1, source_target_pairs={{0,4},{1,5},{2,6},{3,7},{4,0},{5,1},{6,2},{7,3},{8,12},{9,13},{10,... | collective-permute-start | bytes 196616 | tf_op jit(solution)/shard_map/ppermute | solution.py:355
  93.2 7.5 %collective-permute-start.32 = (bf16[256,128]{1,0:T(8,128)(2,1)S(1)}, bf16[256,128]{1,0:T(8,128)(2,1)S(1)}, u32[]{:S(2)}, u32[]{:S(2)}) collective-permute-start(bf16[256,128]{1,0:T(8,128)(2,1)S(1)} %get-tuple-element.197), channel_id=1, source_target_pairs={{0,8},{1,9},{2,10},{3,11},{4,12},{5,13},{6,14},{7,15},{8,0},{9,1},... | collective-permute-start | bytes 196616 | tf_op jit(solution)/shard_map/ppermute | solution.py:355
  95.6 6.2 %collective-permute-start.33 = (bf16[256,128]{1,0:T(8,128)(2,1)S(1)}, bf16[256,128]{1,0:T(8,128)(2,1)S(1)}, u32[]{:S(2)}, u32[]{:S(2)}) collective-permute-start(bf16[256,128]{1,0:T(8,128)(2,1)S(1)} %get-tuple-element.198), channel_id=1, source_target_pairs={{0,12},{1,13},{2,14},{3,15},{4,8},{5,9},{6,10},{7,11},{8,4},{9,5},... | collective-permute-start | bytes 196616 | tf_op jit(solution)/shard_map/ppermute | solution.py:355
  103.0 1.4 %collective-permute-start.34 = (bf16[128,512]{1,0:T(8,128)(2,1)S(1)}, bf16[128,512]{1,0:T(8,128)(2,1)S(1)}, u32[]{:S(2)}, u32[]{:S(2)}) collective-permute-start(bf16[128,512]{1,0:T(8,128)(2,1)S(1)} %get-tuple-element.202), channel_id=1, source_target_pairs={{0,1},{1,0},{2,3},{3,2},{4,5},{5,4},{6,7},{7,6},{8,9},{9,8},{10,11... | collective-permute-start | bytes 393224 | tf_op jit(solution)/shard_map/ppermute | solution.py:352
  103.1 1.5 %collective-permute-start.35 = (bf16[128,512]{1,0:T(8,128)(2,1)S(1)}, bf16[128,512]{1,0:T(8,128)(2,1)S(1)}, u32[]{:S(2)}, u32[]{:S(2)}) collective-permute-start(bf16[128,512]{1,0:T(8,128)(2,1)S(1)} %get-tuple-element.203), channel_id=1, source_target_pairs={{0,1},{1,0},{2,3},{3,2},{4,5},{5,4},{6,7},{7,6},{8,9},{9,8},{10,11... | collective-permute-start | bytes 393224 | tf_op jit(solution)/shard_map/ppermute | solution.py:352
  103.6 1.3 %collective-permute-start.36 = (bf16[128,512]{1,0:T(8,128)(2,1)S(1)}, bf16[128,512]{1,0:T(8,128)(2,1)S(1)}, u32[]{:S(2)}, u32[]{:S(2)}) collective-permute-start(bf16[128,512]{1,0:T(8,128)(2,1)S(1)} %get-tuple-element.204), channel_id=1, source_target_pairs={{0,1},{1,0},{2,3},{3,2},{4,5},{5,4},{6,7},{7,6},{8,9},{9,8},{10,11... | collective-permute-start | bytes 393224 | tf_op jit(solution)/shard_map/ppermute | solution.py:352
  103.7 1.5 %collective-permute-start.37 = (bf16[128,512]{1,0:T(8,128)(2,1)S(1)}, bf16[128,512]{1,0:T(8,128)(2,1)S(1)}, u32[]{:S(2)}, u32[]{:S(2)}) collective-permute-start(bf16[128,512]{1,0:T(8,128)(2,1)S(1)} %get-tuple-element.205), channel_id=1, source_target_pairs={{0,1},{1,0},{2,3},{3,2},{4,5},{5,4},{6,7},{7,6},{8,9},{9,8},{10,11... | collective-permute-start | bytes 393224 | tf_op jit(solution)/shard_map/ppermute | solution.py:352

commit v7 on v6

--- a/solution.py
+++ b/solution.py
@@ -80,28 +80,15 @@
     return copies
 
 
-def start_kernel(share, pos, weight, taps, out_weight, *refs):
-    outs, (own, whole, near, out_half) = refs[:PLANE], refs[PLANE : PLANE + 4]
-    weight_here, taps_here, sems = refs[PLANE + 4 :]
+def start_kernel(pos, taps, out_weight, own, whole, near, out_half, taps_here, sems):
     rows, wide = own.shape
     deep, width = out_half.shape
     quarter = rows // 4
     side = pl.ds(pl.multiple_of(pos[0] * width, width), width)
-    pairs = []
-    for source, here in ((weight, weight_here), (taps, taps_here)):
-        for q in range(4):
-            cut = pl.ds(q * quarter, quarter)
-            pairs.append((source.at[cut], here.at[cut]))
+    cuts = [pl.ds(q * quarter, quarter) for q in range(4)]
+    pairs = [(taps.at[cut], taps_here.at[cut]) for cut in cuts]
     pairs.append((out_weight.at[:, side], out_half))
-    copies = fetch(pairs, sems)
-    for copy in copies[:4]:
-        copy.wait()
-    for d, out in enumerate(outs):
-        place = jnp.bitwise_xor(pos[2], d)
-        for p in range(wide // share):
-            at = pl.multiple_of((p * PLANE + place) * share, share)
-            out[:, p * share : (p + 1) * share] = weight_here[:, pl.ds(at, share)]
-    for copy in copies[4:]:
+    for copy in fetch(pairs, sems):
         copy.wait()
 
     def columns(s):
@@ -113,6 +100,19 @@
     for q in range(2):
         first = pl.multiple_of(pos[0] * (rows // 2) + q * quarter, quarter)
         near[deep:, q * wide : (q + 1) * wide] = taps_here[pl.ds(first, quarter), columns(1)]
+
+
+def split_kernel(share, pos, weight, *refs):
+    outs, (weight_here, sems) = refs[-PLANE - 2 : -2], refs[-2:]
+    quarter = weight.shape[0] // 4
+    cuts = [pl.ds(q * quarter, quarter) for q in range(4)]
+    for copy in fetch([(weight.at[cut], weight_here.at[cut]) for cut in cuts], sems):
+        copy.wait()
+    for d, out in enumerate(outs):
+        place = jnp.bitwise_xor(pos[2], d)
+        for p in range(out.shape[1] // share):
+            at = pl.multiple_of((p * PLANE + place) * share, share)
+            out[:, p * share : (p + 1) * share] = weight_here[:, pl.ds(at, share)]
 
 
 def gate_kernel(share, pos, gate, own, beside, across, sems):
@@ -370,21 +370,26 @@
     )
     part, width, positions = rows // 2, features // 2, blocks * rows
 
-    *cut, taps_own, taps_whole, out_near, out_half = call(
-        functools.partial(start_kernel, share),
-        [shaped(deep, wide)] * PLANE
-        + [shaped(rows, wide), shaped(rows, wide)]
+    taps_own, taps_whole, out_near, out_half = call(
+        start_kernel,
+        [shaped(rows, wide), shaped(rows, wide)]
         + [shaped(deep + rows // 4, width), shaped(deep, width)],
-        [
-            pltpu.VMEM((deep, channels), jnp.bfloat16),
-            pltpu.VMEM((rows, channels), jnp.bfloat16),
-            pltpu.SemaphoreType.DMA((9,)),
-        ],
+        [pltpu.VMEM((rows, channels), jnp.bfloat16), pltpu.SemaphoreType.DMA((5,))],
         pos,
-        [value_weight, filter_taps, output_weight],
+        [filter_taps, output_weight],
         0,
         vmem=53,
-        fetched=3,
+        fetched=2,
+    )
+    cut = call(
+        functools.partial(split_kernel, share),
+        [shaped(deep, wide)] * PLANE,
+        [pltpu.VMEM((deep, channels), jnp.bfloat16), pltpu.SemaphoreType.DMA((4,))],
+        pos,
+        [value_weight],
+        0,
+        vmem=53,
+        fetched=1,
     )
     cut = list(cut)
     out_near = to_plane(out_near, 1)
@@ -435,6 +440,7 @@
         taps_mine,
         taps_other,
         gate_beside,
+        flops=1 << 30,
     )
     other, passed, both = stage((other, passed, both))
     passed_other = to_group(passed)

time: 108 us -> 106 us (0.981)
    ppermute x6, starting transfers between devices: 8.02 us -> 6.23 us  [to_group(): return lax.ppermute(block, 'groups', [(0, 1), (1, 0)])]
    ppermute x1, waiting for transfers between devices: 2.01 us -> 0.44 us  [local(): taps_whole = lax.ppermute(taps_whole, ('groups', 'seq'), route)]
    pallas_call x14 -> x15, Pallas kernels: 17.1 us -> 17.9 us  [call(): pl.pallas_call(kernel, out_shape=outs, in_specs=in_specs, out_specs=[pl.B...]
  transfers between devices with their start and end apart: 39 -> 39, of which waited for: 21 -> 23; matrix products, arithmetic and copies ran while one was open for 0% -> 0% of each run, Pallas kernels for 13% -> 14%
where the time goes in v7:
time: 106 us
  waiting for transfers between devices  46.9 us (44%)
  starting transfers between devices  39.9 us (38%)
  Pallas kernels  17.9 us (17%)
  other arithmetic  1.15 us (1%)
    ppermute x15, waiting for transfers between devices, to_plane(): lax.ppermute(block, 'seq', [(i, i ^ s * PLANE) for i in range(devices)])  29.9 us
    ppermute x15, starting transfers between devices, to_plane(): lax.ppermute(block, 'seq', [(i, i ^ s * PLANE) for i in range(devices)])  22.9 us
    pallas_call x15, Pallas kernels, call(): pl.pallas_call(kernel, out_shape=outs, in_specs=in_specs, out_specs=[pl.B...  17.9 us
    ppermute x17, waiting for transfers between devices, to_place(): return lax.ppermute(block, 'seq', [(i, i ^ d) for i in range(devices)])  11.9 us
    ppermute x17, starting transfers between devices, to_place(): return lax.ppermute(block, 'seq', [(i, i ^ d) for i in range(devices)])  8.25 us
    ppermute x6, starting transfers between devices, to_group(): return lax.ppermute(block, 'groups', [(0, 1), (1, 0)])  6.23 us
    ppermute x6, waiting for transfers between devices, to_group(): return lax.ppermute(block, 'groups', [(0, 1), (1, 0)])  4.69 us
    ppermute x1, starting transfers between devices, local(): taps_whole = lax.ppermute(taps_whole, ('groups', 'seq'), route)  2.59 us
  transfers between devices with their start and end apart: 39, of which 23 were waited for; matrix products, arithmetic and copies ran while one was open for 0% of the time, Pallas kernels for 14%

profile of v7, /device:TPU:0, one launch (start us, length us, event | category | flops | bytes accessed | tf_op | source)
XLA Modules:
  0.0 106.2 jit_solution(15147137768108360119)
XLA Ops:
  0.5 1.8 %shard_map.111 = (bf16[128,512]{1,0:T(8,128)(2,1)S(1)}, bf16[128,512]{1,0:T(8,128)(2,1)S(1)}, bf16[160,1024]{1,0:T(8,128)(2,1)S(1)}, bf16[128,1024]{1,0:T(8,128)(2,1)S(1)}) custom-call(s32[3]{0:T(128)S(1)} %pad_add_fusion.pos, bf16[128,2048]{1,0:T(8,128)(2,1)} %taps.1, bf16[128,2048]{1,0:T(8,128)(2,1)} %refs_6_.1), custom_call_target="tpu_custom_call" | custom-call | tf_op jit(solution)/shard_map/pallas_call | solution.py:60
  2.4 2.7 %collective-permute-start.5 = (bf16[160,1024]{1,0:T(8,128)(2,1)S(1)}, bf16[160,1024]{1,0:T(8,128)(2,1)S(1)}, u32[]{:S(2)}, u32[]{:S(2)}) collective-permute-start(bf16[160,1024]{1,0:T(8,128)(2,1)S(1)} %get-tuple-element.111), channel_id=1, source_target_pairs={{0,4},{1,5},{2,6},{3,7},{4,0},{5,1},{6,2},{7,3},{8,12},{9,13},{10,... | collective-permute-start | bytes 983048 | tf_op jit(solution)/shard_map/ppermute | solution.py:355
  5.0 1.8 %shard_map.109 = (bf16[128,512]{1,0:T(8,128)(2,1)S(1)}, bf16[128,512]{1,0:T(8,128)(2,1)S(1)}, bf16[128,512]{1,0:T(8,128)(2,1)S(1)}, bf16[128,512]{1,0:T(8,128)(2,1)S(1)}) custom-call(s32[3]{0:T(128)S(1)} %pad_add_fusion.pos, bf16[128,2048]{1,0:T(8,128)(2,1)} %weight.1), custom_call_target="tpu_custom_call" | custom-call | tf_op jit(solution)/shard_map/pallas_call | solution.py:60
  7.1 1.5 %collective-permute-start.1 = (bf16[128,512]{1,0:T(8,128)(2,1)S(1)}, bf16[128,512]{1,0:T(8,128)(2,1)S(1)}, u32[]{:S(2)}, u32[]{:S(2)}) collective-permute-start(bf16[128,512]{1,0:T(8,128)(2,1)S(1)} %get-tuple-element.108), channel_id=1, source_target_pairs={{0,2},{1,3},{2,0},{3,1},{4,6},{5,7},{6,4},{7,5},{8,10},{9,11},{10,... | collective-permute-start | bytes 393224 | tf_op jit(solution)/shard_map/ppermute | solution.py:352
  8.8 2.6 %collective-permute-start.3 = (bf16[128,512]{1,0:T(8,128)(2,1)S(1)}, bf16[128,512]{1,0:T(8,128)(2,1)S(1)}, u32[]{:S(2)}, u32[]{:S(2)}) collective-permute-start(bf16[128,512]{1,0:T(8,128)(2,1)S(1)} %get-tuple-element.110), channel_id=1, source_target_pairs={{0,8},{1,9},{2,10},{3,11},{4,12},{5,13},{6,14},{7,15},{8,0},{9,1},... | collective-permute-start | bytes 393224 | tf_op jit(solution)/shard_map/ppermute | solution.py:411
  11.9 0.9 shard_map.113
  12.8 0.6 collective-permute-done.1.refs_2_
  13.4 1.6 %collective-permute-done.2.refs_3_ = bf16[128,512]{1,0:T(8,128)(2,1)S(1)} collective-permute-done((bf16[128,512]{1,0:T(8,128)(2,1)S(1)}, bf16[128,512]{1,0:T(8,128)(2,1)S(1)}, u32[]{:S(2)}, u32[]{:S(2)}) %collective-permute-start.2) | collective-permute-done | bytes 131104 | tf_op jit(solution)/shard_map/ppermute | solution.py:352
  16.2 1.7 %collective-permute-start.6 = (bf16[128,2048]{1,0:T(8,128)(2,1)S(1)}, bf16[128,2048]{1,0:T(8,128)(2,1)S(1)}, u32[]{:S(2)}, u32[]{:S(2)}) collective-permute-start(bf16[128,2048]{1,0:T(8,128)(2,1)S(1)} %copy-done.2), channel_id=1, source_target_pairs={{0,2},{1,3},{2,0},{3,1},{4,6},{5,7},{6,4},{7,5},{8,10},{9,11},{10,... | collective-permute-start | bytes 1572872 | tf_op jit(solution)/shard_map/ppermute | solution.py:352
  17.9 2.6 %collective-permute-start.8 = (bf16[256,512]{1,0:T(8,128)(2,1)S(1)}, bf16[256,512]{1,0:T(8,128)(2,1)S(1)}, u32[]{:S(2)}, u32[]{:S(2)}) collective-permute-start(bf16[256,512]{1,0:T(8,128)(2,1)S(1)} %shard_map.112), channel_id=1, source_target_pairs={{0,8},{1,9},{2,10},{3,11},{4,12},{5,13},{6,14},{7,15},{8,0},{9,1},... | collective-permute-start | bytes 786440 | tf_op jit(solution)/shard_map/ppermute | solution.py:355
  20.5 2.5 %collective-permute-start.7 = (bf16[256,512]{1,0:T(8,128)(2,1)S(1)}, bf16[256,512]{1,0:T(8,128)(2,1)S(1)}, u32[]{:S(2)}, u32[]{:S(2)}) collective-permute-start(bf16[256,512]{1,0:T(8,128)(2,1)S(1)} %shard_map.112), channel_id=1, source_target_pairs={{0,4},{1,5},{2,6},{3,7},{4,0},{5,1},{6,2},{7,3},{8,12},{9,13},{10,... | collective-permute-start | bytes 786440 | tf_op jit(solution)/shard_map/ppermute | solution.py:355
  24.2 1.5 %collective-permute-start.9 = (bf16[192,512]{1,0:T(8,128)(2,1)S(1)}, bf16[192,512]{1,0:T(8,128)(2,1)S(1)}, u32[]{:S(2)}, u32[]{:S(2)}) collective-permute-start(bf16[192,512]{1,0:T(8,128)(2,1)S(1)} %get-tuple-element.120.mine), channel_id=1, source_target_pairs={{0,16},{16,0},{1,17},{17,1},{2,18},{18,2},{3,19},{19,3},{4,20},{20... | collective-permute-start | bytes 589832 | tf_op jit(solution)/shard_map/ppermute | solution.py:358
  25.7 4.6 %collective-permute-done.6.from_x = bf16[128,2048]{1,0:T(8,128)(2,1)S(1)} collective-permute-done((bf16[128,2048]{1,0:T(8,128)(2,1)S(1)}, bf16[128,2048]{1,0:T(8,128)(2,1)S(1)}, u32[]{:S(2)}, u32[]{:S(2)}) %collective-permute-start.6) | collective-permute-done | bytes 524320 | tf_op jit(solution)/shard_map/ppermute | solution.py:352
  30.3 4.7 %collective-permute-done.9.other = bf16[192,512]{1,0:T(8,128)(2,1)S(1)} collective-permute-done((bf16[192,512]{1,0:T(8,128)(2,1)S(1)}, bf16[192,512]{1,0:T(8,128)(2,1)S(1)}, u32[]{:S(2)}, u32[]{:S(2)}) %collective-permute-start.9) | collective-permute-done | bytes 196640 | tf_op jit(solution)/shard_map/ppermute | solution.py:358
  35.5 1.2 %collective-permute-start.11 = (bf16[256,512]{1,0:T(8,128)(2,1)S(1)}, bf16[256,512]{1,0:T(8,128)(2,1)S(1)}, u32[]{:S(2)}, u32[]{:S(2)}) collective-permute-start(bf16[256,512]{1,0:T(8,128)(2,1)S(1)} %collective-permute-done.7.refs_0_), channel_id=1, source_target_pairs={{0,16},{16,0},{1,17},{17,1},{2,18},{18,2},{3,19},{19,3},{4,20},{20... | collective-permute-start | bytes 786440 | tf_op jit(solution)/shard_map/ppermute | solution.py:358
  36.7 0.8 collective-permute-start.12
  37.5 1.2 %collective-permute-start.13 = (bf16[256,512]{1,0:T(8,128)(2,1)S(1)}, bf16[256,512]{1,0:T(8,128)(2,1)S(1)}, u32[]{:S(2)}, u32[]{:S(2)}) collective-permute-start(bf16[256,512]{1,0:T(8,128)(2,1)S(1)} %collective-permute-done.8.refs_1_), channel_id=1, source_target_pairs={{0,4},{1,5},{2,6},{3,7},{4,0},{5,1},{6,2},{7,3},{8,12},{9,13},{10,... | collective-permute-start | bytes 786440 | tf_op jit(solution)/shard_map/ppermute | solution.py:355
  38.7 0.7 shard_map.116
  39.4 8.4 %collective-permute-done.19.refs_0_ = bf16[128,1024]{1,0:T(8,128)(2,1)S(1)} collective-permute-done((bf16[128,1024]{1,0:T(8,128)(2,1)S(1)}, bf16[128,1024]{1,0:T(8,128)(2,1)S(1)}, u32[]{:S(2)}, u32[]{:S(2)}) %collective-permute-start.19) | collective-permute-done | bytes 262176 | tf_op jit(solution)/shard_map/ppermute | solution.py:355
  48.4 0.9 collective-permute-done.13.refs_2_
  49.3 1.4 %collective-permute-start.18 = (bf16[256,512]{1,0:T(8,128)(2,1)S(1)}, bf16[256,512]{1,0:T(8,128)(2,1)S(1)}, u32[]{:S(2)}, u32[]{:S(2)}) collective-permute-start(bf16[256,512]{1,0:T(8,128)(2,1)S(1)} %collective-permute-done.13.refs_2_), channel_id=1, source_target_pairs={{0,16},{16,0},{1,17},{17,1},{2,18},{18,2},{3,19},{19,3},{4,20},{20... | collective-permute-start | bytes 786440 | tf_op jit(solution)/shard_map/ppermute | solution.py:358
  50.7 1.5 %collective-permute-start.16 = (bf16[4,128,128]{2,1,0:T(8,128)(2,1)S(1)}, bf16[4,128,128]{2,1,0:T(8,128)(2,1)S(1)}, u32[]{:S(2)}, u32[]{:S(2)}) collective-permute-start(bf16[4,128,128]{2,1,0:T(8,128)(2,1)S(1)} %get-tuple-element.133), channel_id=1, source_target_pairs={{0,2},{1,3},{2,0},{3,1},{4,6},{5,7},{6,4},{7,5},{8,10},{9,11},{10,... | collective-permute-start | bytes 393224 | tf_op jit(solution)/shard_map/ppermute | solution.py:352
  52.8 3.7 %collective-permute-done.20.refs_1_ = bf16[128,1024]{1,0:T(8,128)(2,1)S(1)} collective-permute-done((bf16[128,1024]{1,0:T(8,128)(2,1)S(1)}, bf16[128,1024]{1,0:T(8,128)(2,1)S(1)}, u32[]{:S(2)}, u32[]{:S(2)}) %collective-permute-start.20) | collective-permute-done | bytes 262176 | tf_op jit(solution)/shard_map/ppermute | solution.py:355
  57.1 0.8 collective-permute-done.17.refs_3_
  58.0 2.0 %shard_map.118 = (bf16[512,128]{1,0:T(8,128)(2,1)S(1)}, bf16[512,128]{1,0:T(8,128)(2,1)S(1)}, bf16[512,128]{1,0:T(8,128)(2,1)S(1)}, bf16[512,128]{1,0:T(8,128)(2,1)S(1)}) custom-call(s32[3]{0:T(128)S(1)} %pad_add_fusion.pos, bf16[128,2048]{1,0:T(8,128)(2,1)S(1)} %copy-done.2, bf16[128,2048]{1,0:T(8,128)(2,1)S(1)} %collective-permute-done.4.core, ...), custom_call_target="tpu_custom_call" | custom-call | flops 1073741824 | bytes 4718592 | tf_op jit(solution)/shard_map/pallas_call | solution.py:60
  60.1 0.7 collective-permute-start.21
  60.8 2.0 %collective-permute-start.22 = (bf16[512,128]{1,0:T(8,128)(2,1)S(1)}, bf16[512,128]{1,0:T(8,128)(2,1)S(1)}, u32[]{:S(2)}, u32[]{:S(2)}) collective-permute-start(bf16[512,128]{1,0:T(8,128)(2,1)S(1)} %get-tuple-element.151), channel_id=1, source_target_pairs={{0,8},{1,9},{2,10},{3,11},{4,12},{5,13},{6,14},{7,15},{8,0},{9,1},... | collective-permute-start | bytes 393224 | tf_op jit(solution)/shard_map/ppermute | solution.py:355
  62.8 1.7 %collective-permute-start.23 = (bf16[512,128]{1,0:T(8,128)(2,1)S(1)}, bf16[512,128]{1,0:T(8,128)(2,1)S(1)}, u32[]{:S(2)}, u32[]{:S(2)}) collective-permute-start(bf16[512,128]{1,0:T(8,128)(2,1)S(1)} %get-tuple-element.152), channel_id=1, source_target_pairs={{0,4},{1,5},{2,6},{3,7},{4,0},{5,1},{6,2},{7,3},{8,12},{9,13},{10,... | collective-permute-start | bytes 393224 | tf_op jit(solution)/shard_map/ppermute | solution.py:355
  64.5 0.8 collective-permute-start.24
  65.3 0.6 collective-permute-start.25
  65.9 1.6 %shard_map.120.refs_6_ = bf16[17,256,128]{2,1,0:T(8,128)(2,1)S(1)} custom-call(s32[3]{0:T(128)S(1)} %pad_add_fusion.pos, bf16[4,128,128]{2,1,0:T(8,128)(2,1)S(1)} %get-tuple-element.154.refs_0_, bf16[8,128,128]{2,1,0:T(8,128)(2,1)S(1)} %collective-permute-done.15.refs_1_.refs_5_, bf16[4,128,128]{2,1,0:T(8,128)(2,1)S(1)} %collective-permute-done.16.refs_2_, ...), custom_call_target="tpu_custom_call" | custom-call | flops 536870912 | bytes 4259840 | tf_op jit(solution)/shard_map/pallas_call | solution.py:60
  67.5 0.9 collective-permute-done.21.refs_3_
  68.4 7.1 %collective-permute-done.22.refs_2_ = bf16[512,128]{1,0:T(8,128)(2,1)S(1)} collective-permute-done((bf16[512,128]{1,0:T(8,128)(2,1)S(1)}, bf16[512,128]{1,0:T(8,128)(2,1)S(1)}, u32[]{:S(2)}, u32[]{:S(2)}) %collective-permute-start.22) | collective-permute-done | bytes 131104 | tf_op jit(solution)/shard_map/ppermute | solution.py:355
  75.5 3.0 %shard_map.121 = (bf16[256,128]{1,0:T(8,128)(2,1)S(1)}, bf16[256,128]{1,0:T(8,128)(2,1)S(1)}, bf16[256,128]{1,0:T(8,128)(2,1)S(1)}, bf16[256,128]{1,0:T(8,128)(2...) custom-call(s32[3]{0:T(128)S(1)} %pad_add_fusion.pos, ...), custom_call_target="tpu_custom_call" | custom-call | flops 4294967296 | bytes 7176192 | tf_op jit(solution)/shard_map/pallas_call | solution.py:60
  78.6 1.4 %collective-permute-start.26 = (bf16[256,128]{1,0:T(8,128)(2,1)S(1)}, bf16[256,128]{1,0:T(8,128)(2,1)S(1)}, u32[]{:S(2)}, u32[]{:S(2)}) collective-permute-start(bf16[256,128]{1,0:T(8,128)(2,1)S(1)} %get-tuple-element.173), channel_id=1, source_target_pairs={{0,12},{1,13},{2,14},{3,15},{4,8},{5,9},{6,10},{7,11},{8,4},{9,5},... | collective-permute-start | bytes 196616 | tf_op jit(solution)/shard_map/ppermute | solution.py:355
  80.3 2.8 %collective-permute-start.28 = (bf16[256,128]{1,0:T(8,128)(2,1)S(1)}, bf16[256,128]{1,0:T(8,128)(2,1)S(1)}, u32[]{:S(2)}, u32[]{:S(2)}) collective-permute-start(bf16[256,128]{1,0:T(8,128)(2,1)S(1)} %get-tuple-element.175), channel_id=1, source_target_pairs={{0,4},{1,5},{2,6},{3,7},{4,0},{5,1},{6,2},{7,3},{8,12},{9,13},{10,... | collective-permute-start | bytes 196616 | tf_op jit(solution)/shard_map/ppermute | solution.py:355
  83.1 2.4 %collective-permute-done.26.refs_3_ = bf16[256,128]{1,0:T(8,128)(2,1)S(1)} collective-permute-done((bf16[256,128]{1,0:T(8,128)(2,1)S(1)}, bf16[256,128]{1,0:T(8,128)(2,1)S(1)}, u32[]{:S(2)}, u32[]{:S(2)}) %collective-permute-start.26) | collective-permute-done | bytes 65568 | tf_op jit(solution)/shard_map/ppermute | solution.py:355
  85.5 2.3 %collective-permute-done.27.refs_2_ = bf16[256,128]{1,0:T(8,128)(2,1)S(1)} collective-permute-done((bf16[256,128]{1,0:T(8,128)(2,1)S(1)}, bf16[256,128]{1,0:T(8,128)(2,1)S(1)}, u32[]{:S(2)}, u32[]{:S(2)}) %collective-permute-start.27) | collective-permute-done | bytes 65568 | tf_op jit(solution)/shard_map/ppermute | solution.py:355
  87.7 1.4 %shard_map.122 = (f32[128,2048]{1,0:T(8,128)S(1)}, bf16[128,2048]{1,0:T(8,128)(2,1)S(1)}, bf16[512,2048]{1,0:T(8,128)(2,1)S(1)}) custom-call(s32[3]{0:T(128)S(1)} %pad_add_fusion.pos, bf16[256,128]{1,0:T(8,128)(2,1)S(1)} %get-tuple-element.182.refs_0_, bf16[256,128]{1,0:T(8,128)(2,1)S(1)} %collective-permute-done.28.refs_1_, ...), custom_call_target="tpu_custom_call" | custom-call | flops 536870912 | bytes 6422528 | tf_op jit(solution)/shard_map/pallas_call | solution.py:60
  89.3 1.9 %collective-permute-done.30 = bf16[128,2048]{1,0:T(8,128)(2,1)S(1)} collective-permute-done((bf16[128,2048]{1,0:T(8,128)(2,1)S(1)}, bf16[128,2048]{1,0:T(8,128)(2,1)S(1)}, u32[]{:S(2)}, u32[]{:S(2)}) %collective-permute-start.30) | collective-permute-done | bytes 524320 | tf_op jit(solution)/shard_map/ppermute | solution.py:352
  91.2 0.8 collective-permute-start.38
  92.1 2.3 %collective-permute-start.32 = (bf16[256,128]{1,0:T(8,128)(2,1)S(1)}, bf16[256,128]{1,0:T(8,128)(2,1)S(1)}, u32[]{:S(2)}, u32[]{:S(2)}) collective-permute-start(bf16[256,128]{1,0:T(8,128)(2,1)S(1)} %get-tuple-element.197), channel_id=1, source_target_pairs={{0,8},{1,9},{2,10},{3,11},{4,12},{5,13},{6,14},{7,15},{8,0},{9,1},... | collective-permute-start | bytes 196616 | tf_op jit(solution)/shard_map/ppermute | solution.py:355
  94.4 2.1 %collective-permute-start.33 = (bf16[256,128]{1,0:T(8,128)(2,1)S(1)}, bf16[256,128]{1,0:T(8,128)(2,1)S(1)}, u32[]{:S(2)}, u32[]{:S(2)}) collective-permute-start(bf16[256,128]{1,0:T(8,128)(2,1)S(1)} %get-tuple-element.198), channel_id=1, source_target_pairs={{0,12},{1,13},{2,14},{3,15},{4,8},{5,9},{6,10},{7,11},{8,4},{9,5},... | collective-permute-start | bytes 196616 | tf_op jit(solution)/shard_map/ppermute | solution.py:355
  96.9 2.7 %collective-permute-done.32.refs_2_ = bf16[256,128]{1,0:T(8,128)(2,1)S(1)} collective-permute-done((bf16[256,128]{1,0:T(8,128)(2,1)S(1)}, bf16[256,128]{1,0:T(8,128)(2,1)S(1)}, u32[]{:S(2)}, u32[]{:S(2)}) %collective-permute-start.32) | collective-permute-done | bytes 65568 | tf_op jit(solution)/shard_map/ppermute | solution.py:355
  99.7 0.9 collective-permute-done.33.refs_3_
  100.5 1.3 %shard_map.123 = (f32[128,2048]{1,0:T(8,128)S(1)}, bf16[128,512]{1,0:T(8,128)(2,1)S(1)}, bf16[128,512]{1,0:T(8,128)(2,1)S(1)}, bf16[128,512]{1,0:T(8,128)(2,1)S(1)}, bf16[128,512]{1,0:T(8,128)(2,1)S(1)}) custom-call(s32[3]{0:T(128)S(1)} %pad_add_fusion.pos, bf16[256,128]{1,0:T(8,128)(2,1)S(1)} %get-tuple-element.195.refs_0_, ...), custom_call_target="tpu_custom_call" | custom-call | tf_op jit(solution)/shard_map/pallas_call | solution.py:60
  103.9 1.4 %collective-permute-done.38 = bf16[128,2048]{1,0:T(8,128)(2,1)S(1)} collective-permute-done((bf16[128,2048]{1,0:T(8,128)(2,1)S(1)}, bf16[128,2048]{1,0:T(8,128)(2,1)S(1)}, u32[]{:S(2)}, u32[]{:S(2)}) %collective-permute-start.38) | collective-permute-done | bytes 524320 | tf_op jit(solution)/shard_map/ppermute | solution.py:352
  105.3 1.0 add_convert_fusion
  (67 shorter events, 9.3 us)
Async XLA Ops:
  0.0 16.2 %copy-start.2 = (bf16[128,2048]{1,0:T(8,128)(2,1)S(1)}, bf16[128,2048]{1,0:T(8,128)(2,1)}, u32[]{:S(2)}) copy-start(bf16[128,2048]{1,0:T(8,128)(2,1)} %x.1) | copy-start | bytes 1572868
  0.0 11.9 %copy-start.3 = (bf16[128,2048]{1,0:T(8,128)(2,1)S(1)}, bf16[128,2048]{1,0:T(8,128)(2,1)}, u32[]{:S(2)}) copy-start(bf16[128,2048]{1,0:T(8,128)(2,1)} %gate.1) | copy-start | bytes 1572868
  0.0 16.2 %collective-permute-start.4 = (bf16[128,2048]{1,0:T(8,128)(2,1)}, bf16[128,2048]{1,0:T(8,128)(2,1)S(1)}, u32[]{:S(2)}, u32[]{:S(2)}) collective-permute-start(bf16[128,2048]{1,0:T(8,128)(2,1)} %x.1), channel_id=1, source_target_pairs={{0,1},{1,0},{2,3},{3,2},{4,5},{5,4},{6,7},{7,6},{8,9},{9,8},{10,11... | collective-permute-start | bytes 1572872 | tf_op jit(solution)/shard_map/ppermute | solution.py:352
  2.4 13.8 %collective-permute-start.5 = (bf16[160,1024]{1,0:T(8,128)(2,1)S(1)}, bf16[160,1024]{1,0:T(8,128)(2,1)S(1)}, u32[]{:S(2)}, u32[]{:S(2)}) collective-permute-start(bf16[160,1024]{1,0:T(8,128)(2,1)S(1)} %get-tuple-element.111), channel_id=1, source_target_pairs={{0,4},{1,5},{2,6},{3,7},{4,0},{5,1},{6,2},{7,3},{8,12},{9,13},{10,... | collective-permute-start | bytes 983048 | tf_op jit(solution)/shard_map/ppermute | solution.py:355
  6.9 1.9 %collective-permute-start = (bf16[128,512]{1,0:T(8,128)(2,1)S(1)}, bf16[128,512]{1,0:T(8,128)(2,1)S(1)}, u32[]{:S(2)}, u32[]{:S(2)}) collective-permute-start(bf16[128,512]{1,0:T(8,128)(2,1)S(1)} %get-tuple-element.107), channel_id=1, source_target_pairs={{0,1},{1,0},{2,3},{3,2},{4,5},{5,4},{6,7},{7,6},{8,9},{9,8},{10,11... | collective-permute-start | bytes 393224 | tf_op jit(solution)/shard_map/ppermute | solution.py:352
  7.1 6.3 %collective-permute-start.1 = (bf16[128,512]{1,0:T(8,128)(2,1)S(1)}, bf16[128,512]{1,0:T(8,128)(2,1)S(1)}, u32[]{:S(2)}, u32[]{:S(2)}) collective-permute-start(bf16[128,512]{1,0:T(8,128)(2,1)S(1)} %get-tuple-element.108), channel_id=1, source_target_pairs={{0,2},{1,3},{2,0},{3,1},{4,6},{5,7},{6,4},{7,5},{8,10},{9,11},{10,... | collective-permute-start | bytes 393224 | tf_op jit(solution)/shard_map/ppermute | solution.py:352
  8.6 6.4 %collective-permute-start.2 = (bf16[128,512]{1,0:T(8,128)(2,1)S(1)}, bf16[128,512]{1,0:T(8,128)(2,1)S(1)}, u32[]{:S(2)}, u32[]{:S(2)}) collective-permute-start(bf16[128,512]{1,0:T(8,128)(2,1)S(1)} %get-tuple-element.109), channel_id=1, source_target_pairs={{0,3},{1,2},{2,1},{3,0},{4,7},{5,6},{6,5},{7,4},{8,11},{9,10},{10,... | collective-permute-start | bytes 393224 | tf_op jit(solution)/shard_map/ppermute | solution.py:352
  8.8 7.3 %collective-permute-start.3 = (bf16[128,512]{1,0:T(8,128)(2,1)S(1)}, bf16[128,512]{1,0:T(8,128)(2,1)S(1)}, u32[]{:S(2)}, u32[]{:S(2)}) collective-permute-start(bf16[128,512]{1,0:T(8,128)(2,1)S(1)} %get-tuple-element.110), channel_id=1, source_target_pairs={{0,8},{1,9},{2,10},{3,11},{4,12},{5,13},{6,14},{7,15},{8,0},{9,1},... | collective-permute-start | bytes 393224 | tf_op jit(solution)/shard_map/ppermute | solution.py:411
  16.2 14.1 %collective-permute-start.6 = (bf16[128,2048]{1,0:T(8,128)(2,1)S(1)}, bf16[128,2048]{1,0:T(8,128)(2,1)S(1)}, u32[]{:S(2)}, u32[]{:S(2)}) collective-permute-start(bf16[128,2048]{1,0:T(8,128)(2,1)S(1)} %copy-done.2), channel_id=1, source_target_pairs={{0,2},{1,3},{2,0},{3,1},{4,6},{5,7},{6,4},{7,5},{8,10},{9,11},{10,... | collective-permute-start | bytes 1572872 | tf_op jit(solution)/shard_map/ppermute | solution.py:352
  17.9 17.1 %collective-permute-start.8 = (bf16[256,512]{1,0:T(8,128)(2,1)S(1)}, bf16[256,512]{1,0:T(8,128)(2,1)S(1)}, u32[]{:S(2)}, u32[]{:S(2)}) collective-permute-start(bf16[256,512]{1,0:T(8,128)(2,1)S(1)} %shard_map.112), channel_id=1, source_target_pairs={{0,8},{1,9},{2,10},{3,11},{4,12},{5,13},{6,14},{7,15},{8,0},{9,1},... | collective-permute-start | bytes 786440 | tf_op jit(solution)/shard_map/ppermute | solution.py:355
  20.5 14.4 %collective-permute-start.7 = (bf16[256,512]{1,0:T(8,128)(2,1)S(1)}, bf16[256,512]{1,0:T(8,128)(2,1)S(1)}, u32[]{:S(2)}, u32[]{:S(2)}) collective-permute-start(bf16[256,512]{1,0:T(8,128)(2,1)S(1)} %shard_map.112), channel_id=1, source_target_pairs={{0,4},{1,5},{2,6},{3,7},{4,0},{5,1},{6,2},{7,3},{8,12},{9,13},{10,... | collective-permute-start | bytes 786440 | tf_op jit(solution)/shard_map/ppermute | solution.py:355
  23.6 11.4 %collective-permute-start.10 = (bf16[128,1024]{1,0:T(8,128)(2,1)S(1)}, bf16[128,1024]{1,0:T(8,128)(2,1)S(1)}, u32[]{:S(2)}, u32[]{:S(2)}) collective-permute-start(bf16[128,1024]{1,0:T(8,128)(2,1)S(1)} %get-tuple-element.122.refs_7_), channel_id=1, source_target_pairs={{0,16},{16,0},{1,17},{17,1},{2,18},{18,2},{3,19},{19,3},{4,20},{20... | collective-permute-start | bytes 786440 | tf_op jit(solution)/shard_map/ppermute | solution.py:358
  24.2 10.7 %collective-permute-start.9 = (bf16[192,512]{1,0:T(8,128)(2,1)S(1)}, bf16[192,512]{1,0:T(8,128)(2,1)S(1)}, u32[]{:S(2)}, u32[]{:S(2)}) collective-permute-start(bf16[192,512]{1,0:T(8,128)(2,1)S(1)} %get-tuple-element.120.mine), channel_id=1, source_target_pairs={{0,16},{16,0},{1,17},{17,1},{2,18},{18,2},{3,19},{19,3},{4,20},{20... | collective-permute-start | bytes 589832 | tf_op jit(solution)/shard_map/ppermute | solution.py:358
  30.3 19.1 %collective-permute-start.14 = (bf16[128,2048]{1,0:T(8,128)(2,1)S(1)}, bf16[128,2048]{1,0:T(8,128)(2,1)S(1)}, u32[]{:S(2)}, u32[]{:S(2)}) collective-permute-start(bf16[128,2048]{1,0:T(8,128)(2,1)S(1)} %collective-permute-done.6.from_x), channel_id=1, source_target_pairs={{0,1},{1,0},{2,3},{3,2},{4,5},{5,4},{6,7},{7,6},{8,9},{9,8},{10,11... | collective-permute-start | bytes 1572872 | tf_op jit(solution)/shard_map/ppermute | solution.py:352
  35.0 12.8 %collective-permute-start.19 = (bf16[128,1024]{1,0:T(8,128)(2,1)S(1)}, bf16[128,1024]{1,0:T(8,128)(2,1)S(1)}, u32[]{:S(2)}, u32[]{:S(2)}) collective-permute-start(bf16[128,1024]{1,0:T(8,128)(2,1)S(1)} %get-tuple-element.148), channel_id=1, source_target_pairs={{0,8},{1,9},{2,10},{3,11},{4,12},{5,13},{6,14},{7,15},{8,0},{9,1},... | collective-permute-start | bytes 786440 | tf_op jit(solution)/shard_map/ppermute | solution.py:355
  35.5 12.4 %collective-permute-start.11 = (bf16[256,512]{1,0:T(8,128)(2,1)S(1)}, bf16[256,512]{1,0:T(8,128)(2,1)S(1)}, u32[]{:S(2)}, u32[]{:S(2)}) collective-permute-start(bf16[256,512]{1,0:T(8,128)(2,1)S(1)} %collective-permute-done.7.refs_0_), channel_id=1, source_target_pairs={{0,16},{16,0},{1,17},{17,1},{2,18},{18,2},{3,19},{19,3},{4,20},{20... | collective-permute-start | bytes 786440 | tf_op jit(solution)/shard_map/ppermute | solution.py:358
  36.7 11.1 %collective-permute-start.12 = (bf16[256,512]{1,0:T(8,128)(2,1)S(1)}, bf16[256,512]{1,0:T(8,128)(2,1)S(1)}, u32[]{:S(2)}, u32[]{:S(2)}) collective-permute-start(bf16[256,512]{1,0:T(8,128)(2,1)S(1)} %collective-permute-done.8.refs_1_), channel_id=1, source_target_pairs={{0,16},{16,0},{1,17},{17,1},{2,18},{18,2},{3,19},{19,3},{4,20},{20... | collective-permute-start | bytes 786440 | tf_op jit(solution)/shard_map/ppermute | solution.py:358
  37.5 11.9 %collective-permute-start.13 = (bf16[256,512]{1,0:T(8,128)(2,1)S(1)}, bf16[256,512]{1,0:T(8,128)(2,1)S(1)}, u32[]{:S(2)}, u32[]{:S(2)}) collective-permute-start(bf16[256,512]{1,0:T(8,128)(2,1)S(1)} %collective-permute-done.8.refs_1_), channel_id=1, source_target_pairs={{0,4},{1,5},{2,6},{3,7},{4,0},{5,1},{6,2},{7,3},{8,12},{9,13},{10,... | collective-permute-start | bytes 786440 | tf_op jit(solution)/shard_map/ppermute | solution.py:355
  47.8 10.2 %collective-permute-start.15 = (bf16[8,128,128]{2,1,0:T(8,128)(2,1)S(1)}, bf16[8,128,128]{2,1,0:T(8,128)(2,1)S(1)}, u32[]{:S(2)}, u32[]{:S(2)}) collective-permute-start(bf16[8,128,128]{2,1,0:T(8,128)(2,1)S(1)} %get-tuple-element.132), channel_id=1, source_target_pairs={{0,1},{1,0},{2,3},{3,2},{4,5},{5,4},{6,7},{7,6},{8,9},{9,8},{10,11... | collective-permute-start | bytes 786440 | tf_op jit(solution)/shard_map/ppermute | solution.py:352
  47.8 8.7 %collective-permute-start.20 = (bf16[128,1024]{1,0:T(8,128)(2,1)S(1)}, bf16[128,1024]{1,0:T(8,128)(2,1)S(1)}, u32[]{:S(2)}, u32[]{:S(2)}) collective-permute-start(bf16[128,1024]{1,0:T(8,128)(2,1)S(1)} %collective-permute-done.19.refs_0_), channel_id=1, source_target_pairs={{0,4},{1,5},{2,6},{3,7},{4,0},{5,1},{6,2},{7,3},{8,12},{9,13},{10,... | collective-permute-start | bytes 786440 | tf_op jit(solution)/shard_map/ppermute | solution.py:355
  49.3 8.6 %collective-permute-start.18 = (bf16[256,512]{1,0:T(8,128)(2,1)S(1)}, bf16[256,512]{1,0:T(8,128)(2,1)S(1)}, u32[]{:S(2)}, u32[]{:S(2)}) collective-permute-start(bf16[256,512]{1,0:T(8,128)(2,1)S(1)} %collective-permute-done.13.refs_2_), channel_id=1, source_target_pairs={{0,16},{16,0},{1,17},{17,1},{2,18},{18,2},{3,19},{19,3},{4,20},{20... | collective-permute-start | bytes 786440 | tf_op jit(solution)/shard_map/ppermute | solution.py:358
  50.7 6.4 %collective-permute-start.16 = (bf16[4,128,128]{2,1,0:T(8,128)(2,1)S(1)}, bf16[4,128,128]{2,1,0:T(8,128)(2,1)S(1)}, u32[]{:S(2)}, u32[]{:S(2)}) collective-permute-start(bf16[4,128,128]{2,1,0:T(8,128)(2,1)S(1)} %get-tuple-element.133), channel_id=1, source_target_pairs={{0,2},{1,3},{2,0},{3,1},{4,6},{5,7},{6,4},{7,5},{8,10},{9,11},{10,... | collective-permute-start | bytes 393224 | tf_op jit(solution)/shard_map/ppermute | solution.py:352
  52.2 5.8 %collective-permute-start.17 = (bf16[4,128,128]{2,1,0:T(8,128)(2,1)S(1)}, bf16[4,128,128]{2,1,0:T(8,128)(2,1)S(1)}, u32[]{:S(2)}, u32[]{:S(2)}) collective-permute-start(bf16[4,128,128]{2,1,0:T(8,128)(2,1)S(1)} %get-tuple-element.134), channel_id=1, source_target_pairs={{0,3},{1,2},{2,1},{3,0},{4,7},{5,6},{6,5},{7,4},{8,11},{9,10},{10,... | collective-permute-start | bytes 393224 | tf_op jit(solution)/shard_map/ppermute | solution.py:352
  57.1 8.8 %copy-start = (bf16[17,256,256]{2,1,0:T(8,128)(2,1)S(1)}, bf16[17,256,256]{2,1,0:T(8,128)(2,1)}, u32[]{:S(2)}) copy-start(bf16[17,256,256]{2,1,0:T(8,128)(2,1)} %constant.45.clone.refs_5_.refs_9_) | copy-start | bytes 6684676
  57.1 8.8 %copy-start.4 = (bf16[512,256]{1,0:T(8,128)(2,1)S(1)}, bf16[512,256]{1,0:T(8,128)(2,1)}, u32[]{:S(2)}) copy-start(bf16[512,256]{1,0:T(8,128)(2,1)} %constant.43.clone.refs_4_.refs_7_) | copy-start | bytes 786436
  60.0 15.4 %copy-start.5 = (f32[3,2048]{1,0:T(4,128)S(1)}, f32[3,2048]{1,0:T(4,128)}, u32[]{:S(2)}) copy-start(f32[3,2048]{1,0:T(4,128)} %refs_4_.2) | copy-start | bytes 73732
  60.0 15.4 %copy-start.6 = (f32[2048]{0:T(1024)S(1)}, f32[2048]{0:T(1024)}, u32[]{:S(2)}) copy-start(f32[2048]{0:T(1024)} %param.16) | copy-start | bytes 24580
  60.0 15.4 %copy-start.7 = (bf16[17,256,256]{2,1,0:T(8,128)(2,1)S(1)}, bf16[17,256,256]{2,1,0:T(8,128)(2,1)}, u32[]{:S(2)}) copy-start(bf16[17,256,256]{2,1,0:T(8,128)(2,1)} %constant.46.clone.refs_10_) | copy-start | bytes 6684676
  60.1 15.4 %copy-start.8 = (bf16[256,512]{1,0:T(8,128)(2,1)S(1)}, bf16[256,512]{1,0:T(8,128)(2,1)}, u32[]{:S(2)}) copy-start(bf16[256,512]{1,0:T(8,128)(2,1)} %constant.44.clone.refs_8_) | copy-start | bytes 786436
  60.1 8.3 %collective-permute-start.21 = (bf16[512,128]{1,0:T(8,128)(2,1)S(1)}, bf16[512,128]{1,0:T(8,128)(2,1)S(1)}, u32[]{:S(2)}, u32[]{:S(2)}) collective-permute-start(bf16[512,128]{1,0:T(8,128)(2,1)S(1)} %get-tuple-element.150), channel_id=1, source_target_pairs={{0,12},{1,13},{2,14},{3,15},{4,8},{5,9},{6,10},{7,11},{8,4},{9,5},... | collective-permute-start | bytes 393224 | tf_op jit(solution)/shard_map/ppermute | solution.py:355
  60.8 14.7 %collective-permute-start.22 = (bf16[512,128]{1,0:T(8,128)(2,1)S(1)}, bf16[512,128]{1,0:T(8,128)(2,1)S(1)}, u32[]{:S(2)}, u32[]{:S(2)}) collective-permute-start(bf16[512,128]{1,0:T(8,128)(2,1)S(1)} %get-tuple-element.151), channel_id=1, source_target_pairs={{0,8},{1,9},{2,10},{3,11},{4,12},{5,13},{6,14},{7,15},{8,0},{9,1},... | collective-permute-start | bytes 393224 | tf_op jit(solution)/shard_map/ppermute | solution.py:355
  62.8 12.7 %collective-permute-start.23 = (bf16[512,128]{1,0:T(8,128)(2,1)S(1)}, bf16[512,128]{1,0:T(8,128)(2,1)S(1)}, u32[]{:S(2)}, u32[]{:S(2)}) collective-permute-start(bf16[512,128]{1,0:T(8,128)(2,1)S(1)} %get-tuple-element.152), channel_id=1, source_target_pairs={{0,4},{1,5},{2,6},{3,7},{4,0},{5,1},{6,2},{7,3},{8,12},{9,13},{10,... | collective-permute-start | bytes 393224 | tf_op jit(solution)/shard_map/ppermute | solution.py:355
  64.5 14.0 %collective-permute-start.24 = (bf16[256,1024]{1,0:T(8,128)(2,1)S(1)}, bf16[256,1024]{1,0:T(8,128)(2,1)S(1)}, u32[]{:S(2)}, u32[]{:S(2)}) collective-permute-start(bf16[256,1024]{1,0:T(8,128)(2,1)S(1)} %shard_map.119.refs_8_), channel_id=1, source_target_pairs={{0,16},{16,0},{1,17},{17,1},{2,18},{18,2},{3,19},{19,3},{4,20},{20... | collective-permute-start | bytes 1572872 | tf_op jit(solution)/shard_map/ppermute | solution.py:358
  65.3 13.2 %collective-permute-start.25 = (bf16[256,512]{1,0:T(8,128)(2,1)S(1)}, bf16[256,512]{1,0:T(8,128)(2,1)S(1)}, u32[]{:S(2)}, u32[]{:S(2)}) collective-permute-start(bf16[256,512]{1,0:T(8,128)(2,1)S(1)} %get-tuple-element.172), channel_id=1, source_target_pairs={{0,2},{1,3},{2,0},{3,1},{4,6},{5,7},{6,4},{7,5},{8,10},{9,11},{10,... | collective-permute-start | bytes 786440 | tf_op jit(solution)/shard_map/ppermute | solution.py:352
  75.5 12.3 %copy-start.1 = (bf16[128,2048]{1,0:T(8,128)(2,1)S(1)}, bf16[128,2048]{1,0:T(8,128)(2,1)}, u32[]{:S(2)}) copy-start(bf16[128,2048]{1,0:T(8,128)(2,1)} %refs_6_.1) | copy-start | bytes 1572868
  78.5 9.2 %collective-permute-start.29 = (bf16[128,512]{1,0:T(8,128)(2,1)S(1)}, bf16[128,512]{1,0:T(8,128)(2,1)S(1)}, u32[]{:S(2)}, u32[]{:S(2)}) collective-permute-start(bf16[128,512]{1,0:T(8,128)(2,1)S(1)} %slice.3), channel_id=1, source_target_pairs={{0,1},{1,0},{2,3},{3,2},{4,5},{5,4},{6,7},{7,6},{8,9},{9,8},{10,11... | collective-permute-start | bytes 393224 | tf_op jit(solution)/shard_map/ppermute | solution.py:352
  78.6 6.9 %collective-permute-start.26 = (bf16[256,128]{1,0:T(8,128)(2,1)S(1)}, bf16[256,128]{1,0:T(8,128)(2,1)S(1)}, u32[]{:S(2)}, u32[]{:S(2)}) collective-permute-start(bf16[256,128]{1,0:T(8,128)(2,1)S(1)} %get-tuple-element.173), channel_id=1, source_target_pairs={{0,12},{1,13},{2,14},{3,15},{4,8},{5,9},{6,10},{7,11},{8,4},{9,5},... | collective-permute-start | bytes 196616 | tf_op jit(solution)/shard_map/ppermute | solution.py:355
  80.0 7.7 %collective-permute-start.27 = (bf16[256,128]{1,0:T(8,128)(2,1)S(1)}, bf16[256,128]{1,0:T(8,128)(2,1)S(1)}, u32[]{:S(2)}, u32[]{:S(2)}) collective-permute-start(bf16[256,128]{1,0:T(8,128)(2,1)S(1)} %get-tuple-element.174), channel_id=1, source_target_pairs={{0,8},{1,9},{2,10},{3,11},{4,12},{5,13},{6,14},{7,15},{8,0},{9,1},... | collective-permute-start | bytes 196616 | tf_op jit(solution)/shard_map/ppermute | solution.py:355
  80.3 7.5 %collective-permute-start.28 = (bf16[256,128]{1,0:T(8,128)(2,1)S(1)}, bf16[256,128]{1,0:T(8,128)(2,1)S(1)}, u32[]{:S(2)}, u32[]{:S(2)}) collective-permute-start(bf16[256,128]{1,0:T(8,128)(2,1)S(1)} %get-tuple-element.175), channel_id=1, source_target_pairs={{0,4},{1,5},{2,6},{3,7},{4,0},{5,1},{6,2},{7,3},{8,12},{9,13},{10,... | collective-permute-start | bytes 196616 | tf_op jit(solution)/shard_map/ppermute | solution.py:355
  89.2 2.0 %collective-permute-start.30 = (bf16[128,2048]{1,0:T(8,128)(2,1)S(1)}, bf16[128,2048]{1,0:T(8,128)(2,1)S(1)}, u32[]{:S(2)}, u32[]{:S(2)}) collective-permute-start(bf16[128,2048]{1,0:T(8,128)(2,1)S(1)} %get-tuple-element.190), channel_id=1, source_target_pairs={{0,1},{1,0},{2,3},{3,2},{4,5},{5,4},{6,7},{7,6},{8,9},{9,8},{10,11... | collective-permute-start | bytes 1572872 | tf_op jit(solution)/shard_map/ppermute | solution.py:352
  91.2 14.0 %collective-permute-start.38 = (bf16[128,2048]{1,0:T(8,128)(2,1)S(1)}, bf16[128,2048]{1,0:T(8,128)(2,1)S(1)}, u32[]{:S(2)}, u32[]{:S(2)}) collective-permute-start(bf16[128,2048]{1,0:T(8,128)(2,1)S(1)} %add_convert_fusion.1), channel_id=1, source_target_pairs={{0,2},{1,3},{2,0},{3,1},{4,6},{5,7},{6,4},{7,5},{8,10},{9,11},{10,... | collective-permute-start | bytes 1572872 | tf_op jit(solution)/shard_map/ppermute | solution.py:352
  92.1 4.8 %collective-permute-start.31 = (bf16[256,128]{1,0:T(8,128)(2,1)S(1)}, bf16[256,128]{1,0:T(8,128)(2,1)S(1)}, u32[]{:S(2)}, u32[]{:S(2)}) collective-permute-start(bf16[256,128]{1,0:T(8,128)(2,1)S(1)} %get-tuple-element.196), channel_id=1, source_target_pairs={{0,4},{1,5},{2,6},{3,7},{4,0},{5,1},{6,2},{7,3},{8,12},{9,13},{10,... | collective-permute-start | bytes 196616 | tf_op jit(solution)/shard_map/ppermute | solution.py:355
  92.1 7.6 %collective-permute-start.32 = (bf16[256,128]{1,0:T(8,128)(2,1)S(1)}, bf16[256,128]{1,0:T(8,128)(2,1)S(1)}, u32[]{:S(2)}, u32[]{:S(2)}) collective-permute-start(bf16[256,128]{1,0:T(8,128)(2,1)S(1)} %get-tuple-element.197), channel_id=1, source_target_pairs={{0,8},{1,9},{2,10},{3,11},{4,12},{5,13},{6,14},{7,15},{8,0},{9,1},... | collective-permute-start | bytes 196616 | tf_op jit(solution)/shard_map/ppermute | solution.py:355
  94.4 6.1 %collective-permute-start.33 = (bf16[256,128]{1,0:T(8,128)(2,1)S(1)}, bf16[256,128]{1,0:T(8,128)(2,1)S(1)}, u32[]{:S(2)}, u32[]{:S(2)}) collective-permute-start(bf16[256,128]{1,0:T(8,128)(2,1)S(1)} %get-tuple-element.198), channel_id=1, source_target_pairs={{0,12},{1,13},{2,14},{3,15},{4,8},{5,9},{6,10},{7,11},{8,4},{9,5},... | collective-permute-start | bytes 196616 | tf_op jit(solution)/shard_map/ppermute | solution.py:355
  101.8 1.4 %collective-permute-start.34 = (bf16[128,512]{1,0:T(8,128)(2,1)S(1)}, bf16[128,512]{1,0:T(8,128)(2,1)S(1)}, u32[]{:S(2)}, u32[]{:S(2)}) collective-permute-start(bf16[128,512]{1,0:T(8,128)(2,1)S(1)} %get-tuple-element.202), channel_id=1, source_target_pairs={{0,1},{1,0},{2,3},{3,2},{4,5},{5,4},{6,7},{7,6},{8,9},{9,8},{10,11... | collective-permute-start | bytes 393224 | tf_op jit(solution)/shard_map/ppermute | solution.py:352
  101.9 1.5 %collective-permute-start.35 = (bf16[128,512]{1,0:T(8,128)(2,1)S(1)}, bf16[128,512]{1,0:T(8,128)(2,1)S(1)}, u32[]{:S(2)}, u32[]{:S(2)}) collective-permute-start(bf16[128,512]{1,0:T(8,128)(2,1)S(1)} %get-tuple-element.203), channel_id=1, source_target_pairs={{0,1},{1,0},{2,3},{3,2},{4,5},{5,4},{6,7},{7,6},{8,9},{9,8},{10,11... | collective-permute-start | bytes 393224 | tf_op jit(solution)/shard_map/ppermute | solution.py:352
  102.4 1.3 %collective-permute-start.36 = (bf16[128,512]{1,0:T(8,128)(2,1)S(1)}, bf16[128,512]{1,0:T(8,128)(2,1)S(1)}, u32[]{:S(2)}, u32[]{:S(2)}) collective-permute-start(bf16[128,512]{1,0:T(8,128)(2,1)S(1)} %get-tuple-element.204), channel_id=1, source_target_pairs={{0,1},{1,0},{2,3},{3,2},{4,5},{5,4},{6,7},{7,6},{8,9},{9,8},{10,11... | collective-permute-start | bytes 393224 | tf_op jit(solution)/shard_map/ppermute | solution.py:352
  102.4 1.5 %collective-permute-start.37 = (bf16[128,512]{1,0:T(8,128)(2,1)S(1)}, bf16[128,512]{1,0:T(8,128)(2,1)S(1)}, u32[]{:S(2)}, u32[]{:S(2)}) collective-permute-start(bf16[128,512]{1,0:T(8,128)(2,1)S(1)} %get-tuple-element.205), channel_id=1, source_target_pairs={{0,1},{1,0},{2,3},{3,2},{4,5},{5,4},{6,7},{7,6},{8,9},{9,8},{10,11... | collective-permute-start | bytes 393224 | tf_op jit(solution)/shard_map/ppermute | solution.py:352

commit v8 on v7

--- a/solution.py
+++ b/solution.py
@@ -294,45 +294,43 @@
             ]
 
 
-def mixed_dots(planes, pos, u, gate, ws, mixed, outs):
-    share = u[0].shape[1]
-    rows = u[0].shape[0] // 2
+def mixed_dot(planes, pos, u, gate, ws, mixed, outs, half):
+    rows, share = mixed.shape[0], u[0].shape[1]
     for s in range(planes):
         plane = jnp.bitwise_xor(pos[1], s)
-        for d in range(2):
-            if len(gate[d].shape) == 3:
-                columns = gate[d][planes + plane]
-            else:
-                columns = gate[d][:rows, pl.ds(pl.multiple_of(plane * share, share), share)]
-            mixed[d * rows : (d + 1) * rows, s * share : (s + 1) * share] = (
-                columns.astype(jnp.float32)
-                * u[s][d * rows : (d + 1) * rows, :].astype(jnp.float32)
-            ).astype(mixed.dtype)
+        if len(gate.shape) == 3:
+            columns = gate[planes + plane]
+        else:
+            columns = gate[:rows, pl.ds(pl.multiple_of(plane * share, share), share)]
+        mixed[:, s * share : (s + 1) * share] = (
+            columns.astype(jnp.float32)
+            * u[s][half * rows : (half + 1) * rows, :].astype(jnp.float32)
+        ).astype(mixed.dtype)
     got = dot(mixed[...], ws[...])
-    outs[0][...] = got[:rows].astype(outs[0].dtype)
-    width = outs[1].shape[1]
-    for i, out in enumerate(outs[1:]):
-        out[...] = got[rows:, i * width : (i + 1) * width].astype(out.dtype)
+    width = outs[0].shape[1]
+    for i, out in enumerate(outs):
+        out[...] = got[:, i * width : (i + 1) * width].astype(out.dtype)
 
 
 def upper_kernel(planes, pos, *refs):
-    u, gate = refs[:planes], refs[planes : planes + 2]
-    own, halves = refs[planes + 2], refs[planes + 3 : planes + 7]
-    outs, ws, mixed = refs[planes + 7 : -2], refs[-2], refs[-1]
+    u, gate = refs[:planes], refs[planes]
+    own, halves = refs[planes + 1], refs[planes + 2 : planes + 6]
+    out, ws, mixed = refs[planes + 6 :]
     share = u[0].shape[1]
     width = halves[0].shape[1]
     ws[:share, :] = own[...]
     for k in range(2):
         side = pos[0] if k == 0 else 1 - pos[0]
         columns = pl.ds(pl.multiple_of(side * width, width), width)
-        ws[share : 2 * share, columns] = halves[2 * k][...]
-        ws[2 * share :, columns] = halves[2 * k + 1][...]
-    mixed_dots(planes, pos, u, gate, ws, mixed, outs)
-
-
-def lower_kernel(planes, pos, *refs):
-    u, gate, ws = refs[:planes], refs[planes : planes + 2], refs[planes + 2]
-    mixed_dots(planes, pos, u, gate, ws, refs[-1], refs[planes + 3 : -1])
+        near, far = halves[2 * k : 2 * k + 2]
+        ws[share : 2 * share, columns] = near[:share, :]
+        ws[2 * share :, columns] = far[...]
+    mixed_dot(planes, pos, u, gate, ws, mixed, (out,), 1)
+
+
+def place_kernel(planes, half, pos, *refs):
+    u, gate, ws = refs[:planes], refs[planes], refs[planes + 1]
+    mixed_dot(planes, pos, u, gate, ws, refs[-1], refs[planes + 2 : -1], half)
 
 
 def local(inputs, gate_in, value_weight, short_taps, filter_taps, skip_scale, output_weight):
@@ -507,33 +505,37 @@
     gate_three = to_place(gate_x[rows:], 1)
     upper, lower, gate_three = stage((upper[::-1], mixed[:planes], gate_three))
     upper = upper[::-1]
-    scratch = [pltpu.VMEM((2 * rows, wide), jnp.bfloat16)]
-    flops = 4 * rows * features * wide
-    partial_two, partial_three, gathered = call(
+    scratch = [pltpu.VMEM((rows, wide), jnp.bfloat16)]
+    flops = 2 * rows * features * wide
+    partial_three, gathered = call(
         functools.partial(upper_kernel, planes),
-        [shaped(rows, features, dtype=jnp.float32), shaped(rows, features)]
-        + [shaped(wide, features)],
+        [shaped(rows, features), shaped(wide, features)],
         scratch,
         pos,
-        [*upper, gate_x, gate_three, output_weight]
-        + [out_near, weights, out_other, weights_other],
+        [*upper, gate_three, output_weight, out_near, weights, out_other, weights_other],
         flops,
         vmem=8,
     )
+
+    def partial_of(parts, half, gate, cost, pieces, dtype):
+        return call(
+            functools.partial(place_kernel, planes, half),
+            [shaped(rows, features // pieces, dtype=dtype)] * pieces,
+            scratch,
+            pos,
+            [*parts, gate, gathered],
+            cost,
+            vmem=8,
+        )
+
+    partial_two = partial_of(upper, 0, gate_x, flops, 1, jnp.float32)[0]
     across = partial_two + to_place(partial_three, 1).astype(jnp.float32)
     across, lower = stage((across.astype(jnp.bfloat16), lower))
 
     across = to_place(across, 2)
     lower = spread(lower)
-    partial_zero, *partial_one = call(
-        functools.partial(lower_kernel, planes),
-        [shaped(rows, features, dtype=jnp.float32)] + [shaped(rows, features // 4)] * 4,
-        scratch,
-        pos,
-        [*lower, gate_own, taps_parts[1], gathered],
-        0,
-        vmem=8,
-    )
+    partial_one = partial_of(lower, 1, taps_parts[1], 0, 4, jnp.bfloat16)
+    partial_zero = partial_of(lower, 0, gate_own, 0, 1, jnp.float32)[0]
     partial_one = jnp.concatenate([to_place(block, 1) for block in partial_one], 1)
     result = partial_zero + partial_one.astype(jnp.float32) + across.astype(jnp.float32)
     return result.astype(jnp.bfloat16)

time: 106 us -> 106 us (level)
  waiting for transfers between devices: 46.9 us -> 44.2 us
  Pallas kernels: 17.9 us -> 19.3 us
    ppermute x15, waiting for transfers between devices: 29.9 us -> 25.3 us  [to_plane(): lax.ppermute(block, 'seq', [(i, i ^ s * PLANE) for i in range(devices)])]
    ppermute x6, waiting for transfers between devices: 4.69 us -> 8.75 us  [to_group(): return lax.ppermute(block, 'groups', [(0, 1), (1, 0)])]
    ppermute x17, waiting for transfers between devices: 11.9 us -> 9.63 us  [to_place(): return lax.ppermute(block, 'seq', [(i, i ^ d) for i in range(devices)])]
    pallas_call x15 -> x17, Pallas kernels: 17.9 us -> 19.3 us  [call(): pl.pallas_call(kernel, out_shape=outs, in_specs=in_specs, out_specs=[pl.B...]
    ppermute x15, starting transfers between devices: 22.9 us -> 24.1 us  [to_plane(): lax.ppermute(block, 'seq', [(i, i ^ s * PLANE) for i in range(devices)])]
  transfers between devices with their start and end apart: 39 -> 39, of which waited for: 23 -> 19; matrix products, arithmetic and copies ran while one was open for 0% -> 0% of each run, Pallas kernels for 14% -> 15%
where the time goes in v8:
time: 106 us
  waiting for transfers between devices  44.2 us (42%)
  starting transfers between devices  40.7 us (38%)
  Pallas kernels  19.3 us (18%)
  other arithmetic  1.14 us (1%)
    ppermute x15, waiting for transfers between devices, to_plane(): lax.ppermute(block, 'seq', [(i, i ^ s * PLANE) for i in range(devices)])  25.3 us
    ppermute x15, starting transfers between devices, to_plane(): lax.ppermute(block, 'seq', [(i, i ^ s * PLANE) for i in range(devices)])  24.1 us
    pallas_call x17, Pallas kernels, call(): pl.pallas_call(kernel, out_shape=outs, in_specs=in_specs, out_specs=[pl.B...  19.3 us
    ppermute x17, waiting for transfers between devices, to_place(): return lax.ppermute(block, 'seq', [(i, i ^ d) for i in range(devices)])  9.63 us
    ppermute x6, waiting for transfers between devices, to_group(): return lax.ppermute(block, 'groups', [(0, 1), (1, 0)])  8.75 us
    ppermute x17, starting transfers between devices, to_place(): return lax.ppermute(block, 'seq', [(i, i ^ d) for i in range(devices)])  8.69 us
    ppermute x6, starting transfers between devices, to_group(): return lax.ppermute(block, 'groups', [(0, 1), (1, 0)])  5.26 us
    ppermute x1, starting transfers between devices, local(): taps_whole = lax.ppermute(taps_whole, ('groups', 'seq'), route)  2.59 us
  transfers between devices with their start and end apart: 39, of which 19 were waited for; matrix products, arithmetic and copies ran while one was open for 0% of the time, Pallas kernels for 15%

profile of v8, /device:TPU:0, one launch (start us, length us, event | category | flops | bytes accessed | tf_op | source)
XLA Modules:
  0.0 105.7 jit_solution(9884932306088657131)
XLA Ops:
  0.5 1.8 %shard_map.111 = (bf16[128,512]{1,0:T(8,128)(2,1)S(1)}, bf16[128,512]{1,0:T(8,128)(2,1)S(1)}, bf16[160,1024]{1,0:T(8,128)(2,1)S(1)}, bf16[128,1024]{1,0:T(8,128)(2,1)S(1)}) custom-call(s32[3]{0:T(128)S(1)} %pad_add_fusion.pos, bf16[128,2048]{1,0:T(8,128)(2,1)} %taps.1, bf16[128,2048]{1,0:T(8,128)(2,1)} %refs_5_.2), custom_call_target="tpu_custom_call" | custom-call | tf_op jit(solution)/shard_map/pallas_call | solution.py:60
  2.4 2.7 %collective-permute-start.5 = (bf16[160,1024]{1,0:T(8,128)(2,1)S(1)}, bf16[160,1024]{1,0:T(8,128)(2,1)S(1)}, u32[]{:S(2)}, u32[]{:S(2)}) collective-permute-start(bf16[160,1024]{1,0:T(8,128)(2,1)S(1)} %get-tuple-element.109), channel_id=1, source_target_pairs={{0,4},{1,5},{2,6},{3,7},{4,0},{5,1},{6,2},{7,3},{8,12},{9,13},{10,... | collective-permute-start | bytes 983048 | tf_op jit(solution)/shard_map/ppermute | solution.py:353
  5.0 1.8 %shard_map.109 = (bf16[128,512]{1,0:T(8,128)(2,1)S(1)}, bf16[128,512]{1,0:T(8,128)(2,1)S(1)}, bf16[128,512]{1,0:T(8,128)(2,1)S(1)}, bf16[128,512]{1,0:T(8,128)(2,1)S(1)}) custom-call(s32[3]{0:T(128)S(1)} %pad_add_fusion.pos, bf16[128,2048]{1,0:T(8,128)(2,1)} %weight.1), custom_call_target="tpu_custom_call" | custom-call | tf_op jit(solution)/shard_map/pallas_call | solution.py:60
  7.1 1.5 %collective-permute-start.1 = (bf16[128,512]{1,0:T(8,128)(2,1)S(1)}, bf16[128,512]{1,0:T(8,128)(2,1)S(1)}, u32[]{:S(2)}, u32[]{:S(2)}) collective-permute-start(bf16[128,512]{1,0:T(8,128)(2,1)S(1)} %get-tuple-element.106), channel_id=1, source_target_pairs={{0,2},{1,3},{2,0},{3,1},{4,6},{5,7},{6,4},{7,5},{8,10},{9,11},{10,... | collective-permute-start | bytes 393224 | tf_op jit(solution)/shard_map/ppermute | solution.py:350
  8.8 2.6 %collective-permute-start.3 = (bf16[128,512]{1,0:T(8,128)(2,1)S(1)}, bf16[128,512]{1,0:T(8,128)(2,1)S(1)}, u32[]{:S(2)}, u32[]{:S(2)}) collective-permute-start(bf16[128,512]{1,0:T(8,128)(2,1)S(1)} %get-tuple-element.108), channel_id=1, source_target_pairs={{0,8},{1,9},{2,10},{3,11},{4,12},{5,13},{6,14},{7,15},{8,0},{9,1},... | collective-permute-start | bytes 393224 | tf_op jit(solution)/shard_map/ppermute | solution.py:409
  11.9 0.9 shard_map.113
  13.4 1.6 %collective-permute-done.2.refs_3_ = bf16[128,512]{1,0:T(8,128)(2,1)S(1)} collective-permute-done((bf16[128,512]{1,0:T(8,128)(2,1)S(1)}, bf16[128,512]{1,0:T(8,128)(2,1)S(1)}, u32[]{:S(2)}, u32[]{:S(2)}) %collective-permute-start.2) | collective-permute-done | bytes 131104 | tf_op jit(solution)/shard_map/ppermute | solution.py:350
  16.2 1.7 %collective-permute-start.6 = (bf16[128,2048]{1,0:T(8,128)(2,1)S(1)}, bf16[128,2048]{1,0:T(8,128)(2,1)S(1)}, u32[]{:S(2)}, u32[]{:S(2)}) collective-permute-start(bf16[128,2048]{1,0:T(8,128)(2,1)S(1)} %copy-done.2), channel_id=1, source_target_pairs={{0,2},{1,3},{2,0},{3,1},{4,6},{5,7},{6,4},{7,5},{8,10},{9,11},{10,... | collective-permute-start | bytes 1572872 | tf_op jit(solution)/shard_map/ppermute | solution.py:350
  17.9 2.7 %collective-permute-start.7 = (bf16[256,512]{1,0:T(8,128)(2,1)S(1)}, bf16[256,512]{1,0:T(8,128)(2,1)S(1)}, u32[]{:S(2)}, u32[]{:S(2)}) collective-permute-start(bf16[256,512]{1,0:T(8,128)(2,1)S(1)} %shard_map.112), channel_id=1, source_target_pairs={{0,4},{1,5},{2,6},{3,7},{4,0},{5,1},{6,2},{7,3},{8,12},{9,13},{10,... | collective-permute-start | bytes 786440 | tf_op jit(solution)/shard_map/ppermute | solution.py:353
  20.6 2.5 %collective-permute-start.8 = (bf16[256,512]{1,0:T(8,128)(2,1)S(1)}, bf16[256,512]{1,0:T(8,128)(2,1)S(1)}, u32[]{:S(2)}, u32[]{:S(2)}) collective-permute-start(bf16[256,512]{1,0:T(8,128)(2,1)S(1)} %shard_map.112), channel_id=1, source_target_pairs={{0,8},{1,9},{2,10},{3,11},{4,12},{5,13},{6,14},{7,15},{8,0},{9,1},... | collective-permute-start | bytes 786440 | tf_op jit(solution)/shard_map/ppermute | solution.py:353
  24.2 1.5 %collective-permute-start.9 = (bf16[192,512]{1,0:T(8,128)(2,1)S(1)}, bf16[192,512]{1,0:T(8,128)(2,1)S(1)}, u32[]{:S(2)}, u32[]{:S(2)}) collective-permute-start(bf16[192,512]{1,0:T(8,128)(2,1)S(1)} %get-tuple-element.118.mine), channel_id=1, source_target_pairs={{0,16},{16,0},{1,17},{17,1},{2,18},{18,2},{3,19},{19,3},{4,20},{20... | collective-permute-start | bytes 589832 | tf_op jit(solution)/shard_map/ppermute | solution.py:356
  25.7 4.6 %collective-permute-done.6.from_x = bf16[128,2048]{1,0:T(8,128)(2,1)S(1)} collective-permute-done((bf16[128,2048]{1,0:T(8,128)(2,1)S(1)}, bf16[128,2048]{1,0:T(8,128)(2,1)S(1)}, u32[]{:S(2)}, u32[]{:S(2)}) %collective-permute-start.6) | collective-permute-done | bytes 524320 | tf_op jit(solution)/shard_map/ppermute | solution.py:350
  30.3 4.7 %collective-permute-done.9.other = bf16[192,512]{1,0:T(8,128)(2,1)S(1)} collective-permute-done((bf16[192,512]{1,0:T(8,128)(2,1)S(1)}, bf16[192,512]{1,0:T(8,128)(2,1)S(1)}, u32[]{:S(2)}, u32[]{:S(2)}) %collective-permute-start.9) | collective-permute-done | bytes 196640 | tf_op jit(solution)/shard_map/ppermute | solution.py:356
  35.4 1.3 %collective-permute-start.19 = (bf16[128,1024]{1,0:T(8,128)(2,1)S(1)}, bf16[128,1024]{1,0:T(8,128)(2,1)S(1)}, u32[]{:S(2)}, u32[]{:S(2)}) collective-permute-start(bf16[128,1024]{1,0:T(8,128)(2,1)S(1)} %get-tuple-element.146), channel_id=1, source_target_pairs={{0,8},{1,9},{2,10},{3,11},{4,12},{5,13},{6,14},{7,15},{8,0},{9,1},... | collective-permute-start | bytes 786440 | tf_op jit(solution)/shard_map/ppermute | solution.py:353
  36.7 0.8 collective-permute-start.12
  37.5 1.8 %collective-permute-start.13 = (bf16[256,512]{1,0:T(8,128)(2,1)S(1)}, bf16[256,512]{1,0:T(8,128)(2,1)S(1)}, u32[]{:S(2)}, u32[]{:S(2)}) collective-permute-start(bf16[256,512]{1,0:T(8,128)(2,1)S(1)} %collective-permute-done.8.refs_1_), channel_id=1, source_target_pairs={{0,4},{1,5},{2,6},{3,7},{4,0},{5,1},{6,2},{7,3},{8,12},{9,13},{10,... | collective-permute-start | bytes 786440 | tf_op jit(solution)/shard_map/ppermute | solution.py:353
  39.3 0.7 shard_map.116
  39.9 4.1 %collective-permute-done.11.refs_0_ = bf16[256,512]{1,0:T(8,128)(2,1)S(1)} collective-permute-done((bf16[256,512]{1,0:T(8,128)(2,1)S(1)}, bf16[256,512]{1,0:T(8,128)(2,1)S(1)}, u32[]{:S(2)}, u32[]{:S(2)}) %collective-permute-start.11) | collective-permute-done | bytes 262176 | tf_op jit(solution)/shard_map/ppermute | solution.py:356
  44.0 4.6 %collective-permute-done.19.refs_0_ = bf16[128,1024]{1,0:T(8,128)(2,1)S(1)} collective-permute-done((bf16[128,1024]{1,0:T(8,128)(2,1)S(1)}, bf16[128,1024]{1,0:T(8,128)(2,1)S(1)}, u32[]{:S(2)}, u32[]{:S(2)}) %collective-permute-start.19) | collective-permute-done | bytes 262176 | tf_op jit(solution)/shard_map/ppermute | solution.py:353
  49.2 1.4 %collective-permute-start.18 = (bf16[256,512]{1,0:T(8,128)(2,1)S(1)}, bf16[256,512]{1,0:T(8,128)(2,1)S(1)}, u32[]{:S(2)}, u32[]{:S(2)}) collective-permute-start(bf16[256,512]{1,0:T(8,128)(2,1)S(1)} %collective-permute-done.13.refs_2_), channel_id=1, source_target_pairs={{0,16},{16,0},{1,17},{17,1},{2,18},{18,2},{3,19},{19,3},{4,20},{20... | collective-permute-start | bytes 786440 | tf_op jit(solution)/shard_map/ppermute | solution.py:356
  50.6 1.5 %collective-permute-start.16 = (bf16[4,128,128]{2,1,0:T(8,128)(2,1)S(1)}, bf16[4,128,128]{2,1,0:T(8,128)(2,1)S(1)}, u32[]{:S(2)}, u32[]{:S(2)}) collective-permute-start(bf16[4,128,128]{2,1,0:T(8,128)(2,1)S(1)} %get-tuple-element.131), channel_id=1, source_target_pairs={{0,2},{1,3},{2,0},{3,1},{4,6},{5,7},{6,4},{7,5},{8,10},{9,11},{10,... | collective-permute-start | bytes 393224 | tf_op jit(solution)/shard_map/ppermute | solution.py:350
  52.6 3.7 %collective-permute-done.20.refs_1_ = bf16[128,1024]{1,0:T(8,128)(2,1)S(1)} collective-permute-done((bf16[128,1024]{1,0:T(8,128)(2,1)S(1)}, bf16[128,1024]{1,0:T(8,128)(2,1)S(1)}, u32[]{:S(2)}, u32[]{:S(2)}) %collective-permute-start.20) | collective-permute-done | bytes 262176 | tf_op jit(solution)/shard_map/ppermute | solution.py:353
  56.9 0.9 collective-permute-done.17.refs_3_
  57.8 2.0 %shard_map.118 = (bf16[512,128]{1,0:T(8,128)(2,1)S(1)}, bf16[512,128]{1,0:T(8,128)(2,1)S(1)}, bf16[512,128]{1,0:T(8,128)(2,1)S(1)}, bf16[512,128]{1,0:T(8,128)(2,1)S(1)}) custom-call(s32[3]{0:T(128)S(1)} %pad_add_fusion.pos, bf16[128,2048]{1,0:T(8,128)(2,1)S(1)} %copy-done.2, bf16[128,2048]{1,0:T(8,128)(2,1)S(1)} %collective-permute-done.4.core, ...), custom_call_target="tpu_custom_call" | custom-call | flops 1073741824 | bytes 4718592 | tf_op jit(solution)/shard_map/pallas_call | solution.py:60
  59.9 2.0 %collective-permute-start.21 = (bf16[512,128]{1,0:T(8,128)(2,1)S(1)}, bf16[512,128]{1,0:T(8,128)(2,1)S(1)}, u32[]{:S(2)}, u32[]{:S(2)}) collective-permute-start(bf16[512,128]{1,0:T(8,128)(2,1)S(1)} %get-tuple-element.148), channel_id=1, source_target_pairs={{0,12},{1,13},{2,14},{3,15},{4,8},{5,9},{6,10},{7,11},{8,4},{9,5},... | collective-permute-start | bytes 393224 | tf_op jit(solution)/shard_map/ppermute | solution.py:353
  61.9 0.6 collective-permute-start.22
  62.6 1.8 %collective-permute-start.23 = (bf16[512,128]{1,0:T(8,128)(2,1)S(1)}, bf16[512,128]{1,0:T(8,128)(2,1)S(1)}, u32[]{:S(2)}, u32[]{:S(2)}) collective-permute-start(bf16[512,128]{1,0:T(8,128)(2,1)S(1)} %get-tuple-element.150), channel_id=1, source_target_pairs={{0,4},{1,5},{2,6},{3,7},{4,0},{5,1},{6,2},{7,3},{8,12},{9,13},{10,... | collective-permute-start | bytes 393224 | tf_op jit(solution)/shard_map/ppermute | solution.py:353
  64.9 0.8 collective-permute-start.25
  65.7 1.6 %shard_map.120.refs_6_ = bf16[17,256,128]{2,1,0:T(8,128)(2,1)S(1)} custom-call(s32[3]{0:T(128)S(1)} %pad_add_fusion.pos, bf16[4,128,128]{2,1,0:T(8,128)(2,1)S(1)} %get-tuple-element.152.refs_0_, bf16[8,128,128]{2,1,0:T(8,128)(2,1)S(1)} %collective-permute-done.15.refs_1_.refs_4_, bf16[4,128,128]{2,1,0:T(8,128)(2,1)S(1)} %collective-permute-done.16.refs_2_, ...), custom_call_target="tpu_custom_call" | custom-call | flops 536870912 | bytes 4259840 | tf_op jit(solution)/shard_map/pallas_call | solution.py:60
  67.3 0.9 collective-permute-done.21.refs_3_
  68.2 7.0 %collective-permute-done.22.refs_2_ = bf16[512,128]{1,0:T(8,128)(2,1)S(1)} collective-permute-done((bf16[512,128]{1,0:T(8,128)(2,1)S(1)}, bf16[512,128]{1,0:T(8,128)(2,1)S(1)}, u32[]{:S(2)}, u32[]{:S(2)}) %collective-permute-start.22) | collective-permute-done | bytes 131104 | tf_op jit(solution)/shard_map/ppermute | solution.py:353
  75.3 3.0 %shard_map.121 = (bf16[256,128]{1,0:T(8,128)(2,1)S(1)}, bf16[256,128]{1,0:T(8,128)(2,1)S(1)}, bf16[256,128]{1,0:T(8,128)(2,1)S(1)}, bf16[256,128]{1,0:T(8,128)(2...) custom-call(s32[3]{0:T(128)S(1)} %pad_add_fusion.pos, ...), custom_call_target="tpu_custom_call" | custom-call | flops 4294967296 | bytes 7176192 | tf_op jit(solution)/shard_map/pallas_call | solution.py:60
  78.4 2.2 %collective-permute-start.26 = (bf16[256,128]{1,0:T(8,128)(2,1)S(1)}, bf16[256,128]{1,0:T(8,128)(2,1)S(1)}, u32[]{:S(2)}, u32[]{:S(2)}) collective-permute-start(bf16[256,128]{1,0:T(8,128)(2,1)S(1)} %get-tuple-element.171), channel_id=1, source_target_pairs={{0,12},{1,13},{2,14},{3,15},{4,8},{5,9},{6,10},{7,11},{8,4},{9,5},... | collective-permute-start | bytes 196616 | tf_op jit(solution)/shard_map/ppermute | solution.py:353
  80.5 2.3 %collective-permute-start.28 = (bf16[256,128]{1,0:T(8,128)(2,1)S(1)}, bf16[256,128]{1,0:T(8,128)(2,1)S(1)}, u32[]{:S(2)}, u32[]{:S(2)}) collective-permute-start(bf16[256,128]{1,0:T(8,128)(2,1)S(1)} %get-tuple-element.173), channel_id=1, source_target_pairs={{0,4},{1,5},{2,6},{3,7},{4,0},{5,1},{6,2},{7,3},{8,12},{9,13},{10,... | collective-permute-start | bytes 196616 | tf_op jit(solution)/shard_map/ppermute | solution.py:353
  82.8 2.4 %collective-permute-done.26.refs_3_ = bf16[256,128]{1,0:T(8,128)(2,1)S(1)} collective-permute-done((bf16[256,128]{1,0:T(8,128)(2,1)S(1)}, bf16[256,128]{1,0:T(8,128)(2,1)S(1)}, u32[]{:S(2)}, u32[]{:S(2)}) %collective-permute-start.26) | collective-permute-done | bytes 65568 | tf_op jit(solution)/shard_map/ppermute | solution.py:353
  85.2 2.3 %collective-permute-done.27.refs_2_ = bf16[256,128]{1,0:T(8,128)(2,1)S(1)} collective-permute-done((bf16[256,128]{1,0:T(8,128)(2,1)S(1)}, bf16[256,128]{1,0:T(8,128)(2,1)S(1)}, u32[]{:S(2)}, u32[]{:S(2)}) %collective-permute-start.27) | collective-permute-done | bytes 65568 | tf_op jit(solution)/shard_map/ppermute | solution.py:353
  87.5 1.1 %shard_map.122 = (bf16[128,2048]{1,0:T(8,128)(2,1)S(1)}, bf16[512,2048]{1,0:T(8,128)(2,1)S(1)}) custom-call(s32[3]{0:T(128)S(1)} %pad_add_fusion.pos, bf16[256,128]{1,0:T(8,128)(2,1)S(1)} %get-tuple-element.180.refs_0_, bf16[256,128]{1,0:T(8,128)(2,1)S(1)} %collective-permute-done.28.refs_1_, bf16[256,128]{1,0:T(8,128)(2,1)S(1)} %collective-permute-done.27.refs_2_, ...), custom_call_target="tpu_custom_call" | custom-call | flops 268435456 | bytes 5111808 | tf_op jit(solution)/shard_map/pallas_call | solution.py:60
  88.8 1.0 shard_map.123
  89.8 0.9 collective-permute-done.30
  90.7 1.1 %collective-permute-start.38 = (bf16[128,2048]{1,0:T(8,128)(2,1)S(1)}, bf16[128,2048]{1,0:T(8,128)(2,1)S(1)}, u32[]{:S(2)}, u32[]{:S(2)}) collective-permute-start(bf16[128,2048]{1,0:T(8,128)(2,1)S(1)} %add_convert_fusion.1), channel_id=1, source_target_pairs={{0,2},{1,3},{2,0},{3,1},{4,6},{5,7},{6,4},{7,5},{8,10},{9,11},{10,... | collective-permute-start | bytes 1572872 | tf_op jit(solution)/shard_map/ppermute | solution.py:350
  92.1 2.4 %collective-permute-start.32 = (bf16[256,128]{1,0:T(8,128)(2,1)S(1)}, bf16[256,128]{1,0:T(8,128)(2,1)S(1)}, u32[]{:S(2)}, u32[]{:S(2)}) collective-permute-start(bf16[256,128]{1,0:T(8,128)(2,1)S(1)} %get-tuple-element.195), channel_id=1, source_target_pairs={{0,8},{1,9},{2,10},{3,11},{4,12},{5,13},{6,14},{7,15},{8,0},{9,1},... | collective-permute-start | bytes 196616 | tf_op jit(solution)/shard_map/ppermute | solution.py:353
  94.4 1.8 %collective-permute-start.33 = (bf16[256,128]{1,0:T(8,128)(2,1)S(1)}, bf16[256,128]{1,0:T(8,128)(2,1)S(1)}, u32[]{:S(2)}, u32[]{:S(2)}) collective-permute-start(bf16[256,128]{1,0:T(8,128)(2,1)S(1)} %get-tuple-element.196), channel_id=1, source_target_pairs={{0,12},{1,13},{2,14},{3,15},{4,8},{5,9},{6,10},{7,11},{8,4},{9,5},... | collective-permute-start | bytes 196616 | tf_op jit(solution)/shard_map/ppermute | solution.py:353
  96.6 2.9 %collective-permute-done.32.refs_2_ = bf16[256,128]{1,0:T(8,128)(2,1)S(1)} collective-permute-done((bf16[256,128]{1,0:T(8,128)(2,1)S(1)}, bf16[256,128]{1,0:T(8,128)(2,1)S(1)}, u32[]{:S(2)}, u32[]{:S(2)}) %collective-permute-start.32) | collective-permute-done | bytes 65568 | tf_op jit(solution)/shard_map/ppermute | solution.py:353
  99.5 1.1 collective-permute-done.33.refs_3_
  100.6 1.0 shard_map.125
  102.7 1.0 shard_map.124
  103.7 1.1 collective-permute-done.38
  104.8 1.0 add_convert_fusion
  (69 shorter events, 9.3 us)
Async XLA Ops:
  0.0 16.2 %copy-start.2 = (bf16[128,2048]{1,0:T(8,128)(2,1)S(1)}, bf16[128,2048]{1,0:T(8,128)(2,1)}, u32[]{:S(2)}) copy-start(bf16[128,2048]{1,0:T(8,128)(2,1)} %x.1) | copy-start | bytes 1572868
  0.0 11.9 %copy-start.3 = (bf16[128,2048]{1,0:T(8,128)(2,1)S(1)}, bf16[128,2048]{1,0:T(8,128)(2,1)}, u32[]{:S(2)}) copy-start(bf16[128,2048]{1,0:T(8,128)(2,1)} %gate.1) | copy-start | bytes 1572868
  0.0 16.2 %collective-permute-start.4 = (bf16[128,2048]{1,0:T(8,128)(2,1)}, bf16[128,2048]{1,0:T(8,128)(2,1)S(1)}, u32[]{:S(2)}, u32[]{:S(2)}) collective-permute-start(bf16[128,2048]{1,0:T(8,128)(2,1)} %x.1), channel_id=1, source_target_pairs={{0,1},{1,0},{2,3},{3,2},{4,5},{5,4},{6,7},{7,6},{8,9},{9,8},{10,11... | collective-permute-start | bytes 1572872 | tf_op jit(solution)/shard_map/ppermute | solution.py:350
  2.4 13.8 %collective-permute-start.5 = (bf16[160,1024]{1,0:T(8,128)(2,1)S(1)}, bf16[160,1024]{1,0:T(8,128)(2,1)S(1)}, u32[]{:S(2)}, u32[]{:S(2)}) collective-permute-start(bf16[160,1024]{1,0:T(8,128)(2,1)S(1)} %get-tuple-element.109), channel_id=1, source_target_pairs={{0,4},{1,5},{2,6},{3,7},{4,0},{5,1},{6,2},{7,3},{8,12},{9,13},{10,... | collective-permute-start | bytes 983048 | tf_op jit(solution)/shard_map/ppermute | solution.py:353
  6.9 1.9 %collective-permute-start = (bf16[128,512]{1,0:T(8,128)(2,1)S(1)}, bf16[128,512]{1,0:T(8,128)(2,1)S(1)}, u32[]{:S(2)}, u32[]{:S(2)}) collective-permute-start(bf16[128,512]{1,0:T(8,128)(2,1)S(1)} %get-tuple-element.105), channel_id=1, source_target_pairs={{0,1},{1,0},{2,3},{3,2},{4,5},{5,4},{6,7},{7,6},{8,9},{9,8},{10,11... | collective-permute-start | bytes 393224 | tf_op jit(solution)/shard_map/ppermute | solution.py:350
  7.1 6.3 %collective-permute-start.1 = (bf16[128,512]{1,0:T(8,128)(2,1)S(1)}, bf16[128,512]{1,0:T(8,128)(2,1)S(1)}, u32[]{:S(2)}, u32[]{:S(2)}) collective-permute-start(bf16[128,512]{1,0:T(8,128)(2,1)S(1)} %get-tuple-element.106), channel_id=1, source_target_pairs={{0,2},{1,3},{2,0},{3,1},{4,6},{5,7},{6,4},{7,5},{8,10},{9,11},{10,... | collective-permute-start | bytes 393224 | tf_op jit(solution)/shard_map/ppermute | solution.py:350
  8.6 6.4 %collective-permute-start.2 = (bf16[128,512]{1,0:T(8,128)(2,1)S(1)}, bf16[128,512]{1,0:T(8,128)(2,1)S(1)}, u32[]{:S(2)}, u32[]{:S(2)}) collective-permute-start(bf16[128,512]{1,0:T(8,128)(2,1)S(1)} %get-tuple-element.107), channel_id=1, source_target_pairs={{0,3},{1,2},{2,1},{3,0},{4,7},{5,6},{6,5},{7,4},{8,11},{9,10},{10,... | collective-permute-start | bytes 393224 | tf_op jit(solution)/shard_map/ppermute | solution.py:350
  8.8 7.3 %collective-permute-start.3 = (bf16[128,512]{1,0:T(8,128)(2,1)S(1)}, bf16[128,512]{1,0:T(8,128)(2,1)S(1)}, u32[]{:S(2)}, u32[]{:S(2)}) collective-permute-start(bf16[128,512]{1,0:T(8,128)(2,1)S(1)} %get-tuple-element.108), channel_id=1, source_target_pairs={{0,8},{1,9},{2,10},{3,11},{4,12},{5,13},{6,14},{7,15},{8,0},{9,1},... | collective-permute-start | bytes 393224 | tf_op jit(solution)/shard_map/ppermute | solution.py:409
  16.2 14.1 %collective-permute-start.6 = (bf16[128,2048]{1,0:T(8,128)(2,1)S(1)}, bf16[128,2048]{1,0:T(8,128)(2,1)S(1)}, u32[]{:S(2)}, u32[]{:S(2)}) collective-permute-start(bf16[128,2048]{1,0:T(8,128)(2,1)S(1)} %copy-done.2), channel_id=1, source_target_pairs={{0,2},{1,3},{2,0},{3,1},{4,6},{5,7},{6,4},{7,5},{8,10},{9,11},{10,... | collective-permute-start | bytes 1572872 | tf_op jit(solution)/shard_map/ppermute | solution.py:350
  17.9 17.1 %collective-permute-start.7 = (bf16[256,512]{1,0:T(8,128)(2,1)S(1)}, bf16[256,512]{1,0:T(8,128)(2,1)S(1)}, u32[]{:S(2)}, u32[]{:S(2)}) collective-permute-start(bf16[256,512]{1,0:T(8,128)(2,1)S(1)} %shard_map.112), channel_id=1, source_target_pairs={{0,4},{1,5},{2,6},{3,7},{4,0},{5,1},{6,2},{7,3},{8,12},{9,13},{10,... | collective-permute-start | bytes 786440 | tf_op jit(solution)/shard_map/ppermute | solution.py:353
  20.6 14.4 %collective-permute-start.8 = (bf16[256,512]{1,0:T(8,128)(2,1)S(1)}, bf16[256,512]{1,0:T(8,128)(2,1)S(1)}, u32[]{:S(2)}, u32[]{:S(2)}) collective-permute-start(bf16[256,512]{1,0:T(8,128)(2,1)S(1)} %shard_map.112), channel_id=1, source_target_pairs={{0,8},{1,9},{2,10},{3,11},{4,12},{5,13},{6,14},{7,15},{8,0},{9,1},... | collective-permute-start | bytes 786440 | tf_op jit(solution)/shard_map/ppermute | solution.py:353
  23.6 11.4 %collective-permute-start.10 = (bf16[128,1024]{1,0:T(8,128)(2,1)S(1)}, bf16[128,1024]{1,0:T(8,128)(2,1)S(1)}, u32[]{:S(2)}, u32[]{:S(2)}) collective-permute-start(bf16[128,1024]{1,0:T(8,128)(2,1)S(1)} %get-tuple-element.120.refs_6_), channel_id=1, source_target_pairs={{0,16},{16,0},{1,17},{17,1},{2,18},{18,2},{3,19},{19,3},{4,20},{20... | collective-permute-start | bytes 786440 | tf_op jit(solution)/shard_map/ppermute | solution.py:356
  24.2 10.7 %collective-permute-start.9 = (bf16[192,512]{1,0:T(8,128)(2,1)S(1)}, bf16[192,512]{1,0:T(8,128)(2,1)S(1)}, u32[]{:S(2)}, u32[]{:S(2)}) collective-permute-start(bf16[192,512]{1,0:T(8,128)(2,1)S(1)} %get-tuple-element.118.mine), channel_id=1, source_target_pairs={{0,16},{16,0},{1,17},{17,1},{2,18},{18,2},{3,19},{19,3},{4,20},{20... | collective-permute-start | bytes 589832 | tf_op jit(solution)/shard_map/ppermute | solution.py:356
  30.3 18.9 %collective-permute-start.14 = (bf16[128,2048]{1,0:T(8,128)(2,1)S(1)}, bf16[128,2048]{1,0:T(8,128)(2,1)S(1)}, u32[]{:S(2)}, u32[]{:S(2)}) collective-permute-start(bf16[128,2048]{1,0:T(8,128)(2,1)S(1)} %collective-permute-done.6.from_x), channel_id=1, source_target_pairs={{0,1},{1,0},{2,3},{3,2},{4,5},{5,4},{6,7},{7,6},{8,9},{9,8},{10,11... | collective-permute-start | bytes 1572872 | tf_op jit(solution)/shard_map/ppermute | solution.py:350
  35.0 9.0 %collective-permute-start.11 = (bf16[256,512]{1,0:T(8,128)(2,1)S(1)}, bf16[256,512]{1,0:T(8,128)(2,1)S(1)}, u32[]{:S(2)}, u32[]{:S(2)}) collective-permute-start(bf16[256,512]{1,0:T(8,128)(2,1)S(1)} %collective-permute-done.7.refs_0_), channel_id=1, source_target_pairs={{0,16},{16,0},{1,17},{17,1},{2,18},{18,2},{3,19},{19,3},{4,20},{20... | collective-permute-start | bytes 786440 | tf_op jit(solution)/shard_map/ppermute | solution.py:356
  35.4 13.2 %collective-permute-start.19 = (bf16[128,1024]{1,0:T(8,128)(2,1)S(1)}, bf16[128,1024]{1,0:T(8,128)(2,1)S(1)}, u32[]{:S(2)}, u32[]{:S(2)}) collective-permute-start(bf16[128,1024]{1,0:T(8,128)(2,1)S(1)} %get-tuple-element.146), channel_id=1, source_target_pairs={{0,8},{1,9},{2,10},{3,11},{4,12},{5,13},{6,14},{7,15},{8,0},{9,1},... | collective-permute-start | bytes 786440 | tf_op jit(solution)/shard_map/ppermute | solution.py:353
  36.7 11.9 %collective-permute-start.12 = (bf16[256,512]{1,0:T(8,128)(2,1)S(1)}, bf16[256,512]{1,0:T(8,128)(2,1)S(1)}, u32[]{:S(2)}, u32[]{:S(2)}) collective-permute-start(bf16[256,512]{1,0:T(8,128)(2,1)S(1)} %collective-permute-done.8.refs_1_), channel_id=1, source_target_pairs={{0,16},{16,0},{1,17},{17,1},{2,18},{18,2},{3,19},{19,3},{4,20},{20... | collective-permute-start | bytes 786440 | tf_op jit(solution)/shard_map/ppermute | solution.py:356
  37.5 11.7 %collective-permute-start.13 = (bf16[256,512]{1,0:T(8,128)(2,1)S(1)}, bf16[256,512]{1,0:T(8,128)(2,1)S(1)}, u32[]{:S(2)}, u32[]{:S(2)}) collective-permute-start(bf16[256,512]{1,0:T(8,128)(2,1)S(1)} %collective-permute-done.8.refs_1_), channel_id=1, source_target_pairs={{0,4},{1,5},{2,6},{3,7},{4,0},{5,1},{6,2},{7,3},{8,12},{9,13},{10,... | collective-permute-start | bytes 786440 | tf_op jit(solution)/shard_map/ppermute | solution.py:353
  44.0 13.8 %collective-permute-start.15 = (bf16[8,128,128]{2,1,0:T(8,128)(2,1)S(1)}, bf16[8,128,128]{2,1,0:T(8,128)(2,1)S(1)}, u32[]{:S(2)}, u32[]{:S(2)}) collective-permute-start(bf16[8,128,128]{2,1,0:T(8,128)(2,1)S(1)} %get-tuple-element.130), channel_id=1, source_target_pairs={{0,1},{1,0},{2,3},{3,2},{4,5},{5,4},{6,7},{7,6},{8,9},{9,8},{10,11... | collective-permute-start | bytes 786440 | tf_op jit(solution)/shard_map/ppermute | solution.py:350
  48.6 7.7 %collective-permute-start.20 = (bf16[128,1024]{1,0:T(8,128)(2,1)S(1)}, bf16[128,1024]{1,0:T(8,128)(2,1)S(1)}, u32[]{:S(2)}, u32[]{:S(2)}) collective-permute-start(bf16[128,1024]{1,0:T(8,128)(2,1)S(1)} %collective-permute-done.19.refs_0_), channel_id=1, source_target_pairs={{0,4},{1,5},{2,6},{3,7},{4,0},{5,1},{6,2},{7,3},{8,12},{9,13},{10,... | collective-permute-start | bytes 786440 | tf_op jit(solution)/shard_map/ppermute | solution.py:353
  49.2 8.6 %collective-permute-start.18 = (bf16[256,512]{1,0:T(8,128)(2,1)S(1)}, bf16[256,512]{1,0:T(8,128)(2,1)S(1)}, u32[]{:S(2)}, u32[]{:S(2)}) collective-permute-start(bf16[256,512]{1,0:T(8,128)(2,1)S(1)} %collective-permute-done.13.refs_2_), channel_id=1, source_target_pairs={{0,16},{16,0},{1,17},{17,1},{2,18},{18,2},{3,19},{19,3},{4,20},{20... | collective-permute-start | bytes 786440 | tf_op jit(solution)/shard_map/ppermute | solution.py:356
  50.6 6.3 %collective-permute-start.16 = (bf16[4,128,128]{2,1,0:T(8,128)(2,1)S(1)}, bf16[4,128,128]{2,1,0:T(8,128)(2,1)S(1)}, u32[]{:S(2)}, u32[]{:S(2)}) collective-permute-start(bf16[4,128,128]{2,1,0:T(8,128)(2,1)S(1)} %get-tuple-element.131), channel_id=1, source_target_pairs={{0,2},{1,3},{2,0},{3,1},{4,6},{5,7},{6,4},{7,5},{8,10},{9,11},{10,... | collective-permute-start | bytes 393224 | tf_op jit(solution)/shard_map/ppermute | solution.py:350
  52.0 5.8 %collective-permute-start.17 = (bf16[4,128,128]{2,1,0:T(8,128)(2,1)S(1)}, bf16[4,128,128]{2,1,0:T(8,128)(2,1)S(1)}, u32[]{:S(2)}, u32[]{:S(2)}) collective-permute-start(bf16[4,128,128]{2,1,0:T(8,128)(2,1)S(1)} %get-tuple-element.132), channel_id=1, source_target_pairs={{0,3},{1,2},{2,1},{3,0},{4,7},{5,6},{6,5},{7,4},{8,11},{9,10},{10,... | collective-permute-start | bytes 393224 | tf_op jit(solution)/shard_map/ppermute | solution.py:350
  56.9 8.9 %copy-start = (bf16[17,256,256]{2,1,0:T(8,128)(2,1)S(1)}, bf16[17,256,256]{2,1,0:T(8,128)(2,1)}, u32[]{:S(2)}) copy-start(bf16[17,256,256]{2,1,0:T(8,128)(2,1)} %constant.45.clone.refs_5_.refs_9_) | copy-start | bytes 6684676
  56.9 8.9 %copy-start.4 = (bf16[512,256]{1,0:T(8,128)(2,1)S(1)}, bf16[512,256]{1,0:T(8,128)(2,1)}, u32[]{:S(2)}) copy-start(bf16[512,256]{1,0:T(8,128)(2,1)} %constant.43.clone.refs_4_.refs_7_) | copy-start | bytes 786436
  59.9 15.4 %copy-start.5 = (f32[3,2048]{1,0:T(4,128)S(1)}, f32[3,2048]{1,0:T(4,128)}, u32[]{:S(2)}) copy-start(f32[3,2048]{1,0:T(4,128)} %refs_4_.2) | copy-start | bytes 73732
  59.9 15.3 %copy-start.6 = (f32[2048]{0:T(1024)S(1)}, f32[2048]{0:T(1024)}, u32[]{:S(2)}) copy-start(f32[2048]{0:T(1024)} %param.16) | copy-start | bytes 24580
  59.9 15.3 %copy-start.7 = (bf16[17,256,256]{2,1,0:T(8,128)(2,1)S(1)}, bf16[17,256,256]{2,1,0:T(8,128)(2,1)}, u32[]{:S(2)}) copy-start(bf16[17,256,256]{2,1,0:T(8,128)(2,1)} %constant.46.clone.refs_10_) | copy-start | bytes 6684676
  59.9 15.3 %copy-start.8 = (bf16[256,512]{1,0:T(8,128)(2,1)S(1)}, bf16[256,512]{1,0:T(8,128)(2,1)}, u32[]{:S(2)}) copy-start(bf16[256,512]{1,0:T(8,128)(2,1)} %constant.44.clone.refs_8_) | copy-start | bytes 786436
  59.9 8.3 %collective-permute-start.21 = (bf16[512,128]{1,0:T(8,128)(2,1)S(1)}, bf16[512,128]{1,0:T(8,128)(2,1)S(1)}, u32[]{:S(2)}, u32[]{:S(2)}) collective-permute-start(bf16[512,128]{1,0:T(8,128)(2,1)S(1)} %get-tuple-element.148), channel_id=1, source_target_pairs={{0,12},{1,13},{2,14},{3,15},{4,8},{5,9},{6,10},{7,11},{8,4},{9,5},... | collective-permute-start | bytes 393224 | tf_op jit(solution)/shard_map/ppermute | solution.py:353
  61.9 13.3 %collective-permute-start.22 = (bf16[512,128]{1,0:T(8,128)(2,1)S(1)}, bf16[512,128]{1,0:T(8,128)(2,1)S(1)}, u32[]{:S(2)}, u32[]{:S(2)}) collective-permute-start(bf16[512,128]{1,0:T(8,128)(2,1)S(1)} %get-tuple-element.149), channel_id=1, source_target_pairs={{0,8},{1,9},{2,10},{3,11},{4,12},{5,13},{6,14},{7,15},{8,0},{9,1},... | collective-permute-start | bytes 393224 | tf_op jit(solution)/shard_map/ppermute | solution.py:353
  62.6 12.7 %collective-permute-start.23 = (bf16[512,128]{1,0:T(8,128)(2,1)S(1)}, bf16[512,128]{1,0:T(8,128)(2,1)S(1)}, u32[]{:S(2)}, u32[]{:S(2)}) collective-permute-start(bf16[512,128]{1,0:T(8,128)(2,1)S(1)} %get-tuple-element.150), channel_id=1, source_target_pairs={{0,4},{1,5},{2,6},{3,7},{4,0},{5,1},{6,2},{7,3},{8,12},{9,13},{10,... | collective-permute-start | bytes 393224 | tf_op jit(solution)/shard_map/ppermute | solution.py:353
  64.4 13.9 %collective-permute-start.24 = (bf16[256,1024]{1,0:T(8,128)(2,1)S(1)}, bf16[256,1024]{1,0:T(8,128)(2,1)S(1)}, u32[]{:S(2)}, u32[]{:S(2)}) collective-permute-start(bf16[256,1024]{1,0:T(8,128)(2,1)S(1)} %shard_map.119.refs_7_), channel_id=1, source_target_pairs={{0,16},{16,0},{1,17},{17,1},{2,18},{18,2},{3,19},{19,3},{4,20},{20... | collective-permute-start | bytes 1572872 | tf_op jit(solution)/shard_map/ppermute | solution.py:356
  64.9 13.4 %collective-permute-start.25 = (bf16[256,512]{1,0:T(8,128)(2,1)S(1)}, bf16[256,512]{1,0:T(8,128)(2,1)S(1)}, u32[]{:S(2)}, u32[]{:S(2)}) collective-permute-start(bf16[256,512]{1,0:T(8,128)(2,1)S(1)} %get-tuple-element.170), channel_id=1, source_target_pairs={{0,2},{1,3},{2,0},{3,1},{4,6},{5,7},{6,4},{7,5},{8,10},{9,11},{10,... | collective-permute-start | bytes 786440 | tf_op jit(solution)/shard_map/ppermute | solution.py:350
  75.2 12.3 %copy-start.1 = (bf16[128,2048]{1,0:T(8,128)(2,1)S(1)}, bf16[128,2048]{1,0:T(8,128)(2,1)}, u32[]{:S(2)}) copy-start(bf16[128,2048]{1,0:T(8,128)(2,1)} %refs_5_.2) | copy-start | bytes 1572868
  78.3 9.2 %collective-permute-start.29 = (bf16[128,512]{1,0:T(8,128)(2,1)S(1)}, bf16[128,512]{1,0:T(8,128)(2,1)S(1)}, u32[]{:S(2)}, u32[]{:S(2)}) collective-permute-start(bf16[128,512]{1,0:T(8,128)(2,1)S(1)} %slice.3), channel_id=1, source_target_pairs={{0,1},{1,0},{2,3},{3,2},{4,5},{5,4},{6,7},{7,6},{8,9},{9,8},{10,11... | collective-permute-start | bytes 393224 | tf_op jit(solution)/shard_map/ppermute | solution.py:350
  78.4 6.9 %collective-permute-start.26 = (bf16[256,128]{1,0:T(8,128)(2,1)S(1)}, bf16[256,128]{1,0:T(8,128)(2,1)S(1)}, u32[]{:S(2)}, u32[]{:S(2)}) collective-permute-start(bf16[256,128]{1,0:T(8,128)(2,1)S(1)} %get-tuple-element.171), channel_id=1, source_target_pairs={{0,12},{1,13},{2,14},{3,15},{4,8},{5,9},{6,10},{7,11},{8,4},{9,5},... | collective-permute-start | bytes 196616 | tf_op jit(solution)/shard_map/ppermute | solution.py:353
  80.5 6.9 %collective-permute-start.27 = (bf16[256,128]{1,0:T(8,128)(2,1)S(1)}, bf16[256,128]{1,0:T(8,128)(2,1)S(1)}, u32[]{:S(2)}, u32[]{:S(2)}) collective-permute-start(bf16[256,128]{1,0:T(8,128)(2,1)S(1)} %get-tuple-element.172), channel_id=1, source_target_pairs={{0,8},{1,9},{2,10},{3,11},{4,12},{5,13},{6,14},{7,15},{8,0},{9,1},... | collective-permute-start | bytes 196616 | tf_op jit(solution)/shard_map/ppermute | solution.py:353
  80.5 6.9 %collective-permute-start.28 = (bf16[256,128]{1,0:T(8,128)(2,1)S(1)}, bf16[256,128]{1,0:T(8,128)(2,1)S(1)}, u32[]{:S(2)}, u32[]{:S(2)}) collective-permute-start(bf16[256,128]{1,0:T(8,128)(2,1)S(1)} %get-tuple-element.173), channel_id=1, source_target_pairs={{0,4},{1,5},{2,6},{3,7},{4,0},{5,1},{6,2},{7,3},{8,12},{9,13},{10,... | collective-permute-start | bytes 196616 | tf_op jit(solution)/shard_map/ppermute | solution.py:353
  88.7 2.0 %collective-permute-start.30 = (bf16[128,2048]{1,0:T(8,128)(2,1)S(1)}, bf16[128,2048]{1,0:T(8,128)(2,1)S(1)}, u32[]{:S(2)}, u32[]{:S(2)}) collective-permute-start(bf16[128,2048]{1,0:T(8,128)(2,1)S(1)} %get-tuple-element.188), channel_id=1, source_target_pairs={{0,1},{1,0},{2,3},{3,2},{4,5},{5,4},{6,7},{7,6},{8,9},{9,8},{10,11... | collective-permute-start | bytes 1572872 | tf_op jit(solution)/shard_map/ppermute | solution.py:350
  90.7 14.0 %collective-permute-start.38 = (bf16[128,2048]{1,0:T(8,128)(2,1)S(1)}, bf16[128,2048]{1,0:T(8,128)(2,1)S(1)}, u32[]{:S(2)}, u32[]{:S(2)}) collective-permute-start(bf16[128,2048]{1,0:T(8,128)(2,1)S(1)} %add_convert_fusion.1), channel_id=1, source_target_pairs={{0,2},{1,3},{2,0},{3,1},{4,6},{5,7},{6,4},{7,5},{8,10},{9,11},{10,... | collective-permute-start | bytes 1572872 | tf_op jit(solution)/shard_map/ppermute | solution.py:350
  91.8 4.8 %collective-permute-start.31 = (bf16[256,128]{1,0:T(8,128)(2,1)S(1)}, bf16[256,128]{1,0:T(8,128)(2,1)S(1)}, u32[]{:S(2)}, u32[]{:S(2)}) collective-permute-start(bf16[256,128]{1,0:T(8,128)(2,1)S(1)} %get-tuple-element.194), channel_id=1, source_target_pairs={{0,4},{1,5},{2,6},{3,7},{4,0},{5,1},{6,2},{7,3},{8,12},{9,13},{10,... | collective-permute-start | bytes 196616 | tf_op jit(solution)/shard_map/ppermute | solution.py:353
  92.1 7.5 %collective-permute-start.32 = (bf16[256,128]{1,0:T(8,128)(2,1)S(1)}, bf16[256,128]{1,0:T(8,128)(2,1)S(1)}, u32[]{:S(2)}, u32[]{:S(2)}) collective-permute-start(bf16[256,128]{1,0:T(8,128)(2,1)S(1)} %get-tuple-element.195), channel_id=1, source_target_pairs={{0,8},{1,9},{2,10},{3,11},{4,12},{5,13},{6,14},{7,15},{8,0},{9,1},... | collective-permute-start | bytes 196616 | tf_op jit(solution)/shard_map/ppermute | solution.py:353
  94.4 6.2 %collective-permute-start.33 = (bf16[256,128]{1,0:T(8,128)(2,1)S(1)}, bf16[256,128]{1,0:T(8,128)(2,1)S(1)}, u32[]{:S(2)}, u32[]{:S(2)}) collective-permute-start(bf16[256,128]{1,0:T(8,128)(2,1)S(1)} %get-tuple-element.196), channel_id=1, source_target_pairs={{0,12},{1,13},{2,14},{3,15},{4,8},{5,9},{6,10},{7,11},{8,4},{9,5},... | collective-permute-start | bytes 196616 | tf_op jit(solution)/shard_map/ppermute | solution.py:353
  101.6 2.1 %collective-permute-start.37 = (bf16[128,512]{1,0:T(8,128)(2,1)S(1)}, bf16[128,512]{1,0:T(8,128)(2,1)S(1)}, u32[]{:S(2)}, u32[]{:S(2)}) collective-permute-start(bf16[128,512]{1,0:T(8,128)(2,1)S(1)} %get-tuple-element.201), channel_id=1, source_target_pairs={{0,1},{1,0},{2,3},{3,2},{4,5},{5,4},{6,7},{7,6},{8,9},{9,8},{10,11... | collective-permute-start | bytes 393224 | tf_op jit(solution)/shard_map/ppermute | solution.py:350
  101.7 2.0 %collective-permute-start.36 = (bf16[128,512]{1,0:T(8,128)(2,1)S(1)}, bf16[128,512]{1,0:T(8,128)(2,1)S(1)}, u32[]{:S(2)}, u32[]{:S(2)}) collective-permute-start(bf16[128,512]{1,0:T(8,128)(2,1)S(1)} %get-tuple-element.200), channel_id=1, source_target_pairs={{0,1},{1,0},{2,3},{3,2},{4,5},{5,4},{6,7},{7,6},{8,9},{9,8},{10,11... | collective-permute-start | bytes 393224 | tf_op jit(solution)/shard_map/ppermute | solution.py:350
  102.2 1.5 %collective-permute-start.35 = (bf16[128,512]{1,0:T(8,128)(2,1)S(1)}, bf16[128,512]{1,0:T(8,128)(2,1)S(1)}, u32[]{:S(2)}, u32[]{:S(2)}) collective-permute-start(bf16[128,512]{1,0:T(8,128)(2,1)S(1)} %get-tuple-element.199), channel_id=1, source_target_pairs={{0,1},{1,0},{2,3},{3,2},{4,5},{5,4},{6,7},{7,6},{8,9},{9,8},{10,11... | collective-permute-start | bytes 393224 | tf_op jit(solution)/shard_map/ppermute | solution.py:350
  102.2 1.5 %collective-permute-start.34 = (bf16[128,512]{1,0:T(8,128)(2,1)S(1)}, bf16[128,512]{1,0:T(8,128)(2,1)S(1)}, u32[]{:S(2)}, u32[]{:S(2)}) collective-permute-start(bf16[128,512]{1,0:T(8,128)(2,1)S(1)} %get-tuple-element.198), channel_id=1, source_target_pairs={{0,1},{1,0},{2,3},{3,2},{4,5},{5,4},{6,7},{7,6},{8,9},{9,8},{10,11... | collective-permute-start | bytes 393224 | tf_op jit(solution)/shard_map/ppermute | solution.py:350

commit v9 on v8

--- a/solution.py
+++ b/solution.py
@@ -312,20 +312,16 @@
         out[...] = got[:, i * width : (i + 1) * width].astype(out.dtype)
 
 
-def upper_kernel(planes, pos, *refs):
-    u, gate = refs[:planes], refs[planes]
-    own, halves = refs[planes + 1], refs[planes + 2 : planes + 6]
-    out, ws, mixed = refs[planes + 6 :]
-    share = u[0].shape[1]
+def gather_kernel(pos, own, *refs):
+    halves, ws = refs[:4], refs[4]
+    share = own.shape[0]
     width = halves[0].shape[1]
     ws[:share, :] = own[...]
     for k in range(2):
         side = pos[0] if k == 0 else 1 - pos[0]
         columns = pl.ds(pl.multiple_of(side * width, width), width)
-        near, far = halves[2 * k : 2 * k + 2]
-        ws[share : 2 * share, columns] = near[:share, :]
-        ws[2 * share :, columns] = far[...]
-    mixed_dot(planes, pos, u, gate, ws, mixed, (out,), 1)
+        ws[share : 2 * share, columns] = halves[2 * k][:share, :]
+        ws[2 * share :, columns] = halves[2 * k + 1][...]
 
 
 def place_kernel(planes, half, pos, *refs):
@@ -503,20 +499,20 @@
 
     upper = spread(mixed[planes:])
     gate_three = to_place(gate_x[rows:], 1)
-    upper, lower, gate_three = stage((upper[::-1], mixed[:planes], gate_three))
+    gathered = small(
+        gather_kernel,
+        [shaped(wide, features)],
+        output_weight,
+        out_near,
+        weights,
+        out_other,
+        weights_other,
+        flops=1,
+    )[0]
+    upper, lower, gate_three, gathered = stage((upper[::-1], mixed[:planes], gate_three, gathered))
     upper = upper[::-1]
     scratch = [pltpu.VMEM((rows, wide), jnp.bfloat16)]
     flops = 2 * rows * features * wide
-    partial_three, gathered = call(
-        functools.partial(upper_kernel, planes),
-        [shaped(rows, features), shaped(wide, features)],
-        scratch,
-        pos,
-        [*upper, gate_three, output_weight, out_near, weights, out_other, weights_other],
-        flops,
-        vmem=8,
-    )
-
     def partial_of(parts, half, gate, cost, pieces, dtype):
         return call(
             functools.partial(place_kernel, planes, half),
@@ -528,6 +524,7 @@
             vmem=8,
         )
 
+    partial_three = partial_of(upper, 1, gate_three, flops, 1, jnp.bfloat16)[0]
     partial_two = partial_of(upper, 0, gate_x, flops, 1, jnp.float32)[0]
     across = partial_two + to_place(partial_three, 1).astype(jnp.float32)
     across, lower = stage((across.astype(jnp.bfloat16), lower))

time: 106 us -> 106 us (level)
    pallas_call x17 -> x18, Pallas kernels: 19.3 us -> 19.9 us  [call(): pl.pallas_call(kernel, out_shape=outs, in_specs=in_specs, out_specs=[pl.B...]
  transfers between devices with their start and end apart: 39 -> 39, of which waited for: 19 -> 19; matrix products, arithmetic and copies ran while one was open for 0% -> 0% of each run, Pallas kernels for 15% -> 16%
where the time goes in v9:
time: 106 us
  waiting for transfers between devices  43.5 us (41%)
  starting transfers between devices  40.7 us (38%)
  Pallas kernels  19.9 us (19%)
  other arithmetic  1.14 us (1%)
    ppermute x15, waiting for transfers between devices, to_plane(): lax.ppermute(block, 'seq', [(i, i ^ s * PLANE) for i in range(devices)])  24.6 us
    ppermute x15, starting transfers between devices, to_plane(): lax.ppermute(block, 'seq', [(i, i ^ s * PLANE) for i in range(devices)])  24.1 us
    pallas_call x18, Pallas kernels, call(): pl.pallas_call(kernel, out_shape=outs, in_specs=in_specs, out_specs=[pl.B...  19.9 us
    ppermute x17, waiting for transfers between devices, to_place(): return lax.ppermute(block, 'seq', [(i, i ^ d) for i in range(devices)])  9.62 us
    ppermute x6, waiting for transfers between devices, to_group(): return lax.ppermute(block, 'groups', [(0, 1), (1, 0)])  8.75 us
    ppermute x17, starting transfers between devices, to_place(): return lax.ppermute(block, 'seq', [(i, i ^ d) for i in range(devices)])  8.7 us
    ppermute x6, starting transfers between devices, to_group(): return lax.ppermute(block, 'groups', [(0, 1), (1, 0)])  5.26 us
    ppermute x1, starting transfers between devices, local(): taps_whole = lax.ppermute(taps_whole, ('groups', 'seq'), route)  2.59 us
  transfers between devices with their start and end apart: 39, of which 19 were waited for; matrix products, arithmetic and copies ran while one was open for 0% of the time, Pallas kernels for 16%

profile of v9, /device:TPU:0, one launch (start us, length us, event | category | flops | bytes accessed | tf_op | source)
XLA Modules:
  0.0 105.6 jit_solution(14292353144990838898)
XLA Ops:
  0.5 1.8 %shard_map.111 = (bf16[128,512]{1,0:T(8,128)(2,1)S(1)}, bf16[128,512]{1,0:T(8,128)(2,1)S(1)}, bf16[160,1024]{1,0:T(8,128)(2,1)S(1)}, bf16[128,1024]{1,0:T(8,128)(2,1)S(1)}) custom-call(s32[3]{0:T(128)S(1)} %pad_add_fusion.pos, bf16[128,2048]{1,0:T(8,128)(2,1)} %taps.1, bf16[128,2048]{1,0:T(8,128)(2,1)} %own.1), custom_call_target="tpu_custom_call" | custom-call | tf_op jit(solution)/shard_map/pallas_call | solution.py:60
  2.4 2.7 %collective-permute-start.5 = (bf16[160,1024]{1,0:T(8,128)(2,1)S(1)}, bf16[160,1024]{1,0:T(8,128)(2,1)S(1)}, u32[]{:S(2)}, u32[]{:S(2)}) collective-permute-start(bf16[160,1024]{1,0:T(8,128)(2,1)S(1)} %get-tuple-element.108), channel_id=1, source_target_pairs={{0,4},{1,5},{2,6},{3,7},{4,0},{5,1},{6,2},{7,3},{8,12},{9,13},{10,... | collective-permute-start | bytes 983048 | tf_op jit(solution)/shard_map/ppermute | solution.py:349
  5.0 1.8 %shard_map.109 = (bf16[128,512]{1,0:T(8,128)(2,1)S(1)}, bf16[128,512]{1,0:T(8,128)(2,1)S(1)}, bf16[128,512]{1,0:T(8,128)(2,1)S(1)}, bf16[128,512]{1,0:T(8,128)(2,1)S(1)}) custom-call(s32[3]{0:T(128)S(1)} %pad_add_fusion.pos, bf16[128,2048]{1,0:T(8,128)(2,1)} %weight.1), custom_call_target="tpu_custom_call" | custom-call | tf_op jit(solution)/shard_map/pallas_call | solution.py:60
  7.1 1.5 %collective-permute-start.1 = (bf16[128,512]{1,0:T(8,128)(2,1)S(1)}, bf16[128,512]{1,0:T(8,128)(2,1)S(1)}, u32[]{:S(2)}, u32[]{:S(2)}) collective-permute-start(bf16[128,512]{1,0:T(8,128)(2,1)S(1)} %get-tuple-element.105), channel_id=1, source_target_pairs={{0,2},{1,3},{2,0},{3,1},{4,6},{5,7},{6,4},{7,5},{8,10},{9,11},{10,... | collective-permute-start | bytes 393224 | tf_op jit(solution)/shard_map/ppermute | solution.py:346
  8.8 2.6 %collective-permute-start.3 = (bf16[128,512]{1,0:T(8,128)(2,1)S(1)}, bf16[128,512]{1,0:T(8,128)(2,1)S(1)}, u32[]{:S(2)}, u32[]{:S(2)}) collective-permute-start(bf16[128,512]{1,0:T(8,128)(2,1)S(1)} %get-tuple-element.107), channel_id=1, source_target_pairs={{0,8},{1,9},{2,10},{3,11},{4,12},{5,13},{6,14},{7,15},{8,0},{9,1},... | collective-permute-start | bytes 393224 | tf_op jit(solution)/shard_map/ppermute | solution.py:405
  11.9 0.9 shard_map.113
  13.4 1.6 %collective-permute-done.2.refs_3_ = bf16[128,512]{1,0:T(8,128)(2,1)S(1)} collective-permute-done((bf16[128,512]{1,0:T(8,128)(2,1)S(1)}, bf16[128,512]{1,0:T(8,128)(2,1)S(1)}, u32[]{:S(2)}, u32[]{:S(2)}) %collective-permute-start.2) | collective-permute-done | bytes 131104 | tf_op jit(solution)/shard_map/ppermute | solution.py:346
  16.2 1.7 %collective-permute-start.6 = (bf16[128,2048]{1,0:T(8,128)(2,1)S(1)}, bf16[128,2048]{1,0:T(8,128)(2,1)S(1)}, u32[]{:S(2)}, u32[]{:S(2)}) collective-permute-start(bf16[128,2048]{1,0:T(8,128)(2,1)S(1)} %copy-done.2), channel_id=1, source_target_pairs={{0,2},{1,3},{2,0},{3,1},{4,6},{5,7},{6,4},{7,5},{8,10},{9,11},{10,... | collective-permute-start | bytes 1572872 | tf_op jit(solution)/shard_map/ppermute | solution.py:346
  17.9 2.7 %collective-permute-start.7 = (bf16[256,512]{1,0:T(8,128)(2,1)S(1)}, bf16[256,512]{1,0:T(8,128)(2,1)S(1)}, u32[]{:S(2)}, u32[]{:S(2)}) collective-permute-start(bf16[256,512]{1,0:T(8,128)(2,1)S(1)} %shard_map.112), channel_id=1, source_target_pairs={{0,4},{1,5},{2,6},{3,7},{4,0},{5,1},{6,2},{7,3},{8,12},{9,13},{10,... | collective-permute-start | bytes 786440 | tf_op jit(solution)/shard_map/ppermute | solution.py:349
  20.6 2.5 %collective-permute-start.8 = (bf16[256,512]{1,0:T(8,128)(2,1)S(1)}, bf16[256,512]{1,0:T(8,128)(2,1)S(1)}, u32[]{:S(2)}, u32[]{:S(2)}) collective-permute-start(bf16[256,512]{1,0:T(8,128)(2,1)S(1)} %shard_map.112), channel_id=1, source_target_pairs={{0,8},{1,9},{2,10},{3,11},{4,12},{5,13},{6,14},{7,15},{8,0},{9,1},... | collective-permute-start | bytes 786440 | tf_op jit(solution)/shard_map/ppermute | solution.py:349
  24.2 1.5 %collective-permute-start.9 = (bf16[192,512]{1,0:T(8,128)(2,1)S(1)}, bf16[192,512]{1,0:T(8,128)(2,1)S(1)}, u32[]{:S(2)}, u32[]{:S(2)}) collective-permute-start(bf16[192,512]{1,0:T(8,128)(2,1)S(1)} %get-tuple-element.117.mine), channel_id=1, source_target_pairs={{0,16},{16,0},{1,17},{17,1},{2,18},{18,2},{3,19},{19,3},{4,20},{20... | collective-permute-start | bytes 589832 | tf_op jit(solution)/shard_map/ppermute | solution.py:352
  25.7 4.6 %collective-permute-done.6.from_x = bf16[128,2048]{1,0:T(8,128)(2,1)S(1)} collective-permute-done((bf16[128,2048]{1,0:T(8,128)(2,1)S(1)}, bf16[128,2048]{1,0:T(8,128)(2,1)S(1)}, u32[]{:S(2)}, u32[]{:S(2)}) %collective-permute-start.6) | collective-permute-done | bytes 524320 | tf_op jit(solution)/shard_map/ppermute | solution.py:346
  30.3 4.7 %collective-permute-done.9.other = bf16[192,512]{1,0:T(8,128)(2,1)S(1)} collective-permute-done((bf16[192,512]{1,0:T(8,128)(2,1)S(1)}, bf16[192,512]{1,0:T(8,128)(2,1)S(1)}, u32[]{:S(2)}, u32[]{:S(2)}) %collective-permute-start.9) | collective-permute-done | bytes 196640 | tf_op jit(solution)/shard_map/ppermute | solution.py:352
  35.4 1.3 %collective-permute-start.19 = (bf16[128,1024]{1,0:T(8,128)(2,1)S(1)}, bf16[128,1024]{1,0:T(8,128)(2,1)S(1)}, u32[]{:S(2)}, u32[]{:S(2)}) collective-permute-start(bf16[128,1024]{1,0:T(8,128)(2,1)S(1)} %get-tuple-element.145), channel_id=1, source_target_pairs={{0,8},{1,9},{2,10},{3,11},{4,12},{5,13},{6,14},{7,15},{8,0},{9,1},... | collective-permute-start | bytes 786440 | tf_op jit(solution)/shard_map/ppermute | solution.py:349
  36.7 0.8 collective-permute-start.12
  37.5 1.8 %collective-permute-start.13 = (bf16[256,512]{1,0:T(8,128)(2,1)S(1)}, bf16[256,512]{1,0:T(8,128)(2,1)S(1)}, u32[]{:S(2)}, u32[]{:S(2)}) collective-permute-start(bf16[256,512]{1,0:T(8,128)(2,1)S(1)} %collective-permute-done.8.refs_1_), channel_id=1, source_target_pairs={{0,4},{1,5},{2,6},{3,7},{4,0},{5,1},{6,2},{7,3},{8,12},{9,13},{10,... | collective-permute-start | bytes 786440 | tf_op jit(solution)/shard_map/ppermute | solution.py:349
  39.3 0.7 shard_map.116
  39.9 4.1 %collective-permute-done.11.refs_0_ = bf16[256,512]{1,0:T(8,128)(2,1)S(1)} collective-permute-done((bf16[256,512]{1,0:T(8,128)(2,1)S(1)}, bf16[256,512]{1,0:T(8,128)(2,1)S(1)}, u32[]{:S(2)}, u32[]{:S(2)}) %collective-permute-start.11) | collective-permute-done | bytes 262176 | tf_op jit(solution)/shard_map/ppermute | solution.py:352
  44.0 4.6 %collective-permute-done.19.refs_0_ = bf16[128,1024]{1,0:T(8,128)(2,1)S(1)} collective-permute-done((bf16[128,1024]{1,0:T(8,128)(2,1)S(1)}, bf16[128,1024]{1,0:T(8,128)(2,1)S(1)}, u32[]{:S(2)}, u32[]{:S(2)}) %collective-permute-start.19) | collective-permute-done | bytes 262176 | tf_op jit(solution)/shard_map/ppermute | solution.py:349
  49.2 1.4 %collective-permute-start.18 = (bf16[256,512]{1,0:T(8,128)(2,1)S(1)}, bf16[256,512]{1,0:T(8,128)(2,1)S(1)}, u32[]{:S(2)}, u32[]{:S(2)}) collective-permute-start(bf16[256,512]{1,0:T(8,128)(2,1)S(1)} %collective-permute-done.13.refs_2_), channel_id=1, source_target_pairs={{0,16},{16,0},{1,17},{17,1},{2,18},{18,2},{3,19},{19,3},{4,20},{20... | collective-permute-start | bytes 786440 | tf_op jit(solution)/shard_map/ppermute | solution.py:352
  50.6 1.5 %collective-permute-start.16 = (bf16[4,128,128]{2,1,0:T(8,128)(2,1)S(1)}, bf16[4,128,128]{2,1,0:T(8,128)(2,1)S(1)}, u32[]{:S(2)}, u32[]{:S(2)}) collective-permute-start(bf16[4,128,128]{2,1,0:T(8,128)(2,1)S(1)} %get-tuple-element.130), channel_id=1, source_target_pairs={{0,2},{1,3},{2,0},{3,1},{4,6},{5,7},{6,4},{7,5},{8,10},{9,11},{10,... | collective-permute-start | bytes 393224 | tf_op jit(solution)/shard_map/ppermute | solution.py:346
  52.6 3.7 %collective-permute-done.20.refs_1_ = bf16[128,1024]{1,0:T(8,128)(2,1)S(1)} collective-permute-done((bf16[128,1024]{1,0:T(8,128)(2,1)S(1)}, bf16[128,1024]{1,0:T(8,128)(2,1)S(1)}, u32[]{:S(2)}, u32[]{:S(2)}) %collective-permute-start.20) | collective-permute-done | bytes 262176 | tf_op jit(solution)/shard_map/ppermute | solution.py:349
  56.9 0.9 collective-permute-done.17.refs_3_
  57.8 2.0 %shard_map.118 = (bf16[512,128]{1,0:T(8,128)(2,1)S(1)}, bf16[512,128]{1,0:T(8,128)(2,1)S(1)}, bf16[512,128]{1,0:T(8,128)(2,1)S(1)}, bf16[512,128]{1,0:T(8,128)(2,1)S(1)}) custom-call(s32[3]{0:T(128)S(1)} %pad_add_fusion.pos, bf16[128,2048]{1,0:T(8,128)(2,1)S(1)} %copy-done.2, bf16[128,2048]{1,0:T(8,128)(2,1)S(1)} %collective-permute-done.4.core, ...), custom_call_target="tpu_custom_call" | custom-call | flops 1073741824 | bytes 4718592 | tf_op jit(solution)/shard_map/pallas_call | solution.py:60
  59.9 2.0 %collective-permute-start.21 = (bf16[512,128]{1,0:T(8,128)(2,1)S(1)}, bf16[512,128]{1,0:T(8,128)(2,1)S(1)}, u32[]{:S(2)}, u32[]{:S(2)}) collective-permute-start(bf16[512,128]{1,0:T(8,128)(2,1)S(1)} %get-tuple-element.147), channel_id=1, source_target_pairs={{0,12},{1,13},{2,14},{3,15},{4,8},{5,9},{6,10},{7,11},{8,4},{9,5},... | collective-permute-start | bytes 393224 | tf_op jit(solution)/shard_map/ppermute | solution.py:349
  62.6 1.8 %collective-permute-start.23 = (bf16[512,128]{1,0:T(8,128)(2,1)S(1)}, bf16[512,128]{1,0:T(8,128)(2,1)S(1)}, u32[]{:S(2)}, u32[]{:S(2)}) collective-permute-start(bf16[512,128]{1,0:T(8,128)(2,1)S(1)} %get-tuple-element.149), channel_id=1, source_target_pairs={{0,4},{1,5},{2,6},{3,7},{4,0},{5,1},{6,2},{7,3},{8,12},{9,13},{10,... | collective-permute-start | bytes 393224 | tf_op jit(solution)/shard_map/ppermute | solution.py:349
  64.9 0.8 collective-permute-start.25
  65.7 1.6 %shard_map.120.refs_6_ = bf16[17,256,128]{2,1,0:T(8,128)(2,1)S(1)} custom-call(s32[3]{0:T(128)S(1)} %pad_add_fusion.pos, bf16[4,128,128]{2,1,0:T(8,128)(2,1)S(1)} %get-tuple-element.151.refs_0_, bf16[8,128,128]{2,1,0:T(8,128)(2,1)S(1)} %collective-permute-done.15.refs_1_.refs_4_, bf16[4,128,128]{2,1,0:T(8,128)(2,1)S(1)} %collective-permute-done.16.refs_2_, ...), custom_call_target="tpu_custom_call" | custom-call | flops 536870912 | bytes 4259840 | tf_op jit(solution)/shard_map/pallas_call | solution.py:60
  67.3 0.9 collective-permute-done.21.refs_3_
  68.2 7.0 %collective-permute-done.22.refs_2_ = bf16[512,128]{1,0:T(8,128)(2,1)S(1)} collective-permute-done((bf16[512,128]{1,0:T(8,128)(2,1)S(1)}, bf16[512,128]{1,0:T(8,128)(2,1)S(1)}, u32[]{:S(2)}, u32[]{:S(2)}) %collective-permute-start.22) | collective-permute-done | bytes 131104 | tf_op jit(solution)/shard_map/ppermute | solution.py:349
  75.3 3.0 %shard_map.121 = (bf16[256,128]{1,0:T(8,128)(2,1)S(1)}, bf16[256,128]{1,0:T(8,128)(2,1)S(1)}, bf16[256,128]{1,0:T(8,128)(2,1)S(1)}, bf16[256,128]{1,0:T(8,128)(2...) custom-call(s32[3]{0:T(128)S(1)} %pad_add_fusion.pos, ...), custom_call_target="tpu_custom_call" | custom-call | flops 4294967296 | bytes 7176192 | tf_op jit(solution)/shard_map/pallas_call | solution.py:60
  78.4 2.2 %collective-permute-start.26 = (bf16[256,128]{1,0:T(8,128)(2,1)S(1)}, bf16[256,128]{1,0:T(8,128)(2,1)S(1)}, u32[]{:S(2)}, u32[]{:S(2)}) collective-permute-start(bf16[256,128]{1,0:T(8,128)(2,1)S(1)} %get-tuple-element.170), channel_id=1, source_target_pairs={{0,12},{1,13},{2,14},{3,15},{4,8},{5,9},{6,10},{7,11},{8,4},{9,5},... | collective-permute-start | bytes 196616 | tf_op jit(solution)/shard_map/ppermute | solution.py:349
  80.5 2.3 %collective-permute-start.28 = (bf16[256,128]{1,0:T(8,128)(2,1)S(1)}, bf16[256,128]{1,0:T(8,128)(2,1)S(1)}, u32[]{:S(2)}, u32[]{:S(2)}) collective-permute-start(bf16[256,128]{1,0:T(8,128)(2,1)S(1)} %get-tuple-element.172), channel_id=1, source_target_pairs={{0,4},{1,5},{2,6},{3,7},{4,0},{5,1},{6,2},{7,3},{8,12},{9,13},{10,... | collective-permute-start | bytes 196616 | tf_op jit(solution)/shard_map/ppermute | solution.py:349
  82.8 0.7 shard_map.122.refs_5_
  83.5 1.7 %collective-permute-done.26.refs_3_ = bf16[256,128]{1,0:T(8,128)(2,1)S(1)} collective-permute-done((bf16[256,128]{1,0:T(8,128)(2,1)S(1)}, bf16[256,128]{1,0:T(8,128)(2,1)S(1)}, u32[]{:S(2)}, u32[]{:S(2)}) %collective-permute-start.26) | collective-permute-done | bytes 65568 | tf_op jit(solution)/shard_map/ppermute | solution.py:349
  85.2 2.3 %collective-permute-done.27.refs_2_ = bf16[256,128]{1,0:T(8,128)(2,1)S(1)} collective-permute-done((bf16[256,128]{1,0:T(8,128)(2,1)S(1)}, bf16[256,128]{1,0:T(8,128)(2,1)S(1)}, u32[]{:S(2)}, u32[]{:S(2)}) %collective-permute-start.27) | collective-permute-done | bytes 65568 | tf_op jit(solution)/shard_map/ppermute | solution.py:349
  87.5 1.0 shard_map.124
  88.6 1.0 shard_map.123
  89.6 0.9 collective-permute-done.30
  90.6 1.1 %collective-permute-start.38 = (bf16[128,2048]{1,0:T(8,128)(2,1)S(1)}, bf16[128,2048]{1,0:T(8,128)(2,1)S(1)}, u32[]{:S(2)}, u32[]{:S(2)}) collective-permute-start(bf16[128,2048]{1,0:T(8,128)(2,1)S(1)} %add_convert_fusion.1), channel_id=1, source_target_pairs={{0,2},{1,3},{2,0},{3,1},{4,6},{5,7},{6,4},{7,5},{8,10},{9,11},{10,... | collective-permute-start | bytes 1572872 | tf_op jit(solution)/shard_map/ppermute | solution.py:346
  91.9 2.3 %collective-permute-start.32 = (bf16[256,128]{1,0:T(8,128)(2,1)S(1)}, bf16[256,128]{1,0:T(8,128)(2,1)S(1)}, u32[]{:S(2)}, u32[]{:S(2)}) collective-permute-start(bf16[256,128]{1,0:T(8,128)(2,1)S(1)} %get-tuple-element.193), channel_id=1, source_target_pairs={{0,8},{1,9},{2,10},{3,11},{4,12},{5,13},{6,14},{7,15},{8,0},{9,1},... | collective-permute-start | bytes 196616 | tf_op jit(solution)/shard_map/ppermute | solution.py:349
  94.3 1.8 %collective-permute-start.33 = (bf16[256,128]{1,0:T(8,128)(2,1)S(1)}, bf16[256,128]{1,0:T(8,128)(2,1)S(1)}, u32[]{:S(2)}, u32[]{:S(2)}) collective-permute-start(bf16[256,128]{1,0:T(8,128)(2,1)S(1)} %get-tuple-element.194), channel_id=1, source_target_pairs={{0,12},{1,13},{2,14},{3,15},{4,8},{5,9},{6,10},{7,11},{8,4},{9,5},... | collective-permute-start | bytes 196616 | tf_op jit(solution)/shard_map/ppermute | solution.py:349
  96.4 2.9 %collective-permute-done.32.refs_2_ = bf16[256,128]{1,0:T(8,128)(2,1)S(1)} collective-permute-done((bf16[256,128]{1,0:T(8,128)(2,1)S(1)}, bf16[256,128]{1,0:T(8,128)(2,1)S(1)}, u32[]{:S(2)}, u32[]{:S(2)}) %collective-permute-start.32) | collective-permute-done | bytes 65568 | tf_op jit(solution)/shard_map/ppermute | solution.py:349
  99.4 1.1 collective-permute-done.33.refs_3_
  100.4 1.0 shard_map.126
  102.5 1.0 shard_map.125
  103.6 1.1 collective-permute-done.38
  104.6 1.0 add_convert_fusion
  (70 shorter events, 9.9 us)
Async XLA Ops:
  0.0 16.2 %copy-start.2 = (bf16[128,2048]{1,0:T(8,128)(2,1)S(1)}, bf16[128,2048]{1,0:T(8,128)(2,1)}, u32[]{:S(2)}) copy-start(bf16[128,2048]{1,0:T(8,128)(2,1)} %x.1) | copy-start | bytes 1572868
  0.0 11.9 %copy-start.3 = (bf16[128,2048]{1,0:T(8,128)(2,1)S(1)}, bf16[128,2048]{1,0:T(8,128)(2,1)}, u32[]{:S(2)}) copy-start(bf16[128,2048]{1,0:T(8,128)(2,1)} %gate.1) | copy-start | bytes 1572868
  0.0 16.2 %collective-permute-start.4 = (bf16[128,2048]{1,0:T(8,128)(2,1)}, bf16[128,2048]{1,0:T(8,128)(2,1)S(1)}, u32[]{:S(2)}, u32[]{:S(2)}) collective-permute-start(bf16[128,2048]{1,0:T(8,128)(2,1)} %x.1), channel_id=1, source_target_pairs={{0,1},{1,0},{2,3},{3,2},{4,5},{5,4},{6,7},{7,6},{8,9},{9,8},{10,11... | collective-permute-start | bytes 1572872 | tf_op jit(solution)/shard_map/ppermute | solution.py:346
  2.4 13.8 %collective-permute-start.5 = (bf16[160,1024]{1,0:T(8,128)(2,1)S(1)}, bf16[160,1024]{1,0:T(8,128)(2,1)S(1)}, u32[]{:S(2)}, u32[]{:S(2)}) collective-permute-start(bf16[160,1024]{1,0:T(8,128)(2,1)S(1)} %get-tuple-element.108), channel_id=1, source_target_pairs={{0,4},{1,5},{2,6},{3,7},{4,0},{5,1},{6,2},{7,3},{8,12},{9,13},{10,... | collective-permute-start | bytes 983048 | tf_op jit(solution)/shard_map/ppermute | solution.py:349
  6.9 1.9 %collective-permute-start = (bf16[128,512]{1,0:T(8,128)(2,1)S(1)}, bf16[128,512]{1,0:T(8,128)(2,1)S(1)}, u32[]{:S(2)}, u32[]{:S(2)}) collective-permute-start(bf16[128,512]{1,0:T(8,128)(2,1)S(1)} %get-tuple-element.104), channel_id=1, source_target_pairs={{0,1},{1,0},{2,3},{3,2},{4,5},{5,4},{6,7},{7,6},{8,9},{9,8},{10,11... | collective-permute-start | bytes 393224 | tf_op jit(solution)/shard_map/ppermute | solution.py:346
  7.1 6.3 %collective-permute-start.1 = (bf16[128,512]{1,0:T(8,128)(2,1)S(1)}, bf16[128,512]{1,0:T(8,128)(2,1)S(1)}, u32[]{:S(2)}, u32[]{:S(2)}) collective-permute-start(bf16[128,512]{1,0:T(8,128)(2,1)S(1)} %get-tuple-element.105), channel_id=1, source_target_pairs={{0,2},{1,3},{2,0},{3,1},{4,6},{5,7},{6,4},{7,5},{8,10},{9,11},{10,... | collective-permute-start | bytes 393224 | tf_op jit(solution)/shard_map/ppermute | solution.py:346
  8.6 6.4 %collective-permute-start.2 = (bf16[128,512]{1,0:T(8,128)(2,1)S(1)}, bf16[128,512]{1,0:T(8,128)(2,1)S(1)}, u32[]{:S(2)}, u32[]{:S(2)}) collective-permute-start(bf16[128,512]{1,0:T(8,128)(2,1)S(1)} %get-tuple-element.106), channel_id=1, source_target_pairs={{0,3},{1,2},{2,1},{3,0},{4,7},{5,6},{6,5},{7,4},{8,11},{9,10},{10,... | collective-permute-start | bytes 393224 | tf_op jit(solution)/shard_map/ppermute | solution.py:346
  8.8 7.3 %collective-permute-start.3 = (bf16[128,512]{1,0:T(8,128)(2,1)S(1)}, bf16[128,512]{1,0:T(8,128)(2,1)S(1)}, u32[]{:S(2)}, u32[]{:S(2)}) collective-permute-start(bf16[128,512]{1,0:T(8,128)(2,1)S(1)} %get-tuple-element.107), channel_id=1, source_target_pairs={{0,8},{1,9},{2,10},{3,11},{4,12},{5,13},{6,14},{7,15},{8,0},{9,1},... | collective-permute-start | bytes 393224 | tf_op jit(solution)/shard_map/ppermute | solution.py:405
  16.2 14.1 %collective-permute-start.6 = (bf16[128,2048]{1,0:T(8,128)(2,1)S(1)}, bf16[128,2048]{1,0:T(8,128)(2,1)S(1)}, u32[]{:S(2)}, u32[]{:S(2)}) collective-permute-start(bf16[128,2048]{1,0:T(8,128)(2,1)S(1)} %copy-done.2), channel_id=1, source_target_pairs={{0,2},{1,3},{2,0},{3,1},{4,6},{5,7},{6,4},{7,5},{8,10},{9,11},{10,... | collective-permute-start | bytes 1572872 | tf_op jit(solution)/shard_map/ppermute | solution.py:346
  17.9 17.1 %collective-permute-start.7 = (bf16[256,512]{1,0:T(8,128)(2,1)S(1)}, bf16[256,512]{1,0:T(8,128)(2,1)S(1)}, u32[]{:S(2)}, u32[]{:S(2)}) collective-permute-start(bf16[256,512]{1,0:T(8,128)(2,1)S(1)} %shard_map.112), channel_id=1, source_target_pairs={{0,4},{1,5},{2,6},{3,7},{4,0},{5,1},{6,2},{7,3},{8,12},{9,13},{10,... | collective-permute-start | bytes 786440 | tf_op jit(solution)/shard_map/ppermute | solution.py:349
  20.6 14.4 %collective-permute-start.8 = (bf16[256,512]{1,0:T(8,128)(2,1)S(1)}, bf16[256,512]{1,0:T(8,128)(2,1)S(1)}, u32[]{:S(2)}, u32[]{:S(2)}) collective-permute-start(bf16[256,512]{1,0:T(8,128)(2,1)S(1)} %shard_map.112), channel_id=1, source_target_pairs={{0,8},{1,9},{2,10},{3,11},{4,12},{5,13},{6,14},{7,15},{8,0},{9,1},... | collective-permute-start | bytes 786440 | tf_op jit(solution)/shard_map/ppermute | solution.py:349
  23.6 11.4 %collective-permute-start.10 = (bf16[128,1024]{1,0:T(8,128)(2,1)S(1)}, bf16[128,1024]{1,0:T(8,128)(2,1)S(1)}, u32[]{:S(2)}, u32[]{:S(2)}) collective-permute-start(bf16[128,1024]{1,0:T(8,128)(2,1)S(1)} %get-tuple-element.119.refs_0_), channel_id=1, source_target_pairs={{0,16},{16,0},{1,17},{17,1},{2,18},{18,2},{3,19},{19,3},{4,20},{20... | collective-permute-start | bytes 786440 | tf_op jit(solution)/shard_map/ppermute | solution.py:352
  24.2 10.7 %collective-permute-start.9 = (bf16[192,512]{1,0:T(8,128)(2,1)S(1)}, bf16[192,512]{1,0:T(8,128)(2,1)S(1)}, u32[]{:S(2)}, u32[]{:S(2)}) collective-permute-start(bf16[192,512]{1,0:T(8,128)(2,1)S(1)} %get-tuple-element.117.mine), channel_id=1, source_target_pairs={{0,16},{16,0},{1,17},{17,1},{2,18},{18,2},{3,19},{19,3},{4,20},{20... | collective-permute-start | bytes 589832 | tf_op jit(solution)/shard_map/ppermute | solution.py:352
  30.3 18.9 %collective-permute-start.14 = (bf16[128,2048]{1,0:T(8,128)(2,1)S(1)}, bf16[128,2048]{1,0:T(8,128)(2,1)S(1)}, u32[]{:S(2)}, u32[]{:S(2)}) collective-permute-start(bf16[128,2048]{1,0:T(8,128)(2,1)S(1)} %collective-permute-done.6.from_x), channel_id=1, source_target_pairs={{0,1},{1,0},{2,3},{3,2},{4,5},{5,4},{6,7},{7,6},{8,9},{9,8},{10,11... | collective-permute-start | bytes 1572872 | tf_op jit(solution)/shard_map/ppermute | solution.py:346
  35.0 9.0 %collective-permute-start.11 = (bf16[256,512]{1,0:T(8,128)(2,1)S(1)}, bf16[256,512]{1,0:T(8,128)(2,1)S(1)}, u32[]{:S(2)}, u32[]{:S(2)}) collective-permute-start(bf16[256,512]{1,0:T(8,128)(2,1)S(1)} %collective-permute-done.7.refs_0_), channel_id=1, source_target_pairs={{0,16},{16,0},{1,17},{17,1},{2,18},{18,2},{3,19},{19,3},{4,20},{20... | collective-permute-start | bytes 786440 | tf_op jit(solution)/shard_map/ppermute | solution.py:352
  35.4 13.2 %collective-permute-start.19 = (bf16[128,1024]{1,0:T(8,128)(2,1)S(1)}, bf16[128,1024]{1,0:T(8,128)(2,1)S(1)}, u32[]{:S(2)}, u32[]{:S(2)}) collective-permute-start(bf16[128,1024]{1,0:T(8,128)(2,1)S(1)} %get-tuple-element.145), channel_id=1, source_target_pairs={{0,8},{1,9},{2,10},{3,11},{4,12},{5,13},{6,14},{7,15},{8,0},{9,1},... | collective-permute-start | bytes 786440 | tf_op jit(solution)/shard_map/ppermute | solution.py:349
  36.7 11.9 %collective-permute-start.12 = (bf16[256,512]{1,0:T(8,128)(2,1)S(1)}, bf16[256,512]{1,0:T(8,128)(2,1)S(1)}, u32[]{:S(2)}, u32[]{:S(2)}) collective-permute-start(bf16[256,512]{1,0:T(8,128)(2,1)S(1)} %collective-permute-done.8.refs_1_), channel_id=1, source_target_pairs={{0,16},{16,0},{1,17},{17,1},{2,18},{18,2},{3,19},{19,3},{4,20},{20... | collective-permute-start | bytes 786440 | tf_op jit(solution)/shard_map/ppermute | solution.py:352
  37.5 11.7 %collective-permute-start.13 = (bf16[256,512]{1,0:T(8,128)(2,1)S(1)}, bf16[256,512]{1,0:T(8,128)(2,1)S(1)}, u32[]{:S(2)}, u32[]{:S(2)}) collective-permute-start(bf16[256,512]{1,0:T(8,128)(2,1)S(1)} %collective-permute-done.8.refs_1_), channel_id=1, source_target_pairs={{0,4},{1,5},{2,6},{3,7},{4,0},{5,1},{6,2},{7,3},{8,12},{9,13},{10,... | collective-permute-start | bytes 786440 | tf_op jit(solution)/shard_map/ppermute | solution.py:349
  44.0 13.8 %collective-permute-start.15 = (bf16[8,128,128]{2,1,0:T(8,128)(2,1)S(1)}, bf16[8,128,128]{2,1,0:T(8,128)(2,1)S(1)}, u32[]{:S(2)}, u32[]{:S(2)}) collective-permute-start(bf16[8,128,128]{2,1,0:T(8,128)(2,1)S(1)} %get-tuple-element.129), channel_id=1, source_target_pairs={{0,1},{1,0},{2,3},{3,2},{4,5},{5,4},{6,7},{7,6},{8,9},{9,8},{10,11... | collective-permute-start | bytes 786440 | tf_op jit(solution)/shard_map/ppermute | solution.py:346
  48.6 7.7 %collective-permute-start.20 = (bf16[128,1024]{1,0:T(8,128)(2,1)S(1)}, bf16[128,1024]{1,0:T(8,128)(2,1)S(1)}, u32[]{:S(2)}, u32[]{:S(2)}) collective-permute-start(bf16[128,1024]{1,0:T(8,128)(2,1)S(1)} %collective-permute-done.19.refs_0_), channel_id=1, source_target_pairs={{0,4},{1,5},{2,6},{3,7},{4,0},{5,1},{6,2},{7,3},{8,12},{9,13},{10,... | collective-permute-start | bytes 786440 | tf_op jit(solution)/shard_map/ppermute | solution.py:349
  49.2 8.6 %collective-permute-start.18 = (bf16[256,512]{1,0:T(8,128)(2,1)S(1)}, bf16[256,512]{1,0:T(8,128)(2,1)S(1)}, u32[]{:S(2)}, u32[]{:S(2)}) collective-permute-start(bf16[256,512]{1,0:T(8,128)(2,1)S(1)} %collective-permute-done.13.refs_2_), channel_id=1, source_target_pairs={{0,16},{16,0},{1,17},{17,1},{2,18},{18,2},{3,19},{19,3},{4,20},{20... | collective-permute-start | bytes 786440 | tf_op jit(solution)/shard_map/ppermute | solution.py:352
  50.6 6.3 %collective-permute-start.16 = (bf16[4,128,128]{2,1,0:T(8,128)(2,1)S(1)}, bf16[4,128,128]{2,1,0:T(8,128)(2,1)S(1)}, u32[]{:S(2)}, u32[]{:S(2)}) collective-permute-start(bf16[4,128,128]{2,1,0:T(8,128)(2,1)S(1)} %get-tuple-element.130), channel_id=1, source_target_pairs={{0,2},{1,3},{2,0},{3,1},{4,6},{5,7},{6,4},{7,5},{8,10},{9,11},{10,... | collective-permute-start | bytes 393224 | tf_op jit(solution)/shard_map/ppermute | solution.py:346
  52.0 5.8 %collective-permute-start.17 = (bf16[4,128,128]{2,1,0:T(8,128)(2,1)S(1)}, bf16[4,128,128]{2,1,0:T(8,128)(2,1)S(1)}, u32[]{:S(2)}, u32[]{:S(2)}) collective-permute-start(bf16[4,128,128]{2,1,0:T(8,128)(2,1)S(1)} %get-tuple-element.131), channel_id=1, source_target_pairs={{0,3},{1,2},{2,1},{3,0},{4,7},{5,6},{6,5},{7,4},{8,11},{9,10},{10,... | collective-permute-start | bytes 393224 | tf_op jit(solution)/shard_map/ppermute | solution.py:346
  56.9 8.9 %copy-start = (bf16[17,256,256]{2,1,0:T(8,128)(2,1)S(1)}, bf16[17,256,256]{2,1,0:T(8,128)(2,1)}, u32[]{:S(2)}) copy-start(bf16[17,256,256]{2,1,0:T(8,128)(2,1)} %constant.45.clone.refs_5_.refs_9_) | copy-start | bytes 6684676
  56.9 8.9 %copy-start.4 = (bf16[512,256]{1,0:T(8,128)(2,1)S(1)}, bf16[512,256]{1,0:T(8,128)(2,1)}, u32[]{:S(2)}) copy-start(bf16[512,256]{1,0:T(8,128)(2,1)} %constant.43.clone.refs_4_.refs_7_) | copy-start | bytes 786436
  59.9 15.4 %copy-start.5 = (f32[3,2048]{1,0:T(4,128)S(1)}, f32[3,2048]{1,0:T(4,128)}, u32[]{:S(2)}) copy-start(f32[3,2048]{1,0:T(4,128)} %refs_4_.2) | copy-start | bytes 73732
  59.9 15.3 %copy-start.6 = (f32[2048]{0:T(1024)S(1)}, f32[2048]{0:T(1024)}, u32[]{:S(2)}) copy-start(f32[2048]{0:T(1024)} %param.16) | copy-start | bytes 24580
  59.9 15.3 %copy-start.7 = (bf16[17,256,256]{2,1,0:T(8,128)(2,1)S(1)}, bf16[17,256,256]{2,1,0:T(8,128)(2,1)}, u32[]{:S(2)}) copy-start(bf16[17,256,256]{2,1,0:T(8,128)(2,1)} %constant.46.clone.refs_10_) | copy-start | bytes 6684676
  59.9 15.3 %copy-start.8 = (bf16[256,512]{1,0:T(8,128)(2,1)S(1)}, bf16[256,512]{1,0:T(8,128)(2,1)}, u32[]{:S(2)}) copy-start(bf16[256,512]{1,0:T(8,128)(2,1)} %constant.44.clone.refs_8_) | copy-start | bytes 786436
  59.9 8.3 %collective-permute-start.21 = (bf16[512,128]{1,0:T(8,128)(2,1)S(1)}, bf16[512,128]{1,0:T(8,128)(2,1)S(1)}, u32[]{:S(2)}, u32[]{:S(2)}) collective-permute-start(bf16[512,128]{1,0:T(8,128)(2,1)S(1)} %get-tuple-element.147), channel_id=1, source_target_pairs={{0,12},{1,13},{2,14},{3,15},{4,8},{5,9},{6,10},{7,11},{8,4},{9,5},... | collective-permute-start | bytes 393224 | tf_op jit(solution)/shard_map/ppermute | solution.py:349
  61.9 13.3 %collective-permute-start.22 = (bf16[512,128]{1,0:T(8,128)(2,1)S(1)}, bf16[512,128]{1,0:T(8,128)(2,1)S(1)}, u32[]{:S(2)}, u32[]{:S(2)}) collective-permute-start(bf16[512,128]{1,0:T(8,128)(2,1)S(1)} %get-tuple-element.148), channel_id=1, source_target_pairs={{0,8},{1,9},{2,10},{3,11},{4,12},{5,13},{6,14},{7,15},{8,0},{9,1},... | collective-permute-start | bytes 393224 | tf_op jit(solution)/shard_map/ppermute | solution.py:349
  62.6 12.7 %collective-permute-start.23 = (bf16[512,128]{1,0:T(8,128)(2,1)S(1)}, bf16[512,128]{1,0:T(8,128)(2,1)S(1)}, u32[]{:S(2)}, u32[]{:S(2)}) collective-permute-start(bf16[512,128]{1,0:T(8,128)(2,1)S(1)} %get-tuple-element.149), channel_id=1, source_target_pairs={{0,4},{1,5},{2,6},{3,7},{4,0},{5,1},{6,2},{7,3},{8,12},{9,13},{10,... | collective-permute-start | bytes 393224 | tf_op jit(solution)/shard_map/ppermute | solution.py:349
  64.4 13.9 %collective-permute-start.24 = (bf16[256,1024]{1,0:T(8,128)(2,1)S(1)}, bf16[256,1024]{1,0:T(8,128)(2,1)S(1)}, u32[]{:S(2)}, u32[]{:S(2)}) collective-permute-start(bf16[256,1024]{1,0:T(8,128)(2,1)S(1)} %shard_map.119.refs_1_), channel_id=1, source_target_pairs={{0,16},{16,0},{1,17},{17,1},{2,18},{18,2},{3,19},{19,3},{4,20},{20... | collective-permute-start | bytes 1572872 | tf_op jit(solution)/shard_map/ppermute | solution.py:352
  64.9 13.4 %collective-permute-start.25 = (bf16[256,512]{1,0:T(8,128)(2,1)S(1)}, bf16[256,512]{1,0:T(8,128)(2,1)S(1)}, u32[]{:S(2)}, u32[]{:S(2)}) collective-permute-start(bf16[256,512]{1,0:T(8,128)(2,1)S(1)} %get-tuple-element.169), channel_id=1, source_target_pairs={{0,2},{1,3},{2,0},{3,1},{4,6},{5,7},{6,4},{7,5},{8,10},{9,11},{10,... | collective-permute-start | bytes 786440 | tf_op jit(solution)/shard_map/ppermute | solution.py:346
  75.2 7.6 %copy-start.1 = (bf16[128,2048]{1,0:T(8,128)(2,1)S(1)}, bf16[128,2048]{1,0:T(8,128)(2,1)}, u32[]{:S(2)}) copy-start(bf16[128,2048]{1,0:T(8,128)(2,1)} %own.1) | copy-start | bytes 1572868
  78.3 9.2 %collective-permute-start.29 = (bf16[128,512]{1,0:T(8,128)(2,1)S(1)}, bf16[128,512]{1,0:T(8,128)(2,1)S(1)}, u32[]{:S(2)}, u32[]{:S(2)}) collective-permute-start(bf16[128,512]{1,0:T(8,128)(2,1)S(1)} %slice.3), channel_id=1, source_target_pairs={{0,1},{1,0},{2,3},{3,2},{4,5},{5,4},{6,7},{7,6},{8,9},{9,8},{10,11... | collective-permute-start | bytes 393224 | tf_op jit(solution)/shard_map/ppermute | solution.py:346
  78.4 6.9 %collective-permute-start.26 = (bf16[256,128]{1,0:T(8,128)(2,1)S(1)}, bf16[256,128]{1,0:T(8,128)(2,1)S(1)}, u32[]{:S(2)}, u32[]{:S(2)}) collective-permute-start(bf16[256,128]{1,0:T(8,128)(2,1)S(1)} %get-tuple-element.170), channel_id=1, source_target_pairs={{0,12},{1,13},{2,14},{3,15},{4,8},{5,9},{6,10},{7,11},{8,4},{9,5},... | collective-permute-start | bytes 196616 | tf_op jit(solution)/shard_map/ppermute | solution.py:349
  80.5 7.0 %collective-permute-start.27 = (bf16[256,128]{1,0:T(8,128)(2,1)S(1)}, bf16[256,128]{1,0:T(8,128)(2,1)S(1)}, u32[]{:S(2)}, u32[]{:S(2)}) collective-permute-start(bf16[256,128]{1,0:T(8,128)(2,1)S(1)} %get-tuple-element.171), channel_id=1, source_target_pairs={{0,8},{1,9},{2,10},{3,11},{4,12},{5,13},{6,14},{7,15},{8,0},{9,1},... | collective-permute-start | bytes 196616 | tf_op jit(solution)/shard_map/ppermute | solution.py:349
  80.5 7.0 %collective-permute-start.28 = (bf16[256,128]{1,0:T(8,128)(2,1)S(1)}, bf16[256,128]{1,0:T(8,128)(2,1)S(1)}, u32[]{:S(2)}, u32[]{:S(2)}) collective-permute-start(bf16[256,128]{1,0:T(8,128)(2,1)S(1)} %get-tuple-element.172), channel_id=1, source_target_pairs={{0,4},{1,5},{2,6},{3,7},{4,0},{5,1},{6,2},{7,3},{8,12},{9,13},{10,... | collective-permute-start | bytes 196616 | tf_op jit(solution)/shard_map/ppermute | solution.py:349
  88.5 2.0 %collective-permute-start.30 = (bf16[128,2048]{1,0:T(8,128)(2,1)S(1)}, bf16[128,2048]{1,0:T(8,128)(2,1)S(1)}, u32[]{:S(2)}, u32[]{:S(2)}) collective-permute-start(bf16[128,2048]{1,0:T(8,128)(2,1)S(1)} %shard_map.124), channel_id=1, source_target_pairs={{0,1},{1,0},{2,3},{3,2},{4,5},{5,4},{6,7},{7,6},{8,9},{9,8},{10,11... | collective-permute-start | bytes 1572872 | tf_op jit(solution)/shard_map/ppermute | solution.py:346
  90.6 14.0 %collective-permute-start.38 = (bf16[128,2048]{1,0:T(8,128)(2,1)S(1)}, bf16[128,2048]{1,0:T(8,128)(2,1)S(1)}, u32[]{:S(2)}, u32[]{:S(2)}) collective-permute-start(bf16[128,2048]{1,0:T(8,128)(2,1)S(1)} %add_convert_fusion.1), channel_id=1, source_target_pairs={{0,2},{1,3},{2,0},{3,1},{4,6},{5,7},{6,4},{7,5},{8,10},{9,11},{10,... | collective-permute-start | bytes 1572872 | tf_op jit(solution)/shard_map/ppermute | solution.py:346
  91.7 4.8 %collective-permute-start.31 = (bf16[256,128]{1,0:T(8,128)(2,1)S(1)}, bf16[256,128]{1,0:T(8,128)(2,1)S(1)}, u32[]{:S(2)}, u32[]{:S(2)}) collective-permute-start(bf16[256,128]{1,0:T(8,128)(2,1)S(1)} %get-tuple-element.192), channel_id=1, source_target_pairs={{0,4},{1,5},{2,6},{3,7},{4,0},{5,1},{6,2},{7,3},{8,12},{9,13},{10,... | collective-permute-start | bytes 196616 | tf_op jit(solution)/shard_map/ppermute | solution.py:349
  91.9 7.5 %collective-permute-start.32 = (bf16[256,128]{1,0:T(8,128)(2,1)S(1)}, bf16[256,128]{1,0:T(8,128)(2,1)S(1)}, u32[]{:S(2)}, u32[]{:S(2)}) collective-permute-start(bf16[256,128]{1,0:T(8,128)(2,1)S(1)} %get-tuple-element.193), channel_id=1, source_target_pairs={{0,8},{1,9},{2,10},{3,11},{4,12},{5,13},{6,14},{7,15},{8,0},{9,1},... | collective-permute-start | bytes 196616 | tf_op jit(solution)/shard_map/ppermute | solution.py:349
  94.3 6.2 %collective-permute-start.33 = (bf16[256,128]{1,0:T(8,128)(2,1)S(1)}, bf16[256,128]{1,0:T(8,128)(2,1)S(1)}, u32[]{:S(2)}, u32[]{:S(2)}) collective-permute-start(bf16[256,128]{1,0:T(8,128)(2,1)S(1)} %get-tuple-element.194), channel_id=1, source_target_pairs={{0,12},{1,13},{2,14},{3,15},{4,8},{5,9},{6,10},{7,11},{8,4},{9,5},... | collective-permute-start | bytes 196616 | tf_op jit(solution)/shard_map/ppermute | solution.py:349
  101.4 2.1 %collective-permute-start.37 = (bf16[128,512]{1,0:T(8,128)(2,1)S(1)}, bf16[128,512]{1,0:T(8,128)(2,1)S(1)}, u32[]{:S(2)}, u32[]{:S(2)}) collective-permute-start(bf16[128,512]{1,0:T(8,128)(2,1)S(1)} %get-tuple-element.199), channel_id=1, source_target_pairs={{0,1},{1,0},{2,3},{3,2},{4,5},{5,4},{6,7},{7,6},{8,9},{9,8},{10,11... | collective-permute-start | bytes 393224 | tf_op jit(solution)/shard_map/ppermute | solution.py:346
  101.5 2.0 %collective-permute-start.36 = (bf16[128,512]{1,0:T(8,128)(2,1)S(1)}, bf16[128,512]{1,0:T(8,128)(2,1)S(1)}, u32[]{:S(2)}, u32[]{:S(2)}) collective-permute-start(bf16[128,512]{1,0:T(8,128)(2,1)S(1)} %get-tuple-element.198), channel_id=1, source_target_pairs={{0,1},{1,0},{2,3},{3,2},{4,5},{5,4},{6,7},{7,6},{8,9},{9,8},{10,11... | collective-permute-start | bytes 393224 | tf_op jit(solution)/shard_map/ppermute | solution.py:346
  102.0 1.5 %collective-permute-start.35 = (bf16[128,512]{1,0:T(8,128)(2,1)S(1)}, bf16[128,512]{1,0:T(8,128)(2,1)S(1)}, u32[]{:S(2)}, u32[]{:S(2)}) collective-permute-start(bf16[128,512]{1,0:T(8,128)(2,1)S(1)} %get-tuple-element.197), channel_id=1, source_target_pairs={{0,1},{1,0},{2,3},{3,2},{4,5},{5,4},{6,7},{7,6},{8,9},{9,8},{10,11... | collective-permute-start | bytes 393224 | tf_op jit(solution)/shard_map/ppermute | solution.py:346
  102.1 1.5 %collective-permute-start.34 = (bf16[128,512]{1,0:T(8,128)(2,1)S(1)}, bf16[128,512]{1,0:T(8,128)(2,1)S(1)}, u32[]{:S(2)}, u32[]{:S(2)}) collective-permute-start(bf16[128,512]{1,0:T(8,128)(2,1)S(1)} %get-tuple-element.196), channel_id=1, source_target_pairs={{0,1},{1,0},{2,3},{3,2},{4,5},{5,4},{6,7},{7,6},{8,9},{9,8},{10,11... | collective-permute-start | bytes 393224 | tf_op jit(solution)/shard_map/ppermute | solution.py:346
